TPU v7x, 32 devices: a whole 2x2x4 slice. The times are simulated.
32 devices in a mesh: fsdp: 4 (over x, core), ctx: 8 (over z, y).
Axes of the slice: x: 2, y: 2, z: 4, core: 2. Of those that a mesh axis runs over, the one named last changes fastest.
Arguments:
- frames: bfloat16 [4, 4096, 1536], P('fsdp', 'ctx'), may hold values from -120 to 120
- lengths: int32 [4], P('fsdp'), may hold values from 1024 to 4096, as said below
- ln_gain: float32 [1536], replicated, may hold values from 0.1 to 1.9
- w_in: bfloat16 [1536, 1536], P('fsdp'), may hold values from -0.15625 to 0.15625
- dw_kernel: float32 [31, 768], replicated, may hold values from -1 to 1
- bn_gain: float32 [768], replicated, may hold values from 0.1 to 1.9
- bn_shift: float32 [768], replicated, may hold values from -3 to 3
- w_out: bfloat16 [768, 1536], P('fsdp'), may hold values from -0.21875 to 0.21875
Outputs:
- result: bfloat16 [4, 4096, 1536], P('fsdp', 'ctx')
Inputs may be any that keep to these rules, and one draw needn't show every extreme that they name: frames 0 to lengths[r] - 1 of recording r are valid; one recording is full and one has exactly 1024 valid frames.
All inputs are finite; a program needn't handle non-finite values.
Results may differ from a plain program's by a relative error of at most 0.0076.
Values may be sent and summed in bfloat16 or wider, within the bound.
No kernel may reach another device: no remote copies, remote signals or barrier semaphores. Data moves between devices by JAX's collectives and lax.ppermute only.
A program may use at most 64 MiB of HBM per device.

v0:
```python
import functools

import jax
import jax.numpy as jnp
from jax import lax
from jax.experimental import pallas as pl
from jax.experimental.pallas import tpu as pltpu
from jax.sharding import PartitionSpec as P

HALO = 16
LANES = 128
MIB = 1024 * 1024
VMEM = pltpu.VMEM


def cost(flops):
    return pl.CostEstimate(flops=flops, bytes_accessed=0, transcendentals=0)


def params(mib):
    return pltpu.CompilerParams(vmem_limit_bytes=mib * MIB)


def swap(value, axis, bit):
    return lax.ppermute(value, axis, [(i, i ^ bit) for i in range(lax.axis_size(axis))])


def cut_kernel(parity_ref, shard_ref, rows_ref, *refs):
    first_ref, second_ref, third_ref, head_ref, tail_ref, sems = refs
    wide = first_ref.shape[1]
    channels = shard_ref.shape[1] // 2
    row_count = rows_ref.shape[0]
    copies = []

    def copy(source, target):
        copies.append(pltpu.make_async_copy(source, target, sems.at[len(copies)]))
        copies[-1].start()

    side = parity_ref[0] * channels
    for block, ref in enumerate((first_ref, second_ref)):
        copy(shard_ref.at[:, pl.ds(pl.multiple_of(side + block * wide, wide), wide)], ref)
    for i in range(2):
        at = i * channels + 2 * wide
        copy(shard_ref.at[:, at : at + wide], third_ref.at[:, i * wide : (i + 1) * wide])
    copy(rows_ref.at[0:HALO, :], head_ref)
    copy(rows_ref.at[row_count - HALO : row_count, :], tail_ref)
    for started in copies:
        started.wait()


def cut(parity, shard, rows, wide):
    depth, width = shard.shape
    shapes = [(depth, wide), (depth, wide), (depth, 2 * wide), (HALO, width), (HALO, width)]
    return pl.pallas_call(
        cut_kernel,
        out_shape=[jax.ShapeDtypeStruct(shape, jnp.bfloat16) for shape in shapes],
        in_specs=[
            pl.BlockSpec(memory_space=pltpu.SMEM),
            pl.BlockSpec(memory_space=pltpu.HBM),
            pl.BlockSpec(memory_space=pltpu.HBM),
        ],
        out_specs=[pl.BlockSpec(memory_space=VMEM)] * 5,
        scratch_shapes=[pltpu.SemaphoreType.DMA((6,))],
        compiler_params=params(56),
        cost_estimate=cost(10**8),
        name="cut",
    )(parity, shard, rows)


def normalize(values, gain):
    values = values.astype(jnp.float32)
    centre = jnp.mean(values, axis=-1, keepdims=True)
    deviate = values - centre
    spread = jnp.mean(deviate * deviate, axis=-1, keepdims=True)
    return (deviate * lax.rsqrt(spread + 1e-05) * gain).astype(jnp.bfloat16)


def norm_kernel(rows_ref, gain_ref, out_ref, held, sems):
    pieces = sems.shape[0]
    step = held.shape[0] // pieces
    parts = [slice(i * step, (i + 1) * step) for i in range(pieces)]
    copies = [
        pltpu.make_async_copy(rows_ref.at[here, :], held.at[here, :], sems.at[i])
        for i, here in enumerate(parts)
    ]
    for copy in copies:
        copy.start()
    for copy, here in zip(copies, parts):
        copy.wait()
        out_ref[here, :] = normalize(held[here, :], gain_ref[...])


def normalize_rows(rows, gain):
    row_count, width = rows.shape
    return pl.pallas_call(
        norm_kernel,
        out_shape=jax.ShapeDtypeStruct((row_count, width), jnp.bfloat16),
        in_specs=[pl.BlockSpec(memory_space=pltpu.HBM), pl.BlockSpec(memory_space=VMEM)],
        out_specs=pl.BlockSpec(memory_space=VMEM),
        scratch_shapes=[VMEM((row_count, width), jnp.bfloat16), pltpu.SemaphoreType.DMA((8,))],
        compiler_params=params(48),
        cost_estimate=cost(10**9),
        name="layer_norm",
    )(rows, gain)


def near_kernel(place_ref, before_ref, rows_ref, after_ref, gain_ref, *refs):
    *weight_refs, ext_ref, first_ref, second_ref, third_ref, weights = refs
    row_count = rows_ref.shape[0]
    gain = gain_ref[...]
    ext_ref[0:HALO, :] = normalize(before_ref[...], gain)
    ext_ref[HALO : HALO + row_count, :] = rows_ref[...]
    ext_ref[HALO + row_count :, :] = normalize(after_ref[...], gain)
    if not weight_refs:
        return
    own = place_ref[0]
    depth, width = weight_refs[0].shape
    for i, weight_ref in enumerate(weight_refs):
        at = pl.multiple_of(lax.bitwise_xor(own % 2, i) * depth, depth)
        weights[pl.ds(at, depth), :] = weight_ref[...]
    near = pl.ds(pl.multiple_of(own // 2 * (2 * depth), 2 * depth), 2 * depth)
    wide = first_ref.shape[1] // 2
    channels = width // 2
    for block, out_ref in enumerate((first_ref, second_ref, third_ref)):
        for i in range(2):
            columns = slice(i * channels + block * wide, i * channels + (block + 1) * wide)
            out_ref[:, i * wide : (i + 1) * wide] = jnp.dot(
                ext_ref[:, near], weights[:, columns], preferred_element_type=jnp.float32
            )


def near_product(place, before, rows, after, gain, shards):
    row_count, width = rows.shape
    ext_rows = row_count + 2 * HALO
    partial = jax.ShapeDtypeStruct((ext_rows, width // 3), jnp.float32)
    depth = 2 * shards[0].shape[0] if shards else 16
    return pl.pallas_call(
        near_kernel,
        out_shape=(jax.ShapeDtypeStruct((ext_rows, width), jnp.bfloat16), partial, partial, partial),
        in_specs=[pl.BlockSpec(memory_space=pltpu.SMEM)]
        + [pl.BlockSpec(memory_space=VMEM)] * (4 + len(shards)),
        out_specs=[pl.BlockSpec(memory_space=VMEM)] * 4,
        scratch_shapes=[VMEM((depth, width), jnp.bfloat16)],
        compiler_params=params(10),
        cost_estimate=cost(10**9),
        name="near",
    )(place, before, rows, after, gain, *shards)


def front_kernel(block, earlier, place_ref, normed_ref, *refs):
    refs, earlier_refs = refs[earlier:], refs[:earlier]
    *weight_refs, taps_ref, conv_ref, stats_ref, weights, gated = refs
    ext_rows = normed_ref.shape[0]
    row_count, wide = conv_ref.shape
    taps, channels = taps_ref.shape
    if len(weight_refs) > 1:
        near_ref, *far_refs = weight_refs
        own = place_ref[0]
        depth = far_refs[0].shape[0]
        halves = len(far_refs) // 2
        for i in range(2):
            at = pl.multiple_of(lax.bitwise_xor(own % 2, i) * depth, depth)
            if halves == 1:
                weights[pl.ds(at, depth), :] = far_refs[i][...]
                continue
            for j in range(2):
                column = pl.multiple_of(lax.bitwise_xor(place_ref[3], j) * wide, wide)
                weights[pl.ds(at, depth), pl.ds(column, wide)] = far_refs[2 * i + j][...]
        far = pl.ds(pl.multiple_of((1 - own // 2) * (2 * depth), 2 * depth), 2 * depth)
        normed = normed_ref[:, far]
        value = near_ref[:, 0:wide] + jnp.dot(normed, weights[:, 0:wide], preferred_element_type=jnp.float32)
        gate = near_ref[:, wide:] + jnp.dot(normed, weights[:, wide:], preferred_element_type=jnp.float32)
    else:
        columns = slice(block * wide, (block + 1) * wide)
        value = jnp.dot(normed_ref[...], weight_refs[0][:, columns], preferred_element_type=jnp.float32)
        columns = slice(channels + block * wide, channels + (block + 1) * wide)
        gate = jnp.dot(normed_ref[...], weight_refs[0][:, columns], preferred_element_type=jnp.float32)
    start, length = place_ref[1], place_ref[2]
    position = start - HALO + lax.broadcasted_iota(jnp.int32, (ext_rows, 1), 0)
    valid = (position >= 0) & (position < length)
    kept = jnp.where(valid, value * jax.nn.sigmoid(gate), 0.0)
    kept = kept.astype(jnp.bfloat16).astype(jnp.float32)
    units = wide // LANES
    for unit in range(units):
        gated[unit] = kept[:, unit * LANES : (unit + 1) * LANES]
    first = HALO - (taps - 1) // 2
    step = 64
    for unit in range(units):
        lanes = slice(unit * LANES, (unit + 1) * LANES)
        tap_lanes = slice(block * wide + unit * LANES, block * wide + (unit + 1) * LANES)
        for at in range(0, row_count, step):
            acc = jnp.zeros((step, LANES), jnp.float32)
            for phase in range(8):
                offsets = [k for k in range(phase, first + taps, 8) if k >= first]
                extent = step + 8 if phase else step
                part = None
                for offset in offsets:
                    base = at + offset - phase
                    tap = offset - first
                    term = gated[unit, base : base + extent, :] * taps_ref[tap : tap + 1, tap_lanes]
                    part = term if part is None else part + term
                if phase:
                    part = pltpu.roll(part, extent - phase, 0)[:step]
                acc = acc + part
            conv_ref[at : at + step, lanes] = acc
    here = start + lax.broadcasted_iota(jnp.int32, (row_count, 1), 0) < length
    count = jnp.clip(length - start, 0, row_count).astype(jnp.float32)
    conv = conv_ref[...]
    mean = jnp.sum(jnp.where(here, conv, 0.0), axis=0, keepdims=True) / jnp.maximum(count, 1.0)
    deviate = jnp.where(here, conv - mean, 0.0)
    square = jnp.sum(deviate * deviate, axis=0, keepdims=True)
    stats = [mean, square, jnp.full((1, wide), count)]
    if not earlier_refs:
        for i, row in enumerate(stats):
            stats_ref[i : i + 1, :] = row
        return
    for copy in range(stats_ref.shape[0]):
        for i, row in enumerate(stats):
            parts = [ref[i : i + 1, :] for ref in earlier_refs] + [row]
            stats_ref[copy, i : i + 1, :] = jnp.concatenate(parts, axis=1)


def front_block(block, wide, place, normed, weights, dw_kernel, earlier=(), copies=1):
    ext_rows, width = normed.shape
    row_count = ext_rows - 2 * HALO
    depth = 2 * weights[1].shape[0] if len(weights) > 1 else 16
    stats_shape = (copies, 3, dw_kernel.shape[1]) if earlier else (3, wide)
    return pl.pallas_call(
        functools.partial(front_kernel, block, len(earlier)),
        out_shape=(
            jax.ShapeDtypeStruct((row_count, wide), jnp.float32),
            jax.ShapeDtypeStruct(stats_shape, jnp.float32),
        ),
        in_specs=[pl.BlockSpec(memory_space=pltpu.SMEM)]
        + [pl.BlockSpec(memory_space=VMEM)] * (2 + len(weights) + len(earlier)),
        out_specs=[pl.BlockSpec(memory_space=VMEM)] * 2,
        scratch_shapes=[
            VMEM((depth, 2 * wide), jnp.bfloat16),
            VMEM((wide // LANES, ext_rows, LANES), jnp.float32),
        ],
        compiler_params=params(10),
        cost_estimate=cost(4 * 10**9),
        name="front",
    )(place, normed, *earlier, *weights, dw_kernel)


def merged(stats_ref):
    means, squares, counts = stats_ref[:, 0, :], stats_ref[:, 1, :], stats_ref[:, 2, :]
    count = jnp.sum(counts, axis=0, keepdims=True)
    mean = jnp.sum(counts * means, axis=0, keepdims=True) / jnp.maximum(count, 1.0)
    between = means - mean
    square = jnp.sum(squares + counts * between * between, axis=0, keepdims=True)
    return mean, square, count


def merge_kernel(stats_ref, out_ref):
    for i, row in enumerate(merged(stats_ref)):
        for copy in range(out_ref.shape[0]):
            out_ref[copy, i : i + 1, :] = row


def merge(stats, copies):
    return pl.pallas_call(
        merge_kernel,
        out_shape=jax.ShapeDtypeStruct((copies,) + stats.shape[1:], jnp.float32),
        in_specs=[pl.BlockSpec(memory_space=VMEM)],
        out_specs=pl.BlockSpec(memory_space=VMEM),
        compiler_params=params(8),
        cost_estimate=cost(10**8),
        name="merge",
    )(stats)


def back_kernel(place_ref, stats_ref, gain_ref, shift_ref, *refs):
    *conv_refs, out_ref, rows_out, sems, weights = refs
    convs, weight_refs = conv_refs[:3], conv_refs[3:]
    row_count, wide = convs[0].shape
    if len(weight_refs) == 4:
        depth = weight_refs[0].shape[0]
        for i, weight_ref in enumerate(weight_refs):
            at = pl.multiple_of(lax.bitwise_xor(place_ref[0], i) * depth, depth)
            weights[pl.ds(at, depth), :] = weight_ref[...]
    else:
        weights[...] = weight_refs[0][...]
    mean, square, count = merged(stats_ref)
    scale = lax.rsqrt(square / count + 1e-05) * gain_ref[...]
    shift = shift_ref[...]
    pieces, rows, columns = rows_out.shape
    across = out_ref.shape[1] // columns
    copies = []
    for piece in range(pieces // across):
        here = slice(piece * rows, (piece + 1) * rows)
        parts = []
        for i, conv_ref in enumerate(convs):
            lanes = slice(i * wide, (i + 1) * wide)
            scaled = (conv_ref[here, :] - mean[:, lanes]) * scale[:, lanes] + shift[:, lanes]
            parts.append((scaled * jax.nn.sigmoid(scaled)).astype(jnp.bfloat16))
        activated = jnp.concatenate(parts, axis=1)
        position = place_ref[1] + piece * rows + lax.broadcasted_iota(jnp.int32, (rows, 1), 0)
        for j in range(across):
            lanes = slice(j * columns, (j + 1) * columns)
            result = jnp.dot(activated, weights[:, lanes], preferred_element_type=jnp.float32)
            slot = piece * across + j
            rows_out[slot] = jnp.where(position < place_ref[2], result, 0.0).astype(jnp.bfloat16)
            copy = pltpu.make_async_copy(rows_out.at[slot], out_ref.at[here, lanes], sems.at[slot])
            copy.start()
            copies.append(copy)
    for copy in copies:
        copy.wait()


def back(place, stats, gain, shift, convs, weights):
    row_count = convs[0].shape[0]
    channels, width = gain.shape[1], weights[0].shape[1]
    pieces, across = 4, 2
    return pl.pallas_call(
        back_kernel,
        out_shape=jax.ShapeDtypeStruct((row_count, width), jnp.bfloat16),
        in_specs=[pl.BlockSpec(memory_space=pltpu.SMEM)]
        + [pl.BlockSpec(memory_space=VMEM)] * (3 + len(convs) + len(weights)),
        out_specs=pl.BlockSpec(memory_space=pl.ANY),
        scratch_shapes=[
            VMEM((pieces, row_count * across // pieces, width // across), jnp.bfloat16),
            pltpu.SemaphoreType.DMA((pieces,)),
            VMEM((channels, width), jnp.bfloat16),
        ],
        compiler_params=params(10),
        cost_estimate=cost(10**9),
        name="back",
    )(place, stats, gain, shift, *convs, *weights)


def everyones(copies, groups):
    return lax.all_to_all(copies, ("fsdp", "ctx"), 0, 0, axis_index_groups=groups, tiled=True)


def tie(*values):
    return lax.optimization_barrier(values)


def body(frames, lengths, ln_gain, w_in, dw_kernel, bn_gain, bn_shift, w_out):
    _, row_count, model_width = frames.shape
    channels = dw_kernel.shape[1]
    wide = channels // 3
    ctx, fsdp = lax.axis_index("ctx"), lax.axis_index("fsdp")
    ctx_count, fsdp_count = lax.axis_size("ctx"), lax.axis_size("fsdp")
    direct = fsdp_count == 4 and ctx_count % 2 == 0
    rows = frames[0]
    gain = ln_gain[None]
    parity = lax.rem(ctx, 2)
    place = jnp.stack([fsdp, ctx * row_count, lengths[0], parity]).astype(jnp.int32)
    ends = ctx_count - 1
    down, up = [(i, i + 1) for i in range(ends)], [(i + 1, i) for i in range(ends)]
    if direct:
        *parts, head, tail = cut(parity[None].astype(jnp.int32), w_in, rows, wide)
        over_x = [swap(part, "fsdp", 2) for part in parts]
        shards = [w_in, swap(w_in, "fsdp", 1)]
        normed = normalize_rows(rows, gain)
        normed, head, tail, over_x[0] = tie(normed, head, tail, over_x[0])
        over_y = [swap(over_x[0], "ctx", 1)]
        before, after = lax.ppermute(tail, "ctx", down), lax.ppermute(head, "ctx", up)
        normed, over_x[1], over_y[0] = tie(normed, over_x[1], over_y[0])
        over_y.append(swap(over_x[1], "ctx", 1))
        normed, *partials = near_product(place, before, normed, after, gain, shards)
        partials[0], over_x[2], over_y[1] = tie(partials[0], over_x[2], over_y[1])
        halves = [(over_x[0], over_y[0]), (over_x[1], over_y[1]), (over_x[2],)]
        weights = [
            [partial, *half, *(swap(part, "fsdp", 1) for part in half)]
            for partial, half in zip(partials, halves)
        ]
        _, later = tie(over_x[2], w_out)
        out_weights = [w_out, swap(later, "fsdp", 1), swap(later, "fsdp", 2)]
    else:
        full_in = lax.all_gather(w_in, "fsdp", axis=0, tiled=True)
        out_weights = [lax.all_gather(w_out, "fsdp", axis=0, tiled=True)]
        before = lax.ppermute(rows[-HALO:], "ctx", down)
        after = lax.ppermute(rows[:HALO], "ctx", up)
        normed = normalize_rows(rows, gain)
        normed, *_ = near_product(place, before, normed, after, gain, [])
        weights = [[full_in]] * 3
    near_by = 2 if ctx_count % 2 == 0 else 1
    member = lambda f, p: f * ctx_count + p
    groups = [
        [member(f, p + i) for f in range(fsdp_count) for i in range(near_by)]
        for p in range(0, ctx_count, near_by)
    ]
    convs, stats = [], []
    for i in range(3):
        extra = (stats, len(groups[0])) if i == 2 else ()
        conv, stat = front_block(i, wide, place, normed, weights[i], dw_kernel, *extra)
        convs.append(conv)
        stats.append(stat)
    stats = merge(everyones(stats[2], groups), len(groups))
    if direct:
        stats, out_weights[2] = tie(stats, out_weights[2])
        out_weights.append(swap(out_weights[2], "fsdp", 1))
    groups = [
        [member(f, p + i) for p in range(0, ctx_count, near_by)]
        for f in range(fsdp_count)
        for i in range(near_by)
    ]
    stats = everyones(stats, groups)
    result = back(place, stats, bn_gain[None], bn_shift[None], convs, out_weights)
    return result[None]


def solution(mesh):
    return jax.shard_map(
        body,
        mesh=mesh,
        in_specs=(
            P("fsdp", "ctx", None),
            P("fsdp"),
            P(),
            P("fsdp", None),
            P(),
            P(),
            P(),
            P("fsdp", None),
        ),
        out_specs=P("fsdp", "ctx", None),
        check_vma=False,
    )
```

profile of v0, /device:TPU:0, one launch (start us, length us, event | category | flops | bytes accessed | tf_op | source)
XLA Modules:
  0.0 67.8 jit_solution(10516977869313183399)
XLA Ops:
  0.5 2.3 %cut.1 = (bf16[384,256]{1,0:T(8,128)(2,1)}, bf16[384,256]{1,0:T(8,128)(2,1)}, bf16[384,512]{1,0:T(8,128)(2,1)}, bf16[16,1536]{1,0:T(8,128)(2,1)}, bf16[16,1536]{1,0:T(8,128)(2,1)}) custom-call(s32[1]{0:T(128)} %bitcast.2.parity_ref, bf16[384,1536]{1,0:T(8,128)(2,1)} %refs_0_.1, bf16[512,1536]{1,0:T(8,128)(2,1)} %bitcast.5), custom_call_target="tpu_custom_call" | custom-call | flops 100000000 | tf_op jit(solution)/shard_map/cut/pallas_call | solution.py:54
  2.8 2.6 %collective-permute-start = (bf16[384,256]{1,0:T(8,128)(2,1)}, bf16[384,256]{1,0:T(8,128)(2,1)}, u32[]{:S(2)}, u32[]{:S(2)}) collective-permute-start(bf16[384,256]{1,0:T(8,128)(2,1)} %get-tuple-element.35), channel_id=1, source_target_pairs={{0,16},{8,24},{16,0},{24,8},{1,17},{9,25},{17,1},{25,9},{2,18},{10... | collective-permute-start | bytes 589832 | tf_op jit(solution)/shard_map/ppermute | solution.py:25
  5.4 3.9 %layer_norm.1.rows_ref = bf16[512,1536]{1,0:T(8,128)(2,1)S(1)} custom-call(bf16[512,1536]{1,0:T(8,128)(2,1)S(1)} %bitcast.6, f32[1,1536]{1,0:T(1,128)S(1)} %broadcast_in_dim.13.gain_ref), custom_call_target="tpu_custom_call" | custom-call | flops 1000000000 | tf_op jit(solution)/shard_map/layer_norm/pallas_call | solution.py:95
  9.4 2.0 %collective-permute-done.refs_1_ = bf16[384,256]{1,0:T(8,128)(2,1)} collective-permute-done((bf16[384,256]{1,0:T(8,128)(2,1)}, bf16[384,256]{1,0:T(8,128)(2,1)}, u32[]{:S(2)}, u32[]{:S(2)}) %collective-permute-start) | collective-permute-done | bytes 196640 | tf_op jit(solution)/shard_map/ppermute | solution.py:25
  11.4 2.0 %collective-permute-start.3 = (bf16[384,256]{1,0:T(8,128)(2,1)}, bf16[384,256]{1,0:T(8,128)(2,1)}, u32[]{:S(2)}, u32[]{:S(2)}) collective-permute-start(bf16[384,256]{1,0:T(8,128)(2,1)} %collective-permute-done.refs_1_), channel_id=1, source_target_pairs={{0,1},{1,0},{2,3},{3,2},{4,5},{5,4},{6,7},{7,6},{8,9},{9,8},{10,11... | collective-permute-start | bytes 589832 | tf_op jit(solution)/shard_map/ppermute | solution.py:25
  13.4 1.5 %collective-permute-start.6 = (bf16[384,512]{1,0:T(8,128)(2,1)}, bf16[384,512]{1,0:T(8,128)(2,1)}, u32[]{:S(2)}, u32[]{:S(2)}) collective-permute-start(bf16[384,512]{1,0:T(8,128)(2,1)} %get-tuple-element.44), channel_id=1, source_target_pairs={{0,16},{8,24},{16,0},{24,8},{1,17},{9,25},{17,1},{25,9},{2,18},{10... | collective-permute-start | bytes 1179656 | tf_op jit(solution)/shard_map/ppermute | solution.py:25
  14.9 2.4 %collective-permute-start.1 = (bf16[16,1536]{1,0:T(8,128)(2,1)S(1)}, bf16[16,1536]{1,0:T(8,128)(2,1)S(1)}, u32[]{:S(2)}, u32[]{:S(2)}) collective-permute-start(bf16[16,1536]{1,0:T(8,128)(2,1)S(1)} %copy-done.12), channel_id=1, source_target_pairs={{0,1},{1,2},{2,3},{3,4},{4,5},{5,6},{6,7},{8,9},{9,10},{10,11},{11... | collective-permute-start | bytes 147464 | tf_op jit(solution)/shard_map/ppermute | solution.py:361
  17.3 1.3 %collective-permute-start.4 = (bf16[16,1536]{1,0:T(8,128)(2,1)S(1)}, bf16[16,1536]{1,0:T(8,128)(2,1)S(1)}, u32[]{:S(2)}, u32[]{:S(2)}) collective-permute-start(bf16[16,1536]{1,0:T(8,128)(2,1)S(1)} %copy-done.11), channel_id=1, source_target_pairs={{1,0},{2,1},{3,2},{4,3},{5,4},{6,5},{7,6},{9,8},{10,9},{11,10},{12... | collective-permute-start | bytes 147464 | tf_op jit(solution)/shard_map/ppermute | solution.py:361
  19.3 3.2 %collective-permute-start.7 = (bf16[384,256]{1,0:T(8,128)(2,1)}, bf16[384,256]{1,0:T(8,128)(2,1)S(1)}, u32[]{:S(2)}, u32[]{:S(2)}) collective-permute-start(bf16[384,256]{1,0:T(8,128)(2,1)} %collective-permute-done.2.refs_1_), channel_id=1, source_target_pairs={{0,1},{1,0},{2,3},{3,2},{4,5},{5,4},{6,7},{7,6},{8,9},{9,8},{10,11... | collective-permute-start | bytes 589832 | tf_op jit(solution)/shard_map/ppermute | solution.py:25
  22.6 1.2 %collective-permute-done.4.after_ref = bf16[16,1536]{1,0:T(8,128)(2,1)S(1)} collective-permute-done((bf16[16,1536]{1,0:T(8,128)(2,1)S(1)}, bf16[16,1536]{1,0:T(8,128)(2,1)S(1)}, u32[]{:S(2)}, u32[]{:S(2)}) %collective-permute-start.4) | collective-permute-done | bytes 49184 | tf_op jit(solution)/shard_map/ppermute | solution.py:361
  24.5 3.0 %near.1 = (bf16[544,1536]{1,0:T(8,128)(2,1)S(1)}, f32[544,512]{1,0:T(8,128)S(1)}, f32[544,512]{1,0:T(8,128)S(1)}, f32[544,512]{1,0:T(8,128)S(1)}) custom-call(s32[4]{0:T(128)S(1)} %pad_add_fusion.place_ref, bf16[16,1536]{1,0:T(8,128)(2,1)S(1)} %collective-permute-done.1.before_ref, bf16[512,1536]{1,0:T(8,128)(2,1)S(1)} %layer_norm.1.rows_ref, ...), custom_call_target="tpu_custom_call" | custom-call | flops 1000000000 | tf_op jit(solution)/shard_map/near/pallas_call | solution.py:137
  27.5 0.8 %collective-permute-done.7.refs_2_ = bf16[384,256]{1,0:T(8,128)(2,1)S(1)} collective-permute-done((bf16[384,256]{1,0:T(8,128)(2,1)}, bf16[384,256]{1,0:T(8,128)(2,1)S(1)}, u32[]{:S(2)}, u32[]{:S(2)}) %collective-permute-start.7) | collective-permute-done | bytes 196640 | tf_op jit(solution)/shard_map/ppermute | solution.py:25
  29.3 3.4 %front.3 = (f32[512,256]{1,0:T(8,128)S(1)}, f32[3,256]{1,0:T(4,128)S(1)}) custom-call(s32[4]{0:T(128)S(1)} %pad_add_fusion.place_ref, bf16[544,1536]{1,0:T(8,128)(2,1)S(1)} %get-tuple-element.42.normed_ref, f32[544,512]{1,0:T(8,128)S(1)} %get-tuple-element.46.refs_0_, bf16[384,256]{1,0:T(8,128)(2,1)} %collective-permute-done.refs_1_, ...), custom_call_target="tpu_custom_call" | custom-call | flops 4000000000 | tf_op jit(solution)/shard_map/front/pallas_call | solution.py:228
  32.7 3.3 %front.4 = (f32[512,256]{1,0:T(8,128)S(1)}, f32[3,256]{1,0:T(4,128)S(1)}) custom-call(s32[4]{0:T(128)S(1)} %pad_add_fusion.place_ref, bf16[544,1536]{1,0:T(8,128)(2,1)S(1)} %get-tuple-element.42.normed_ref, f32[544,512]{1,0:T(8,128)S(1)} %get-tuple-element.49.refs_0_, bf16[384,256]{1,0:T(8,128)(2,1)} %collective-permute-done.2.refs_1_, ...), custom_call_target="tpu_custom_call" | custom-call | flops 4000000000 | tf_op jit(solution)/shard_map/front/pallas_call | solution.py:228
  36.0 0.8 %copy-done.3 = f32[512,256]{1,0:T(8,128)} copy-done((f32[512,256]{1,0:T(8,128)}, f32[512,256]{1,0:T(8,128)S(1)}, u32[]{:S(2)}) %copy-start.3) | copy-done | bytes 524312
  36.8 4.1 %front.5 = (f32[512,256]{1,0:T(8,128)S(1)}, f32[8,3,768]{2,1,0:T(4,128)}) custom-call(s32[4]{0:T(128)S(1)} %pad_add_fusion.place_ref, bf16[544,1536]{1,0:T(8,128)(2,1)S(1)} %get-tuple-element.42.normed_ref, f32[3,256]{1,0:T(4,128)S(1)} %get-tuple-element.48.refs_0_, f32[3,256]{1,0:T(4,128)S(1)} %get-tuple-element.51.refs_1_, ...), custom_call_target="tpu_custom_call" | custom-call | flops 4000000000 | tf_op jit(solution)/shard_map/front/pallas_call | solution.py:228
  40.9 0.8 %copy-done.5 = f32[512,256]{1,0:T(8,128)} copy-done((f32[512,256]{1,0:T(8,128)}, f32[512,256]{1,0:T(8,128)S(1)}, u32[]{:S(2)}) %copy-start.5) | copy-done | bytes 524312
  41.7 4.5 %all-to-all-start = ((f32[8,3,768]{2,1,0:T(4,128)}), f32[8,3,768]{2,1,0:T(4,128)S(1)}, u32[]{:S(2)}, u32[]{:S(2)}) async-start(f32[8,3,768]{2,1,0:T(4,128)} %get-tuple-element.54), calls=%async_computation | async-start | bytes 196608 | tf_op jit(solution)/shard_map/all_to_all | solution.py:334
  46.7 4.3 %all-to-all-done.stats_ref = f32[8,3,768]{2,1,0:T(4,128)S(1)} async-done(((f32[8,3,768]{2,1,0:T(4,128)}), f32[8,3,768]{2,1,0:T(4,128)S(1)}, u32[]{:S(2)}, u32[]{:S(2)}) %all-to-all-start) | async-done | bytes 73760 | tf_op jit(solution)/shard_map/all_to_all | solution.py:334
  51.8 5.3 %all-to-all-start.1 = ((f32[4,3,768]{2,1,0:T(4,128)}), f32[4,3,768]{2,1,0:T(4,128)S(1)}, u32[]{:S(2)}, u32[]{:S(2)}) async-start(f32[4,3,768]{2,1,0:T(4,128)} %merge.1), calls=%async_computation.1 | async-start | bytes 98304 | tf_op jit(solution)/shard_map/all_to_all | solution.py:334
  57.1 5.7 %all-to-all-done.1.stats_ref = f32[4,3,768]{2,1,0:T(4,128)S(1)} async-done(((f32[4,3,768]{2,1,0:T(4,128)}), f32[4,3,768]{2,1,0:T(4,128)S(1)}, u32[]{:S(2)}, u32[]{:S(2)}) %all-to-all-start.1) | async-done | bytes 36896 | tf_op jit(solution)/shard_map/all_to_all | solution.py:334
  62.8 1.0 %copy-done.4 = f32[512,256]{1,0:T(8,128)S(1)} copy-done((f32[512,256]{1,0:T(8,128)S(1)}, f32[512,256]{1,0:T(8,128)}, u32[]{:S(2)}) %copy-start.4) | copy-done | bytes 524312
  63.9 1.0 %copy-done.6 = f32[512,256]{1,0:T(8,128)S(1)} copy-done((f32[512,256]{1,0:T(8,128)S(1)}, f32[512,256]{1,0:T(8,128)}, u32[]{:S(2)}) %copy-start.6) | copy-done | bytes 524312
  64.9 2.9 %back.1 = bf16[512,1536]{1,0:T(8,128)(2,1)} custom-call(s32[4]{0:T(128)S(1)} %pad_add_fusion.place_ref, f32[4,3,768]{2,1,0:T(4,128)S(1)} %all-to-all-done.1.stats_ref, f32[1,768]{1,0:T(1,128)S(1)} %broadcast_in_dim.14.gain_ref, f32[1,768]{1,0:T(1,128)S(1)} %broadcast_in_dim.15.shift_ref, f32[512,256]{1,0:T(8,128)S(1)} %get-tuple-element.57.refs_0_, ...), custom_call_target="tpu_custom_call" | custom-call | flops 1000000000 | tf_op jit(solution)/shard_map/back/pallas_call | solution.py:316
  (50 shorter events, 3.7 us)
Async XLA Ops:
  0.0 23.9 %collective-permute-start.5 = (bf16[384,1536]{1,0:T(8,128)(2,1)}, bf16[384,1536]{1,0:T(8,128)(2,1)}, u32[]{:S(2)}, u32[]{:S(2)}) collective-permute-start(bf16[384,1536]{1,0:T(8,128)(2,1)} %refs_0_.1), channel_id=1, source_target_pairs={{0,8},{8,0},{16,24},{24,16},{1,9},{9,1},{17,25},{25,17},{2,10},{10... | collective-permute-start | bytes 3538952 | tf_op jit(solution)/shard_map/ppermute | solution.py:25
  2.8 8.6 %collective-permute-start = (bf16[384,256]{1,0:T(8,128)(2,1)}, bf16[384,256]{1,0:T(8,128)(2,1)}, u32[]{:S(2)}, u32[]{:S(2)}) collective-permute-start(bf16[384,256]{1,0:T(8,128)(2,1)} %get-tuple-element.35), channel_id=1, source_target_pairs={{0,16},{8,24},{16,0},{24,8},{1,17},{9,25},{17,1},{25,9},{2,18},{10... | collective-permute-start | bytes 589832 | tf_op jit(solution)/shard_map/ppermute | solution.py:25
  5.3 11.9 %collective-permute-start.2 = (bf16[384,256]{1,0:T(8,128)(2,1)}, bf16[384,256]{1,0:T(8,128)(2,1)}, u32[]{:S(2)}, u32[]{:S(2)}) collective-permute-start(bf16[384,256]{1,0:T(8,128)(2,1)} %get-tuple-element.38), channel_id=1, source_target_pairs={{0,16},{8,24},{16,0},{24,8},{1,17},{9,25},{17,1},{25,9},{2,18},{10... | collective-permute-start | bytes 589832 | tf_op jit(solution)/shard_map/ppermute | solution.py:25
  5.4 9.4 %copy-start.12 = (bf16[16,1536]{1,0:T(8,128)(2,1)S(1)}, bf16[16,1536]{1,0:T(8,128)(2,1)}, u32[]{:S(2)}) copy-start(bf16[16,1536]{1,0:T(8,128)(2,1)} %get-tuple-element.36) | copy-start | bytes 147460
  5.4 11.8 %copy-start.11 = (bf16[16,1536]{1,0:T(8,128)(2,1)S(1)}, bf16[16,1536]{1,0:T(8,128)(2,1)}, u32[]{:S(2)}) copy-start(bf16[16,1536]{1,0:T(8,128)(2,1)} %get-tuple-element.41) | copy-start | bytes 147460
  5.4 19.0 %copy-start = (bf16[384,1536]{1,0:T(8,128)(2,1)S(1)}, bf16[384,1536]{1,0:T(8,128)(2,1)}, u32[]{:S(2)}) copy-start(bf16[384,1536]{1,0:T(8,128)(2,1)} %refs_0_.1) | copy-start | bytes 3538948
  11.4 7.9 %collective-permute-start.3 = (bf16[384,256]{1,0:T(8,128)(2,1)}, bf16[384,256]{1,0:T(8,128)(2,1)}, u32[]{:S(2)}, u32[]{:S(2)}) collective-permute-start(bf16[384,256]{1,0:T(8,128)(2,1)} %collective-permute-done.refs_1_), channel_id=1, source_target_pairs={{0,1},{1,0},{2,3},{3,2},{4,5},{5,4},{6,7},{7,6},{8,9},{9,8},{10,11... | collective-permute-start | bytes 589832 | tf_op jit(solution)/shard_map/ppermute | solution.py:25
  13.4 14.1 %collective-permute-start.6 = (bf16[384,512]{1,0:T(8,128)(2,1)}, bf16[384,512]{1,0:T(8,128)(2,1)}, u32[]{:S(2)}, u32[]{:S(2)}) collective-permute-start(bf16[384,512]{1,0:T(8,128)(2,1)} %get-tuple-element.44), channel_id=1, source_target_pairs={{0,16},{8,24},{16,0},{24,8},{1,17},{9,25},{17,1},{25,9},{2,18},{10... | collective-permute-start | bytes 1179656 | tf_op jit(solution)/shard_map/ppermute | solution.py:25
  14.9 4.5 %collective-permute-start.1 = (bf16[16,1536]{1,0:T(8,128)(2,1)S(1)}, bf16[16,1536]{1,0:T(8,128)(2,1)S(1)}, u32[]{:S(2)}, u32[]{:S(2)}) collective-permute-start(bf16[16,1536]{1,0:T(8,128)(2,1)S(1)} %copy-done.12), channel_id=1, source_target_pairs={{0,1},{1,2},{2,3},{3,4},{4,5},{5,6},{6,7},{8,9},{9,10},{10,11},{11... | collective-permute-start | bytes 147464 | tf_op jit(solution)/shard_map/ppermute | solution.py:361
  17.3 6.5 %collective-permute-start.4 = (bf16[16,1536]{1,0:T(8,128)(2,1)S(1)}, bf16[16,1536]{1,0:T(8,128)(2,1)S(1)}, u32[]{:S(2)}, u32[]{:S(2)}) collective-permute-start(bf16[16,1536]{1,0:T(8,128)(2,1)S(1)} %copy-done.11), channel_id=1, source_target_pairs={{1,0},{2,1},{3,2},{4,3},{5,4},{6,5},{7,6},{9,8},{10,9},{11,10},{12... | collective-permute-start | bytes 147464 | tf_op jit(solution)/shard_map/ppermute | solution.py:361
  19.2 9.5 %collective-permute-start.8 = (bf16[384,256]{1,0:T(8,128)(2,1)}, bf16[384,256]{1,0:T(8,128)(2,1)S(1)}, u32[]{:S(2)}, u32[]{:S(2)}) collective-permute-start(bf16[384,256]{1,0:T(8,128)(2,1)} %collective-permute-done.refs_1_), channel_id=1, source_target_pairs={{0,8},{8,0},{16,24},{24,16},{1,9},{9,1},{17,25},{25,17},{2,10},{10... | collective-permute-start | bytes 589832 | tf_op jit(solution)/shard_map/ppermute | solution.py:25
  19.3 8.9 %collective-permute-start.7 = (bf16[384,256]{1,0:T(8,128)(2,1)}, bf16[384,256]{1,0:T(8,128)(2,1)S(1)}, u32[]{:S(2)}, u32[]{:S(2)}) collective-permute-start(bf16[384,256]{1,0:T(8,128)(2,1)} %collective-permute-done.2.refs_1_), channel_id=1, source_target_pairs={{0,1},{1,0},{2,3},{3,2},{4,5},{5,4},{6,7},{7,6},{8,9},{9,8},{10,11... | collective-permute-start | bytes 589832 | tf_op jit(solution)/shard_map/ppermute | solution.py:25
  23.8 5.5 %collective-permute-start.9 = (bf16[384,256]{1,0:T(8,128)(2,1)}, bf16[384,256]{1,0:T(8,128)(2,1)S(1)}, u32[]{:S(2)}, u32[]{:S(2)}) collective-permute-start(bf16[384,256]{1,0:T(8,128)(2,1)} %collective-permute-done.3.refs_2_), channel_id=1, source_target_pairs={{0,8},{8,0},{16,24},{24,16},{1,9},{9,1},{17,25},{25,17},{2,10},{10... | collective-permute-start | bytes 589832 | tf_op jit(solution)/shard_map/ppermute | solution.py:25
  23.9 5.5 %copy-start.7 = (f32[31,768]{1,0:T(8,128)S(1)}, f32[31,768]{1,0:T(8,128)}, u32[]{:S(2)}) copy-start(f32[31,768]{1,0:T(8,128)} %refs_5_.5) | copy-start | bytes 285700
  23.9 8.8 %collective-permute-start.10 = (bf16[384,256]{1,0:T(8,128)(2,1)}, bf16[384,256]{1,0:T(8,128)(2,1)S(1)}, u32[]{:S(2)}, u32[]{:S(2)}) collective-permute-start(bf16[384,256]{1,0:T(8,128)(2,1)} %collective-permute-done.2.refs_1_), channel_id=1, source_target_pairs={{0,8},{8,0},{16,24},{24,16},{1,9},{9,1},{17,25},{25,17},{2,10},{10... | collective-permute-start | bytes 589832 | tf_op jit(solution)/shard_map/ppermute | solution.py:25
  28.3 4.4 %collective-permute-start.11 = (bf16[384,256]{1,0:T(8,128)(2,1)S(1)}, bf16[384,256]{1,0:T(8,128)(2,1)S(1)}, u32[]{:S(2)}, u32[]{:S(2)}) collective-permute-start(bf16[384,256]{1,0:T(8,128)(2,1)S(1)} %collective-permute-done.7.refs_2_), channel_id=1, source_target_pairs={{0,8},{8,0},{16,24},{24,16},{1,9},{9,1},{17,25},{25,17},{2,10},{10... | collective-permute-start | bytes 589832 | tf_op jit(solution)/shard_map/ppermute | solution.py:25
  28.3 8.5 %collective-permute-start.12 = (bf16[384,512]{1,0:T(8,128)(2,1)}, bf16[384,512]{1,0:T(8,128)(2,1)S(1)}, u32[]{:S(2)}, u32[]{:S(2)}) collective-permute-start(bf16[384,512]{1,0:T(8,128)(2,1)} %collective-permute-done.6.refs_3_), channel_id=1, source_target_pairs={{0,8},{8,0},{16,24},{24,16},{1,9},{9,1},{17,25},{25,17},{2,10},{10... | collective-permute-start | bytes 1179656 | tf_op jit(solution)/shard_map/ppermute | solution.py:25
  28.8 22.9 %collective-permute-start.13 = (bf16[192,1536]{1,0:T(8,128)(2,1)S(1)}, bf16[192,1536]{1,0:T(8,128)(2,1)S(1)}, u32[]{:S(2)}, u32[]{:S(2)}) collective-permute-start(bf16[192,1536]{1,0:T(8,128)(2,1)S(1)} %copy-done.2), channel_id=1, source_target_pairs={{0,16},{8,24},{16,0},{24,8},{1,17},{9,25},{17,1},{25,9},{2,18},{10... | collective-permute-start | bytes 1769480 | tf_op jit(solution)/shard_map/ppermute | solution.py:25
  36.8 20.3 %copy-start.9 = (f32[768]{0:T(1024)S(1)}, f32[768]{0:T(1024)}, u32[]{:S(2)}) copy-start(f32[768]{0:T(1024)} %param.13) | copy-start | bytes 9220
  36.8 20.3 %copy-start.10 = (f32[768]{0:T(1024)S(1)}, f32[768]{0:T(1024)}, u32[]{:S(2)}) copy-start(f32[768]{0:T(1024)} %param.14) | copy-start | bytes 9220
  41.7 9.3 %all-to-all-start = ((f32[8,3,768]{2,1,0:T(4,128)}), f32[8,3,768]{2,1,0:T(4,128)S(1)}, u32[]{:S(2)}, u32[]{:S(2)}) async-start(f32[8,3,768]{2,1,0:T(4,128)} %get-tuple-element.54), calls=%async_computation | async-start | bytes 196608 | tf_op jit(solution)/shard_map/all_to_all | solution.py:334
  46.2 10.9 %collective-permute-start.14 = (bf16[192,1536]{1,0:T(8,128)(2,1)S(1)}, bf16[192,1536]{1,0:T(8,128)(2,1)S(1)}, u32[]{:S(2)}, u32[]{:S(2)}) collective-permute-start(bf16[192,1536]{1,0:T(8,128)(2,1)S(1)} %copy-done.2), channel_id=1, source_target_pairs={{0,8},{8,0},{16,24},{24,16},{1,9},{9,1},{17,25},{25,17},{2,10},{10... | collective-permute-start | bytes 1769480 | tf_op jit(solution)/shard_map/ppermute | solution.py:25
  51.7 11.1 %collective-permute-start.15 = (bf16[192,1536]{1,0:T(8,128)(2,1)S(1)}, bf16[192,1536]{1,0:T(8,128)(2,1)S(1)}, u32[]{:S(2)}, u32[]{:S(2)}) collective-permute-start(bf16[192,1536]{1,0:T(8,128)(2,1)S(1)} %collective-permute-done.13.refs_5_), channel_id=1, source_target_pairs={{0,8},{8,0},{16,24},{24,16},{1,9},{9,1},{17,25},{25,17},{2,10},{10... | collective-permute-start | bytes 1769480 | tf_op jit(solution)/shard_map/ppermute | solution.py:25
  51.8 11.0 %all-to-all-start.1 = ((f32[4,3,768]{2,1,0:T(4,128)}), f32[4,3,768]{2,1,0:T(4,128)S(1)}, u32[]{:S(2)}, u32[]{:S(2)}) async-start(f32[4,3,768]{2,1,0:T(4,128)} %merge.1), calls=%async_computation.1 | async-start | bytes 98304 | tf_op jit(solution)/shard_map/all_to_all | solution.py:334
  (7 other events, 18.5 us)
where the time goes:
time: 68.4 us; the launch traced here: 67.8 us
  starting transfers between devices  25.6 us (37%)
  Pallas kernels  23.6 us (35%)
  waiting for transfers between devices  14 us (20%)
  local copies, waits for them, and re-layouts  3.71 us (5%)
  between operations  0.85 us (1%)
    ppermute x14, starting transfers between devices, swap(): lax.ppermute(value, axis, [(i, i ^ bit) for i in range(lax.axis_size(axis...  12.1 us
    pallas_call x3, Pallas kernels, front_block(): pl.pallas_call(functools.partial(front_kernel, block, len(earlier)), out_...  10.7 us
    all_to_all x2, waiting for transfers between devices, everyones(): lax.all_to_all(copies, ('fsdp', 'ctx'), 0, 0, axis_index_groups=groups, t...  9.95 us
    all_to_all x2, starting transfers between devices, everyones(): lax.all_to_all(copies, ('fsdp', 'ctx'), 0, 0, axis_index_groups=groups, t...  9.83 us
    pallas_call x1, Pallas kernels, normalize_rows(): pl.pallas_call(norm_kernel, out_shape=jax.ShapeDtypeStruct((row_count, wi...  3.94 us
    unnamed x26, local copies, waits for them, and re-layouts  3.7 us
    pallas_call x1, Pallas kernels, near_product(): pl.pallas_call(near_kernel, out_shape=(jax.ShapeDtypeStruct((ext_rows, wi...  3.02 us
    pallas_call x1, Pallas kernels, back(): pl.pallas_call(back_kernel, out_shape=jax.ShapeDtypeStruct((row_count, wi...  2.95 us
  transfers between devices with their start and end apart: 18, of which 5 were waited for; matrix products, arithmetic and copies ran while one was open for 0% of the time, Pallas kernels for 30%

commit v1 on v0

--- a/solution.py
+++ b/solution.py
@@ -11,6 +11,8 @@
 LANES = 128
 MIB = 1024 * 1024
 VMEM = pltpu.VMEM
+ORDER = (0, 1, 2)
+SPLIT = (0, 1)
 
 
 def cost(flops):
@@ -25,9 +27,8 @@
     return lax.ppermute(value, axis, [(i, i ^ bit) for i in range(lax.axis_size(axis))])
 
 
-def cut_kernel(parity_ref, shard_ref, rows_ref, *refs):
-    first_ref, second_ref, third_ref, head_ref, tail_ref, sems = refs
-    wide = first_ref.shape[1]
+def cut_kernel(order, split, wide, parity_ref, shard_ref, rows_ref, out_shard_ref, *refs):
+    *part_refs, head_ref, tail_ref, upper_ref, lower_ref, sems = refs
     channels = shard_ref.shape[1] // 2
     row_count = rows_ref.shape[0]
     copies = []
@@ -37,34 +38,41 @@
         copies[-1].start()
 
     side = parity_ref[0] * channels
-    for block, ref in enumerate((first_ref, second_ref)):
-        copy(shard_ref.at[:, pl.ds(pl.multiple_of(side + block * wide, wide), wide)], ref)
-    for i in range(2):
-        at = i * channels + 2 * wide
-        copy(shard_ref.at[:, at : at + wide], third_ref.at[:, i * wide : (i + 1) * wide])
+    for block, ref in zip(order, part_refs):
+        if block in split:
+            copy(shard_ref.at[:, pl.ds(pl.multiple_of(side + block * wide, wide), wide)], ref)
+        else:
+            for i in range(2):
+                at = i * channels + block * wide
+                copy(shard_ref.at[:, at : at + wide], ref.at[:, i * wide : (i + 1) * wide])
     copy(rows_ref.at[0:HALO, :], head_ref)
     copy(rows_ref.at[row_count - HALO : row_count, :], tail_ref)
+    depth = upper_ref.shape[0]
+    copy(out_shard_ref.at[0:depth, :], upper_ref)
+    copy(out_shard_ref.at[depth : 2 * depth, :], lower_ref)
     for started in copies:
         started.wait()
 
 
-def cut(parity, shard, rows, wide):
+def cut(parity, shard, rows, out_shard, wide):
     depth, width = shard.shape
-    shapes = [(depth, wide), (depth, wide), (depth, 2 * wide), (HALO, width), (HALO, width)]
-    return pl.pallas_call(
-        cut_kernel,
+    shapes = [(depth, wide if block in SPLIT else 2 * wide) for block in ORDER]
+    shapes += [(HALO, width)] * 2 + [(out_shard.shape[0] // 2, out_shard.shape[1])] * 2
+    return pl.pallas_call(
+        functools.partial(cut_kernel, ORDER, SPLIT, wide),
         out_shape=[jax.ShapeDtypeStruct(shape, jnp.bfloat16) for shape in shapes],
         in_specs=[
             pl.BlockSpec(memory_space=pltpu.SMEM),
             pl.BlockSpec(memory_space=pltpu.HBM),
             pl.BlockSpec(memory_space=pltpu.HBM),
+            pl.BlockSpec(memory_space=pltpu.HBM),
         ],
-        out_specs=[pl.BlockSpec(memory_space=VMEM)] * 5,
-        scratch_shapes=[pltpu.SemaphoreType.DMA((6,))],
+        out_specs=[pl.BlockSpec(memory_space=VMEM)] * len(shapes),
+        scratch_shapes=[pltpu.SemaphoreType.DMA((8,))],
         compiler_params=params(56),
         cost_estimate=cost(10**8),
         name="cut",
-    )(parity, shard, rows)
+    )(parity, shard, rows, out_shard)
 
 
 def normalize(values, gain):
@@ -75,19 +83,13 @@
     return (deviate * lax.rsqrt(spread + 1e-05) * gain).astype(jnp.bfloat16)
 
 
-def norm_kernel(rows_ref, gain_ref, out_ref, held, sems):
-    pieces = sems.shape[0]
-    step = held.shape[0] // pieces
-    parts = [slice(i * step, (i + 1) * step) for i in range(pieces)]
-    copies = [
-        pltpu.make_async_copy(rows_ref.at[here, :], held.at[here, :], sems.at[i])
-        for i, here in enumerate(parts)
-    ]
-    for copy in copies:
-        copy.start()
-    for copy, here in zip(copies, parts):
-        copy.wait()
-        out_ref[here, :] = normalize(held[here, :], gain_ref[...])
+def norm_kernel(rows_ref, gain_ref, out_ref):
+    step = 64
+
+    @pl.loop(0, rows_ref.shape[0] // step)
+    def _(i):
+        here = pl.ds(pl.multiple_of(i * step, step), step)
+        out_ref[here, :] = normalize(rows_ref[here, :], gain_ref[...])
 
 
 def normalize_rows(rows, gain):
@@ -95,11 +97,10 @@
     return pl.pallas_call(
         norm_kernel,
         out_shape=jax.ShapeDtypeStruct((row_count, width), jnp.bfloat16),
-        in_specs=[pl.BlockSpec(memory_space=pltpu.HBM), pl.BlockSpec(memory_space=VMEM)],
+        in_specs=[pl.BlockSpec(memory_space=VMEM)] * 2,
         out_specs=pl.BlockSpec(memory_space=VMEM),
-        scratch_shapes=[VMEM((row_count, width), jnp.bfloat16), pltpu.SemaphoreType.DMA((8,))],
-        compiler_params=params(48),
-        cost_estimate=cost(10**9),
+        compiler_params=params(4),
+        cost_estimate=cost(4 * 10**9),
         name="layer_norm",
     )(rows, gain)
 
@@ -141,8 +142,8 @@
         + [pl.BlockSpec(memory_space=VMEM)] * (4 + len(shards)),
         out_specs=[pl.BlockSpec(memory_space=VMEM)] * 4,
         scratch_shapes=[VMEM((depth, width), jnp.bfloat16)],
-        compiler_params=params(10),
-        cost_estimate=cost(10**9),
+        compiler_params=params(8),
+        cost_estimate=cost(10**8),
         name="near",
     )(place, before, rows, after, gain, *shards)
 
@@ -180,28 +181,21 @@
     valid = (position >= 0) & (position < length)
     kept = jnp.where(valid, value * jax.nn.sigmoid(gate), 0.0)
     kept = kept.astype(jnp.bfloat16).astype(jnp.float32)
-    units = wide // LANES
-    for unit in range(units):
-        gated[unit] = kept[:, unit * LANES : (unit + 1) * LANES]
     first = HALO - (taps - 1) // 2
     step = 64
-    for unit in range(units):
+    for unit in range(wide // LANES):
         lanes = slice(unit * LANES, (unit + 1) * LANES)
         tap_lanes = slice(block * wide + unit * LANES, block * wide + (unit + 1) * LANES)
+        column = kept[:, lanes]
+        gated[0] = column
+        for phase in range(1, 8):
+            gated[phase] = pltpu.roll(column, ext_rows - phase, 0)
         for at in range(0, row_count, step):
-            acc = jnp.zeros((step, LANES), jnp.float32)
-            for phase in range(8):
-                offsets = [k for k in range(phase, first + taps, 8) if k >= first]
-                extent = step + 8 if phase else step
-                part = None
-                for offset in offsets:
-                    base = at + offset - phase
-                    tap = offset - first
-                    term = gated[unit, base : base + extent, :] * taps_ref[tap : tap + 1, tap_lanes]
-                    part = term if part is None else part + term
-                if phase:
-                    part = pltpu.roll(part, extent - phase, 0)[:step]
-                acc = acc + part
+            acc = None
+            for tap in range(taps):
+                base = at + (first + tap) // 8 * 8
+                term = gated[(first + tap) % 8, base : base + step, :] * taps_ref[tap : tap + 1, tap_lanes]
+                acc = term if acc is None else acc + term
             conv_ref[at : at + step, lanes] = acc
     here = start + lax.broadcasted_iota(jnp.int32, (row_count, 1), 0) < length
     count = jnp.clip(length - start, 0, row_count).astype(jnp.float32)
@@ -214,10 +208,11 @@
         for i, row in enumerate(stats):
             stats_ref[i : i + 1, :] = row
         return
-    for copy in range(stats_ref.shape[0]):
-        for i, row in enumerate(stats):
-            parts = [ref[i : i + 1, :] for ref in earlier_refs] + [row]
-            stats_ref[copy, i : i + 1, :] = jnp.concatenate(parts, axis=1)
+    for i, row in enumerate(stats):
+        for copy in range(stats_ref.shape[0]):
+            stats_ref[copy, i : i + 1, block * wide : (block + 1) * wide] = row
+            for other, ref in zip([j for j in ORDER if j != block], earlier_refs):
+                stats_ref[copy, i : i + 1, other * wide : (other + 1) * wide] = ref[i : i + 1, :]
 
 
 def front_block(block, wide, place, normed, weights, dw_kernel, earlier=(), copies=1):
@@ -236,25 +231,28 @@
         out_specs=[pl.BlockSpec(memory_space=VMEM)] * 2,
         scratch_shapes=[
             VMEM((depth, 2 * wide), jnp.bfloat16),
-            VMEM((wide // LANES, ext_rows, LANES), jnp.float32),
+            VMEM((8, ext_rows, LANES), jnp.float32),
         ],
         compiler_params=params(10),
-        cost_estimate=cost(4 * 10**9),
+        cost_estimate=cost(10**8),
         name="front",
     )(place, normed, *earlier, *weights, dw_kernel)
 
 
-def merged(stats_ref):
-    means, squares, counts = stats_ref[:, 0, :], stats_ref[:, 1, :], stats_ref[:, 2, :]
-    count = jnp.sum(counts, axis=0, keepdims=True)
-    mean = jnp.sum(counts * means, axis=0, keepdims=True) / jnp.maximum(count, 1.0)
-    between = means - mean
-    square = jnp.sum(squares + counts * between * between, axis=0, keepdims=True)
+def merged(parts):
+    means, squares, counts = zip(*parts)
+    count = sum(counts)
+    mean = sum(n * m for n, m in zip(counts, means)) / jnp.maximum(count, 1.0)
+    square = sum(squares) + sum(n * (m - mean) * (m - mean) for n, m in zip(counts, means))
     return mean, square, count
 
 
+def rows_of(refs):
+    return [[ref[copy, i : i + 1, :] for i in range(3)] for ref in refs for copy in range(ref.shape[0])]
+
+
 def merge_kernel(stats_ref, out_ref):
-    for i, row in enumerate(merged(stats_ref)):
+    for i, row in enumerate(merged(rows_of([stats_ref]))):
         for copy in range(out_ref.shape[0]):
             out_ref[copy, i : i + 1, :] = row
 
@@ -271,18 +269,23 @@
     )(stats)
 
 
-def back_kernel(place_ref, stats_ref, gain_ref, shift_ref, *refs):
+def back_kernel(stat_count, place_ref, gain_ref, shift_ref, *refs):
+    stat_refs, refs = refs[:stat_count], refs[stat_count:]
     *conv_refs, out_ref, rows_out, sems, weights = refs
     convs, weight_refs = conv_refs[:3], conv_refs[3:]
     row_count, wide = convs[0].shape
-    if len(weight_refs) == 4:
+    if len(weight_refs) > 1:
         depth = weight_refs[0].shape[0]
-        for i, weight_ref in enumerate(weight_refs):
+        for i, weight_ref in enumerate(weight_refs[:2]):
             at = pl.multiple_of(lax.bitwise_xor(place_ref[0], i) * depth, depth)
             weights[pl.ds(at, depth), :] = weight_ref[...]
+        half = depth // 2
+        for i, weight_ref in enumerate(weight_refs[2:]):
+            at = lax.bitwise_xor(place_ref[0], 2 + i // 2) * depth + i % 2 * half
+            weights[pl.ds(pl.multiple_of(at, half), half), :] = weight_ref[...]
     else:
         weights[...] = weight_refs[0][...]
-    mean, square, count = merged(stats_ref)
+    mean, square, count = merged(rows_of(stat_refs))
     scale = lax.rsqrt(square / count + 1e-05) * gain_ref[...]
     shift = shift_ref[...]
     pieces, rows, columns = rows_out.shape
@@ -314,10 +317,10 @@
     channels, width = gain.shape[1], weights[0].shape[1]
     pieces, across = 4, 2
     return pl.pallas_call(
-        back_kernel,
+        functools.partial(back_kernel, len(stats)),
         out_shape=jax.ShapeDtypeStruct((row_count, width), jnp.bfloat16),
         in_specs=[pl.BlockSpec(memory_space=pltpu.SMEM)]
-        + [pl.BlockSpec(memory_space=VMEM)] * (3 + len(convs) + len(weights)),
+        + [pl.BlockSpec(memory_space=VMEM)] * (2 + len(stats) + len(convs) + len(weights)),
         out_specs=pl.BlockSpec(memory_space=pl.ANY),
         scratch_shapes=[
             VMEM((pieces, row_count * across // pieces, width // across), jnp.bfloat16),
@@ -327,7 +330,7 @@
         compiler_params=params(10),
         cost_estimate=cost(10**9),
         name="back",
-    )(place, stats, gain, shift, *convs, *weights)
+    )(place, gain, shift, *stats, *convs, *weights)
 
 
 def everyones(copies, groups):
@@ -344,32 +347,69 @@
     wide = channels // 3
     ctx, fsdp = lax.axis_index("ctx"), lax.axis_index("fsdp")
     ctx_count, fsdp_count = lax.axis_size("ctx"), lax.axis_size("fsdp")
-    direct = fsdp_count == 4 and ctx_count % 2 == 0
+    direct = fsdp_count == 4 and ctx_count == 8
     rows = frames[0]
     gain = ln_gain[None]
     parity = lax.rem(ctx, 2)
     place = jnp.stack([fsdp, ctx * row_count, lengths[0], parity]).astype(jnp.int32)
     ends = ctx_count - 1
     down, up = [(i, i + 1) for i in range(ends)], [(i + 1, i) for i in range(ends)]
+    both = ("fsdp", "ctx")
+    member = lambda f, p: f * ctx_count + p
+
+    def front(block, weights, *extra):
+        return front_block(block, wide, place, normed, weights, dw_kernel, *extra)
+
     if direct:
-        *parts, head, tail = cut(parity[None].astype(jnp.int32), w_in, rows, wide)
-        over_x = [swap(part, "fsdp", 2) for part in parts]
-        shards = [w_in, swap(w_in, "fsdp", 1)]
+        *parts, head, tail, upper, lower = cut(parity[None].astype(jnp.int32), w_in, rows, w_out, wide)
+        over_x = {block: [swap(part, "fsdp", 2)] for block, part in zip(ORDER, parts)}
+        parts[0], shard = tie(parts[0], w_in)
+        shards = [w_in, swap(shard, "fsdp", 1)]
+        before, after = lax.ppermute(tail, "ctx", down), lax.ppermute(head, "ctx", up)
         normed = normalize_rows(rows, gain)
-        normed, head, tail, over_x[0] = tie(normed, head, tail, over_x[0])
-        over_y = [swap(over_x[0], "ctx", 1)]
-        before, after = lax.ppermute(tail, "ctx", down), lax.ppermute(head, "ctx", up)
-        normed, over_x[1], over_y[0] = tie(normed, over_x[1], over_y[0])
-        over_y.append(swap(over_x[1], "ctx", 1))
+        normed, before, after, over_x[0][0] = tie(normed, before, after, over_x[0][0])
+        over_x[0].append(swap(over_x[0][0], "ctx", 1))
+        normed, over_x[1][0] = tie(normed, over_x[1][0])
+        over_x[1].append(swap(over_x[1][0], "ctx", 1))
         normed, *partials = near_product(place, before, normed, after, gain, shards)
-        partials[0], over_x[2], over_y[1] = tie(partials[0], over_x[2], over_y[1])
-        halves = [(over_x[0], over_y[0]), (over_x[1], over_y[1]), (over_x[2],)]
-        weights = [
-            [partial, *half, *(swap(part, "fsdp", 1) for part in half)]
-            for partial, half in zip(partials, halves)
-        ]
-        _, later = tie(over_x[2], w_out)
-        out_weights = [w_out, swap(later, "fsdp", 1), swap(later, "fsdp", 2)]
+        partials[0], over_x[0][1], over_x[1][1], w_out, upper = tie(
+            partials[0], over_x[0][1], over_x[1][1], w_out, upper
+        )
+        upper = swap(upper, "fsdp", 2)
+        out_weights = [w_out, swap(w_out, "fsdp", 1)]
+
+        def weights_of(block):
+            return [partials[block], *over_x[block], *(swap(part, "fsdp", 1) for part in over_x[block])]
+
+        weights = [weights_of(0), weights_of(1)]
+        conv_one, stat_one = front(0, weights[0])
+        conv_one, weights[1][0], over_x[2][0] = tie(conv_one, weights[1][0], over_x[2][0])
+        _, lower = tie(over_x[2][0], lower)
+        lower = swap(lower, "fsdp", 2)
+        weights.append(weights_of(2))
+        conv_two, stat_two = front(1, weights[1])
+        conv_three, stats = front(2, weights[2], (stat_one, stat_two), 1)
+        convs = [conv_one, conv_two, conv_three]
+
+        def others(flips):
+            return [
+                lax.ppermute(
+                    stats,
+                    both,
+                    [(member(f, p), member(f ^ df, p ^ dp)) for f in range(4) for p in range(8)],
+                )
+                for df, dp in flips
+            ]
+
+        def union(parts):
+            return jnp.stack(merged([[part[:, i] for i in range(3)] for part in parts]), 1)
+
+        stats, upper = tie(stats, upper)
+        stats = union([stats] + others([(1, 0)]))
+        stats = union([stats] + others([(2, 0), (0, 1), (2, 1)]))
+        stats, lower = tie(stats, lower)
+        out_weights += [upper, lower, swap(upper, "fsdp", 1), swap(lower, "fsdp", 1)]
+        stats = [stats] + others([(0, 2), (0, 4), (0, 6)])
     else:
         full_in = lax.all_gather(w_in, "fsdp", axis=0, tiled=True)
         out_weights = [lax.all_gather(w_out, "fsdp", axis=0, tiled=True)]
@@ -377,29 +417,23 @@
         after = lax.ppermute(rows[:HALO], "ctx", up)
         normed = normalize_rows(rows, gain)
         normed, *_ = near_product(place, before, normed, after, gain, [])
-        weights = [[full_in]] * 3
-    near_by = 2 if ctx_count % 2 == 0 else 1
-    member = lambda f, p: f * ctx_count + p
-    groups = [
-        [member(f, p + i) for f in range(fsdp_count) for i in range(near_by)]
-        for p in range(0, ctx_count, near_by)
-    ]
-    convs, stats = [], []
-    for i in range(3):
-        extra = (stats, len(groups[0])) if i == 2 else ()
-        conv, stat = front_block(i, wide, place, normed, weights[i], dw_kernel, *extra)
-        convs.append(conv)
-        stats.append(stat)
-    stats = merge(everyones(stats[2], groups), len(groups))
-    if direct:
-        stats, out_weights[2] = tie(stats, out_weights[2])
-        out_weights.append(swap(out_weights[2], "fsdp", 1))
-    groups = [
-        [member(f, p + i) for p in range(0, ctx_count, near_by)]
-        for f in range(fsdp_count)
-        for i in range(near_by)
-    ]
-    stats = everyones(stats, groups)
+        near_by = 2 if ctx_count % 2 == 0 else 1
+        groups = [
+            [member(f, p + i) for f in range(fsdp_count) for i in range(near_by)]
+            for p in range(0, ctx_count, near_by)
+        ]
+        convs, stats = [None] * 3, []
+        for block in ORDER:
+            extra = (stats, len(groups[0])) if block == ORDER[-1] else ()
+            convs[block], stat = front(block, [full_in], *extra)
+            stats.append(stat)
+        stats = merge(everyones(stats[2], groups), len(groups))
+        groups = [
+            [member(f, p + i) for p in range(0, ctx_count, near_by)]
+            for f in range(fsdp_count)
+            for i in range(near_by)
+        ]
+        stats = [everyones(stats, groups)]
     result = back(place, stats, bn_gain[None], bn_shift[None], convs, out_weights)
     return result[None]
 

time: 68.4 us -> 70.8 us (1.035)
  waiting for transfers between devices: 14 us -> 24.5 us
  Pallas kernels: 23.6 us -> 19.8 us
  starting transfers between devices: 25.6 us -> 22.2 us
  local copies, waits for them, and re-layouts: 3.71 us -> 2.9 us
    ppermute x14 -> x16, waiting for transfers between devices: 2.8 us -> 13.6 us  [swap(): lax.ppermute(value, axis, [(i, i ^ bit) for i in range(lax.axis_size(axis...]
    all_to_all x2 -> x0, waiting for transfers between devices: 9.95 us -> none  [everyones(): lax.all_to_all(copies, ('fsdp', 'ctx'), 0, 0, axis_index_groups=groups, t...]
    all_to_all x2 -> x0, starting transfers between devices: 9.83 us -> none  [everyones(): lax.all_to_all(copies, ('fsdp', 'ctx'), 0, 0, axis_index_groups=groups, t...]
    ppermute x0 -> x7, waiting for transfers between devices: none -> 9.23 us  [others(): lax.ppermute(stats, both, [(member(f, p), member(f ^ df, p ^ dp)) for f i...]
    ppermute x0 -> x7, starting transfers between devices: none -> 8.85 us  [others(): lax.ppermute(stats, both, [(member(f, p), member(f ^ df, p ^ dp)) for f i...]
    ppermute x14 -> x16, starting transfers between devices: 12.1 us -> 8.67 us  [swap(): lax.ppermute(value, axis, [(i, i ^ bit) for i in range(lax.axis_size(axis...]
    pallas_call x1, Pallas kernels: 3.94 us -> 1.91 us  [normalize_rows(): pl.pallas_call(norm_kernel, out_shape=jax.ShapeDtypeStruct((row_count, wi...]
    pallas_call x3, Pallas kernels: 10.7 us -> 9.18 us  [front_block(): pl.pallas_call(functools.partial(front_kernel, block, len(earlier)), out_...]
  transfers between devices with their start and end apart: 18 -> 25, of which waited for: 5 -> 12; matrix products, arithmetic and copies ran while one was open for 0% -> 0% of each run, Pallas kernels for 30% -> 20%
where the time goes in v1:
time: 70.8 us; the launch traced here: 70.5 us
  waiting for transfers between devices  24.5 us (35%)
  starting transfers between devices  22.2 us (31%)
  Pallas kernels  19.8 us (28%)
  local copies, waits for them, and re-layouts  2.9 us (4%)
  between operations  0.89 us (1%)
    ppermute x16, waiting for transfers between devices, swap(): lax.ppermute(value, axis, [(i, i ^ bit) for i in range(lax.axis_size(axis...  13.6 us
    ppermute x7, waiting for transfers between devices, others(): lax.ppermute(stats, both, [(member(f, p), member(f ^ df, p ^ dp)) for f i...  9.23 us
    pallas_call x3, Pallas kernels, front_block(): pl.pallas_call(functools.partial(front_kernel, block, len(earlier)), out_...  9.18 us
    ppermute x7, starting transfers between devices, others(): lax.ppermute(stats, both, [(member(f, p), member(f ^ df, p ^ dp)) for f i...  8.85 us
    ppermute x16, starting transfers between devices, swap(): lax.ppermute(value, axis, [(i, i ^ bit) for i in range(lax.axis_size(axis...  8.67 us
    ppermute x1, starting transfers between devices, body(): lax.ppermute(tail, 'ctx', down)  3.41 us
    pallas_call x1, Pallas kernels, near_product(): pl.pallas_call(near_kernel, out_shape=(jax.ShapeDtypeStruct((ext_rows, wi...  3.02 us
    pallas_call x1, Pallas kernels, back(): pl.pallas_call(functools.partial(back_kernel, len(stats)), out_shape=jax....  2.94 us
  transfers between devices with their start and end apart: 25, of which 12 were waited for; matrix products, arithmetic and copies ran while one was open for 0% of the time, Pallas kernels for 20%

profile of v1, /device:TPU:0, one launch (start us, length us, event | category | flops | bytes accessed | tf_op | source)
XLA Modules:
  0.0 70.5 jit_solution(1256698750321533123)
XLA Ops:
  0.0 2.8 %cut.1 = (bf16[384,256]{1,0:T(8,128)(2,1)}, bf16[384,256]{1,0:T(8,128)(2,1)}, bf16[384,512]{1,0:T(8,128)(2,1)}, bf16[16,1536]{1,0:T(8,128)(2,1)}, bf16[16,1536]{...) custom-call(s32[1]{0:T(128)} %bitcast.2.parity_ref, bf16[384,1536]{1,0:T(8,128)(2,1)} %refs_0_.1, ...), custom_call_target="tpu_custom_call" | custom-call | flops 100000000 | tf_op jit(solution)/shard_map/cut/pallas_call | solution.py:61
  3.3 2.6 %collective-permute-start.2 = (bf16[384,256]{1,0:T(8,128)(2,1)}, bf16[384,256]{1,0:T(8,128)(2,1)}, u32[]{:S(2)}, u32[]{:S(2)}) collective-permute-start(bf16[384,256]{1,0:T(8,128)(2,1)} %get-tuple-element.44), channel_id=1, source_target_pairs={{0,16},{8,24},{16,0},{24,8},{1,17},{9,25},{17,1},{25,9},{2,18},{10... | collective-permute-start | bytes 589832 | tf_op jit(solution)/shard_map/ppermute | solution.py:27
  5.9 3.4 %collective-permute-start = (bf16[16,1536]{1,0:T(8,128)(2,1)}, bf16[16,1536]{1,0:T(8,128)(2,1)S(1)}, u32[]{:S(2)}, u32[]{:S(2)}) collective-permute-start(bf16[16,1536]{1,0:T(8,128)(2,1)} %get-tuple-element.42), channel_id=1, source_target_pairs={{0,1},{1,2},{2,3},{3,4},{4,5},{5,6},{6,7},{8,9},{9,10},{10,11},{11... | collective-permute-start | bytes 147464 | tf_op jit(solution)/shard_map/ppermute | solution.py:368
  9.3 1.3 %collective-permute-start.1 = (bf16[16,1536]{1,0:T(8,128)(2,1)}, bf16[16,1536]{1,0:T(8,128)(2,1)S(1)}, u32[]{:S(2)}, u32[]{:S(2)}) collective-permute-start(bf16[16,1536]{1,0:T(8,128)(2,1)} %get-tuple-element.43), channel_id=1, source_target_pairs={{1,0},{2,1},{3,2},{4,3},{5,4},{6,5},{7,6},{9,8},{10,9},{11,10},{12... | collective-permute-start | bytes 147464 | tf_op jit(solution)/shard_map/ppermute | solution.py:368
  11.2 1.9 %layer_norm.1.rows_ref = bf16[512,1536]{1,0:T(8,128)(2,1)S(1)} custom-call(bf16[512,1536]{1,0:T(8,128)(2,1)S(1)} %bitcast.6, f32[1,1536]{1,0:T(1,128)S(1)} %broadcast_in_dim.15.gain_ref), custom_call_target="tpu_custom_call" | custom-call | flops 4000000000 | tf_op jit(solution)/shard_map/layer_norm/pallas_call | solution.py:97
  13.8 1.7 %collective-permute-done.1.after_ref = bf16[16,1536]{1,0:T(8,128)(2,1)S(1)} collective-permute-done((bf16[16,1536]{1,0:T(8,128)(2,1)}, bf16[16,1536]{1,0:T(8,128)(2,1)S(1)}, u32[]{:S(2)}, u32[]{:S(2)}) %collective-permute-start.1) | collective-permute-done | bytes 49184 | tf_op jit(solution)/shard_map/ppermute | solution.py:368
  16.1 1.5 %collective-permute-done.3.refs_1_ = bf16[384,256]{1,0:T(8,128)(2,1)S(1)} collective-permute-done((bf16[384,256]{1,0:T(8,128)(2,1)}, bf16[384,256]{1,0:T(8,128)(2,1)S(1)}, u32[]{:S(2)}, u32[]{:S(2)}) %collective-permute-start.3) | collective-permute-done | bytes 196640 | tf_op jit(solution)/shard_map/ppermute | solution.py:27
  17.6 2.4 %collective-permute-start.6 = (bf16[384,256]{1,0:T(8,128)(2,1)S(1)}, bf16[384,256]{1,0:T(8,128)(2,1)S(1)}, u32[]{:S(2)}, u32[]{:S(2)}) collective-permute-start(bf16[384,256]{1,0:T(8,128)(2,1)S(1)} %collective-permute-done.3.refs_1_), channel_id=1, source_target_pairs={{0,1},{1,0},{2,3},{3,2},{4,5},{5,4},{6,7},{7,6},{8,9},{9,8},{10,11... | collective-permute-start | bytes 589832 | tf_op jit(solution)/shard_map/ppermute | solution.py:27
  22.9 3.0 %near.1 = (bf16[544,1536]{1,0:T(8,128)(2,1)S(1)}, f32[544,512]{1,0:T(8,128)S(1)}, f32[544,512]{1,0:T(8,128)S(1)}, f32[544,512]{1,0:T(8,128)S(1)}) custom-call(s32[4]{0:T(128)S(1)} %pad_add_fusion.place_ref, bf16[16,1536]{1,0:T(8,128)(2,1)S(1)} %copy-done.5, bf16[512,1536]{1,0:T(8,128)(2,1)S(1)} %layer_norm.1.rows_ref, bf16[16,1536]{1,0:T(8,128)(2,1)S(1)} %copy-done.7, ...), custom_call_target="tpu_custom_call" | custom-call | flops 100000000 | tf_op jit(solution)/shard_map/near/pallas_call | solution.py:138
  25.9 2.1 %collective-permute-done.5.refs_2_ = bf16[384,256]{1,0:T(8,128)(2,1)} collective-permute-done((bf16[384,256]{1,0:T(8,128)(2,1)}, bf16[384,256]{1,0:T(8,128)(2,1)}, u32[]{:S(2)}, u32[]{:S(2)}) %collective-permute-start.5) | collective-permute-done | bytes 196640 | tf_op jit(solution)/shard_map/ppermute | solution.py:27
  28.0 1.6 %collective-permute-done.8.refs_4_ = bf16[384,256]{1,0:T(8,128)(2,1)S(1)} collective-permute-done((bf16[384,256]{1,0:T(8,128)(2,1)}, bf16[384,256]{1,0:T(8,128)(2,1)S(1)}, u32[]{:S(2)}, u32[]{:S(2)}) %collective-permute-start.8) | collective-permute-done | bytes 196640 | tf_op jit(solution)/shard_map/ppermute | solution.py:27
  29.7 3.4 %front.3 = (f32[512,256]{1,0:T(8,128)S(1)}, f32[3,256]{1,0:T(4,128)S(1)}) custom-call(s32[4]{0:T(128)S(1)} %pad_add_fusion.place_ref, bf16[544,1536]{1,0:T(8,128)(2,1)S(1)} %get-tuple-element.51.normed_ref, f32[544,512]{1,0:T(8,128)S(1)} %get-tuple-element.56.refs_0_, bf16[384,256]{1,0:T(8,128)(2,1)} %collective-permute-done.2.refs_1_, ...), custom_call_target="tpu_custom_call" | custom-call | flops 100000000 | tf_op jit(solution)/shard_map/front/pallas_call | solution.py:223
  35.6 2.9 %front.4 = (f32[512,256]{1,0:T(8,128)S(1)}, f32[3,256]{1,0:T(4,128)S(1)}) custom-call(s32[4]{0:T(128)S(1)} %pad_add_fusion.place_ref, bf16[544,1536]{1,0:T(8,128)(2,1)S(1)} %get-tuple-element.51.normed_ref, f32[544,512]{1,0:T(8,128)S(1)} %get-tuple-element.62.refs_0_, bf16[384,256]{1,0:T(8,128)(2,1)S(1)} %collective-permute-done.3.refs_1_, ...), custom_call_target="tpu_custom_call" | custom-call | flops 100000000 | tf_op jit(solution)/shard_map/front/pallas_call | solution.py:223
  38.5 2.9 %front.5 = (f32[512,256]{1,0:T(8,128)S(1)}, f32[1,3,768]{2,1,0:T(4,128)S(1)}) custom-call(s32[4]{0:T(128)S(1)} %pad_add_fusion.place_ref, bf16[544,1536]{1,0:T(8,128)(2,1)S(1)} %get-tuple-element.51.normed_ref, f32[3,256]{1,0:T(4,128)S(1)} %get-tuple-element.58.refs_0_, f32[3,256]{1,0:T(4,128)S(1)} %get-tuple-element.64.refs_1_, ...), custom_call_target="tpu_custom_call" | custom-call | flops 100000000 | tf_op jit(solution)/shard_map/front/pallas_call | solution.py:223
  41.4 1.2 %collective-permute-done.13.refs_9_ = bf16[96,1536]{1,0:T(8,128)(2,1)S(1)} collective-permute-done((bf16[96,1536]{1,0:T(8,128)(2,1)S(1)}, bf16[96,1536]{1,0:T(8,128)(2,1)S(1)}, u32[]{:S(2)}, u32[]{:S(2)}) %collective-permute-start.13) | collective-permute-done | bytes 294944 | tf_op jit(solution)/shard_map/ppermute | solution.py:27
  44.4 1.7 %collective-permute-start.16 = (f32[1,3,768]{2,1,0:T(4,128)S(1)}, f32[1,3,768]{2,1,0:T(4,128)S(1)}, u32[]{:S(2)}, u32[]{:S(2)}) collective-permute-start(f32[1,3,768]{2,1,0:T(4,128)S(1)} %pad_maximum_fusion), channel_id=1, source_target_pairs={{0,1},{1,0},{2,3},{3,2},{4,5},{5,4},{6,7},{7,6},{8,9},{9,8},{10,11... | collective-permute-start | bytes 27656 | tf_op jit(solution)/shard_map/ppermute | solution.py:396
  46.1 1.2 %collective-permute-start.17 = (f32[1,3,768]{2,1,0:T(4,128)S(1)}, f32[1,3,768]{2,1,0:T(4,128)S(1)}, u32[]{:S(2)}, u32[]{:S(2)}) collective-permute-start(f32[1,3,768]{2,1,0:T(4,128)S(1)} %pad_maximum_fusion), channel_id=1, source_target_pairs={{0,17},{1,16},{2,19},{3,18},{4,21},{5,20},{6,23},{7,22},{8,25},{9,... | collective-permute-start | bytes 27656 | tf_op jit(solution)/shard_map/ppermute | solution.py:396
  48.1 2.6 %collective-permute-done.17 = f32[1,3,768]{2,1,0:T(4,128)S(1)} collective-permute-done((f32[1,3,768]{2,1,0:T(4,128)S(1)}, f32[1,3,768]{2,1,0:T(4,128)S(1)}, u32[]{:S(2)}, u32[]{:S(2)}) %collective-permute-start.17) | collective-permute-done | bytes 9248 | tf_op jit(solution)/shard_map/ppermute | solution.py:396
  50.8 6.0 %collective-permute-done.18.refs_10_ = bf16[96,1536]{1,0:T(8,128)(2,1)S(1)} collective-permute-done((bf16[96,1536]{1,0:T(8,128)(2,1)S(1)}, bf16[96,1536]{1,0:T(8,128)(2,1)S(1)}, u32[]{:S(2)}, u32[]{:S(2)}) %collective-permute-start.18) | collective-permute-done | bytes 294944 | tf_op jit(solution)/shard_map/ppermute | solution.py:27
  56.8 2.7 %collective-permute-start.19 = (f32[1,3,768]{2,1,0:T(4,128)S(1)}, f32[1,3,768]{2,1,0:T(4,128)S(1)}, u32[]{:S(2)}, u32[]{:S(2)}) collective-permute-start(f32[1,3,768]{2,1,0:T(4,128)S(1)} %pad_maximum_fusion.1.refs_0_), channel_id=1, source_target_pairs={{0,2},{1,3},{2,0},{3,1},{4,6},{5,7},{6,4},{7,5},{8,10},{9,11},{10,... | collective-permute-start | bytes 27656 | tf_op jit(solution)/shard_map/ppermute | solution.py:396
  59.5 2.6 %collective-permute-start.20 = (f32[1,3,768]{2,1,0:T(4,128)S(1)}, f32[1,3,768]{2,1,0:T(4,128)S(1)}, u32[]{:S(2)}, u32[]{:S(2)}) collective-permute-start(f32[1,3,768]{2,1,0:T(4,128)S(1)} %pad_maximum_fusion.1.refs_0_), channel_id=1, source_target_pairs={{0,4},{1,5},{2,6},{3,7},{4,0},{5,1},{6,2},{7,3},{8,12},{9,13},{10,... | collective-permute-start | bytes 27656 | tf_op jit(solution)/shard_map/ppermute | solution.py:396
  62.1 1.9 %collective-permute-done.20.refs_2_ = f32[1,3,768]{2,1,0:T(4,128)S(1)} collective-permute-done((f32[1,3,768]{2,1,0:T(4,128)S(1)}, f32[1,3,768]{2,1,0:T(4,128)S(1)}, u32[]{:S(2)}, u32[]{:S(2)}) %collective-permute-start.20) | collective-permute-done | bytes 9248 | tf_op jit(solution)/shard_map/ppermute | solution.py:396
  64.1 3.5 %collective-permute-done.21.refs_3_ = f32[1,3,768]{2,1,0:T(4,128)S(1)} collective-permute-done((f32[1,3,768]{2,1,0:T(4,128)S(1)}, f32[1,3,768]{2,1,0:T(4,128)S(1)}, u32[]{:S(2)}, u32[]{:S(2)}) %collective-permute-start.21) | collective-permute-done | bytes 9248 | tf_op jit(solution)/shard_map/ppermute | solution.py:396
  67.6 2.9 %back.1 = bf16[512,1536]{1,0:T(8,128)(2,1)} custom-call(s32[4]{0:T(128)S(1)} %pad_add_fusion.place_ref, f32[1,768]{1,0:T(1,128)S(1)} %broadcast_in_dim.13.gain_ref, f32[1,768]{1,0:T(1,128)S(1)} %broadcast_in_dim.14.shift_ref, f32[1,3,768]{2,1,0:T(4,128)S(1)} %pad_maximum_fusion.1.refs_0_, f32[1,3,768]{2,1,0:T(4,128)S(1)} %collective-permute-done.19.refs_1_, ...), custom_call_target="tpu_custom_call" | custom-call | flops 1000000000 | tf_op jit(solution)/shard_map/back/pallas_call | solution.py:319
  (67 shorter events, 9.8 us)
Async XLA Ops:
  2.8 18.5 %collective-permute-start.4 = (bf16[384,1536]{1,0:T(8,128)(2,1)S(1)}, bf16[384,1536]{1,0:T(8,128)(2,1)}, u32[]{:S(2)}, u32[]{:S(2)}) collective-permute-start(bf16[384,1536]{1,0:T(8,128)(2,1)S(1)} %copy-done), channel_id=1, source_target_pairs={{0,8},{8,0},{16,24},{24,16},{1,9},{9,1},{17,25},{25,17},{2,10},{10... | collective-permute-start | bytes 3538952 | tf_op jit(solution)/shard_map/ppermute | solution.py:27
  3.3 12.8 %collective-permute-start.2 = (bf16[384,256]{1,0:T(8,128)(2,1)}, bf16[384,256]{1,0:T(8,128)(2,1)}, u32[]{:S(2)}, u32[]{:S(2)}) collective-permute-start(bf16[384,256]{1,0:T(8,128)(2,1)} %get-tuple-element.44), channel_id=1, source_target_pairs={{0,16},{8,24},{16,0},{24,8},{1,17},{9,25},{17,1},{25,9},{2,18},{10... | collective-permute-start | bytes 589832 | tf_op jit(solution)/shard_map/ppermute | solution.py:27
  5.9 7.3 %collective-permute-start = (bf16[16,1536]{1,0:T(8,128)(2,1)}, bf16[16,1536]{1,0:T(8,128)(2,1)S(1)}, u32[]{:S(2)}, u32[]{:S(2)}) collective-permute-start(bf16[16,1536]{1,0:T(8,128)(2,1)} %get-tuple-element.42), channel_id=1, source_target_pairs={{0,1},{1,2},{2,3},{3,4},{4,5},{5,6},{6,7},{8,9},{9,10},{10,11},{11... | collective-permute-start | bytes 147464 | tf_op jit(solution)/shard_map/ppermute | solution.py:368
  9.3 6.2 %collective-permute-start.1 = (bf16[16,1536]{1,0:T(8,128)(2,1)}, bf16[16,1536]{1,0:T(8,128)(2,1)S(1)}, u32[]{:S(2)}, u32[]{:S(2)}) collective-permute-start(bf16[16,1536]{1,0:T(8,128)(2,1)} %get-tuple-element.43), channel_id=1, source_target_pairs={{1,0},{2,1},{3,2},{4,3},{5,4},{6,5},{7,6},{9,8},{10,9},{11,10},{12... | collective-permute-start | bytes 147464 | tf_op jit(solution)/shard_map/ppermute | solution.py:368
  10.6 7.0 %collective-permute-start.3 = (bf16[384,256]{1,0:T(8,128)(2,1)}, bf16[384,256]{1,0:T(8,128)(2,1)S(1)}, u32[]{:S(2)}, u32[]{:S(2)}) collective-permute-start(bf16[384,256]{1,0:T(8,128)(2,1)} %get-tuple-element.47), channel_id=1, source_target_pairs={{0,16},{8,24},{16,0},{24,8},{1,17},{9,25},{17,1},{25,9},{2,18},{10... | collective-permute-start | bytes 589832 | tf_op jit(solution)/shard_map/ppermute | solution.py:27
  17.6 8.4 %collective-permute-start.6 = (bf16[384,256]{1,0:T(8,128)(2,1)S(1)}, bf16[384,256]{1,0:T(8,128)(2,1)S(1)}, u32[]{:S(2)}, u32[]{:S(2)}) collective-permute-start(bf16[384,256]{1,0:T(8,128)(2,1)S(1)} %collective-permute-done.3.refs_1_), channel_id=1, source_target_pairs={{0,1},{1,0},{2,3},{3,2},{4,5},{5,4},{6,7},{7,6},{8,9},{9,8},{10,11... | collective-permute-start | bytes 589832 | tf_op jit(solution)/shard_map/ppermute | solution.py:27
  19.9 8.1 %collective-permute-start.5 = (bf16[384,256]{1,0:T(8,128)(2,1)}, bf16[384,256]{1,0:T(8,128)(2,1)}, u32[]{:S(2)}, u32[]{:S(2)}) collective-permute-start(bf16[384,256]{1,0:T(8,128)(2,1)} %collective-permute-done.2.refs_1_), channel_id=1, source_target_pairs={{0,1},{1,0},{2,3},{3,2},{4,5},{5,4},{6,7},{7,6},{8,9},{9,8},{10,11... | collective-permute-start | bytes 589832 | tf_op jit(solution)/shard_map/ppermute | solution.py:27
  20.0 13.1 %collective-permute-start.9 = (bf16[384,512]{1,0:T(8,128)(2,1)}, bf16[384,512]{1,0:T(8,128)(2,1)S(1)}, u32[]{:S(2)}, u32[]{:S(2)}) collective-permute-start(bf16[384,512]{1,0:T(8,128)(2,1)} %get-tuple-element.61), channel_id=1, source_target_pairs={{0,16},{8,24},{16,0},{24,8},{1,17},{9,25},{17,1},{25,9},{2,18},{10... | collective-permute-start | bytes 1179656 | tf_op jit(solution)/shard_map/ppermute | solution.py:27
  21.2 6.8 %collective-permute-start.7 = (bf16[384,256]{1,0:T(8,128)(2,1)}, bf16[384,256]{1,0:T(8,128)(2,1)S(1)}, u32[]{:S(2)}, u32[]{:S(2)}) collective-permute-start(bf16[384,256]{1,0:T(8,128)(2,1)} %collective-permute-done.2.refs_1_), channel_id=1, source_target_pairs={{0,8},{8,0},{16,24},{24,16},{1,9},{9,1},{17,25},{25,17},{2,10},{10... | collective-permute-start | bytes 589832 | tf_op jit(solution)/shard_map/ppermute | solution.py:27
  28.0 1.7 %collective-permute-start.8 = (bf16[384,256]{1,0:T(8,128)(2,1)}, bf16[384,256]{1,0:T(8,128)(2,1)S(1)}, u32[]{:S(2)}, u32[]{:S(2)}) collective-permute-start(bf16[384,256]{1,0:T(8,128)(2,1)} %collective-permute-done.5.refs_2_), channel_id=1, source_target_pairs={{0,8},{8,0},{16,24},{24,16},{1,9},{9,1},{17,25},{25,17},{2,10},{10... | collective-permute-start | bytes 589832 | tf_op jit(solution)/shard_map/ppermute | solution.py:27
  33.1 5.4 %collective-permute-start.12 = (bf16[384,512]{1,0:T(8,128)(2,1)S(1)}, bf16[384,512]{1,0:T(8,128)(2,1)S(1)}, u32[]{:S(2)}, u32[]{:S(2)}) collective-permute-start(bf16[384,512]{1,0:T(8,128)(2,1)S(1)} %collective-permute-done.9.refs_3_), channel_id=1, source_target_pairs={{0,8},{8,0},{16,24},{24,16},{1,9},{9,1},{17,25},{25,17},{2,10},{10... | collective-permute-start | bytes 1179656 | tf_op jit(solution)/shard_map/ppermute | solution.py:27
  33.3 9.3 %collective-permute-start.13 = (bf16[96,1536]{1,0:T(8,128)(2,1)S(1)}, bf16[96,1536]{1,0:T(8,128)(2,1)S(1)}, u32[]{:S(2)}, u32[]{:S(2)}) collective-permute-start(bf16[96,1536]{1,0:T(8,128)(2,1)S(1)} %copy-done.12), channel_id=1, source_target_pairs={{0,16},{8,24},{16,0},{24,8},{1,17},{9,25},{17,1},{25,9},{2,18},{10... | collective-permute-start | bytes 884744 | tf_op jit(solution)/shard_map/ppermute | solution.py:27
  33.8 1.4 %collective-permute-start.10 = (bf16[384,256]{1,0:T(8,128)(2,1)S(1)}, bf16[384,256]{1,0:T(8,128)(2,1)S(1)}, u32[]{:S(2)}, u32[]{:S(2)}) collective-permute-start(bf16[384,256]{1,0:T(8,128)(2,1)S(1)} %collective-permute-done.3.refs_1_), channel_id=1, source_target_pairs={{0,8},{8,0},{16,24},{24,16},{1,9},{9,1},{17,25},{25,17},{2,10},{10... | collective-permute-start | bytes 589832 | tf_op jit(solution)/shard_map/ppermute | solution.py:27
  33.9 1.7 %collective-permute-start.11 = (bf16[384,256]{1,0:T(8,128)(2,1)S(1)}, bf16[384,256]{1,0:T(8,128)(2,1)S(1)}, u32[]{:S(2)}, u32[]{:S(2)}) collective-permute-start(bf16[384,256]{1,0:T(8,128)(2,1)S(1)} %collective-permute-done.6.refs_2_), channel_id=1, source_target_pairs={{0,8},{8,0},{16,24},{24,16},{1,9},{9,1},{17,25},{25,17},{2,10},{10... | collective-permute-start | bytes 589832 | tf_op jit(solution)/shard_map/ppermute | solution.py:27
  43.8 4.2 %collective-permute-start.15 = (f32[1,3,768]{2,1,0:T(4,128)S(1)}, f32[1,3,768]{2,1,0:T(4,128)S(1)}, u32[]{:S(2)}, u32[]{:S(2)}) collective-permute-start(f32[1,3,768]{2,1,0:T(4,128)S(1)} %pad_maximum_fusion), channel_id=1, source_target_pairs={{0,16},{1,17},{2,18},{3,19},{4,20},{5,21},{6,22},{7,23},{8,24},{9,... | collective-permute-start | bytes 27656 | tf_op jit(solution)/shard_map/ppermute | solution.py:396
  44.4 3.7 %collective-permute-start.16 = (f32[1,3,768]{2,1,0:T(4,128)S(1)}, f32[1,3,768]{2,1,0:T(4,128)S(1)}, u32[]{:S(2)}, u32[]{:S(2)}) collective-permute-start(f32[1,3,768]{2,1,0:T(4,128)S(1)} %pad_maximum_fusion), channel_id=1, source_target_pairs={{0,1},{1,0},{2,3},{3,2},{4,5},{5,4},{6,7},{7,6},{8,9},{9,8},{10,11... | collective-permute-start | bytes 27656 | tf_op jit(solution)/shard_map/ppermute | solution.py:396
  46.1 4.6 %collective-permute-start.17 = (f32[1,3,768]{2,1,0:T(4,128)S(1)}, f32[1,3,768]{2,1,0:T(4,128)S(1)}, u32[]{:S(2)}, u32[]{:S(2)}) collective-permute-start(f32[1,3,768]{2,1,0:T(4,128)S(1)} %pad_maximum_fusion), channel_id=1, source_target_pairs={{0,17},{1,16},{2,19},{3,18},{4,21},{5,20},{6,23},{7,22},{8,25},{9,... | collective-permute-start | bytes 27656 | tf_op jit(solution)/shard_map/ppermute | solution.py:396
  47.4 14.7 %collective-permute-start.22 = (bf16[192,1536]{1,0:T(8,128)(2,1)S(1)}, bf16[192,1536]{1,0:T(8,128)(2,1)S(1)}, u32[]{:S(2)}, u32[]{:S(2)}) collective-permute-start(bf16[192,1536]{1,0:T(8,128)(2,1)S(1)} %copy-done.1), channel_id=1, source_target_pairs={{0,8},{8,0},{16,24},{24,16},{1,9},{9,1},{17,25},{25,17},{2,10},{10... | collective-permute-start | bytes 1769480 | tf_op jit(solution)/shard_map/ppermute | solution.py:27
  47.4 9.4 %collective-permute-start.18 = (bf16[96,1536]{1,0:T(8,128)(2,1)S(1)}, bf16[96,1536]{1,0:T(8,128)(2,1)S(1)}, u32[]{:S(2)}, u32[]{:S(2)}) collective-permute-start(bf16[96,1536]{1,0:T(8,128)(2,1)S(1)} %copy-done.11), channel_id=1, source_target_pairs={{0,16},{8,24},{16,0},{24,8},{1,17},{9,25},{17,1},{25,9},{2,18},{10... | collective-permute-start | bytes 884744 | tf_op jit(solution)/shard_map/ppermute | solution.py:27
  48.0 19.6 %collective-permute-start.23 = (bf16[96,1536]{1,0:T(8,128)(2,1)S(1)}, bf16[96,1536]{1,0:T(8,128)(2,1)S(1)}, u32[]{:S(2)}, u32[]{:S(2)}) collective-permute-start(bf16[96,1536]{1,0:T(8,128)(2,1)S(1)} %collective-permute-done.13.refs_9_), channel_id=1, source_target_pairs={{0,8},{8,0},{16,24},{24,16},{1,9},{9,1},{17,25},{25,17},{2,10},{10... | collective-permute-start | bytes 884744 | tf_op jit(solution)/shard_map/ppermute | solution.py:27
  56.8 10.8 %collective-permute-start.24 = (bf16[96,1536]{1,0:T(8,128)(2,1)S(1)}, bf16[96,1536]{1,0:T(8,128)(2,1)S(1)}, u32[]{:S(2)}, u32[]{:S(2)}) collective-permute-start(bf16[96,1536]{1,0:T(8,128)(2,1)S(1)} %collective-permute-done.18.refs_10_), channel_id=1, source_target_pairs={{0,8},{8,0},{16,24},{24,16},{1,9},{9,1},{17,25},{25,17},{2,10},{10... | collective-permute-start | bytes 884744 | tf_op jit(solution)/shard_map/ppermute | solution.py:27
  56.8 5.3 %collective-permute-start.19 = (f32[1,3,768]{2,1,0:T(4,128)S(1)}, f32[1,3,768]{2,1,0:T(4,128)S(1)}, u32[]{:S(2)}, u32[]{:S(2)}) collective-permute-start(f32[1,3,768]{2,1,0:T(4,128)S(1)} %pad_maximum_fusion.1.refs_0_), channel_id=1, source_target_pairs={{0,2},{1,3},{2,0},{3,1},{4,6},{5,7},{6,4},{7,5},{8,10},{9,11},{10,... | collective-permute-start | bytes 27656 | tf_op jit(solution)/shard_map/ppermute | solution.py:396
  59.5 4.6 %collective-permute-start.20 = (f32[1,3,768]{2,1,0:T(4,128)S(1)}, f32[1,3,768]{2,1,0:T(4,128)S(1)}, u32[]{:S(2)}, u32[]{:S(2)}) collective-permute-start(f32[1,3,768]{2,1,0:T(4,128)S(1)} %pad_maximum_fusion.1.refs_0_), channel_id=1, source_target_pairs={{0,4},{1,5},{2,6},{3,7},{4,0},{5,1},{6,2},{7,3},{8,12},{9,13},{10,... | collective-permute-start | bytes 27656 | tf_op jit(solution)/shard_map/ppermute | solution.py:396
  62.1 5.5 %collective-permute-start.21 = (f32[1,3,768]{2,1,0:T(4,128)S(1)}, f32[1,3,768]{2,1,0:T(4,128)S(1)}, u32[]{:S(2)}, u32[]{:S(2)}) collective-permute-start(f32[1,3,768]{2,1,0:T(4,128)S(1)} %pad_maximum_fusion.1.refs_0_), channel_id=1, source_target_pairs={{0,6},{1,7},{2,4},{3,5},{4,2},{5,3},{6,0},{7,1},{8,14},{9,15},{10,... | collective-permute-start | bytes 27656 | tf_op jit(solution)/shard_map/ppermute | solution.py:396
  (14 other events, 106.3 us)

commit v2 on v1

--- a/solution.py
+++ b/solution.py
@@ -11,8 +11,7 @@
 LANES = 128
 MIB = 1024 * 1024
 VMEM = pltpu.VMEM
-ORDER = (0, 1, 2)
-SPLIT = (0, 1)
+ORDER = (2, 0, 1)
 
 
 def cost(flops):
@@ -25,54 +24,6 @@
 
 def swap(value, axis, bit):
     return lax.ppermute(value, axis, [(i, i ^ bit) for i in range(lax.axis_size(axis))])
-
-
-def cut_kernel(order, split, wide, parity_ref, shard_ref, rows_ref, out_shard_ref, *refs):
-    *part_refs, head_ref, tail_ref, upper_ref, lower_ref, sems = refs
-    channels = shard_ref.shape[1] // 2
-    row_count = rows_ref.shape[0]
-    copies = []
-
-    def copy(source, target):
-        copies.append(pltpu.make_async_copy(source, target, sems.at[len(copies)]))
-        copies[-1].start()
-
-    side = parity_ref[0] * channels
-    for block, ref in zip(order, part_refs):
-        if block in split:
-            copy(shard_ref.at[:, pl.ds(pl.multiple_of(side + block * wide, wide), wide)], ref)
-        else:
-            for i in range(2):
-                at = i * channels + block * wide
-                copy(shard_ref.at[:, at : at + wide], ref.at[:, i * wide : (i + 1) * wide])
-    copy(rows_ref.at[0:HALO, :], head_ref)
-    copy(rows_ref.at[row_count - HALO : row_count, :], tail_ref)
-    depth = upper_ref.shape[0]
-    copy(out_shard_ref.at[0:depth, :], upper_ref)
-    copy(out_shard_ref.at[depth : 2 * depth, :], lower_ref)
-    for started in copies:
-        started.wait()
-
-
-def cut(parity, shard, rows, out_shard, wide):
-    depth, width = shard.shape
-    shapes = [(depth, wide if block in SPLIT else 2 * wide) for block in ORDER]
-    shapes += [(HALO, width)] * 2 + [(out_shard.shape[0] // 2, out_shard.shape[1])] * 2
-    return pl.pallas_call(
-        functools.partial(cut_kernel, ORDER, SPLIT, wide),
-        out_shape=[jax.ShapeDtypeStruct(shape, jnp.bfloat16) for shape in shapes],
-        in_specs=[
-            pl.BlockSpec(memory_space=pltpu.SMEM),
-            pl.BlockSpec(memory_space=pltpu.HBM),
-            pl.BlockSpec(memory_space=pltpu.HBM),
-            pl.BlockSpec(memory_space=pltpu.HBM),
-        ],
-        out_specs=[pl.BlockSpec(memory_space=VMEM)] * len(shapes),
-        scratch_shapes=[pltpu.SemaphoreType.DMA((8,))],
-        compiler_params=params(56),
-        cost_estimate=cost(10**8),
-        name="cut",
-    )(parity, shard, rows, out_shard)
 
 
 def normalize(values, gain):
@@ -100,29 +51,33 @@
         in_specs=[pl.BlockSpec(memory_space=VMEM)] * 2,
         out_specs=pl.BlockSpec(memory_space=VMEM),
         compiler_params=params(4),
-        cost_estimate=cost(4 * 10**9),
+        cost_estimate=cost(10**8),
         name="layer_norm",
     )(rows, gain)
 
 
-def near_kernel(place_ref, before_ref, rows_ref, after_ref, gain_ref, *refs):
-    *weight_refs, ext_ref, first_ref, second_ref, third_ref, weights = refs
+def near_kernel(place_ref, rows_ref, inner_ref, outer_ref, gain_ref, *refs):
     row_count = rows_ref.shape[0]
     gain = gain_ref[...]
-    ext_ref[0:HALO, :] = normalize(before_ref[...], gain)
+    *weight_refs, ext_ref = refs[:3] if len(refs) > 1 else refs
+    odd = place_ref[3]
+    at = pl.multiple_of((1 - odd) * (HALO + row_count), HALO)
+    ext_ref[pl.ds(at, HALO), :] = normalize(inner_ref[...], gain)
+    at = pl.multiple_of(odd * (HALO + row_count), HALO)
+    ext_ref[pl.ds(at, HALO), :] = normalize(outer_ref[...], gain)
     ext_ref[HALO : HALO + row_count, :] = rows_ref[...]
-    ext_ref[HALO + row_count :, :] = normalize(after_ref[...], gain)
     if not weight_refs:
         return
+    *out_refs, weights = refs[3:]
     own = place_ref[0]
     depth, width = weight_refs[0].shape
     for i, weight_ref in enumerate(weight_refs):
         at = pl.multiple_of(lax.bitwise_xor(own % 2, i) * depth, depth)
         weights[pl.ds(at, depth), :] = weight_ref[...]
     near = pl.ds(pl.multiple_of(own // 2 * (2 * depth), 2 * depth), 2 * depth)
-    wide = first_ref.shape[1] // 2
+    wide = out_refs[0].shape[1] // 2
     channels = width // 2
-    for block, out_ref in enumerate((first_ref, second_ref, third_ref)):
+    for block, out_ref in enumerate(out_refs):
         for i in range(2):
             columns = slice(i * channels + block * wide, i * channels + (block + 1) * wide)
             out_ref[:, i * wide : (i + 1) * wide] = jnp.dot(
@@ -130,22 +85,25 @@
             )
 
 
-def near_product(place, before, rows, after, gain, shards):
+def near_product(place, rows, inner, outer, gain, *shards):
     row_count, width = rows.shape
     ext_rows = row_count + 2 * HALO
-    partial = jax.ShapeDtypeStruct((ext_rows, width // 3), jnp.float32)
-    depth = 2 * shards[0].shape[0] if shards else 16
+    shapes = [jax.ShapeDtypeStruct((ext_rows, width), jnp.bfloat16)]
+    scratch = []
+    if shards:
+        shapes += [jax.ShapeDtypeStruct((ext_rows, width // 3), jnp.float32)] * 3
+        scratch.append(VMEM((2 * shards[0].shape[0], width), jnp.bfloat16))
     return pl.pallas_call(
         near_kernel,
-        out_shape=(jax.ShapeDtypeStruct((ext_rows, width), jnp.bfloat16), partial, partial, partial),
+        out_shape=shapes,
         in_specs=[pl.BlockSpec(memory_space=pltpu.SMEM)]
         + [pl.BlockSpec(memory_space=VMEM)] * (4 + len(shards)),
-        out_specs=[pl.BlockSpec(memory_space=VMEM)] * 4,
-        scratch_shapes=[VMEM((depth, width), jnp.bfloat16)],
+        out_specs=[pl.BlockSpec(memory_space=VMEM)] * len(shapes),
+        scratch_shapes=scratch,
         compiler_params=params(8),
         cost_estimate=cost(10**8),
         name="near",
-    )(place, before, rows, after, gain, *shards)
+    )(place, rows, inner, outer, gain, *shards)
 
 
 def front_kernel(block, earlier, place_ref, normed_ref, *refs):
@@ -275,14 +233,17 @@
     convs, weight_refs = conv_refs[:3], conv_refs[3:]
     row_count, wide = convs[0].shape
     if len(weight_refs) > 1:
-        depth = weight_refs[0].shape[0]
+        depth, width = weight_refs[0].shape
         for i, weight_ref in enumerate(weight_refs[:2]):
             at = pl.multiple_of(lax.bitwise_xor(place_ref[0], i) * depth, depth)
             weights[pl.ds(at, depth), :] = weight_ref[...]
-        half = depth // 2
         for i, weight_ref in enumerate(weight_refs[2:]):
-            at = lax.bitwise_xor(place_ref[0], 2 + i // 2) * depth + i % 2 * half
-            weights[pl.ds(pl.multiple_of(at, half), half), :] = weight_ref[...]
+            rows, columns = weight_ref.shape
+            at = lax.bitwise_xor(place_ref[0], 2 + i // 4) * depth
+            at += lax.bitwise_xor(place_ref[3], i // 2 % 2) * rows
+            column = lax.bitwise_xor(place_ref[4], i % 2) * columns
+            here = pl.ds(pl.multiple_of(at, rows), rows), pl.ds(pl.multiple_of(column, columns), columns)
+            weights[here] = weight_ref[...]
     else:
         weights[...] = weight_refs[0][...]
     mean, square, count = merged(rows_of(stat_refs))
@@ -350,8 +311,8 @@
     direct = fsdp_count == 4 and ctx_count == 8
     rows = frames[0]
     gain = ln_gain[None]
-    parity = lax.rem(ctx, 2)
-    place = jnp.stack([fsdp, ctx * row_count, lengths[0], parity]).astype(jnp.int32)
+    parity, pair = lax.rem(ctx, 2), lax.rem(ctx // 2, 2)
+    place = jnp.stack([fsdp, ctx * row_count, lengths[0], parity, pair]).astype(jnp.int32)
     ends = ctx_count - 1
     down, up = [(i, i + 1) for i in range(ends)], [(i + 1, i) for i in range(ends)]
     both = ("fsdp", "ctx")
@@ -361,35 +322,55 @@
         return front_block(block, wide, place, normed, weights, dw_kernel, *extra)
 
     if direct:
-        *parts, head, tail, upper, lower = cut(parity[None].astype(jnp.int32), w_in, rows, w_out, wide)
-        over_x = {block: [swap(part, "fsdp", 2)] for block, part in zip(ORDER, parts)}
-        parts[0], shard = tie(parts[0], w_in)
-        shards = [w_in, swap(shard, "fsdp", 1)]
-        before, after = lax.ppermute(tail, "ctx", down), lax.ppermute(head, "ctx", up)
+        last = row_count - HALO
+        out_depth, out_width = w_out.shape[0] // 2, model_width // 2
+
+        def columns(shard, block):
+            at = block * wide
+            return jnp.concatenate([shard[:, at : at + wide], shard[:, channels + at : channels + at + wide]], 1)
+
+        half = lax.dynamic_slice_in_dim(w_in, parity * channels + 2 * wide, wide, axis=1)
+        over_x = {2: [swap(half, "fsdp", 2)]}
+        half, later_in, later_out, later_rows = tie(half, w_in, w_out, rows)
+        block = columns(later_in, 0)
+        over_x[0] = [swap(block, "fsdp", 2)]
+        quarter = lax.dynamic_slice(later_out, (parity * out_depth, pair * out_width), (out_depth, out_width))
+        quarter = swap(quarter, "fsdp", 2)
+        inner = lax.dynamic_slice_in_dim(later_rows, (1 - parity) * last, HALO, axis=0)
+        outer = lax.dynamic_slice_in_dim(later_rows, parity * last, HALO, axis=0)
+        inner = swap(inner, "ctx", 1)
+        pairs = [(i, i + 1) for i in range(1, ends, 2)]
+        outer = lax.ppermute(outer, "ctx", pairs + [(j, i) for i, j in pairs])
+        across = swap(later_in, "fsdp", 1)
         normed = normalize_rows(rows, gain)
-        normed, before, after, over_x[0][0] = tie(normed, before, after, over_x[0][0])
-        over_x[0].append(swap(over_x[0][0], "ctx", 1))
-        normed, over_x[1][0] = tie(normed, over_x[1][0])
-        over_x[1].append(swap(over_x[1][0], "ctx", 1))
-        normed, *partials = near_product(place, before, normed, after, gain, shards)
-        partials[0], over_x[0][1], over_x[1][1], w_out, upper = tie(
-            partials[0], over_x[0][1], over_x[1][1], w_out, upper
+        normed, over_x[2][0], later_in = tie(normed, over_x[2][0], later_in)
+        over_x[2].append(swap(over_x[2][0], "ctx", 1))
+        beyond_half = swap(over_x[2][0], "fsdp", 1)
+        normed, part = tie(normed, columns(later_in, 1))
+        over_x[1] = [swap(part, "fsdp", 2)]
+        normed, *partials = near_product(place, normed, inner, outer, gain, w_in, across)
+        partials[2], beyond_half, quarter = tie(partials[2], beyond_half, quarter)
+        quarters = [quarter, swap(quarter, "ctx", 2), swap(quarter, "ctx", 1)]
+        partials[2], over_x[2][1], w_out = tie(partials[2], over_x[2][1], w_out)
+
+        beyond_two = [beyond_half, swap(over_x[2][1], "fsdp", 1)]
+        partials[2], over_x[0][0] = tie(partials[2], over_x[0][0])
+        beyond_zero = swap(over_x[0][0], "fsdp", 1)
+        conv_one, stat_one = front(2, [partials[2], *over_x[2], *beyond_two])
+        conv_one, partials[0], *quarters = tie(conv_one, partials[0], *quarters)
+        quarters.append(swap(quarters[1], "ctx", 1))
+        beyond_quarters = [swap(part, "fsdp", 1) for part in quarters[:3]]
+        conv_two, stat_two = front(0, [partials[0], *over_x[0], beyond_zero])
+        conv_two, over_x[1][0] = tie(conv_two, over_x[1][0])
+        across_out = swap(w_out, "fsdp", 1)
+        beyond_one = swap(over_x[1][0], "fsdp", 1)
+        conv_three, stats = front(1, [partials[1], *over_x[1], beyond_one], (stat_one, stat_two), 1)
+        stats, across_out, quarters[3], *beyond_quarters = tie(
+            stats, across_out, quarters[3], *beyond_quarters
         )
-        upper = swap(upper, "fsdp", 2)
-        out_weights = [w_out, swap(w_out, "fsdp", 1)]
-
-        def weights_of(block):
-            return [partials[block], *over_x[block], *(swap(part, "fsdp", 1) for part in over_x[block])]
-
-        weights = [weights_of(0), weights_of(1)]
-        conv_one, stat_one = front(0, weights[0])
-        conv_one, weights[1][0], over_x[2][0] = tie(conv_one, weights[1][0], over_x[2][0])
-        _, lower = tie(over_x[2][0], lower)
-        lower = swap(lower, "fsdp", 2)
-        weights.append(weights_of(2))
-        conv_two, stat_two = front(1, weights[1])
-        conv_three, stats = front(2, weights[2], (stat_one, stat_two), 1)
-        convs = [conv_one, conv_two, conv_three]
+        beyond_quarters.append(swap(quarters[3], "fsdp", 1))
+        out_weights = [w_out, across_out, *quarters, *beyond_quarters]
+        convs = [conv_two, conv_three, conv_one]
 
         def others(flips):
             return [
@@ -404,19 +385,17 @@
         def union(parts):
             return jnp.stack(merged([[part[:, i] for i in range(3)] for part in parts]), 1)
 
-        stats, upper = tie(stats, upper)
         stats = union([stats] + others([(1, 0)]))
         stats = union([stats] + others([(2, 0), (0, 1), (2, 1)]))
-        stats, lower = tie(stats, lower)
-        out_weights += [upper, lower, swap(upper, "fsdp", 1), swap(lower, "fsdp", 1)]
         stats = [stats] + others([(0, 2), (0, 4), (0, 6)])
     else:
         full_in = lax.all_gather(w_in, "fsdp", axis=0, tiled=True)
         out_weights = [lax.all_gather(w_out, "fsdp", axis=0, tiled=True)]
         before = lax.ppermute(rows[-HALO:], "ctx", down)
         after = lax.ppermute(rows[:HALO], "ctx", up)
-        normed = normalize_rows(rows, gain)
-        normed, *_ = near_product(place, before, normed, after, gain, [])
+        inner = jnp.where(parity == 0, after, before)
+        outer = jnp.where(parity == 0, before, after)
+        (normed,) = near_product(place, normalize_rows(rows, gain), inner, outer, gain)
         near_by = 2 if ctx_count % 2 == 0 else 1
         groups = [
             [member(f, p + i) for f in range(fsdp_count) for i in range(near_by)]

time: 70.8 us -> 64.7 us (0.914)
  waiting for transfers between devices: 24.5 us -> 13.6 us
  starting transfers between devices: 22.2 us -> 27.4 us
  Pallas kernels: 19.8 us -> 16.6 us
  local copies, waits for them, and re-layouts: 2.9 us -> 5.05 us
  other arithmetic: 0.18 us -> 0.91 us
    ppermute x16 -> x19, starting transfers between devices: 8.67 us -> 18 us  [swap(): lax.ppermute(value, axis, [(i, i ^ bit) for i in range(lax.axis_size(axis...]
    ppermute x16 -> x19, waiting for transfers between devices: 13.6 us -> 5.24 us  [swap(): lax.ppermute(value, axis, [(i, i ^ bit) for i in range(lax.axis_size(axis...]
    dynamic_slice x0 -> x3, local copies, waits for them, and re-layouts: none -> 3.85 us  [the longest x1 1.69 us: body(): lax.dynamic_slice_in_dim(w_in, parity * channels + 2 * wide, wide, axis=1)]
    ppermute x2 -> x1, starting transfers between devices: 4.71 us -> 1.26 us  [body(): outer = lax.ppermute(outer, 'ctx', pairs + [(j, i) for i, j in pairs])]
    pallas_call x2 -> x1, Pallas kernels: 5.77 us -> 2.66 us  [near_product(): pl.pallas_call(near_kernel, out_shape=shapes, in_specs=[pl.BlockSpec(memo...]
    unnamed x26 -> x16, local copies, waits for them, and re-layouts: 2.88 us -> 0.03 us
    ppermute x2 -> x1, waiting for transfers between devices: 1.73 us -> 0.01 us  [body(): outer = lax.ppermute(outer, 'ctx', pairs + [(j, i) for i, j in pairs])]
    slice x0 -> x2, local copies, waits for them, and re-layouts: none -> 1.08 us  [columns(): shard[:, at:at + wide]]
  transfers between devices with their start and end apart: 25 -> 27, of which waited for: 12 -> 10; matrix products, arithmetic and copies ran while one was open for 0% -> 7% of each run, Pallas kernels for 20% -> 21%
where the time goes in v2:
time: 64.7 us; the launch traced here: 64.4 us
  starting transfers between devices  27.4 us (42%)
  Pallas kernels  16.6 us (26%)
  waiting for transfers between devices  13.6 us (21%)
  local copies, waits for them, and re-layouts  5.05 us (8%)
  other arithmetic  0.91 us (1%)
  between operations  0.86 us (1%)
    ppermute x19, starting transfers between devices, swap(): lax.ppermute(value, axis, [(i, i ^ bit) for i in range(lax.axis_size(axis...  18 us
    pallas_call x3, Pallas kernels, front_block(): pl.pallas_call(functools.partial(front_kernel, block, len(earlier)), out_...  9.12 us
    ppermute x7, waiting for transfers between devices, others(): lax.ppermute(stats, both, [(member(f, p), member(f ^ df, p ^ dp)) for f i...  8.37 us
    ppermute x7, starting transfers between devices, others(): lax.ppermute(stats, both, [(member(f, p), member(f ^ df, p ^ dp)) for f i...  8.08 us
    ppermute x19, waiting for transfers between devices, swap(): lax.ppermute(value, axis, [(i, i ^ bit) for i in range(lax.axis_size(axis...  5.24 us
    pallas_call x1, Pallas kernels, back(): pl.pallas_call(functools.partial(back_kernel, len(stats)), out_shape=jax....  2.93 us
    pallas_call x1, Pallas kernels, near_product(): pl.pallas_call(near_kernel, out_shape=shapes, in_specs=[pl.BlockSpec(memo...  2.66 us
    pallas_call x1, Pallas kernels, normalize_rows(): pl.pallas_call(norm_kernel, out_shape=jax.ShapeDtypeStruct((row_count, wi...  1.91 us
  transfers between devices with their start and end apart: 27, of which 10 were waited for; matrix products, arithmetic and copies ran while one was open for 7% of the time, Pallas kernels for 21%

profile of v2, /device:TPU:0, one launch (start us, length us, event | category | flops | bytes accessed | tf_op | source)
XLA Modules:
  0.0 64.4 jit_solution(5599160853193211786)
XLA Ops:
  0.0 1.7 %constant_dynamic-slice_fusion.2 = bf16[384,256]{1,0:T(8,128)(2,1)} fusion(bf16[384,1536]{1,0:T(8,128)(2,1)} %refs_0_.1, s32[]{:T(128)S(6)} %select_n.21), kind=kLoop, calls=%fused_computation.25 | loop fusion | bytes 393220 | tf_op jit(solution)/shard_map/dynamic_slice | solution.py:332
  2.2 2.5 %collective-permute-start = (bf16[384,256]{1,0:T(8,128)(2,1)}, bf16[384,256]{1,0:T(8,128)(2,1)S(1)}, u32[]{:S(2)}, u32[]{:S(2)}) collective-permute-start(bf16[384,256]{1,0:T(8,128)(2,1)} %constant_dynamic-slice_fusion.2), channel_id=1, source_target_pairs={{0,16},{8,24},{16,0},{24,8},{1,17},{9,25},{17,1},{25,9},{2,18},{10... | collective-permute-start | bytes 589832 | tf_op jit(solution)/shard_map/ppermute | solution.py:26
  4.6 1.5 %constant_dynamic-slice_fusion = (bf16[16,1536]{1,0:T(8,128)(2,1)}, bf16[16,1536]{1,0:T(8,128)(2,1)}) fusion(bf16[512,1536]{1,0:T(8,128)(2,1)} %bitcast.6, s32[]{:T(128)S(6)} %select_n.23, s32[]{:T(128)S(6)} %select_n.22), kind=kLoop, calls=%fused_computation.23 | loop fusion | bytes 196616 | tf_op jit(solution)/shard_map/dynamic_slice | solution.py:340
  6.1 1.5 %collective-permute-start.1 = (bf16[16,1536]{1,0:T(8,128)(2,1)}, bf16[16,1536]{1,0:T(8,128)(2,1)}, u32[]{:S(2)}, u32[]{:S(2)}) collective-permute-start(bf16[16,1536]{1,0:T(8,128)(2,1)} %get-tuple-element.90), channel_id=1, source_target_pairs={{0,1},{1,0},{2,3},{3,2},{4,5},{5,4},{6,7},{7,6},{8,9},{9,8},{10,11... | collective-permute-start | bytes 147464 | tf_op jit(solution)/shard_map/ppermute | solution.py:26
  12.7 1.9 %layer_norm.1.rows_ref = bf16[512,1536]{1,0:T(8,128)(2,1)S(1)} custom-call(bf16[512,1536]{1,0:T(8,128)(2,1)S(1)} %bitcast.7, f32[1,1536]{1,0:T(1,128)S(1)} %broadcast_in_dim.14.gain_ref), custom_call_target="tpu_custom_call" | custom-call | flops 100000000 | tf_op jit(solution)/shard_map/layer_norm/pallas_call | solution.py:48
  14.7 1.6 %collective-permute-start.5 = (bf16[96,768]{1,0:T(8,128)(2,1)S(1)}, bf16[96,768]{1,0:T(8,128)(2,1)S(1)}, u32[]{:S(2)}, u32[]{:S(2)}) collective-permute-start(bf16[96,768]{1,0:T(8,128)(2,1)S(1)} %copy-done.4), channel_id=1, source_target_pairs={{0,16},{8,24},{16,0},{24,8},{1,17},{9,25},{17,1},{25,9},{2,18},{10... | collective-permute-start | bytes 442376 | tf_op jit(solution)/shard_map/ppermute | solution.py:26
  16.2 3.7 %collective-permute-start.6 = (bf16[384,256]{1,0:T(8,128)(2,1)S(1)}, bf16[384,256]{1,0:T(8,128)(2,1)S(1)}, u32[]{:S(2)}, u32[]{:S(2)}) collective-permute-start(bf16[384,256]{1,0:T(8,128)(2,1)S(1)} %collective-permute-done.refs_1_), channel_id=1, source_target_pairs={{0,1},{1,0},{2,3},{3,2},{4,5},{5,4},{6,7},{7,6},{8,9},{9,8},{10,11... | collective-permute-start | bytes 589832 | tf_op jit(solution)/shard_map/ppermute | solution.py:26
  20.1 2.7 %near.1 = (bf16[544,1536]{1,0:T(8,128)(2,1)S(1)}, f32[544,512]{1,0:T(8,128)S(1)}, f32[544,512]{1,0:T(8,128)S(1)}, f32[544,512]{1,0:T(8,128)S(1)}) custom-call(s32[5]{0:T(128)S(1)} %stack.31.place_ref, bf16[512,1536]{1,0:T(8,128)(2,1)S(1)} %layer_norm.1.rows_ref, bf16[16,1536]{1,0:T(8,128)(2,1)} %collective-permute-done.1.inner_ref, ...), custom_call_target="tpu_custom_call" | custom-call | flops 100000000 | tf_op jit(solution)/shard_map/near/pallas_call | solution.py:96
  22.7 2.3 %collective-permute-done.5.refs_9_ = bf16[96,768]{1,0:T(8,128)(2,1)S(1)} collective-permute-done((bf16[96,768]{1,0:T(8,128)(2,1)S(1)}, bf16[96,768]{1,0:T(8,128)(2,1)S(1)}, u32[]{:S(2)}, u32[]{:S(2)}) %collective-permute-start.5) | collective-permute-done | bytes 147488 | tf_op jit(solution)/shard_map/ppermute | solution.py:26
  26.3 3.1 %collective-permute-start.10 = (bf16[96,768]{1,0:T(8,128)(2,1)S(1)}, bf16[96,768]{1,0:T(8,128)(2,1)S(1)}, u32[]{:S(2)}, u32[]{:S(2)}) collective-permute-start(bf16[96,768]{1,0:T(8,128)(2,1)S(1)} %collective-permute-done.5.refs_9_), channel_id=1, source_target_pairs={{0,1},{1,0},{2,3},{3,2},{4,5},{5,4},{6,7},{7,6},{8,9},{9,8},{10,11... | collective-permute-start | bytes 442376 | tf_op jit(solution)/shard_map/ppermute | solution.py:26
  29.3 1.6 %collective-permute-start.9 = (bf16[96,768]{1,0:T(8,128)(2,1)S(1)}, bf16[96,768]{1,0:T(8,128)(2,1)S(1)}, u32[]{:S(2)}, u32[]{:S(2)}) collective-permute-start(bf16[96,768]{1,0:T(8,128)(2,1)S(1)} %collective-permute-done.5.refs_9_), channel_id=1, source_target_pairs={{0,2},{1,3},{2,0},{3,1},{4,6},{5,7},{6,4},{7,5},{8,10},{9,11},{10,... | collective-permute-start | bytes 442376 | tf_op jit(solution)/shard_map/ppermute | solution.py:26
  30.9 2.9 %front.3 = (f32[512,256]{1,0:T(8,128)S(1)}, f32[3,256]{1,0:T(4,128)S(1)}) custom-call(s32[5]{0:T(128)S(1)} %stack.31.place_ref, bf16[544,1536]{1,0:T(8,128)(2,1)S(1)} %get-tuple-element.49.normed_ref, f32[544,512]{1,0:T(8,128)S(1)} %get-tuple-element.55.refs_0_, bf16[384,256]{1,0:T(8,128)(2,1)S(1)} %collective-permute-done.refs_1_, ...), custom_call_target="tpu_custom_call" | custom-call | flops 100000000 | tf_op jit(solution)/shard_map/front/pallas_call | solution.py:181
  35.2 3.4 %front.4 = (f32[512,256]{1,0:T(8,128)S(1)}, f32[3,256]{1,0:T(4,128)S(1)}) custom-call(s32[5]{0:T(128)S(1)} %stack.31.place_ref, bf16[544,1536]{1,0:T(8,128)(2,1)S(1)} %get-tuple-element.49.normed_ref, f32[544,512]{1,0:T(8,128)S(1)} %get-tuple-element.62.refs_0_, bf16[384,512]{1,0:T(8,128)(2,1)} %collective-permute-done.7.refs_1_, ...), custom_call_target="tpu_custom_call" | custom-call | flops 100000000 | tf_op jit(solution)/shard_map/front/pallas_call | solution.py:181
  38.6 1.5 %collective-permute-start.15 = (bf16[96,768]{1,0:T(8,128)(2,1)S(1)}, bf16[96,768]{1,0:T(8,128)(2,1)S(1)}, u32[]{:S(2)}, u32[]{:S(2)}) collective-permute-start(bf16[96,768]{1,0:T(8,128)(2,1)S(1)} %collective-permute-done.9.refs_10_), channel_id=1, source_target_pairs={{0,1},{1,0},{2,3},{3,2},{4,5},{5,4},{6,7},{7,6},{8,9},{9,8},{10,11... | collective-permute-start | bytes 442376 | tf_op jit(solution)/shard_map/ppermute | solution.py:26
  40.8 2.9 %front.5 = (f32[512,256]{1,0:T(8,128)S(1)}, f32[1,3,768]{2,1,0:T(4,128)S(1)}) custom-call(s32[5]{0:T(128)S(1)} %stack.31.place_ref, bf16[544,1536]{1,0:T(8,128)(2,1)S(1)} %get-tuple-element.49.normed_ref, f32[3,256]{1,0:T(4,128)S(1)} %get-tuple-element.58.refs_0_, f32[3,256]{1,0:T(4,128)S(1)} %get-tuple-element.64.refs_1_, ...), custom_call_target="tpu_custom_call" | custom-call | flops 100000000 | tf_op jit(solution)/shard_map/front/pallas_call | solution.py:181
  46.2 1.6 %collective-permute-start.20 = (f32[1,3,768]{2,1,0:T(4,128)S(1)}, f32[1,3,768]{2,1,0:T(4,128)S(1)}, u32[]{:S(2)}, u32[]{:S(2)}) collective-permute-start(f32[1,3,768]{2,1,0:T(4,128)S(1)} %pad_maximum_fusion.2), channel_id=1, source_target_pairs={{0,16},{1,17},{2,18},{3,19},{4,20},{5,21},{6,22},{7,23},{8,24},{9,... | collective-permute-start | bytes 27656 | tf_op jit(solution)/shard_map/ppermute | solution.py:377
  48.3 1.4 %collective-permute-start.22 = (f32[1,3,768]{2,1,0:T(4,128)S(1)}, f32[1,3,768]{2,1,0:T(4,128)S(1)}, u32[]{:S(2)}, u32[]{:S(2)}) collective-permute-start(f32[1,3,768]{2,1,0:T(4,128)S(1)} %pad_maximum_fusion.2), channel_id=1, source_target_pairs={{0,17},{1,16},{2,19},{3,18},{4,21},{5,20},{6,23},{7,22},{8,25},{9,... | collective-permute-start | bytes 27656 | tf_op jit(solution)/shard_map/ppermute | solution.py:377
  49.9 1.5 %collective-permute-done.21 = f32[1,3,768]{2,1,0:T(4,128)S(1)} collective-permute-done((f32[1,3,768]{2,1,0:T(4,128)S(1)}, f32[1,3,768]{2,1,0:T(4,128)S(1)}, u32[]{:S(2)}, u32[]{:S(2)}) %collective-permute-start.21) | collective-permute-done | bytes 9248 | tf_op jit(solution)/shard_map/ppermute | solution.py:377
  51.4 1.4 %collective-permute-done.22 = f32[1,3,768]{2,1,0:T(4,128)S(1)} collective-permute-done((f32[1,3,768]{2,1,0:T(4,128)S(1)}, f32[1,3,768]{2,1,0:T(4,128)S(1)}, u32[]{:S(2)}, u32[]{:S(2)}) %collective-permute-start.22) | collective-permute-done | bytes 9248 | tf_op jit(solution)/shard_map/ppermute | solution.py:377
  52.9 1.6 %collective-permute-start.23 = (f32[1,3,768]{2,1,0:T(4,128)S(1)}, f32[1,3,768]{2,1,0:T(4,128)S(1)}, u32[]{:S(2)}, u32[]{:S(2)}) collective-permute-start(f32[1,3,768]{2,1,0:T(4,128)S(1)} %pad_maximum_fusion.3.refs_0_), channel_id=1, source_target_pairs={{0,2},{1,3},{2,0},{3,1},{4,6},{5,7},{6,4},{7,5},{8,10},{9,11},{10,... | collective-permute-start | bytes 27656 | tf_op jit(solution)/shard_map/ppermute | solution.py:377
  54.6 1.4 %collective-permute-start.24 = (f32[1,3,768]{2,1,0:T(4,128)S(1)}, f32[1,3,768]{2,1,0:T(4,128)S(1)}, u32[]{:S(2)}, u32[]{:S(2)}) collective-permute-start(f32[1,3,768]{2,1,0:T(4,128)S(1)} %pad_maximum_fusion.3.refs_0_), channel_id=1, source_target_pairs={{0,4},{1,5},{2,6},{3,7},{4,0},{5,1},{6,2},{7,3},{8,12},{9,13},{10,... | collective-permute-start | bytes 27656 | tf_op jit(solution)/shard_map/ppermute | solution.py:377
  57.4 1.8 %collective-permute-done.24.refs_2_ = f32[1,3,768]{2,1,0:T(4,128)S(1)} collective-permute-done((f32[1,3,768]{2,1,0:T(4,128)S(1)}, f32[1,3,768]{2,1,0:T(4,128)S(1)}, u32[]{:S(2)}, u32[]{:S(2)}) %collective-permute-start.24) | collective-permute-done | bytes 9248 | tf_op jit(solution)/shard_map/ppermute | solution.py:377
  59.2 2.3 %collective-permute-done.25.refs_3_ = f32[1,3,768]{2,1,0:T(4,128)S(1)} collective-permute-done((f32[1,3,768]{2,1,0:T(4,128)S(1)}, f32[1,3,768]{2,1,0:T(4,128)S(1)}, u32[]{:S(2)}, u32[]{:S(2)}) %collective-permute-start.25) | collective-permute-done | bytes 9248 | tf_op jit(solution)/shard_map/ppermute | solution.py:377
  61.5 2.9 %back.1 = bf16[512,1536]{1,0:T(8,128)(2,1)} custom-call(s32[5]{0:T(128)S(1)} %stack.31.place_ref, f32[1,768]{1,0:T(1,128)S(1)} %broadcast_in_dim.12.gain_ref, f32[1,768]{1,0:T(1,128)S(1)} %broadcast_in_dim.13.shift_ref, f32[1,3,768]{2,1,0:T(4,128)S(1)} %pad_maximum_fusion.3.refs_0_, f32[1,3,768]{2,1,0:T(4,128)S(1)} %collective-permute-done.23.refs_1_, ...), custom_call_target="tpu_custom_call" | custom-call | flops 1000000000 | tf_op jit(solution)/shard_map/back/pallas_call | solution.py:280
  (67 shorter events, 12.9 us)
Async XLA Ops:
  1.7 18.4 %collective-permute-start.3 = (bf16[384,1536]{1,0:T(8,128)(2,1)}, bf16[384,1536]{1,0:T(8,128)(2,1)S(1)}, u32[]{:S(2)}, u32[]{:S(2)}) collective-permute-start(bf16[384,1536]{1,0:T(8,128)(2,1)} %refs_0_.1), channel_id=1, source_target_pairs={{0,8},{8,0},{16,24},{24,16},{1,9},{9,1},{17,25},{25,17},{2,10},{10... | collective-permute-start | bytes 3538952 | tf_op jit(solution)/shard_map/ppermute | solution.py:26
  2.2 12.5 %collective-permute-start = (bf16[384,256]{1,0:T(8,128)(2,1)}, bf16[384,256]{1,0:T(8,128)(2,1)S(1)}, u32[]{:S(2)}, u32[]{:S(2)}) collective-permute-start(bf16[384,256]{1,0:T(8,128)(2,1)} %constant_dynamic-slice_fusion.2), channel_id=1, source_target_pairs={{0,16},{8,24},{16,0},{24,8},{1,17},{9,25},{17,1},{25,9},{2,18},{10... | collective-permute-start | bytes 589832 | tf_op jit(solution)/shard_map/ppermute | solution.py:26
  6.1 10.1 %collective-permute-start.1 = (bf16[16,1536]{1,0:T(8,128)(2,1)}, bf16[16,1536]{1,0:T(8,128)(2,1)}, u32[]{:S(2)}, u32[]{:S(2)}) collective-permute-start(bf16[16,1536]{1,0:T(8,128)(2,1)} %get-tuple-element.90), channel_id=1, source_target_pairs={{0,1},{1,0},{2,3},{3,2},{4,5},{5,4},{6,7},{7,6},{8,9},{9,8},{10,11... | collective-permute-start | bytes 147464 | tf_op jit(solution)/shard_map/ppermute | solution.py:26
  7.6 8.6 %collective-permute-start.2 = (bf16[16,1536]{1,0:T(8,128)(2,1)}, bf16[16,1536]{1,0:T(8,128)(2,1)}, u32[]{:S(2)}, u32[]{:S(2)}) collective-permute-start(bf16[16,1536]{1,0:T(8,128)(2,1)} %get-tuple-element.89), channel_id=1, source_target_pairs={{1,2},{3,4},{5,6},{2,1},{4,3},{6,5},{9,10},{11,12},{13,14},{10,9},... | collective-permute-start | bytes 147464 | tf_op jit(solution)/shard_map/ppermute | solution.py:343
  10.7 14.8 %collective-permute-start.7 = (bf16[384,512]{1,0:T(8,128)(2,1)}, bf16[384,512]{1,0:T(8,128)(2,1)}, u32[]{:S(2)}, u32[]{:S(2)}) collective-permute-start(bf16[384,512]{1,0:T(8,128)(2,1)} %pad_maximum_fusion.1), channel_id=1, source_target_pairs={{0,16},{8,24},{16,0},{24,8},{1,17},{9,25},{17,1},{25,9},{2,18},{10... | collective-permute-start | bytes 1179656 | tf_op jit(solution)/shard_map/ppermute | solution.py:26
  14.7 10.4 %collective-permute-start.5 = (bf16[96,768]{1,0:T(8,128)(2,1)S(1)}, bf16[96,768]{1,0:T(8,128)(2,1)S(1)}, u32[]{:S(2)}, u32[]{:S(2)}) collective-permute-start(bf16[96,768]{1,0:T(8,128)(2,1)S(1)} %copy-done.4), channel_id=1, source_target_pairs={{0,16},{8,24},{16,0},{24,8},{1,17},{9,25},{17,1},{25,9},{2,18},{10... | collective-permute-start | bytes 442376 | tf_op jit(solution)/shard_map/ppermute | solution.py:26
  16.2 8.8 %collective-permute-start.4 = (bf16[384,256]{1,0:T(8,128)(2,1)S(1)}, bf16[384,256]{1,0:T(8,128)(2,1)S(1)}, u32[]{:S(2)}, u32[]{:S(2)}) collective-permute-start(bf16[384,256]{1,0:T(8,128)(2,1)S(1)} %collective-permute-done.refs_1_), channel_id=1, source_target_pairs={{0,8},{8,0},{16,24},{24,16},{1,9},{9,1},{17,25},{25,17},{2,10},{10... | collective-permute-start | bytes 589832 | tf_op jit(solution)/shard_map/ppermute | solution.py:26
  16.2 9.3 %collective-permute-start.6 = (bf16[384,256]{1,0:T(8,128)(2,1)S(1)}, bf16[384,256]{1,0:T(8,128)(2,1)S(1)}, u32[]{:S(2)}, u32[]{:S(2)}) collective-permute-start(bf16[384,256]{1,0:T(8,128)(2,1)S(1)} %collective-permute-done.refs_1_), channel_id=1, source_target_pairs={{0,1},{1,0},{2,3},{3,2},{4,5},{5,4},{6,7},{7,6},{8,9},{9,8},{10,11... | collective-permute-start | bytes 589832 | tf_op jit(solution)/shard_map/ppermute | solution.py:26
  25.5 9.7 %collective-permute-start.11 = (bf16[384,512]{1,0:T(8,128)(2,1)}, bf16[384,512]{1,0:T(8,128)(2,1)S(1)}, u32[]{:S(2)}, u32[]{:S(2)}) collective-permute-start(bf16[384,512]{1,0:T(8,128)(2,1)} %collective-permute-done.7.refs_1_), channel_id=1, source_target_pairs={{0,8},{8,0},{16,24},{24,16},{1,9},{9,1},{17,25},{25,17},{2,10},{10... | collective-permute-start | bytes 1179656 | tf_op jit(solution)/shard_map/ppermute | solution.py:26
  25.5 13.0 %collective-permute-start.12 = (bf16[384,512]{1,0:T(8,128)(2,1)S(1)}, bf16[384,512]{1,0:T(8,128)(2,1)S(1)}, u32[]{:S(2)}, u32[]{:S(2)}) collective-permute-start(bf16[384,512]{1,0:T(8,128)(2,1)S(1)} %pad_maximum_fusion), channel_id=1, source_target_pairs={{0,16},{8,24},{16,0},{24,8},{1,17},{9,25},{17,1},{25,9},{2,18},{10... | collective-permute-start | bytes 1179656 | tf_op jit(solution)/shard_map/ppermute | solution.py:26
  26.0 4.9 %collective-permute-start.8 = (bf16[384,256]{1,0:T(8,128)(2,1)S(1)}, bf16[384,256]{1,0:T(8,128)(2,1)S(1)}, u32[]{:S(2)}, u32[]{:S(2)}) collective-permute-start(bf16[384,256]{1,0:T(8,128)(2,1)S(1)} %collective-permute-done.6.refs_2_), channel_id=1, source_target_pairs={{0,8},{8,0},{16,24},{24,16},{1,9},{9,1},{17,25},{25,17},{2,10},{10... | collective-permute-start | bytes 589832 | tf_op jit(solution)/shard_map/ppermute | solution.py:26
  26.3 7.5 %collective-permute-start.10 = (bf16[96,768]{1,0:T(8,128)(2,1)S(1)}, bf16[96,768]{1,0:T(8,128)(2,1)S(1)}, u32[]{:S(2)}, u32[]{:S(2)}) collective-permute-start(bf16[96,768]{1,0:T(8,128)(2,1)S(1)} %collective-permute-done.5.refs_9_), channel_id=1, source_target_pairs={{0,1},{1,0},{2,3},{3,2},{4,5},{5,4},{6,7},{7,6},{8,9},{9,8},{10,11... | collective-permute-start | bytes 442376 | tf_op jit(solution)/shard_map/ppermute | solution.py:26
  29.3 5.8 %collective-permute-start.9 = (bf16[96,768]{1,0:T(8,128)(2,1)S(1)}, bf16[96,768]{1,0:T(8,128)(2,1)S(1)}, u32[]{:S(2)}, u32[]{:S(2)}) collective-permute-start(bf16[96,768]{1,0:T(8,128)(2,1)S(1)} %collective-permute-done.5.refs_9_), channel_id=1, source_target_pairs={{0,2},{1,3},{2,0},{3,1},{4,6},{5,7},{6,4},{7,5},{8,10},{9,11},{10,... | collective-permute-start | bytes 442376 | tf_op jit(solution)/shard_map/ppermute | solution.py:26
  30.9 14.0 %collective-permute-start.14 = (bf16[192,1536]{1,0:T(8,128)(2,1)S(1)}, bf16[192,1536]{1,0:T(8,128)(2,1)S(1)}, u32[]{:S(2)}, u32[]{:S(2)}) collective-permute-start(bf16[192,1536]{1,0:T(8,128)(2,1)S(1)} %copy-done.2), channel_id=1, source_target_pairs={{0,8},{8,0},{16,24},{24,16},{1,9},{9,1},{17,25},{25,17},{2,10},{10... | collective-permute-start | bytes 1769480 | tf_op jit(solution)/shard_map/ppermute | solution.py:26
  38.6 6.3 %collective-permute-start.15 = (bf16[96,768]{1,0:T(8,128)(2,1)S(1)}, bf16[96,768]{1,0:T(8,128)(2,1)S(1)}, u32[]{:S(2)}, u32[]{:S(2)}) collective-permute-start(bf16[96,768]{1,0:T(8,128)(2,1)S(1)} %collective-permute-done.9.refs_10_), channel_id=1, source_target_pairs={{0,1},{1,0},{2,3},{3,2},{4,5},{5,4},{6,7},{7,6},{8,9},{9,8},{10,11... | collective-permute-start | bytes 442376 | tf_op jit(solution)/shard_map/ppermute | solution.py:26
  40.1 4.8 %collective-permute-start.17 = (bf16[96,768]{1,0:T(8,128)(2,1)S(1)}, bf16[96,768]{1,0:T(8,128)(2,1)S(1)}, u32[]{:S(2)}, u32[]{:S(2)}) collective-permute-start(bf16[96,768]{1,0:T(8,128)(2,1)S(1)} %collective-permute-done.9.refs_10_), channel_id=1, source_target_pairs={{0,8},{8,0},{16,24},{24,16},{1,9},{9,1},{17,25},{25,17},{2,10},{10... | collective-permute-start | bytes 442376 | tf_op jit(solution)/shard_map/ppermute | solution.py:26
  40.3 4.5 %collective-permute-start.16 = (bf16[96,768]{1,0:T(8,128)(2,1)S(1)}, bf16[96,768]{1,0:T(8,128)(2,1)S(1)}, u32[]{:S(2)}, u32[]{:S(2)}) collective-permute-start(bf16[96,768]{1,0:T(8,128)(2,1)S(1)} %collective-permute-done.5.refs_9_), channel_id=1, source_target_pairs={{0,8},{8,0},{16,24},{24,16},{1,9},{9,1},{17,25},{25,17},{2,10},{10... | collective-permute-start | bytes 442376 | tf_op jit(solution)/shard_map/ppermute | solution.py:26
  40.6 4.3 %collective-permute-start.18 = (bf16[96,768]{1,0:T(8,128)(2,1)S(1)}, bf16[96,768]{1,0:T(8,128)(2,1)S(1)}, u32[]{:S(2)}, u32[]{:S(2)}) collective-permute-start(bf16[96,768]{1,0:T(8,128)(2,1)S(1)} %collective-permute-done.10.refs_11_), channel_id=1, source_target_pairs={{0,8},{8,0},{16,24},{24,16},{1,9},{9,1},{17,25},{25,17},{2,10},{10... | collective-permute-start | bytes 442376 | tf_op jit(solution)/shard_map/ppermute | solution.py:26
  46.2 3.8 %collective-permute-start.20 = (f32[1,3,768]{2,1,0:T(4,128)S(1)}, f32[1,3,768]{2,1,0:T(4,128)S(1)}, u32[]{:S(2)}, u32[]{:S(2)}) collective-permute-start(f32[1,3,768]{2,1,0:T(4,128)S(1)} %pad_maximum_fusion.2), channel_id=1, source_target_pairs={{0,16},{1,17},{2,18},{3,19},{4,20},{5,21},{6,22},{7,23},{8,24},{9,... | collective-permute-start | bytes 27656 | tf_op jit(solution)/shard_map/ppermute | solution.py:377
  48.3 4.6 %collective-permute-start.22 = (f32[1,3,768]{2,1,0:T(4,128)S(1)}, f32[1,3,768]{2,1,0:T(4,128)S(1)}, u32[]{:S(2)}, u32[]{:S(2)}) collective-permute-start(f32[1,3,768]{2,1,0:T(4,128)S(1)} %pad_maximum_fusion.2), channel_id=1, source_target_pairs={{0,17},{1,16},{2,19},{3,18},{4,21},{5,20},{6,23},{7,22},{8,25},{9,... | collective-permute-start | bytes 27656 | tf_op jit(solution)/shard_map/ppermute | solution.py:377
  49.7 11.8 %collective-permute-start.26 = (bf16[96,768]{1,0:T(8,128)(2,1)S(1)}, bf16[96,768]{1,0:T(8,128)(2,1)S(1)}, u32[]{:S(2)}, u32[]{:S(2)}) collective-permute-start(bf16[96,768]{1,0:T(8,128)(2,1)S(1)} %collective-permute-done.15.refs_12_), channel_id=1, source_target_pairs={{0,8},{8,0},{16,24},{24,16},{1,9},{9,1},{17,25},{25,17},{2,10},{10... | collective-permute-start | bytes 442376 | tf_op jit(solution)/shard_map/ppermute | solution.py:26
  52.9 4.5 %collective-permute-start.23 = (f32[1,3,768]{2,1,0:T(4,128)S(1)}, f32[1,3,768]{2,1,0:T(4,128)S(1)}, u32[]{:S(2)}, u32[]{:S(2)}) collective-permute-start(f32[1,3,768]{2,1,0:T(4,128)S(1)} %pad_maximum_fusion.3.refs_0_), channel_id=1, source_target_pairs={{0,2},{1,3},{2,0},{3,1},{4,6},{5,7},{6,4},{7,5},{8,10},{9,11},{10,... | collective-permute-start | bytes 27656 | tf_op jit(solution)/shard_map/ppermute | solution.py:377
  54.6 4.6 %collective-permute-start.24 = (f32[1,3,768]{2,1,0:T(4,128)S(1)}, f32[1,3,768]{2,1,0:T(4,128)S(1)}, u32[]{:S(2)}, u32[]{:S(2)}) collective-permute-start(f32[1,3,768]{2,1,0:T(4,128)S(1)} %pad_maximum_fusion.3.refs_0_), channel_id=1, source_target_pairs={{0,4},{1,5},{2,6},{3,7},{4,0},{5,1},{6,2},{7,3},{8,12},{9,13},{10,... | collective-permute-start | bytes 27656 | tf_op jit(solution)/shard_map/ppermute | solution.py:377
  56.0 5.5 %collective-permute-start.25 = (f32[1,3,768]{2,1,0:T(4,128)S(1)}, f32[1,3,768]{2,1,0:T(4,128)S(1)}, u32[]{:S(2)}, u32[]{:S(2)}) collective-permute-start(f32[1,3,768]{2,1,0:T(4,128)S(1)} %pad_maximum_fusion.3.refs_0_), channel_id=1, source_target_pairs={{0,6},{1,7},{2,4},{3,5},{4,2},{5,3},{6,0},{7,1},{8,14},{9,15},{10,... | collective-permute-start | bytes 27656 | tf_op jit(solution)/shard_map/ppermute | solution.py:377
  (11 other events, 94.5 us)

commit v3 on v2

--- a/solution.py
+++ b/solution.py
@@ -11,7 +11,7 @@
 LANES = 128
 MIB = 1024 * 1024
 VMEM = pltpu.VMEM
-ORDER = (2, 0, 1)
+ORDER = (0, 2, 1)
 
 
 def cost(flops):
@@ -233,17 +233,15 @@
     convs, weight_refs = conv_refs[:3], conv_refs[3:]
     row_count, wide = convs[0].shape
     if len(weight_refs) > 1:
-        depth, width = weight_refs[0].shape
+        depth = weight_refs[0].shape[0]
         for i, weight_ref in enumerate(weight_refs[:2]):
             at = pl.multiple_of(lax.bitwise_xor(place_ref[0], i) * depth, depth)
             weights[pl.ds(at, depth), :] = weight_ref[...]
         for i, weight_ref in enumerate(weight_refs[2:]):
-            rows, columns = weight_ref.shape
+            rows = weight_ref.shape[0]
             at = lax.bitwise_xor(place_ref[0], 2 + i // 4) * depth
-            at += lax.bitwise_xor(place_ref[3], i // 2 % 2) * rows
-            column = lax.bitwise_xor(place_ref[4], i % 2) * columns
-            here = pl.ds(pl.multiple_of(at, rows), rows), pl.ds(pl.multiple_of(column, columns), columns)
-            weights[here] = weight_ref[...]
+            at += lax.bitwise_xor(2 * place_ref[3] + place_ref[4], i % 4) * rows
+            weights[pl.ds(pl.multiple_of(at, rows), rows), :] = weight_ref[...]
     else:
         weights[...] = weight_refs[0][...]
     mean, square, count = merged(rows_of(stat_refs))
@@ -323,54 +321,52 @@
 
     if direct:
         last = row_count - HALO
-        out_depth, out_width = w_out.shape[0] // 2, model_width // 2
+        depth = w_out.shape[0] // 4
 
         def columns(shard, block):
             at = block * wide
             return jnp.concatenate([shard[:, at : at + wide], shard[:, channels + at : channels + at + wide]], 1)
 
-        half = lax.dynamic_slice_in_dim(w_in, parity * channels + 2 * wide, wide, axis=1)
-        over_x = {2: [swap(half, "fsdp", 2)]}
-        half, later_in, later_out, later_rows = tie(half, w_in, w_out, rows)
+        quarter = lax.dynamic_slice_in_dim(w_out, (2 * parity + pair) * depth, depth, axis=0)
+        quarter, later_in = tie(quarter, w_in)
+        half = lax.dynamic_slice_in_dim(later_in, parity * channels + 2 * wide, wide, axis=1)
+        half, later_in = tie(half, later_in)
         block = columns(later_in, 0)
-        over_x[0] = [swap(block, "fsdp", 2)]
-        quarter = lax.dynamic_slice(later_out, (parity * out_depth, pair * out_width), (out_depth, out_width))
-        quarter = swap(quarter, "fsdp", 2)
+        quarter, half, block = (swap(part, "fsdp", 2) for part in (quarter, half, block))
+        across = swap(later_in, "fsdp", 1)
+        normed = normalize_rows(rows, gain)
+        normed, later_rows, quarter = tie(normed, rows, quarter)
         inner = lax.dynamic_slice_in_dim(later_rows, (1 - parity) * last, HALO, axis=0)
         outer = lax.dynamic_slice_in_dim(later_rows, parity * last, HALO, axis=0)
         inner = swap(inner, "ctx", 1)
         pairs = [(i, i + 1) for i in range(1, ends, 2)]
         outer = lax.ppermute(outer, "ctx", pairs + [(j, i) for i, j in pairs])
-        across = swap(later_in, "fsdp", 1)
-        normed = normalize_rows(rows, gain)
-        normed, over_x[2][0], later_in = tie(normed, over_x[2][0], later_in)
-        over_x[2].append(swap(over_x[2][0], "ctx", 1))
-        beyond_half = swap(over_x[2][0], "fsdp", 1)
+        quarters = [quarter, swap(quarter, "ctx", 2), swap(quarter, "ctx", 1)]
+        normed, half, later_in = tie(normed, half, later_in)
+        over_x = {2: [half, swap(half, "ctx", 1)]}
+        beyond_half = swap(half, "fsdp", 1)
         normed, part = tie(normed, columns(later_in, 1))
         over_x[1] = [swap(part, "fsdp", 2)]
+        normed, block = tie(normed, block)
+        over_x[0] = [block]
+        beyond_zero = swap(block, "fsdp", 1)
         normed, *partials = near_product(place, normed, inner, outer, gain, w_in, across)
-        partials[2], beyond_half, quarter = tie(partials[2], beyond_half, quarter)
-        quarters = [quarter, swap(quarter, "ctx", 2), swap(quarter, "ctx", 1)]
-        partials[2], over_x[2][1], w_out = tie(partials[2], over_x[2][1], w_out)
+        partials[0], beyond_half, *quarters = tie(partials[0], beyond_half, *quarters)
+        quarters.append(swap(quarters[1], "ctx", 1))
+        partials[0], over_x[2][1], w_out = tie(partials[0], over_x[2][1], w_out)
 
         beyond_two = [beyond_half, swap(over_x[2][1], "fsdp", 1)]
-        partials[2], over_x[0][0] = tie(partials[2], over_x[0][0])
-        beyond_zero = swap(over_x[0][0], "fsdp", 1)
-        conv_one, stat_one = front(2, [partials[2], *over_x[2], *beyond_two])
-        conv_one, partials[0], *quarters = tie(conv_one, partials[0], *quarters)
-        quarters.append(swap(quarters[1], "ctx", 1))
-        beyond_quarters = [swap(part, "fsdp", 1) for part in quarters[:3]]
-        conv_two, stat_two = front(0, [partials[0], *over_x[0], beyond_zero])
+        conv_one, stat_one = front(0, [partials[0], *over_x[0], beyond_zero])
+        conv_one, partials[2], quarters[3] = tie(conv_one, partials[2], quarters[3])
+        beyond_quarters = [swap(part, "fsdp", 1) for part in quarters]
+        conv_two, stat_two = front(2, [partials[2], *over_x[2], *beyond_two])
         conv_two, over_x[1][0] = tie(conv_two, over_x[1][0])
         across_out = swap(w_out, "fsdp", 1)
         beyond_one = swap(over_x[1][0], "fsdp", 1)
         conv_three, stats = front(1, [partials[1], *over_x[1], beyond_one], (stat_one, stat_two), 1)
-        stats, across_out, quarters[3], *beyond_quarters = tie(
-            stats, across_out, quarters[3], *beyond_quarters
-        )
-        beyond_quarters.append(swap(quarters[3], "fsdp", 1))
+        stats, across_out, *beyond_quarters = tie(stats, across_out, *beyond_quarters)
         out_weights = [w_out, across_out, *quarters, *beyond_quarters]
-        convs = [conv_two, conv_three, conv_one]
+        convs = [conv_one, conv_three, conv_two]
 
         def others(flips):
             return [

time: 64.7 us -> 72.4 us (1.12)
  local copies, waits for them, and re-layouts: 5.05 us -> 8.89 us
  waiting for transfers between devices: 13.6 us -> 16.1 us
  Pallas kernels: 16.6 us -> 18 us
  starting transfers between devices: 27.4 us -> 26.4 us
  other arithmetic: 0.91 us -> 1.7 us
    unnamed x16 -> x26, local copies, waits for them, and re-layouts: 0.03 us -> 4.27 us
    ppermute x7, waiting for transfers between devices: 8.37 us -> 10.4 us  [others(): lax.ppermute(stats, both, [(member(f, p), member(f ^ df, p ^ dp)) for f i...]
    concatenate x2, other arithmetic: 0.8 us -> 1.59 us  [columns(): jnp.concatenate([shard[:, at:at + wide], shard[:, channels + at:channels...]
    ppermute x19, starting transfers between devices: 18 us -> 17.3 us  [swap(): lax.ppermute(value, axis, [(i, i ^ bit) for i in range(lax.axis_size(axis...]
  transfers between devices with their start and end apart: 27 -> 27, of which waited for: 10 -> 10; matrix products, arithmetic and copies ran while one was open for 7% -> 5% of each run, Pallas kernels for 21% -> 20%
where the time goes in v3:
time: 72.4 us; the launch traced here: 71.9 us
  starting transfers between devices  26.4 us (36%)
  Pallas kernels  18 us (25%)
  waiting for transfers between devices  16.1 us (22%)
  local copies, waits for them, and re-layouts  8.89 us (12%)
  other arithmetic  1.7 us (2%)
  between operations  0.87 us (1%)
    ppermute x19, starting transfers between devices, swap(): lax.ppermute(value, axis, [(i, i ^ bit) for i in range(lax.axis_size(axis...  17.3 us
    ppermute x7, waiting for transfers between devices, others(): lax.ppermute(stats, both, [(member(f, p), member(f ^ df, p ^ dp)) for f i...  10.4 us
    pallas_call x3, Pallas kernels, front_block(): pl.pallas_call(functools.partial(front_kernel, block, len(earlier)), out_...  9.63 us
    ppermute x7, starting transfers between devices, others(): lax.ppermute(stats, both, [(member(f, p), member(f ^ df, p ^ dp)) for f i...  8.44 us
    ppermute x19, waiting for transfers between devices, swap(): lax.ppermute(value, axis, [(i, i ^ bit) for i in range(lax.axis_size(axis...  5.65 us
    unnamed x26, local copies, waits for them, and re-layouts  4.27 us
    pallas_call x1, Pallas kernels, back(): pl.pallas_call(functools.partial(back_kernel, len(stats)), out_shape=jax....  3.38 us
    pallas_call x1, Pallas kernels, near_product(): pl.pallas_call(near_kernel, out_shape=shapes, in_specs=[pl.BlockSpec(memo...  3.14 us
  transfers between devices with their start and end apart: 27, of which 10 were waited for; matrix products, arithmetic and copies ran while one was open for 5% of the time, Pallas kernels for 20%

profile of v3, /device:TPU:0, one launch (start us, length us, event | category | flops | bytes accessed | tf_op | source)
XLA Modules:
  0.0 71.9 jit_solution(8307365554375629030)
XLA Ops:
  0.9 1.6 %constant_dynamic-slice_fusion.2 = bf16[384,256]{1,0:T(8,128)(2,1)} fusion(bf16[384,1536]{1,0:T(8,128)(2,1)} %refs_0_.1, s32[]{:T(128)S(6)} %select_n.19), kind=kLoop, calls=%fused_computation.25 | loop fusion | bytes 393220 | tf_op jit(solution)/shard_map/dynamic_slice | solution.py:332
  3.0 2.5 %collective-permute-start = (bf16[48,1536]{1,0:T(8,128)(2,1)S(1)}, bf16[48,1536]{1,0:T(8,128)(2,1)S(1)}, u32[]{:S(2)}, u32[]{:S(2)}) collective-permute-start(bf16[48,1536]{1,0:T(8,128)(2,1)S(1)} %constant_dynamic-slice_fusion.3), channel_id=1, source_target_pairs={{0,16},{8,24},{16,0},{24,8},{1,17},{9,25},{17,1},{25,9},{2,18},{10... | collective-permute-start | bytes 442376 | tf_op jit(solution)/shard_map/ppermute | solution.py:26
  7.4 2.0 %collective-permute-start.2 = (bf16[384,512]{1,0:T(8,128)(2,1)}, bf16[384,512]{1,0:T(8,128)(2,1)S(1)}, u32[]{:S(2)}, u32[]{:S(2)}) collective-permute-start(bf16[384,512]{1,0:T(8,128)(2,1)} %pad_maximum_fusion.1), channel_id=1, source_target_pairs={{0,16},{8,24},{16,0},{24,8},{1,17},{9,25},{17,1},{25,9},{2,18},{10... | collective-permute-start | bytes 1179656 | tf_op jit(solution)/shard_map/ppermute | solution.py:26
  9.4 1.4 %copy-done.1 = bf16[1,512,1536]{2,1,0:T(8,128)(2,1)S(1)} copy-done((bf16[1,512,1536]{2,1,0:T(8,128)(2,1)S(1)}, bf16[1,512,1536]{2,1,0:T(8,128)(2,1)}, u32[]{:S(2)}) %copy-start.1) | copy-done | bytes 1572888
  10.8 1.9 %layer_norm.1.rows_ref = bf16[512,1536]{1,0:T(8,128)(2,1)S(1)} custom-call(bf16[512,1536]{1,0:T(8,128)(2,1)S(1)} %bitcast.7, f32[1,1536]{1,0:T(1,128)S(1)} %broadcast_in_dim.14.gain_ref), custom_call_target="tpu_custom_call" | custom-call | flops 100000000 | tf_op jit(solution)/shard_map/layer_norm/pallas_call | solution.py:48
  13.6 1.6 %collective-permute-start.3 = (bf16[16,1536]{1,0:T(8,128)(2,1)S(1)}, bf16[16,1536]{1,0:T(8,128)(2,1)S(1)}, u32[]{:S(2)}, u32[]{:S(2)}) collective-permute-start(bf16[16,1536]{1,0:T(8,128)(2,1)S(1)} %get-tuple-element.98), channel_id=1, source_target_pairs={{0,1},{1,0},{2,3},{3,2},{4,5},{5,4},{6,7},{7,6},{8,9},{9,8},{10,11... | collective-permute-start | bytes 147464 | tf_op jit(solution)/shard_map/ppermute | solution.py:26
  15.9 3.3 %collective-permute-start.7 = (bf16[48,1536]{1,0:T(8,128)(2,1)S(1)}, bf16[48,1536]{1,0:T(8,128)(2,1)}, u32[]{:S(2)}, u32[]{:S(2)}) collective-permute-start(bf16[48,1536]{1,0:T(8,128)(2,1)S(1)} %collective-permute-done.refs_9_), channel_id=1, source_target_pairs={{0,2},{1,3},{2,0},{3,1},{4,6},{5,7},{6,4},{7,5},{8,10},{9,11},{10,... | collective-permute-start | bytes 442376 | tf_op jit(solution)/shard_map/ppermute | solution.py:26
  20.0 2.7 %collective-permute-done.2.refs_1_ = bf16[384,512]{1,0:T(8,128)(2,1)S(1)} collective-permute-done((bf16[384,512]{1,0:T(8,128)(2,1)}, bf16[384,512]{1,0:T(8,128)(2,1)S(1)}, u32[]{:S(2)}, u32[]{:S(2)}) %collective-permute-start.2) | collective-permute-done | bytes 393248 | tf_op jit(solution)/shard_map/ppermute | solution.py:26
  24.4 1.8 %collective-permute-start.9 = (bf16[384,256]{1,0:T(8,128)(2,1)}, bf16[384,256]{1,0:T(8,128)(2,1)}, u32[]{:S(2)}, u32[]{:S(2)}) collective-permute-start(bf16[384,256]{1,0:T(8,128)(2,1)} %collective-permute-done.1.refs_1_), channel_id=1, source_target_pairs={{0,1},{1,0},{2,3},{3,2},{4,5},{5,4},{6,7},{7,6},{8,9},{9,8},{10,11... | collective-permute-start | bytes 589832 | tf_op jit(solution)/shard_map/ppermute | solution.py:26
  26.2 1.5 %collective-permute-start.13 = (bf16[384,512]{1,0:T(8,128)(2,1)}, bf16[384,512]{1,0:T(8,128)(2,1)S(1)}, u32[]{:S(2)}, u32[]{:S(2)}) collective-permute-start(bf16[384,512]{1,0:T(8,128)(2,1)} %pad_maximum_fusion), channel_id=1, source_target_pairs={{0,16},{8,24},{16,0},{24,8},{1,17},{9,25},{17,1},{25,9},{2,18},{10... | collective-permute-start | bytes 1179656 | tf_op jit(solution)/shard_map/ppermute | solution.py:26
  30.5 3.1 %near.1 = (bf16[544,1536]{1,0:T(8,128)(2,1)S(1)}, f32[544,512]{1,0:T(8,128)S(1)}, f32[544,512]{1,0:T(8,128)S(1)}, f32[544,512]{1,0:T(8,128)S(1)}) custom-call(s32[5]{0:T(128)S(1)} %stack.31.place_ref, bf16[512,1536]{1,0:T(8,128)(2,1)S(1)} %layer_norm.1.rows_ref, bf16[16,1536]{1,0:T(8,128)(2,1)S(1)} %copy-done.7, bf16[16,1536]{1,0:T(8,128)(2,1)S(1)} %copy-done.9, ...), custom_call_target="tpu_custom_call" | custom-call | flops 100000000 | tf_op jit(solution)/shard_map/near/pallas_call | solution.py:96
  34.8 1.8 %collective-permute-start.11 = (bf16[48,1536]{1,0:T(8,128)(2,1)}, bf16[48,1536]{1,0:T(8,128)(2,1)S(1)}, u32[]{:S(2)}, u32[]{:S(2)}) collective-permute-start(bf16[48,1536]{1,0:T(8,128)(2,1)} %collective-permute-done.7.refs_10_), channel_id=1, source_target_pairs={{0,1},{1,0},{2,3},{3,2},{4,5},{5,4},{6,7},{7,6},{8,9},{9,8},{10,11... | collective-permute-start | bytes 442376 | tf_op jit(solution)/shard_map/ppermute | solution.py:26
  36.7 3.3 %front.3 = (f32[512,256]{1,0:T(8,128)S(1)}, f32[3,256]{1,0:T(4,128)S(1)}) custom-call(s32[5]{0:T(128)S(1)} %stack.31.place_ref, bf16[544,1536]{1,0:T(8,128)(2,1)S(1)} %get-tuple-element.58.normed_ref, f32[544,512]{1,0:T(8,128)S(1)} %get-tuple-element.63.refs_0_, bf16[384,512]{1,0:T(8,128)(2,1)S(1)} %collective-permute-done.2.refs_1_, ...), custom_call_target="tpu_custom_call" | custom-call | flops 100000000 | tf_op jit(solution)/shard_map/front/pallas_call | solution.py:181
  41.2 3.5 %front.4 = (f32[512,256]{1,0:T(8,128)S(1)}, f32[3,256]{1,0:T(4,128)S(1)}) custom-call(s32[5]{0:T(128)S(1)} %stack.31.place_ref, bf16[544,1536]{1,0:T(8,128)(2,1)S(1)} %get-tuple-element.58.normed_ref, f32[544,512]{1,0:T(8,128)S(1)} %get-tuple-element.69.refs_0_, bf16[384,256]{1,0:T(8,128)(2,1)} %collective-permute-done.1.refs_1_, ...), custom_call_target="tpu_custom_call" | custom-call | flops 100000000 | tf_op jit(solution)/shard_map/front/pallas_call | solution.py:181
  46.6 2.8 %front.5 = (f32[512,256]{1,0:T(8,128)S(1)}, f32[1,3,768]{2,1,0:T(4,128)S(1)}) custom-call(s32[5]{0:T(128)S(1)} %stack.31.place_ref, bf16[544,1536]{1,0:T(8,128)(2,1)S(1)} %get-tuple-element.58.normed_ref, f32[3,256]{1,0:T(4,128)S(1)} %get-tuple-element.65.refs_0_, f32[3,256]{1,0:T(4,128)S(1)} %get-tuple-element.72.refs_1_, ...), custom_call_target="tpu_custom_call" | custom-call | flops 100000000 | tf_op jit(solution)/shard_map/front/pallas_call | solution.py:181
  50.9 1.8 %collective-permute-start.21 = (f32[1,3,768]{2,1,0:T(4,128)S(1)}, f32[1,3,768]{2,1,0:T(4,128)S(1)}, u32[]{:S(2)}, u32[]{:S(2)}) collective-permute-start(f32[1,3,768]{2,1,0:T(4,128)S(1)} %pad_maximum_fusion.2), channel_id=1, source_target_pairs={{0,16},{1,17},{2,18},{3,19},{4,20},{5,21},{6,22},{7,23},{8,24},{9,... | collective-permute-start | bytes 27656 | tf_op jit(solution)/shard_map/ppermute | solution.py:373
  52.6 1.5 %collective-permute-start.22 = (f32[1,3,768]{2,1,0:T(4,128)S(1)}, f32[1,3,768]{2,1,0:T(4,128)S(1)}, u32[]{:S(2)}, u32[]{:S(2)}) collective-permute-start(f32[1,3,768]{2,1,0:T(4,128)S(1)} %pad_maximum_fusion.2), channel_id=1, source_target_pairs={{0,1},{1,0},{2,3},{3,2},{4,5},{5,4},{6,7},{7,6},{8,9},{9,8},{10,11... | collective-permute-start | bytes 27656 | tf_op jit(solution)/shard_map/ppermute | solution.py:373
  54.6 1.7 %collective-permute-done.22 = f32[1,3,768]{2,1,0:T(4,128)S(1)} collective-permute-done((f32[1,3,768]{2,1,0:T(4,128)S(1)}, f32[1,3,768]{2,1,0:T(4,128)S(1)}, u32[]{:S(2)}, u32[]{:S(2)}) %collective-permute-start.22) | collective-permute-done | bytes 9248 | tf_op jit(solution)/shard_map/ppermute | solution.py:373
  56.3 2.4 %collective-permute-done.23 = f32[1,3,768]{2,1,0:T(4,128)S(1)} collective-permute-done((f32[1,3,768]{2,1,0:T(4,128)S(1)}, f32[1,3,768]{2,1,0:T(4,128)S(1)}, u32[]{:S(2)}, u32[]{:S(2)}) %collective-permute-start.23) | collective-permute-done | bytes 9248 | tf_op jit(solution)/shard_map/ppermute | solution.py:373
  58.8 1.6 %collective-permute-start.24 = (f32[1,3,768]{2,1,0:T(4,128)S(1)}, f32[1,3,768]{2,1,0:T(4,128)S(1)}, u32[]{:S(2)}, u32[]{:S(2)}) collective-permute-start(f32[1,3,768]{2,1,0:T(4,128)S(1)} %pad_maximum_fusion.3.refs_0_), channel_id=1, source_target_pairs={{0,2},{1,3},{2,0},{3,1},{4,6},{5,7},{6,4},{7,5},{8,10},{9,11},{10,... | collective-permute-start | bytes 27656 | tf_op jit(solution)/shard_map/ppermute | solution.py:373
  60.5 2.6 %collective-permute-start.25 = (f32[1,3,768]{2,1,0:T(4,128)S(1)}, f32[1,3,768]{2,1,0:T(4,128)S(1)}, u32[]{:S(2)}, u32[]{:S(2)}) collective-permute-start(f32[1,3,768]{2,1,0:T(4,128)S(1)} %pad_maximum_fusion.3.refs_0_), channel_id=1, source_target_pairs={{0,4},{1,5},{2,6},{3,7},{4,0},{5,1},{6,2},{7,3},{8,12},{9,13},{10,... | collective-permute-start | bytes 27656 | tf_op jit(solution)/shard_map/ppermute | solution.py:373
  63.3 1.8 %collective-permute-done.25.refs_2_ = f32[1,3,768]{2,1,0:T(4,128)S(1)} collective-permute-done((f32[1,3,768]{2,1,0:T(4,128)S(1)}, f32[1,3,768]{2,1,0:T(4,128)S(1)}, u32[]{:S(2)}, u32[]{:S(2)}) %collective-permute-start.25) | collective-permute-done | bytes 9248 | tf_op jit(solution)/shard_map/ppermute | solution.py:373
  65.1 3.5 %collective-permute-done.26.refs_3_ = f32[1,3,768]{2,1,0:T(4,128)S(1)} collective-permute-done((f32[1,3,768]{2,1,0:T(4,128)S(1)}, f32[1,3,768]{2,1,0:T(4,128)S(1)}, u32[]{:S(2)}, u32[]{:S(2)}) %collective-permute-start.26) | collective-permute-done | bytes 9248 | tf_op jit(solution)/shard_map/ppermute | solution.py:373
  68.6 3.4 %back.1 = bf16[512,1536]{1,0:T(8,128)(2,1)} custom-call(s32[5]{0:T(128)S(1)} %stack.31.place_ref, f32[1,768]{1,0:T(1,128)S(1)} %broadcast_in_dim.12.gain_ref, f32[1,768]{1,0:T(1,128)S(1)} %broadcast_in_dim.13.shift_ref, f32[1,3,768]{2,1,0:T(4,128)S(1)} %pad_maximum_fusion.3.refs_0_, f32[1,3,768]{2,1,0:T(4,128)S(1)} %collective-permute-done.24.refs_1_, ...), custom_call_target="tpu_custom_call" | custom-call | flops 1000000000 | tf_op jit(solution)/shard_map/back/pallas_call | solution.py:278
  (77 shorter events, 16.0 us)
Async XLA Ops:
  2.6 25.1 %collective-permute-start.5 = (bf16[384,1536]{1,0:T(8,128)(2,1)}, bf16[384,1536]{1,0:T(8,128)(2,1)}, u32[]{:S(2)}, u32[]{:S(2)}) collective-permute-start(bf16[384,1536]{1,0:T(8,128)(2,1)} %refs_0_.1), channel_id=1, source_target_pairs={{0,8},{8,0},{16,24},{24,16},{1,9},{9,1},{17,25},{25,17},{2,10},{10... | collective-permute-start | bytes 3538952 | tf_op jit(solution)/shard_map/ppermute | solution.py:26
  3.0 9.7 %collective-permute-start = (bf16[48,1536]{1,0:T(8,128)(2,1)S(1)}, bf16[48,1536]{1,0:T(8,128)(2,1)S(1)}, u32[]{:S(2)}, u32[]{:S(2)}) collective-permute-start(bf16[48,1536]{1,0:T(8,128)(2,1)S(1)} %constant_dynamic-slice_fusion.3), channel_id=1, source_target_pairs={{0,16},{8,24},{16,0},{24,8},{1,17},{9,25},{17,1},{25,9},{2,18},{10... | collective-permute-start | bytes 442376 | tf_op jit(solution)/shard_map/ppermute | solution.py:26
  5.5 10.3 %collective-permute-start.1 = (bf16[384,256]{1,0:T(8,128)(2,1)}, bf16[384,256]{1,0:T(8,128)(2,1)}, u32[]{:S(2)}, u32[]{:S(2)}) collective-permute-start(bf16[384,256]{1,0:T(8,128)(2,1)} %constant_dynamic-slice_fusion.2), channel_id=1, source_target_pairs={{0,16},{8,24},{16,0},{24,8},{1,17},{9,25},{17,1},{25,9},{2,18},{10... | collective-permute-start | bytes 589832 | tf_op jit(solution)/shard_map/ppermute | solution.py:26
  7.4 15.3 %collective-permute-start.2 = (bf16[384,512]{1,0:T(8,128)(2,1)}, bf16[384,512]{1,0:T(8,128)(2,1)S(1)}, u32[]{:S(2)}, u32[]{:S(2)}) collective-permute-start(bf16[384,512]{1,0:T(8,128)(2,1)} %pad_maximum_fusion.1), channel_id=1, source_target_pairs={{0,16},{8,24},{16,0},{24,8},{1,17},{9,25},{17,1},{25,9},{2,18},{10... | collective-permute-start | bytes 1179656 | tf_op jit(solution)/shard_map/ppermute | solution.py:26
  13.6 9.1 %collective-permute-start.3 = (bf16[16,1536]{1,0:T(8,128)(2,1)S(1)}, bf16[16,1536]{1,0:T(8,128)(2,1)S(1)}, u32[]{:S(2)}, u32[]{:S(2)}) collective-permute-start(bf16[16,1536]{1,0:T(8,128)(2,1)S(1)} %get-tuple-element.98), channel_id=1, source_target_pairs={{0,1},{1,0},{2,3},{3,2},{4,5},{5,4},{6,7},{7,6},{8,9},{9,8},{10,11... | collective-permute-start | bytes 147464 | tf_op jit(solution)/shard_map/ppermute | solution.py:26
  15.2 8.6 %collective-permute-start.4 = (bf16[16,1536]{1,0:T(8,128)(2,1)S(1)}, bf16[16,1536]{1,0:T(8,128)(2,1)S(1)}, u32[]{:S(2)}, u32[]{:S(2)}) collective-permute-start(bf16[16,1536]{1,0:T(8,128)(2,1)S(1)} %get-tuple-element.97), channel_id=1, source_target_pairs={{1,2},{3,4},{5,6},{2,1},{4,3},{6,5},{9,10},{11,12},{13,14},{10,9},... | collective-permute-start | bytes 147464 | tf_op jit(solution)/shard_map/ppermute | solution.py:343
  15.9 10.3 %collective-permute-start.7 = (bf16[48,1536]{1,0:T(8,128)(2,1)S(1)}, bf16[48,1536]{1,0:T(8,128)(2,1)}, u32[]{:S(2)}, u32[]{:S(2)}) collective-permute-start(bf16[48,1536]{1,0:T(8,128)(2,1)S(1)} %collective-permute-done.refs_9_), channel_id=1, source_target_pairs={{0,2},{1,3},{2,0},{3,1},{4,6},{5,7},{6,4},{7,5},{8,10},{9,11},{10,... | collective-permute-start | bytes 442376 | tf_op jit(solution)/shard_map/ppermute | solution.py:26
  22.7 14.1 %collective-permute-start.10 = (bf16[384,512]{1,0:T(8,128)(2,1)S(1)}, bf16[384,512]{1,0:T(8,128)(2,1)}, u32[]{:S(2)}, u32[]{:S(2)}) collective-permute-start(bf16[384,512]{1,0:T(8,128)(2,1)S(1)} %collective-permute-done.2.refs_1_), channel_id=1, source_target_pairs={{0,8},{8,0},{16,24},{24,16},{1,9},{9,1},{17,25},{25,17},{2,10},{10... | collective-permute-start | bytes 1179656 | tf_op jit(solution)/shard_map/ppermute | solution.py:26
  23.3 11.4 %collective-permute-start.6 = (bf16[384,256]{1,0:T(8,128)(2,1)}, bf16[384,256]{1,0:T(8,128)(2,1)}, u32[]{:S(2)}, u32[]{:S(2)}) collective-permute-start(bf16[384,256]{1,0:T(8,128)(2,1)} %collective-permute-done.1.refs_1_), channel_id=1, source_target_pairs={{0,8},{8,0},{16,24},{24,16},{1,9},{9,1},{17,25},{25,17},{2,10},{10... | collective-permute-start | bytes 589832 | tf_op jit(solution)/shard_map/ppermute | solution.py:26
  24.4 10.3 %collective-permute-start.9 = (bf16[384,256]{1,0:T(8,128)(2,1)}, bf16[384,256]{1,0:T(8,128)(2,1)}, u32[]{:S(2)}, u32[]{:S(2)}) collective-permute-start(bf16[384,256]{1,0:T(8,128)(2,1)} %collective-permute-done.1.refs_1_), channel_id=1, source_target_pairs={{0,1},{1,0},{2,3},{3,2},{4,5},{5,4},{6,7},{7,6},{8,9},{9,8},{10,11... | collective-permute-start | bytes 589832 | tf_op jit(solution)/shard_map/ppermute | solution.py:26
  26.2 18.5 %collective-permute-start.13 = (bf16[384,512]{1,0:T(8,128)(2,1)}, bf16[384,512]{1,0:T(8,128)(2,1)S(1)}, u32[]{:S(2)}, u32[]{:S(2)}) collective-permute-start(bf16[384,512]{1,0:T(8,128)(2,1)} %pad_maximum_fusion), channel_id=1, source_target_pairs={{0,16},{8,24},{16,0},{24,8},{1,17},{9,25},{17,1},{25,9},{2,18},{10... | collective-permute-start | bytes 1179656 | tf_op jit(solution)/shard_map/ppermute | solution.py:26
  27.7 7.0 %collective-permute-start.8 = (bf16[48,1536]{1,0:T(8,128)(2,1)}, bf16[48,1536]{1,0:T(8,128)(2,1)}, u32[]{:S(2)}, u32[]{:S(2)}) collective-permute-start(bf16[48,1536]{1,0:T(8,128)(2,1)} %copy-done.4), channel_id=1, source_target_pairs={{0,1},{1,0},{2,3},{3,2},{4,5},{5,4},{6,7},{7,6},{8,9},{9,8},{10,11... | collective-permute-start | bytes 442376 | tf_op jit(solution)/shard_map/ppermute | solution.py:26
  34.8 6.5 %collective-permute-start.12 = (bf16[384,256]{1,0:T(8,128)(2,1)}, bf16[384,256]{1,0:T(8,128)(2,1)S(1)}, u32[]{:S(2)}, u32[]{:S(2)}) collective-permute-start(bf16[384,256]{1,0:T(8,128)(2,1)} %collective-permute-done.9.refs_2_), channel_id=1, source_target_pairs={{0,8},{8,0},{16,24},{24,16},{1,9},{9,1},{17,25},{25,17},{2,10},{10... | collective-permute-start | bytes 589832 | tf_op jit(solution)/shard_map/ppermute | solution.py:26
  34.8 6.5 %collective-permute-start.11 = (bf16[48,1536]{1,0:T(8,128)(2,1)}, bf16[48,1536]{1,0:T(8,128)(2,1)S(1)}, u32[]{:S(2)}, u32[]{:S(2)}) collective-permute-start(bf16[48,1536]{1,0:T(8,128)(2,1)} %collective-permute-done.7.refs_10_), channel_id=1, source_target_pairs={{0,1},{1,0},{2,3},{3,2},{4,5},{5,4},{6,7},{7,6},{8,9},{9,8},{10,11... | collective-permute-start | bytes 442376 | tf_op jit(solution)/shard_map/ppermute | solution.py:26
  36.6 13.0 %collective-permute-start.15 = (bf16[192,1536]{1,0:T(8,128)(2,1)S(1)}, bf16[192,1536]{1,0:T(8,128)(2,1)S(1)}, u32[]{:S(2)}, u32[]{:S(2)}) collective-permute-start(bf16[192,1536]{1,0:T(8,128)(2,1)S(1)} %copy-done.2), channel_id=1, source_target_pairs={{0,8},{8,0},{16,24},{24,16},{1,9},{9,1},{17,25},{25,17},{2,10},{10... | collective-permute-start | bytes 1769480 | tf_op jit(solution)/shard_map/ppermute | solution.py:26
  44.8 4.7 %collective-permute-start.17 = (bf16[48,1536]{1,0:T(8,128)(2,1)}, bf16[48,1536]{1,0:T(8,128)(2,1)S(1)}, u32[]{:S(2)}, u32[]{:S(2)}) collective-permute-start(bf16[48,1536]{1,0:T(8,128)(2,1)} %collective-permute-done.7.refs_10_), channel_id=1, source_target_pairs={{0,8},{8,0},{16,24},{24,16},{1,9},{9,1},{17,25},{25,17},{2,10},{10... | collective-permute-start | bytes 442376 | tf_op jit(solution)/shard_map/ppermute | solution.py:26
  45.3 4.2 %collective-permute-start.16 = (bf16[48,1536]{1,0:T(8,128)(2,1)S(1)}, bf16[48,1536]{1,0:T(8,128)(2,1)S(1)}, u32[]{:S(2)}, u32[]{:S(2)}) collective-permute-start(bf16[48,1536]{1,0:T(8,128)(2,1)S(1)} %copy-done.5), channel_id=1, source_target_pairs={{0,8},{8,0},{16,24},{24,16},{1,9},{9,1},{17,25},{25,17},{2,10},{10... | collective-permute-start | bytes 442376 | tf_op jit(solution)/shard_map/ppermute | solution.py:26
  45.4 4.1 %collective-permute-start.18 = (bf16[48,1536]{1,0:T(8,128)(2,1)}, bf16[48,1536]{1,0:T(8,128)(2,1)S(1)}, u32[]{:S(2)}, u32[]{:S(2)}) collective-permute-start(bf16[48,1536]{1,0:T(8,128)(2,1)} %collective-permute-done.8.refs_11_), channel_id=1, source_target_pairs={{0,8},{8,0},{16,24},{24,16},{1,9},{9,1},{17,25},{25,17},{2,10},{10... | collective-permute-start | bytes 442376 | tf_op jit(solution)/shard_map/ppermute | solution.py:26
  50.9 3.8 %collective-permute-start.21 = (f32[1,3,768]{2,1,0:T(4,128)S(1)}, f32[1,3,768]{2,1,0:T(4,128)S(1)}, u32[]{:S(2)}, u32[]{:S(2)}) collective-permute-start(f32[1,3,768]{2,1,0:T(4,128)S(1)} %pad_maximum_fusion.2), channel_id=1, source_target_pairs={{0,16},{1,17},{2,18},{3,19},{4,20},{5,21},{6,22},{7,23},{8,24},{9,... | collective-permute-start | bytes 27656 | tf_op jit(solution)/shard_map/ppermute | solution.py:373
  52.6 3.7 %collective-permute-start.22 = (f32[1,3,768]{2,1,0:T(4,128)S(1)}, f32[1,3,768]{2,1,0:T(4,128)S(1)}, u32[]{:S(2)}, u32[]{:S(2)}) collective-permute-start(f32[1,3,768]{2,1,0:T(4,128)S(1)} %pad_maximum_fusion.2), channel_id=1, source_target_pairs={{0,1},{1,0},{2,3},{3,2},{4,5},{5,4},{6,7},{7,6},{8,9},{9,8},{10,11... | collective-permute-start | bytes 27656 | tf_op jit(solution)/shard_map/ppermute | solution.py:373
  54.2 4.6 %collective-permute-start.23 = (f32[1,3,768]{2,1,0:T(4,128)S(1)}, f32[1,3,768]{2,1,0:T(4,128)S(1)}, u32[]{:S(2)}, u32[]{:S(2)}) collective-permute-start(f32[1,3,768]{2,1,0:T(4,128)S(1)} %pad_maximum_fusion.2), channel_id=1, source_target_pairs={{0,17},{1,16},{2,19},{3,18},{4,21},{5,20},{6,23},{7,22},{8,25},{9,... | collective-permute-start | bytes 27656 | tf_op jit(solution)/shard_map/ppermute | solution.py:373
  58.8 4.5 %collective-permute-start.24 = (f32[1,3,768]{2,1,0:T(4,128)S(1)}, f32[1,3,768]{2,1,0:T(4,128)S(1)}, u32[]{:S(2)}, u32[]{:S(2)}) collective-permute-start(f32[1,3,768]{2,1,0:T(4,128)S(1)} %pad_maximum_fusion.3.refs_0_), channel_id=1, source_target_pairs={{0,2},{1,3},{2,0},{3,1},{4,6},{5,7},{6,4},{7,5},{8,10},{9,11},{10,... | collective-permute-start | bytes 27656 | tf_op jit(solution)/shard_map/ppermute | solution.py:373
  60.5 4.6 %collective-permute-start.25 = (f32[1,3,768]{2,1,0:T(4,128)S(1)}, f32[1,3,768]{2,1,0:T(4,128)S(1)}, u32[]{:S(2)}, u32[]{:S(2)}) collective-permute-start(f32[1,3,768]{2,1,0:T(4,128)S(1)} %pad_maximum_fusion.3.refs_0_), channel_id=1, source_target_pairs={{0,4},{1,5},{2,6},{3,7},{4,0},{5,1},{6,2},{7,3},{8,12},{9,13},{10,... | collective-permute-start | bytes 27656 | tf_op jit(solution)/shard_map/ppermute | solution.py:373
  63.1 5.5 %collective-permute-start.26 = (f32[1,3,768]{2,1,0:T(4,128)S(1)}, f32[1,3,768]{2,1,0:T(4,128)S(1)}, u32[]{:S(2)}, u32[]{:S(2)}) collective-permute-start(f32[1,3,768]{2,1,0:T(4,128)S(1)} %pad_maximum_fusion.3.refs_0_), channel_id=1, source_target_pairs={{0,6},{1,7},{2,4},{3,5},{4,2},{5,3},{6,0},{7,1},{8,14},{9,15},{10,... | collective-permute-start | bytes 27656 | tf_op jit(solution)/shard_map/ppermute | solution.py:373
  (16 other events, 91.1 us)

commit v4 on v3

--- a/solution.py
+++ b/solution.py
@@ -26,6 +26,31 @@
     return lax.ppermute(value, axis, [(i, i ^ bit) for i in range(lax.axis_size(axis))])
 
 
+def cut_kernel(place_ref, shard_ref, half_ref, zero_ref, one_ref):
+    wide = half_ref.shape[1]
+    channels = shard_ref.shape[1] // 2
+    at = pl.multiple_of(place_ref[3] * channels + 2 * wide, wide)
+    half_ref[...] = shard_ref[:, pl.ds(at, wide)]
+    for block, ref in enumerate((zero_ref, one_ref)):
+        for i in range(2):
+            at = i * channels + block * wide
+            ref[:, i * wide : (i + 1) * wide] = shard_ref[:, at : at + wide]
+
+
+def cut(place, shard, wide):
+    depth = shard.shape[0]
+    shapes = [(depth, wide), (depth, 2 * wide), (depth, 2 * wide)]
+    return pl.pallas_call(
+        cut_kernel,
+        out_shape=[jax.ShapeDtypeStruct(shape, jnp.bfloat16) for shape in shapes],
+        in_specs=[pl.BlockSpec(memory_space=pltpu.SMEM), pl.BlockSpec(memory_space=VMEM)],
+        out_specs=[pl.BlockSpec(memory_space=VMEM)] * 3,
+        compiler_params=params(4),
+        cost_estimate=cost(10**8),
+        name="cut",
+    )(place, shard)
+
+
 def normalize(values, gain):
     values = values.astype(jnp.float32)
     centre = jnp.mean(values, axis=-1, keepdims=True)
@@ -34,26 +59,33 @@
     return (deviate * lax.rsqrt(spread + 1e-05) * gain).astype(jnp.bfloat16)
 
 
-def norm_kernel(rows_ref, gain_ref, out_ref):
+def norm_kernel(place_ref, rows_ref, gain_ref, out_ref, inner_ref, outer_ref):
     step = 64
-
-    @pl.loop(0, rows_ref.shape[0] // step)
+    row_count = rows_ref.shape[0]
+
+    @pl.loop(0, row_count // step)
     def _(i):
         here = pl.ds(pl.multiple_of(i * step, step), step)
         out_ref[here, :] = normalize(rows_ref[here, :], gain_ref[...])
 
-
-def normalize_rows(rows, gain):
+    odd = place_ref[3]
+    last = row_count - HALO
+    inner_ref[...] = rows_ref[pl.ds(pl.multiple_of((1 - odd) * last, HALO), HALO), :]
+    outer_ref[...] = rows_ref[pl.ds(pl.multiple_of(odd * last, HALO), HALO), :]
+
+
+def normalize_rows(place, rows, gain):
     row_count, width = rows.shape
+    shapes = [(row_count, width), (HALO, width), (HALO, width)]
     return pl.pallas_call(
         norm_kernel,
-        out_shape=jax.ShapeDtypeStruct((row_count, width), jnp.bfloat16),
-        in_specs=[pl.BlockSpec(memory_space=VMEM)] * 2,
-        out_specs=pl.BlockSpec(memory_space=VMEM),
+        out_shape=[jax.ShapeDtypeStruct(shape, jnp.bfloat16) for shape in shapes],
+        in_specs=[pl.BlockSpec(memory_space=pltpu.SMEM)] + [pl.BlockSpec(memory_space=VMEM)] * 2,
+        out_specs=[pl.BlockSpec(memory_space=VMEM)] * 3,
         compiler_params=params(4),
         cost_estimate=cost(10**8),
         name="layer_norm",
-    )(rows, gain)
+    )(place, rows, gain)
 
 
 def near_kernel(place_ref, rows_ref, inner_ref, outer_ref, gain_ref, *refs):
@@ -234,14 +266,9 @@
     row_count, wide = convs[0].shape
     if len(weight_refs) > 1:
         depth = weight_refs[0].shape[0]
-        for i, weight_ref in enumerate(weight_refs[:2]):
+        for i, weight_ref in enumerate(weight_refs):
             at = pl.multiple_of(lax.bitwise_xor(place_ref[0], i) * depth, depth)
             weights[pl.ds(at, depth), :] = weight_ref[...]
-        for i, weight_ref in enumerate(weight_refs[2:]):
-            rows = weight_ref.shape[0]
-            at = lax.bitwise_xor(place_ref[0], 2 + i // 4) * depth
-            at += lax.bitwise_xor(2 * place_ref[3] + place_ref[4], i % 4) * rows
-            weights[pl.ds(pl.multiple_of(at, rows), rows), :] = weight_ref[...]
     else:
         weights[...] = weight_refs[0][...]
     mean, square, count = merged(rows_of(stat_refs))
@@ -309,8 +336,8 @@
     direct = fsdp_count == 4 and ctx_count == 8
     rows = frames[0]
     gain = ln_gain[None]
-    parity, pair = lax.rem(ctx, 2), lax.rem(ctx // 2, 2)
-    place = jnp.stack([fsdp, ctx * row_count, lengths[0], parity, pair]).astype(jnp.int32)
+    parity = lax.rem(ctx, 2)
+    place = jnp.stack([fsdp, ctx * row_count, lengths[0], parity]).astype(jnp.int32)
     ends = ctx_count - 1
     down, up = [(i, i + 1) for i in range(ends)], [(i + 1, i) for i in range(ends)]
     both = ("fsdp", "ctx")
@@ -320,53 +347,26 @@
         return front_block(block, wide, place, normed, weights, dw_kernel, *extra)
 
     if direct:
-        last = row_count - HALO
-        depth = w_out.shape[0] // 4
-
-        def columns(shard, block):
-            at = block * wide
-            return jnp.concatenate([shard[:, at : at + wide], shard[:, channels + at : channels + at + wide]], 1)
-
-        quarter = lax.dynamic_slice_in_dim(w_out, (2 * parity + pair) * depth, depth, axis=0)
-        quarter, later_in = tie(quarter, w_in)
-        half = lax.dynamic_slice_in_dim(later_in, parity * channels + 2 * wide, wide, axis=1)
-        half, later_in = tie(half, later_in)
-        block = columns(later_in, 0)
-        quarter, half, block = (swap(part, "fsdp", 2) for part in (quarter, half, block))
-        across = swap(later_in, "fsdp", 1)
-        normed = normalize_rows(rows, gain)
-        normed, later_rows, quarter = tie(normed, rows, quarter)
-        inner = lax.dynamic_slice_in_dim(later_rows, (1 - parity) * last, HALO, axis=0)
-        outer = lax.dynamic_slice_in_dim(later_rows, parity * last, HALO, axis=0)
+        half, zero, one = (swap(part, "fsdp", 2) for part in cut(place, w_in, wide))
+        across = swap(w_in, "fsdp", 1)
+        normed, inner, outer = normalize_rows(place, rows, gain)
+        normed, half = tie(normed, half)
+        rest = swap(half, "ctx", 1)
         inner = swap(inner, "ctx", 1)
         pairs = [(i, i + 1) for i in range(1, ends, 2)]
         outer = lax.ppermute(outer, "ctx", pairs + [(j, i) for i, j in pairs])
-        quarters = [quarter, swap(quarter, "ctx", 2), swap(quarter, "ctx", 1)]
-        normed, half, later_in = tie(normed, half, later_in)
-        over_x = {2: [half, swap(half, "ctx", 1)]}
         beyond_half = swap(half, "fsdp", 1)
-        normed, part = tie(normed, columns(later_in, 1))
-        over_x[1] = [swap(part, "fsdp", 2)]
-        normed, block = tie(normed, block)
-        over_x[0] = [block]
-        beyond_zero = swap(block, "fsdp", 1)
+        normed, zero, rest = tie(normed, zero, rest)
+        beyond_zero, beyond_rest = swap(zero, "fsdp", 1), swap(rest, "fsdp", 1)
         normed, *partials = near_product(place, normed, inner, outer, gain, w_in, across)
-        partials[0], beyond_half, *quarters = tie(partials[0], beyond_half, *quarters)
-        quarters.append(swap(quarters[1], "ctx", 1))
-        partials[0], over_x[2][1], w_out = tie(partials[0], over_x[2][1], w_out)
-
-        beyond_two = [beyond_half, swap(over_x[2][1], "fsdp", 1)]
-        conv_one, stat_one = front(0, [partials[0], *over_x[0], beyond_zero])
-        conv_one, partials[2], quarters[3] = tie(conv_one, partials[2], quarters[3])
-        beyond_quarters = [swap(part, "fsdp", 1) for part in quarters]
-        conv_two, stat_two = front(2, [partials[2], *over_x[2], *beyond_two])
-        conv_two, over_x[1][0] = tie(conv_two, over_x[1][0])
-        across_out = swap(w_out, "fsdp", 1)
-        beyond_one = swap(over_x[1][0], "fsdp", 1)
-        conv_three, stats = front(1, [partials[1], *over_x[1], beyond_one], (stat_one, stat_two), 1)
-        stats, across_out, *beyond_quarters = tie(stats, across_out, *beyond_quarters)
-        out_weights = [w_out, across_out, *quarters, *beyond_quarters]
-        convs = [conv_one, conv_three, conv_two]
+        partials[0], beyond_half, w_out = tie(partials[0], beyond_half, w_out)
+        conv_zero, stat_zero = front(0, [partials[0], zero, beyond_zero])
+        conv_zero, partials[2] = tie(conv_zero, partials[2])
+        conv_two, stat_two = front(2, [partials[2], half, rest, beyond_half, beyond_rest])
+        conv_two, one, w_out = tie(conv_two, one, w_out)
+        remote_out, across_out = swap(w_out, "fsdp", 2), swap(w_out, "fsdp", 1)
+        conv_one, stats = front(1, [partials[1], one, swap(one, "fsdp", 1)], (stat_zero, stat_two), 1)
+        convs = [conv_zero, conv_one, conv_two]
 
         def others(flips):
             return [
@@ -384,6 +384,8 @@
         stats = union([stats] + others([(1, 0)]))
         stats = union([stats] + others([(2, 0), (0, 1), (2, 1)]))
         stats = [stats] + others([(0, 2), (0, 4), (0, 6)])
+        *stats, remote_out = tie(*stats, remote_out)
+        out_weights = [w_out, across_out, remote_out, swap(remote_out, "fsdp", 1)]
     else:
         full_in = lax.all_gather(w_in, "fsdp", axis=0, tiled=True)
         out_weights = [lax.all_gather(w_out, "fsdp", axis=0, tiled=True)]
@@ -391,7 +393,8 @@
         after = lax.ppermute(rows[:HALO], "ctx", up)
         inner = jnp.where(parity == 0, after, before)
         outer = jnp.where(parity == 0, before, after)
-        (normed,) = near_product(place, normalize_rows(rows, gain), inner, outer, gain)
+        normed, _, _ = normalize_rows(place, rows, gain)
+        (normed,) = near_product(place, normed, inner, outer, gain)
         near_by = 2 if ctx_count % 2 == 0 else 1
         groups = [
             [member(f, p + i) for f in range(fsdp_count) for i in range(near_by)]

time: 72.4 us -> 74.1 us (1.023)
  waiting for transfers between devices: 16.1 us -> 32.4 us
  local copies, waits for them, and re-layouts: 8.89 us -> 2.71 us
  starting transfers between devices: 26.4 us -> 20.8 us
  other arithmetic: 1.7 us -> 0.18 us
  Pallas kernels: 18 us -> 17 us
    ppermute x7, waiting for transfers between devices: 10.4 us -> 18.9 us  [others(): lax.ppermute(stats, both, [(member(f, p), member(f ^ df, p ^ dp)) for f i...]
    ppermute x19 -> x13, starting transfers between devices: 17.3 us -> 9.21 us  [swap(): lax.ppermute(value, axis, [(i, i ^ bit) for i in range(lax.axis_size(axis...]
    ppermute x19 -> x13, waiting for transfers between devices: 5.65 us -> 13.5 us  [swap(): lax.ppermute(value, axis, [(i, i ^ bit) for i in range(lax.axis_size(axis...]
    dynamic_slice x3 -> x0, local copies, waits for them, and re-layouts: 3.45 us -> none  [the longest x1 1.62 us: body(): lax.dynamic_slice_in_dim(later_in, parity * channels + 2 * wide, wide, ax...]
    ppermute x7, starting transfers between devices: 8.44 us -> 10.8 us  [others(): lax.ppermute(stats, both, [(member(f, p), member(f ^ df, p ^ dp)) for f i...]
    concatenate x2 -> x0, other arithmetic: 1.59 us -> none  [columns(): jnp.concatenate([shard[:, at:at + wide], shard[:, channels + at:channels...]
    unnamed x26 -> x16, local copies, waits for them, and re-layouts: 4.27 us -> 2.7 us
    pallas_call x1 -> x2, Pallas kernels: 1.9 us -> 3.05 us  [the longest x1 2.45 us: normalize_rows(): pl.pallas_call(norm_kernel, out_shape=[jax.ShapeDtypeStruct(shape, jnp.bf...]
  transfers between devices with their start and end apart: 27 -> 21, of which waited for: 10 -> 11; matrix products, arithmetic and copies ran while one was open for 5% -> 0% of each run, Pallas kernels for 20% -> 15%
where the time goes in v4:
time: 74.1 us; the launch traced here: 73.8 us
  waiting for transfers between devices  32.4 us (44%)
  starting transfers between devices  20.8 us (28%)
  Pallas kernels  17 us (23%)
  local copies, waits for them, and re-layouts  2.71 us (4%)
  between operations  0.81 us (1%)
    ppermute x7, waiting for transfers between devices, others(): lax.ppermute(stats, both, [(member(f, p), member(f ^ df, p ^ dp)) for f i...  18.9 us
    ppermute x13, waiting for transfers between devices, swap(): lax.ppermute(value, axis, [(i, i ^ bit) for i in range(lax.axis_size(axis...  13.5 us
    ppermute x7, starting transfers between devices, others(): lax.ppermute(stats, both, [(member(f, p), member(f ^ df, p ^ dp)) for f i...  10.8 us
    ppermute x13, starting transfers between devices, swap(): lax.ppermute(value, axis, [(i, i ^ bit) for i in range(lax.axis_size(axis...  9.21 us
    pallas_call x3, Pallas kernels, front_block(): pl.pallas_call(functools.partial(front_kernel, block, len(earlier)), out_...  8.66 us
    pallas_call x1, Pallas kernels, back(): pl.pallas_call(functools.partial(back_kernel, len(stats)), out_shape=jax....  2.93 us
    unnamed x16, local copies, waits for them, and re-layouts  2.7 us
    pallas_call x1, Pallas kernels, normalize_rows(): pl.pallas_call(norm_kernel, out_shape=[jax.ShapeDtypeStruct(shape, jnp.bf...  2.45 us
  transfers between devices with their start and end apart: 21, of which 11 were waited for; matrix products, arithmetic and copies ran while one was open for 0% of the time, Pallas kernels for 15%

profile of v4, /device:TPU:0, one launch (start us, length us, event | category | flops | bytes accessed | tf_op | source)
XLA Modules:
  0.0 73.8 jit_solution(10722550569969970067)
XLA Ops:
  3.1 2.6 %collective-permute-start = (bf16[384,256]{1,0:T(8,128)(2,1)S(1)}, bf16[384,256]{1,0:T(8,128)(2,1)S(1)}, u32[]{:S(2)}, u32[]{:S(2)}) collective-permute-start(bf16[384,256]{1,0:T(8,128)(2,1)S(1)} %get-tuple-element.40), channel_id=1, source_target_pairs={{0,16},{8,24},{16,0},{24,8},{1,17},{9,25},{17,1},{25,9},{2,18},{10... | collective-permute-start | bytes 589832 | tf_op jit(solution)/shard_map/ppermute | solution.py:26
  5.7 1.4 %copy-done.2 = bf16[1,512,1536]{2,1,0:T(8,128)(2,1)S(1)} copy-done((bf16[1,512,1536]{2,1,0:T(8,128)(2,1)S(1)}, bf16[1,512,1536]{2,1,0:T(8,128)(2,1)}, u32[]{:S(2)}) %copy-start.2) | copy-done | bytes 1572888
  7.1 2.5 %layer_norm.1 = (bf16[512,1536]{1,0:T(8,128)(2,1)S(1)}, bf16[16,1536]{1,0:T(8,128)(2,1)S(1)}, bf16[16,1536]{1,0:T(8,128)(2,1)S(1)}) custom-call(s32[4]{0:T(128)S(1)} %pad_add_fusion.place_ref, bf16[512,1536]{1,0:T(8,128)(2,1)S(1)} %bitcast.5, f32[1,1536]{1,0:T(1,128)S(1)} %broadcast_in_dim.14.gain_ref), custom_call_target="tpu_custom_call" | custom-call | flops 100000000 | tf_op jit(solution)/shard_map/layer_norm/pallas_call | solution.py:80
  9.6 1.8 %collective-permute-done.refs_1_ = bf16[384,256]{1,0:T(8,128)(2,1)S(1)} collective-permute-done((bf16[384,256]{1,0:T(8,128)(2,1)S(1)}, bf16[384,256]{1,0:T(8,128)(2,1)S(1)}, u32[]{:S(2)}, u32[]{:S(2)}) %collective-permute-start) | collective-permute-done | bytes 196640 | tf_op jit(solution)/shard_map/ppermute | solution.py:26
  11.4 2.0 %collective-permute-start.2 = (bf16[384,256]{1,0:T(8,128)(2,1)S(1)}, bf16[384,256]{1,0:T(8,128)(2,1)S(1)}, u32[]{:S(2)}, u32[]{:S(2)}) collective-permute-start(bf16[384,256]{1,0:T(8,128)(2,1)S(1)} %collective-permute-done.refs_1_), channel_id=1, source_target_pairs={{0,1},{1,0},{2,3},{3,2},{4,5},{5,4},{6,7},{7,6},{8,9},{9,8},{10,11... | collective-permute-start | bytes 589832 | tf_op jit(solution)/shard_map/ppermute | solution.py:26
  13.4 4.6 %collective-permute-done.2.refs_2_ = bf16[384,256]{1,0:T(8,128)(2,1)S(1)} collective-permute-done((bf16[384,256]{1,0:T(8,128)(2,1)S(1)}, bf16[384,256]{1,0:T(8,128)(2,1)S(1)}, u32[]{:S(2)}, u32[]{:S(2)}) %collective-permute-start.2) | collective-permute-done | bytes 196640 | tf_op jit(solution)/shard_map/ppermute | solution.py:26
  17.9 1.7 %collective-permute-done.1.refs_1_ = bf16[384,512]{1,0:T(8,128)(2,1)S(1)} collective-permute-done((bf16[384,512]{1,0:T(8,128)(2,1)S(1)}, bf16[384,512]{1,0:T(8,128)(2,1)S(1)}, u32[]{:S(2)}, u32[]{:S(2)}) %collective-permute-start.1) | collective-permute-done | bytes 393248 | tf_op jit(solution)/shard_map/ppermute | solution.py:26
  19.6 1.8 %collective-permute-start.9 = (bf16[384,512]{1,0:T(8,128)(2,1)S(1)}, bf16[384,512]{1,0:T(8,128)(2,1)S(1)}, u32[]{:S(2)}, u32[]{:S(2)}) collective-permute-start(bf16[384,512]{1,0:T(8,128)(2,1)S(1)} %get-tuple-element.60), channel_id=1, source_target_pairs={{0,16},{8,24},{16,0},{24,8},{1,17},{9,25},{17,1},{25,9},{2,18},{10... | collective-permute-start | bytes 1179656 | tf_op jit(solution)/shard_map/ppermute | solution.py:26
  21.4 1.5 %collective-permute-start.3 = (bf16[16,1536]{1,0:T(8,128)(2,1)S(1)}, bf16[16,1536]{1,0:T(8,128)(2,1)S(1)}, u32[]{:S(2)}, u32[]{:S(2)}) collective-permute-start(bf16[16,1536]{1,0:T(8,128)(2,1)S(1)} %get-tuple-element.45), channel_id=1, source_target_pairs={{0,1},{1,0},{2,3},{3,2},{4,5},{5,4},{6,7},{7,6},{8,9},{9,8},{10,11... | collective-permute-start | bytes 147464 | tf_op jit(solution)/shard_map/ppermute | solution.py:26
  23.7 1.8 %collective-permute-done.3.inner_ref = bf16[16,1536]{1,0:T(8,128)(2,1)S(1)} collective-permute-done((bf16[16,1536]{1,0:T(8,128)(2,1)S(1)}, bf16[16,1536]{1,0:T(8,128)(2,1)S(1)}, u32[]{:S(2)}, u32[]{:S(2)}) %collective-permute-start.3) | collective-permute-done | bytes 49184 | tf_op jit(solution)/shard_map/ppermute | solution.py:26
  26.0 2.3 %near.1 = (bf16[544,1536]{1,0:T(8,128)(2,1)S(1)}, f32[544,512]{1,0:T(8,128)S(1)}, f32[544,512]{1,0:T(8,128)S(1)}, f32[544,512]{1,0:T(8,128)S(1)}) custom-call(s32[4]{0:T(128)S(1)} %pad_add_fusion.place_ref, bf16[512,1536]{1,0:T(8,128)(2,1)S(1)} %get-tuple-element.44.rows_ref, bf16[16,1536]{1,0:T(8,128)(2,1)S(1)} %collective-permute-done.3.inner_ref, ...), custom_call_target="tpu_custom_call" | custom-call | flops 100000000 | tf_op jit(solution)/shard_map/near/pallas_call | solution.py:128
  28.4 2.9 %front.3 = (f32[512,256]{1,0:T(8,128)S(1)}, f32[3,256]{1,0:T(4,128)S(1)}) custom-call(s32[4]{0:T(128)S(1)} %pad_add_fusion.place_ref, bf16[544,1536]{1,0:T(8,128)(2,1)S(1)} %get-tuple-element.47.normed_ref, f32[544,512]{1,0:T(8,128)S(1)} %get-tuple-element.49.refs_0_, bf16[384,512]{1,0:T(8,128)(2,1)S(1)} %collective-permute-done.1.refs_1_, ...), custom_call_target="tpu_custom_call" | custom-call | flops 100000000 | tf_op jit(solution)/shard_map/front/pallas_call | solution.py:213
  31.3 2.9 %front.4 = (f32[512,256]{1,0:T(8,128)S(1)}, f32[3,256]{1,0:T(4,128)S(1)}) custom-call(s32[4]{0:T(128)S(1)} %pad_add_fusion.place_ref, bf16[544,1536]{1,0:T(8,128)(2,1)S(1)} %get-tuple-element.47.normed_ref, f32[544,512]{1,0:T(8,128)S(1)} %get-tuple-element.54.refs_0_, bf16[384,256]{1,0:T(8,128)(2,1)S(1)} %collective-permute-done.refs_1_, ...), custom_call_target="tpu_custom_call" | custom-call | flops 100000000 | tf_op jit(solution)/shard_map/front/pallas_call | solution.py:213
  34.2 1.7 %collective-permute-done.10.refs_4_ = bf16[384,512]{1,0:T(8,128)(2,1)S(1)} collective-permute-done((bf16[384,512]{1,0:T(8,128)(2,1)S(1)}, bf16[384,512]{1,0:T(8,128)(2,1)S(1)}, u32[]{:S(2)}, u32[]{:S(2)}) %collective-permute-start.10) | collective-permute-done | bytes 393248 | tf_op jit(solution)/shard_map/ppermute | solution.py:26
  36.0 2.9 %front.5 = (f32[512,256]{1,0:T(8,128)S(1)}, f32[1,3,768]{2,1,0:T(4,128)S(1)}) custom-call(s32[4]{0:T(128)S(1)} %pad_add_fusion.place_ref, bf16[544,1536]{1,0:T(8,128)(2,1)S(1)} %get-tuple-element.47.normed_ref, f32[3,256]{1,0:T(4,128)S(1)} %get-tuple-element.51.refs_0_, f32[3,256]{1,0:T(4,128)S(1)} %get-tuple-element.57.refs_1_, ...), custom_call_target="tpu_custom_call" | custom-call | flops 100000000 | tf_op jit(solution)/shard_map/front/pallas_call | solution.py:213
  41.2 4.8 %collective-permute-start.13 = (f32[1,3,768]{2,1,0:T(4,128)S(1)}, f32[1,3,768]{2,1,0:T(4,128)S(1)}, u32[]{:S(2)}, u32[]{:S(2)}) collective-permute-start(f32[1,3,768]{2,1,0:T(4,128)S(1)} %pad_maximum_fusion), channel_id=1, source_target_pairs={{0,1},{1,0},{2,3},{3,2},{4,5},{5,4},{6,7},{7,6},{8,9},{9,8},{10,11... | collective-permute-start | bytes 27656 | tf_op jit(solution)/shard_map/ppermute | solution.py:373
  46.3 8.8 %collective-permute-done.12 = f32[1,3,768]{2,1,0:T(4,128)S(1)} collective-permute-done((f32[1,3,768]{2,1,0:T(4,128)S(1)}, f32[1,3,768]{2,1,0:T(4,128)S(1)}, u32[]{:S(2)}, u32[]{:S(2)}) %collective-permute-start.12) | collective-permute-done | bytes 9248 | tf_op jit(solution)/shard_map/ppermute | solution.py:373
  55.0 4.1 %collective-permute-done.14 = f32[1,3,768]{2,1,0:T(4,128)S(1)} collective-permute-done((f32[1,3,768]{2,1,0:T(4,128)S(1)}, f32[1,3,768]{2,1,0:T(4,128)S(1)}, u32[]{:S(2)}, u32[]{:S(2)}) %collective-permute-start.14) | collective-permute-done | bytes 9248 | tf_op jit(solution)/shard_map/ppermute | solution.py:373
  59.2 1.6 %collective-permute-start.15 = (f32[1,3,768]{2,1,0:T(4,128)S(1)}, f32[1,3,768]{2,1,0:T(4,128)S(1)}, u32[]{:S(2)}, u32[]{:S(2)}) collective-permute-start(f32[1,3,768]{2,1,0:T(4,128)S(1)} %pad_maximum_fusion.1.refs_0_), channel_id=1, source_target_pairs={{0,2},{1,3},{2,0},{3,1},{4,6},{5,7},{6,4},{7,5},{8,10},{9,11},{10,... | collective-permute-start | bytes 27656 | tf_op jit(solution)/shard_map/ppermute | solution.py:373
  60.9 2.5 %collective-permute-start.16 = (f32[1,3,768]{2,1,0:T(4,128)S(1)}, f32[1,3,768]{2,1,0:T(4,128)S(1)}, u32[]{:S(2)}, u32[]{:S(2)}) collective-permute-start(f32[1,3,768]{2,1,0:T(4,128)S(1)} %pad_maximum_fusion.1.refs_0_), channel_id=1, source_target_pairs={{0,4},{1,5},{2,6},{3,7},{4,0},{5,1},{6,2},{7,3},{8,12},{9,13},{10,... | collective-permute-start | bytes 27656 | tf_op jit(solution)/shard_map/ppermute | solution.py:373
  63.7 1.8 %collective-permute-done.16.refs_2_ = f32[1,3,768]{2,1,0:T(4,128)S(1)} collective-permute-done((f32[1,3,768]{2,1,0:T(4,128)S(1)}, f32[1,3,768]{2,1,0:T(4,128)S(1)}, u32[]{:S(2)}, u32[]{:S(2)}) %collective-permute-start.16) | collective-permute-done | bytes 9248 | tf_op jit(solution)/shard_map/ppermute | solution.py:373
  65.5 3.4 %collective-permute-done.17.refs_3_ = f32[1,3,768]{2,1,0:T(4,128)S(1)} collective-permute-done((f32[1,3,768]{2,1,0:T(4,128)S(1)}, f32[1,3,768]{2,1,0:T(4,128)S(1)}, u32[]{:S(2)}, u32[]{:S(2)}) %collective-permute-start.17) | collective-permute-done | bytes 9248 | tf_op jit(solution)/shard_map/ppermute | solution.py:373
  68.9 2.0 %collective-permute-done.20.refs_10_ = bf16[192,1536]{1,0:T(8,128)(2,1)S(1)} collective-permute-done((bf16[192,1536]{1,0:T(8,128)(2,1)S(1)}, bf16[192,1536]{1,0:T(8,128)(2,1)S(1)}, u32[]{:S(2)}, u32[]{:S(2)}) %collective-permute-start.20) | collective-permute-done | bytes 589856 | tf_op jit(solution)/shard_map/ppermute | solution.py:26
  70.9 2.9 %back.1 = bf16[512,1536]{1,0:T(8,128)(2,1)} custom-call(s32[4]{0:T(128)S(1)} %pad_add_fusion.place_ref, f32[1,768]{1,0:T(1,128)S(1)} %broadcast_in_dim.12.gain_ref, f32[1,768]{1,0:T(1,128)S(1)} %broadcast_in_dim.13.shift_ref, f32[1,3,768]{2,1,0:T(4,128)S(1)} %pad_maximum_fusion.1.refs_0_, f32[1,3,768]{2,1,0:T(4,128)S(1)} %collective-permute-done.15.refs_1_, ...), custom_call_target="tpu_custom_call" | custom-call | flops 1000000000 | tf_op jit(solution)/shard_map/back/pallas_call | solution.py:305
  (49 shorter events, 6.9 us)
Async XLA Ops:
  0.0 26.0 %collective-permute-start.5 = (bf16[384,1536]{1,0:T(8,128)(2,1)}, bf16[384,1536]{1,0:T(8,128)(2,1)S(1)}, u32[]{:S(2)}, u32[]{:S(2)}) collective-permute-start(bf16[384,1536]{1,0:T(8,128)(2,1)} %refs_0_.1), channel_id=1, source_target_pairs={{0,8},{8,0},{16,24},{24,16},{1,9},{9,1},{17,25},{25,17},{2,10},{10... | collective-permute-start | bytes 3538952 | tf_op jit(solution)/shard_map/ppermute | solution.py:26
  2.5 23.5 %copy-start.1 = (bf16[384,1536]{1,0:T(8,128)(2,1)S(1)}, bf16[384,1536]{1,0:T(8,128)(2,1)}, u32[]{:S(2)}) copy-start(bf16[384,1536]{1,0:T(8,128)(2,1)} %refs_0_.1) | copy-start | bytes 3538948
  3.1 8.3 %collective-permute-start = (bf16[384,256]{1,0:T(8,128)(2,1)S(1)}, bf16[384,256]{1,0:T(8,128)(2,1)S(1)}, u32[]{:S(2)}, u32[]{:S(2)}) collective-permute-start(bf16[384,256]{1,0:T(8,128)(2,1)S(1)} %get-tuple-element.40), channel_id=1, source_target_pairs={{0,16},{8,24},{16,0},{24,8},{1,17},{9,25},{17,1},{25,9},{2,18},{10... | collective-permute-start | bytes 589832 | tf_op jit(solution)/shard_map/ppermute | solution.py:26
  5.6 14.0 %collective-permute-start.1 = (bf16[384,512]{1,0:T(8,128)(2,1)S(1)}, bf16[384,512]{1,0:T(8,128)(2,1)S(1)}, u32[]{:S(2)}, u32[]{:S(2)}) collective-permute-start(bf16[384,512]{1,0:T(8,128)(2,1)S(1)} %get-tuple-element.42), channel_id=1, source_target_pairs={{0,16},{8,24},{16,0},{24,8},{1,17},{9,25},{17,1},{25,9},{2,18},{10... | collective-permute-start | bytes 1179656 | tf_op jit(solution)/shard_map/ppermute | solution.py:26
  11.4 6.5 %collective-permute-start.2 = (bf16[384,256]{1,0:T(8,128)(2,1)S(1)}, bf16[384,256]{1,0:T(8,128)(2,1)S(1)}, u32[]{:S(2)}, u32[]{:S(2)}) collective-permute-start(bf16[384,256]{1,0:T(8,128)(2,1)S(1)} %collective-permute-done.refs_1_), channel_id=1, source_target_pairs={{0,1},{1,0},{2,3},{3,2},{4,5},{5,4},{6,7},{7,6},{8,9},{9,8},{10,11... | collective-permute-start | bytes 589832 | tf_op jit(solution)/shard_map/ppermute | solution.py:26
  19.6 8.7 %collective-permute-start.7 = (bf16[384,512]{1,0:T(8,128)(2,1)S(1)}, bf16[384,512]{1,0:T(8,128)(2,1)S(1)}, u32[]{:S(2)}, u32[]{:S(2)}) collective-permute-start(bf16[384,512]{1,0:T(8,128)(2,1)S(1)} %collective-permute-done.1.refs_1_), channel_id=1, source_target_pairs={{0,8},{8,0},{16,24},{24,16},{1,9},{9,1},{17,25},{25,17},{2,10},{10... | collective-permute-start | bytes 1179656 | tf_op jit(solution)/shard_map/ppermute | solution.py:26
  19.6 14.5 %collective-permute-start.9 = (bf16[384,512]{1,0:T(8,128)(2,1)S(1)}, bf16[384,512]{1,0:T(8,128)(2,1)S(1)}, u32[]{:S(2)}, u32[]{:S(2)}) collective-permute-start(bf16[384,512]{1,0:T(8,128)(2,1)S(1)} %get-tuple-element.60), channel_id=1, source_target_pairs={{0,16},{8,24},{16,0},{24,8},{1,17},{9,25},{17,1},{25,9},{2,18},{10... | collective-permute-start | bytes 1179656 | tf_op jit(solution)/shard_map/ppermute | solution.py:26
  21.4 4.1 %collective-permute-start.3 = (bf16[16,1536]{1,0:T(8,128)(2,1)S(1)}, bf16[16,1536]{1,0:T(8,128)(2,1)S(1)}, u32[]{:S(2)}, u32[]{:S(2)}) collective-permute-start(bf16[16,1536]{1,0:T(8,128)(2,1)S(1)} %get-tuple-element.45), channel_id=1, source_target_pairs={{0,1},{1,0},{2,3},{3,2},{4,5},{5,4},{6,7},{7,6},{8,9},{9,8},{10,11... | collective-permute-start | bytes 147464 | tf_op jit(solution)/shard_map/ppermute | solution.py:26
  22.9 2.6 %collective-permute-start.4 = (bf16[16,1536]{1,0:T(8,128)(2,1)S(1)}, bf16[16,1536]{1,0:T(8,128)(2,1)S(1)}, u32[]{:S(2)}, u32[]{:S(2)}) collective-permute-start(bf16[16,1536]{1,0:T(8,128)(2,1)S(1)} %get-tuple-element.46), channel_id=1, source_target_pairs={{1,2},{3,4},{5,6},{2,1},{4,3},{6,5},{9,10},{11,12},{13,14},{10,9},... | collective-permute-start | bytes 147464 | tf_op jit(solution)/shard_map/ppermute | solution.py:357
  25.5 2.9 %collective-permute-start.6 = (bf16[384,256]{1,0:T(8,128)(2,1)S(1)}, bf16[384,256]{1,0:T(8,128)(2,1)S(1)}, u32[]{:S(2)}, u32[]{:S(2)}) collective-permute-start(bf16[384,256]{1,0:T(8,128)(2,1)S(1)} %collective-permute-done.refs_1_), channel_id=1, source_target_pairs={{0,8},{8,0},{16,24},{24,16},{1,9},{9,1},{17,25},{25,17},{2,10},{10... | collective-permute-start | bytes 589832 | tf_op jit(solution)/shard_map/ppermute | solution.py:26
  25.5 5.8 %collective-permute-start.8 = (bf16[384,256]{1,0:T(8,128)(2,1)S(1)}, bf16[384,256]{1,0:T(8,128)(2,1)S(1)}, u32[]{:S(2)}, u32[]{:S(2)}) collective-permute-start(bf16[384,256]{1,0:T(8,128)(2,1)S(1)} %collective-permute-done.2.refs_2_), channel_id=1, source_target_pairs={{0,8},{8,0},{16,24},{24,16},{1,9},{9,1},{17,25},{25,17},{2,10},{10... | collective-permute-start | bytes 589832 | tf_op jit(solution)/shard_map/ppermute | solution.py:26
  34.2 1.8 %collective-permute-start.10 = (bf16[384,512]{1,0:T(8,128)(2,1)S(1)}, bf16[384,512]{1,0:T(8,128)(2,1)S(1)}, u32[]{:S(2)}, u32[]{:S(2)}) collective-permute-start(bf16[384,512]{1,0:T(8,128)(2,1)S(1)} %collective-permute-done.9.refs_3_), channel_id=1, source_target_pairs={{0,8},{8,0},{16,24},{24,16},{1,9},{9,1},{17,25},{25,17},{2,10},{10... | collective-permute-start | bytes 1179656 | tf_op jit(solution)/shard_map/ppermute | solution.py:26
  35.9 33.0 %copy-start.6 = (f32[768]{0:T(1024)S(1)}, f32[768]{0:T(1024)}, u32[]{:S(2)}) copy-start(f32[768]{0:T(1024)} %param.13) | copy-start | bytes 9220
  36.0 33.0 %copy-start.7 = (f32[768]{0:T(1024)S(1)}, f32[768]{0:T(1024)}, u32[]{:S(2)}) copy-start(f32[768]{0:T(1024)} %param.14) | copy-start | bytes 9220
  38.8 1.2 %collective-permute-start.11 = (f32[1,3,768]{2,1,0:T(4,128)S(1)}, f32[1,3,768]{2,1,0:T(4,128)S(1)}, u32[]{:S(2)}, u32[]{:S(2)}) collective-permute-start(f32[1,3,768]{2,1,0:T(4,128)S(1)} %get-tuple-element.63), channel_id=1, source_target_pairs={{0,8},{1,9},{2,10},{3,11},{4,12},{5,13},{6,14},{7,15},{8,0},{9,1},... | collective-permute-start | bytes 27656 | tf_op jit(solution)/shard_map/ppermute | solution.py:373
  39.0 29.9 %collective-permute-start.18 = (bf16[192,1536]{1,0:T(8,128)(2,1)S(1)}, bf16[192,1536]{1,0:T(8,128)(2,1)S(1)}, u32[]{:S(2)}, u32[]{:S(2)}) collective-permute-start(bf16[192,1536]{1,0:T(8,128)(2,1)S(1)} %copy-done.4), channel_id=1, source_target_pairs={{0,16},{8,24},{16,0},{24,8},{1,17},{9,25},{17,1},{25,9},{2,18},{10... | collective-permute-start | bytes 1769480 | tf_op jit(solution)/shard_map/ppermute | solution.py:26
  40.1 14.9 %collective-permute-start.12 = (f32[1,3,768]{2,1,0:T(4,128)S(1)}, f32[1,3,768]{2,1,0:T(4,128)S(1)}, u32[]{:S(2)}, u32[]{:S(2)}) collective-permute-start(f32[1,3,768]{2,1,0:T(4,128)S(1)} %pad_maximum_fusion), channel_id=1, source_target_pairs={{0,16},{1,17},{2,18},{3,19},{4,20},{5,21},{6,22},{7,23},{8,24},{9,... | collective-permute-start | bytes 27656 | tf_op jit(solution)/shard_map/ppermute | solution.py:373
  41.2 13.8 %collective-permute-start.13 = (f32[1,3,768]{2,1,0:T(4,128)S(1)}, f32[1,3,768]{2,1,0:T(4,128)S(1)}, u32[]{:S(2)}, u32[]{:S(2)}) collective-permute-start(f32[1,3,768]{2,1,0:T(4,128)S(1)} %pad_maximum_fusion), channel_id=1, source_target_pairs={{0,1},{1,0},{2,3},{3,2},{4,5},{5,4},{6,7},{7,6},{8,9},{9,8},{10,11... | collective-permute-start | bytes 27656 | tf_op jit(solution)/shard_map/ppermute | solution.py:373
  46.0 13.2 %collective-permute-start.14 = (f32[1,3,768]{2,1,0:T(4,128)S(1)}, f32[1,3,768]{2,1,0:T(4,128)S(1)}, u32[]{:S(2)}, u32[]{:S(2)}) collective-permute-start(f32[1,3,768]{2,1,0:T(4,128)S(1)} %pad_maximum_fusion), channel_id=1, source_target_pairs={{0,17},{1,16},{2,19},{3,18},{4,21},{5,20},{6,23},{7,22},{8,25},{9,... | collective-permute-start | bytes 27656 | tf_op jit(solution)/shard_map/ppermute | solution.py:373
  59.2 4.5 %collective-permute-start.15 = (f32[1,3,768]{2,1,0:T(4,128)S(1)}, f32[1,3,768]{2,1,0:T(4,128)S(1)}, u32[]{:S(2)}, u32[]{:S(2)}) collective-permute-start(f32[1,3,768]{2,1,0:T(4,128)S(1)} %pad_maximum_fusion.1.refs_0_), channel_id=1, source_target_pairs={{0,2},{1,3},{2,0},{3,1},{4,6},{5,7},{6,4},{7,5},{8,10},{9,11},{10,... | collective-permute-start | bytes 27656 | tf_op jit(solution)/shard_map/ppermute | solution.py:373
  60.9 4.6 %collective-permute-start.16 = (f32[1,3,768]{2,1,0:T(4,128)S(1)}, f32[1,3,768]{2,1,0:T(4,128)S(1)}, u32[]{:S(2)}, u32[]{:S(2)}) collective-permute-start(f32[1,3,768]{2,1,0:T(4,128)S(1)} %pad_maximum_fusion.1.refs_0_), channel_id=1, source_target_pairs={{0,4},{1,5},{2,6},{3,7},{4,0},{5,1},{6,2},{7,3},{8,12},{9,13},{10,... | collective-permute-start | bytes 27656 | tf_op jit(solution)/shard_map/ppermute | solution.py:373
  63.4 5.5 %collective-permute-start.17 = (f32[1,3,768]{2,1,0:T(4,128)S(1)}, f32[1,3,768]{2,1,0:T(4,128)S(1)}, u32[]{:S(2)}, u32[]{:S(2)}) collective-permute-start(f32[1,3,768]{2,1,0:T(4,128)S(1)} %pad_maximum_fusion.1.refs_0_), channel_id=1, source_target_pairs={{0,6},{1,7},{2,4},{3,5},{4,2},{5,3},{6,0},{7,1},{8,14},{9,15},{10,... | collective-permute-start | bytes 27656 | tf_op jit(solution)/shard_map/ppermute | solution.py:373
  63.7 5.2 %collective-permute-start.19 = (bf16[192,1536]{1,0:T(8,128)(2,1)S(1)}, bf16[192,1536]{1,0:T(8,128)(2,1)S(1)}, u32[]{:S(2)}, u32[]{:S(2)}) collective-permute-start(bf16[192,1536]{1,0:T(8,128)(2,1)S(1)} %copy-done.4), channel_id=1, source_target_pairs={{0,8},{8,0},{16,24},{24,16},{1,9},{9,1},{17,25},{25,17},{2,10},{10... | collective-permute-start | bytes 1769480 | tf_op jit(solution)/shard_map/ppermute | solution.py:26
  68.9 2.0 %collective-permute-start.20 = (bf16[192,1536]{1,0:T(8,128)(2,1)S(1)}, bf16[192,1536]{1,0:T(8,128)(2,1)S(1)}, u32[]{:S(2)}, u32[]{:S(2)}) collective-permute-start(bf16[192,1536]{1,0:T(8,128)(2,1)S(1)} %collective-permute-done.18.refs_9_), channel_id=1, source_target_pairs={{0,8},{8,0},{16,24},{24,16},{1,9},{9,1},{17,25},{25,17},{2,10},{10... | collective-permute-start | bytes 1769480 | tf_op jit(solution)/shard_map/ppermute | solution.py:26
  (5 other events, 17.0 us)

commit v5 on v4

--- a/solution.py
+++ b/solution.py
@@ -11,7 +11,7 @@
 LANES = 128
 MIB = 1024 * 1024
 VMEM = pltpu.VMEM
-ORDER = (0, 2, 1)
+ORDER = (2, 0, 1)
 
 
 def cost(flops):
@@ -26,20 +26,20 @@
     return lax.ppermute(value, axis, [(i, i ^ bit) for i in range(lax.axis_size(axis))])
 
 
-def cut_kernel(place_ref, shard_ref, half_ref, zero_ref, one_ref):
-    wide = half_ref.shape[1]
+def cut_kernel(place_ref, shard_ref, two_ref, zero_ref, one_ref):
+    wide = two_ref.shape[1]
     channels = shard_ref.shape[1] // 2
-    at = pl.multiple_of(place_ref[3] * channels + 2 * wide, wide)
-    half_ref[...] = shard_ref[:, pl.ds(at, wide)]
-    for block, ref in enumerate((zero_ref, one_ref)):
-        for i in range(2):
-            at = i * channels + block * wide
-            ref[:, i * wide : (i + 1) * wide] = shard_ref[:, at : at + wide]
+    for block, ref in ((2, two_ref), (0, zero_ref)):
+        at = pl.multiple_of(place_ref[3] * channels + block * wide, wide)
+        ref[...] = shard_ref[:, pl.ds(at, wide)]
+    for i in range(2):
+        at = i * channels + wide
+        one_ref[:, i * wide : (i + 1) * wide] = shard_ref[:, at : at + wide]
 
 
 def cut(place, shard, wide):
     depth = shard.shape[0]
-    shapes = [(depth, wide), (depth, 2 * wide), (depth, 2 * wide)]
+    shapes = [(depth, wide), (depth, wide), (depth, 2 * wide)]
     return pl.pallas_call(
         cut_kernel,
         out_shape=[jax.ShapeDtypeStruct(shape, jnp.bfloat16) for shape in shapes],
@@ -347,25 +347,30 @@
         return front_block(block, wide, place, normed, weights, dw_kernel, *extra)
 
     if direct:
-        half, zero, one = (swap(part, "fsdp", 2) for part in cut(place, w_in, wide))
+        two, zero, one = (swap(part, "fsdp", 2) for part in cut(place, w_in, wide))
         across = swap(w_in, "fsdp", 1)
         normed, inner, outer = normalize_rows(place, rows, gain)
-        normed, half = tie(normed, half)
-        rest = swap(half, "ctx", 1)
+        normed, two = tie(normed, two)
+        two = [two, swap(two, "ctx", 1)]
         inner = swap(inner, "ctx", 1)
         pairs = [(i, i + 1) for i in range(1, ends, 2)]
         outer = lax.ppermute(outer, "ctx", pairs + [(j, i) for i, j in pairs])
-        beyond_half = swap(half, "fsdp", 1)
-        normed, zero, rest = tie(normed, zero, rest)
-        beyond_zero, beyond_rest = swap(zero, "fsdp", 1), swap(rest, "fsdp", 1)
+        normed, inner, outer, zero = tie(normed, inner, outer, zero)
+        zero = [zero, swap(zero, "ctx", 1)]
+        two.append(swap(two[0], "fsdp", 1))
+        zero.append(swap(zero[0], "fsdp", 1))
         normed, *partials = near_product(place, normed, inner, outer, gain, w_in, across)
-        partials[0], beyond_half, w_out = tie(partials[0], beyond_half, w_out)
-        conv_zero, stat_zero = front(0, [partials[0], zero, beyond_zero])
-        conv_zero, partials[2] = tie(conv_zero, partials[2])
-        conv_two, stat_two = front(2, [partials[2], half, rest, beyond_half, beyond_rest])
-        conv_two, one, w_out = tie(conv_two, one, w_out)
+        partials[2], *parts = tie(partials[2], *two, *zero, w_out)
+        two, zero, w_out = parts[:3], parts[3:6], parts[6]
+        two.append(swap(two[1], "fsdp", 1))
+        zero.append(swap(zero[1], "fsdp", 1))
+        conv_two, stat_two = front(2, [partials[2], *two])
+        conv_two, partials[0], one = tie(conv_two, partials[0], one)
+        beyond_one = swap(one, "fsdp", 1)
+        conv_zero, stat_zero = front(0, [partials[0], *zero])
+        conv_zero, w_out = tie(conv_zero, w_out)
         remote_out, across_out = swap(w_out, "fsdp", 2), swap(w_out, "fsdp", 1)
-        conv_one, stats = front(1, [partials[1], one, swap(one, "fsdp", 1)], (stat_zero, stat_two), 1)
+        conv_one, stats = front(1, [partials[1], one, beyond_one], (stat_two, stat_zero), 1)
         convs = [conv_zero, conv_one, conv_two]
 
         def others(flips):
@@ -382,9 +387,8 @@
             return jnp.stack(merged([[part[:, i] for i in range(3)] for part in parts]), 1)
 
         stats = union([stats] + others([(1, 0)]))
-        stats = union([stats] + others([(2, 0), (0, 1), (2, 1)]))
-        stats = [stats] + others([(0, 2), (0, 4), (0, 6)])
-        *stats, remote_out = tie(*stats, remote_out)
+        stats = union([stats] + others([(0, 2), (0, 4), (0, 6)]))
+        stats = [stats] + others([(2, 0), (0, 1), (2, 1)])
         out_weights = [w_out, across_out, remote_out, swap(remote_out, "fsdp", 1)]
     else:
         full_in = lax.all_gather(w_in, "fsdp", axis=0, tiled=True)

time: 74.1 us -> 70.3 us (0.949)
  waiting for transfers between devices: 32.4 us -> 25.8 us
  starting transfers between devices: 20.8 us -> 23.6 us
    ppermute x7, waiting for transfers between devices: 18.9 us -> 8.18 us  [others(): lax.ppermute(stats, both, [(member(f, p), member(f ^ df, p ^ dp)) for f i...]
    ppermute x13 -> x15, starting transfers between devices: 9.21 us -> 13.4 us  [swap(): lax.ppermute(value, axis, [(i, i ^ bit) for i in range(lax.axis_size(axis...]
    ppermute x13 -> x15, waiting for transfers between devices: 13.5 us -> 17.6 us  [swap(): lax.ppermute(value, axis, [(i, i ^ bit) for i in range(lax.axis_size(axis...]
    ppermute x7, starting transfers between devices: 10.8 us -> 9.56 us  [others(): lax.ppermute(stats, both, [(member(f, p), member(f ^ df, p ^ dp)) for f i...]
  transfers between devices with their start and end apart: 21 -> 23, of which waited for: 11 -> 12; matrix products, arithmetic and copies ran while one was open for 0% -> 0% of each run, Pallas kernels for 15% -> 16%
where the time goes in v5:
time: 70.3 us; the launch traced here: 70.1 us
  waiting for transfers between devices  25.8 us (37%)
  starting transfers between devices  23.6 us (34%)
  Pallas kernels  17 us (24%)
  local copies, waits for them, and re-layouts  2.71 us (4%)
  between operations  0.79 us (1%)
    ppermute x15, waiting for transfers between devices, swap(): lax.ppermute(value, axis, [(i, i ^ bit) for i in range(lax.axis_size(axis...  17.6 us
    ppermute x15, starting transfers between devices, swap(): lax.ppermute(value, axis, [(i, i ^ bit) for i in range(lax.axis_size(axis...  13.4 us
    ppermute x7, starting transfers between devices, others(): lax.ppermute(stats, both, [(member(f, p), member(f ^ df, p ^ dp)) for f i...  9.56 us
    pallas_call x3, Pallas kernels, front_block(): pl.pallas_call(functools.partial(front_kernel, block, len(earlier)), out_...  8.66 us
    ppermute x7, waiting for transfers between devices, others(): lax.ppermute(stats, both, [(member(f, p), member(f ^ df, p ^ dp)) for f i...  8.18 us
    pallas_call x1, Pallas kernels, back(): pl.pallas_call(functools.partial(back_kernel, len(stats)), out_shape=jax....  2.94 us
    unnamed x16, local copies, waits for them, and re-layouts  2.7 us
    pallas_call x1, Pallas kernels, normalize_rows(): pl.pallas_call(norm_kernel, out_shape=[jax.ShapeDtypeStruct(shape, jnp.bf...  2.45 us
  transfers between devices with their start and end apart: 23, of which 12 were waited for; matrix products, arithmetic and copies ran while one was open for 0% of the time, Pallas kernels for 16%

profile of v5, /device:TPU:0, one launch (start us, length us, event | category | flops | bytes accessed | tf_op | source)
XLA Modules:
  0.0 70.1 jit_solution(16972554384396285427)
XLA Ops:
  3.1 2.6 %collective-permute-start = (bf16[384,256]{1,0:T(8,128)(2,1)S(1)}, bf16[384,256]{1,0:T(8,128)(2,1)S(1)}, u32[]{:S(2)}, u32[]{:S(2)}) collective-permute-start(bf16[384,256]{1,0:T(8,128)(2,1)S(1)} %get-tuple-element.41), channel_id=1, source_target_pairs={{0,16},{8,24},{16,0},{24,8},{1,17},{9,25},{17,1},{25,9},{2,18},{10... | collective-permute-start | bytes 589832 | tf_op jit(solution)/shard_map/ppermute | solution.py:26
  5.7 1.4 %copy-done.2 = bf16[1,512,1536]{2,1,0:T(8,128)(2,1)S(1)} copy-done((bf16[1,512,1536]{2,1,0:T(8,128)(2,1)S(1)}, bf16[1,512,1536]{2,1,0:T(8,128)(2,1)}, u32[]{:S(2)}) %copy-start.2) | copy-done | bytes 1572888
  7.1 2.5 %layer_norm.1 = (bf16[512,1536]{1,0:T(8,128)(2,1)S(1)}, bf16[16,1536]{1,0:T(8,128)(2,1)S(1)}, bf16[16,1536]{1,0:T(8,128)(2,1)S(1)}) custom-call(s32[4]{0:T(128)S(1)} %pad_add_fusion.place_ref, bf16[512,1536]{1,0:T(8,128)(2,1)S(1)} %bitcast.5, f32[1,1536]{1,0:T(1,128)S(1)} %broadcast_in_dim.14.gain_ref), custom_call_target="tpu_custom_call" | custom-call | flops 100000000 | tf_op jit(solution)/shard_map/layer_norm/pallas_call | solution.py:80
  9.6 2.0 %collective-permute-start.1 = (bf16[16,1536]{1,0:T(8,128)(2,1)S(1)}, bf16[16,1536]{1,0:T(8,128)(2,1)S(1)}, u32[]{:S(2)}, u32[]{:S(2)}) collective-permute-start(bf16[16,1536]{1,0:T(8,128)(2,1)S(1)} %get-tuple-element.43), channel_id=1, source_target_pairs={{0,1},{1,0},{2,3},{3,2},{4,5},{5,4},{6,7},{7,6},{8,9},{9,8},{10,11... | collective-permute-start | bytes 147464 | tf_op jit(solution)/shard_map/ppermute | solution.py:26
  12.3 1.4 %collective-permute-done.1.inner_ref = bf16[16,1536]{1,0:T(8,128)(2,1)S(1)} collective-permute-done((bf16[16,1536]{1,0:T(8,128)(2,1)S(1)}, bf16[16,1536]{1,0:T(8,128)(2,1)S(1)}, u32[]{:S(2)}, u32[]{:S(2)}) %collective-permute-start.1) | collective-permute-done | bytes 49184 | tf_op jit(solution)/shard_map/ppermute | solution.py:26
  13.7 1.7 %collective-permute-done.3.refs_1_ = bf16[384,256]{1,0:T(8,128)(2,1)S(1)} collective-permute-done((bf16[384,256]{1,0:T(8,128)(2,1)S(1)}, bf16[384,256]{1,0:T(8,128)(2,1)S(1)}, u32[]{:S(2)}, u32[]{:S(2)}) %collective-permute-start.3) | collective-permute-done | bytes 196640 | tf_op jit(solution)/shard_map/ppermute | solution.py:26
  15.4 3.2 %collective-permute-start.7 = (bf16[384,256]{1,0:T(8,128)(2,1)S(1)}, bf16[384,256]{1,0:T(8,128)(2,1)S(1)}, u32[]{:S(2)}, u32[]{:S(2)}) collective-permute-start(bf16[384,256]{1,0:T(8,128)(2,1)S(1)} %collective-permute-done.3.refs_1_), channel_id=1, source_target_pairs={{0,1},{1,0},{2,3},{3,2},{4,5},{5,4},{6,7},{7,6},{8,9},{9,8},{10,11... | collective-permute-start | bytes 589832 | tf_op jit(solution)/shard_map/ppermute | solution.py:26
  19.1 1.9 %collective-permute-start.10 = (bf16[384,512]{1,0:T(8,128)(2,1)S(1)}, bf16[384,512]{1,0:T(8,128)(2,1)S(1)}, u32[]{:S(2)}, u32[]{:S(2)}) collective-permute-start(bf16[384,512]{1,0:T(8,128)(2,1)S(1)} %get-tuple-element.60), channel_id=1, source_target_pairs={{0,16},{8,24},{16,0},{24,8},{1,17},{9,25},{17,1},{25,9},{2,18},{10... | collective-permute-start | bytes 1179656 | tf_op jit(solution)/shard_map/ppermute | solution.py:26
  21.0 2.3 %near.1 = (bf16[544,1536]{1,0:T(8,128)(2,1)S(1)}, f32[544,512]{1,0:T(8,128)S(1)}, f32[544,512]{1,0:T(8,128)S(1)}, f32[544,512]{1,0:T(8,128)S(1)}) custom-call(s32[4]{0:T(128)S(1)} %pad_add_fusion.place_ref, bf16[512,1536]{1,0:T(8,128)(2,1)S(1)} %get-tuple-element.46.rows_ref, bf16[16,1536]{1,0:T(8,128)(2,1)S(1)} %collective-permute-done.1.inner_ref, ...), custom_call_target="tpu_custom_call" | custom-call | flops 100000000 | tf_op jit(solution)/shard_map/near/pallas_call | solution.py:128
  23.9 2.8 %collective-permute-done.5.refs_2_ = bf16[384,256]{1,0:T(8,128)(2,1)S(1)} collective-permute-done((bf16[384,256]{1,0:T(8,128)(2,1)S(1)}, bf16[384,256]{1,0:T(8,128)(2,1)S(1)}, u32[]{:S(2)}, u32[]{:S(2)}) %collective-permute-start.5) | collective-permute-done | bytes 196640 | tf_op jit(solution)/shard_map/ppermute | solution.py:26
  28.1 2.9 %front.3 = (f32[512,256]{1,0:T(8,128)S(1)}, f32[3,256]{1,0:T(4,128)S(1)}) custom-call(s32[4]{0:T(128)S(1)} %pad_add_fusion.place_ref, bf16[544,1536]{1,0:T(8,128)(2,1)S(1)} %get-tuple-element.49.normed_ref, f32[544,512]{1,0:T(8,128)S(1)} %get-tuple-element.53.refs_0_, bf16[384,256]{1,0:T(8,128)(2,1)S(1)} %collective-permute-done.refs_1_, ...), custom_call_target="tpu_custom_call" | custom-call | flops 100000000 | tf_op jit(solution)/shard_map/front/pallas_call | solution.py:213
  31.1 2.9 %front.4 = (f32[512,256]{1,0:T(8,128)S(1)}, f32[3,256]{1,0:T(4,128)S(1)}) custom-call(s32[4]{0:T(128)S(1)} %pad_add_fusion.place_ref, bf16[544,1536]{1,0:T(8,128)(2,1)S(1)} %get-tuple-element.49.normed_ref, f32[544,512]{1,0:T(8,128)S(1)} %get-tuple-element.61.refs_0_, bf16[384,256]{1,0:T(8,128)(2,1)S(1)} %collective-permute-done.3.refs_1_, ...), custom_call_target="tpu_custom_call" | custom-call | flops 100000000 | tf_op jit(solution)/shard_map/front/pallas_call | solution.py:213
  34.0 1.7 %collective-permute-start.21 = (bf16[192,1536]{1,0:T(8,128)(2,1)S(1)}, bf16[192,1536]{1,0:T(8,128)(2,1)S(1)}, u32[]{:S(2)}, u32[]{:S(2)}) collective-permute-start(bf16[192,1536]{1,0:T(8,128)(2,1)S(1)} %copy-done.4), channel_id=1, source_target_pairs={{0,16},{8,24},{16,0},{24,8},{1,17},{9,25},{17,1},{25,9},{2,18},{10... | collective-permute-start | bytes 1769480 | tf_op jit(solution)/shard_map/ppermute | solution.py:26
  35.7 1.7 %collective-permute-done.12.refs_4_ = bf16[384,512]{1,0:T(8,128)(2,1)S(1)} collective-permute-done((bf16[384,512]{1,0:T(8,128)(2,1)S(1)}, bf16[384,512]{1,0:T(8,128)(2,1)S(1)}, u32[]{:S(2)}, u32[]{:S(2)}) %collective-permute-start.12) | collective-permute-done | bytes 393248 | tf_op jit(solution)/shard_map/ppermute | solution.py:26
  37.4 2.9 %front.5 = (f32[512,256]{1,0:T(8,128)S(1)}, f32[1,3,768]{2,1,0:T(4,128)S(1)}) custom-call(s32[4]{0:T(128)S(1)} %pad_add_fusion.place_ref, bf16[544,1536]{1,0:T(8,128)(2,1)S(1)} %get-tuple-element.49.normed_ref, f32[3,256]{1,0:T(4,128)S(1)} %get-tuple-element.57.refs_0_, f32[3,256]{1,0:T(4,128)S(1)} %get-tuple-element.65.refs_1_, ...), custom_call_target="tpu_custom_call" | custom-call | flops 100000000 | tf_op jit(solution)/shard_map/front/pallas_call | solution.py:213
  40.9 8.5 %collective-permute-done.21.refs_9_ = bf16[192,1536]{1,0:T(8,128)(2,1)S(1)} collective-permute-done((bf16[192,1536]{1,0:T(8,128)(2,1)S(1)}, bf16[192,1536]{1,0:T(8,128)(2,1)S(1)}, u32[]{:S(2)}, u32[]{:S(2)}) %collective-permute-start.21) | collective-permute-done | bytes 589856 | tf_op jit(solution)/shard_map/ppermute | solution.py:26
  49.5 3.3 %collective-permute-start.14 = (f32[1,3,768]{2,1,0:T(4,128)S(1)}, f32[1,3,768]{2,1,0:T(4,128)S(1)}, u32[]{:S(2)}, u32[]{:S(2)}) collective-permute-start(f32[1,3,768]{2,1,0:T(4,128)S(1)} %pad_maximum_fusion), channel_id=1, source_target_pairs={{0,2},{1,3},{2,0},{3,1},{4,6},{5,7},{6,4},{7,5},{8,10},{9,11},{10,... | collective-permute-start | bytes 27656 | tf_op jit(solution)/shard_map/ppermute | solution.py:378
  52.8 2.4 %collective-permute-start.15 = (f32[1,3,768]{2,1,0:T(4,128)S(1)}, f32[1,3,768]{2,1,0:T(4,128)S(1)}, u32[]{:S(2)}, u32[]{:S(2)}) collective-permute-start(f32[1,3,768]{2,1,0:T(4,128)S(1)} %pad_maximum_fusion), channel_id=1, source_target_pairs={{0,4},{1,5},{2,6},{3,7},{4,0},{5,1},{6,2},{7,3},{8,12},{9,13},{10,... | collective-permute-start | bytes 27656 | tf_op jit(solution)/shard_map/ppermute | solution.py:378
  55.3 2.1 %collective-permute-done.15 = f32[1,3,768]{2,1,0:T(4,128)S(1)} collective-permute-done((f32[1,3,768]{2,1,0:T(4,128)S(1)}, f32[1,3,768]{2,1,0:T(4,128)S(1)}, u32[]{:S(2)}, u32[]{:S(2)}) %collective-permute-start.15) | collective-permute-done | bytes 9248 | tf_op jit(solution)/shard_map/ppermute | solution.py:378
  57.4 3.3 %collective-permute-done.16 = f32[1,3,768]{2,1,0:T(4,128)S(1)} collective-permute-done((f32[1,3,768]{2,1,0:T(4,128)S(1)}, f32[1,3,768]{2,1,0:T(4,128)S(1)}, u32[]{:S(2)}, u32[]{:S(2)}) %collective-permute-start.16) | collective-permute-done | bytes 9248 | tf_op jit(solution)/shard_map/ppermute | solution.py:378
  60.8 1.6 %collective-permute-start.17 = (f32[1,3,768]{2,1,0:T(4,128)S(1)}, f32[1,3,768]{2,1,0:T(4,128)S(1)}, u32[]{:S(2)}, u32[]{:S(2)}) collective-permute-start(f32[1,3,768]{2,1,0:T(4,128)S(1)} %pad_maximum_fusion.1.refs_0_), channel_id=1, source_target_pairs={{0,16},{1,17},{2,18},{3,19},{4,20},{5,21},{6,22},{7,23},{8,24},{9,... | collective-permute-start | bytes 27656 | tf_op jit(solution)/shard_map/ppermute | solution.py:378
  62.5 1.8 %collective-permute-start.19 = (f32[1,3,768]{2,1,0:T(4,128)S(1)}, f32[1,3,768]{2,1,0:T(4,128)S(1)}, u32[]{:S(2)}, u32[]{:S(2)}) collective-permute-start(f32[1,3,768]{2,1,0:T(4,128)S(1)} %pad_maximum_fusion.1.refs_0_), channel_id=1, source_target_pairs={{0,17},{1,16},{2,19},{3,18},{4,21},{5,20},{6,23},{7,22},{8,25},{9,... | collective-permute-start | bytes 27656 | tf_op jit(solution)/shard_map/ppermute | solution.py:378
  64.5 1.5 %collective-permute-done.18.refs_2_ = f32[1,3,768]{2,1,0:T(4,128)S(1)} collective-permute-done((f32[1,3,768]{2,1,0:T(4,128)S(1)}, f32[1,3,768]{2,1,0:T(4,128)S(1)}, u32[]{:S(2)}, u32[]{:S(2)}) %collective-permute-start.18) | collective-permute-done | bytes 9248 | tf_op jit(solution)/shard_map/ppermute | solution.py:378
  67.1 2.9 %back.1 = bf16[512,1536]{1,0:T(8,128)(2,1)} custom-call(s32[4]{0:T(128)S(1)} %pad_add_fusion.place_ref, f32[1,768]{1,0:T(1,128)S(1)} %broadcast_in_dim.12.gain_ref, f32[1,768]{1,0:T(1,128)S(1)} %broadcast_in_dim.13.shift_ref, f32[1,3,768]{2,1,0:T(4,128)S(1)} %pad_maximum_fusion.1.refs_0_, f32[1,3,768]{2,1,0:T(4,128)S(1)} %collective-permute-done.17.refs_1_, ...), custom_call_target="tpu_custom_call" | custom-call | flops 1000000000 | tf_op jit(solution)/shard_map/back/pallas_call | solution.py:305
  (53 shorter events, 7.8 us)
Async XLA Ops:
  0.0 19.1 %collective-permute-start.4 = (bf16[384,1536]{1,0:T(8,128)(2,1)}, bf16[384,1536]{1,0:T(8,128)(2,1)S(1)}, u32[]{:S(2)}, u32[]{:S(2)}) collective-permute-start(bf16[384,1536]{1,0:T(8,128)(2,1)} %refs_0_.1), channel_id=1, source_target_pairs={{0,8},{8,0},{16,24},{24,16},{1,9},{9,1},{17,25},{25,17},{2,10},{10... | collective-permute-start | bytes 3538952 | tf_op jit(solution)/shard_map/ppermute | solution.py:26
  3.1 9.2 %collective-permute-start = (bf16[384,256]{1,0:T(8,128)(2,1)S(1)}, bf16[384,256]{1,0:T(8,128)(2,1)S(1)}, u32[]{:S(2)}, u32[]{:S(2)}) collective-permute-start(bf16[384,256]{1,0:T(8,128)(2,1)S(1)} %get-tuple-element.41), channel_id=1, source_target_pairs={{0,16},{8,24},{16,0},{24,8},{1,17},{9,25},{17,1},{25,9},{2,18},{10... | collective-permute-start | bytes 589832 | tf_op jit(solution)/shard_map/ppermute | solution.py:26
  5.6 9.8 %collective-permute-start.3 = (bf16[384,256]{1,0:T(8,128)(2,1)S(1)}, bf16[384,256]{1,0:T(8,128)(2,1)S(1)}, u32[]{:S(2)}, u32[]{:S(2)}) collective-permute-start(bf16[384,256]{1,0:T(8,128)(2,1)S(1)} %get-tuple-element.45), channel_id=1, source_target_pairs={{0,16},{8,24},{16,0},{24,8},{1,17},{9,25},{17,1},{25,9},{2,18},{10... | collective-permute-start | bytes 589832 | tf_op jit(solution)/shard_map/ppermute | solution.py:26
  9.6 4.2 %collective-permute-start.1 = (bf16[16,1536]{1,0:T(8,128)(2,1)S(1)}, bf16[16,1536]{1,0:T(8,128)(2,1)S(1)}, u32[]{:S(2)}, u32[]{:S(2)}) collective-permute-start(bf16[16,1536]{1,0:T(8,128)(2,1)S(1)} %get-tuple-element.43), channel_id=1, source_target_pairs={{0,1},{1,0},{2,3},{3,2},{4,5},{5,4},{6,7},{7,6},{8,9},{9,8},{10,11... | collective-permute-start | bytes 147464 | tf_op jit(solution)/shard_map/ppermute | solution.py:26
  11.6 2.1 %collective-permute-start.2 = (bf16[16,1536]{1,0:T(8,128)(2,1)S(1)}, bf16[16,1536]{1,0:T(8,128)(2,1)S(1)}, u32[]{:S(2)}, u32[]{:S(2)}) collective-permute-start(bf16[16,1536]{1,0:T(8,128)(2,1)S(1)} %get-tuple-element.44), channel_id=1, source_target_pairs={{1,2},{3,4},{5,6},{2,1},{4,3},{6,5},{9,10},{11,12},{13,14},{10,9},... | collective-permute-start | bytes 147464 | tf_op jit(solution)/shard_map/ppermute | solution.py:357
  15.4 8.4 %collective-permute-start.7 = (bf16[384,256]{1,0:T(8,128)(2,1)S(1)}, bf16[384,256]{1,0:T(8,128)(2,1)S(1)}, u32[]{:S(2)}, u32[]{:S(2)}) collective-permute-start(bf16[384,256]{1,0:T(8,128)(2,1)S(1)} %collective-permute-done.3.refs_1_), channel_id=1, source_target_pairs={{0,1},{1,0},{2,3},{3,2},{4,5},{5,4},{6,7},{7,6},{8,9},{9,8},{10,11... | collective-permute-start | bytes 589832 | tf_op jit(solution)/shard_map/ppermute | solution.py:26
  18.6 5.2 %collective-permute-start.8 = (bf16[384,256]{1,0:T(8,128)(2,1)S(1)}, bf16[384,256]{1,0:T(8,128)(2,1)S(1)}, u32[]{:S(2)}, u32[]{:S(2)}) collective-permute-start(bf16[384,256]{1,0:T(8,128)(2,1)S(1)} %collective-permute-done.3.refs_1_), channel_id=1, source_target_pairs={{0,8},{8,0},{16,24},{24,16},{1,9},{9,1},{17,25},{25,17},{2,10},{10... | collective-permute-start | bytes 589832 | tf_op jit(solution)/shard_map/ppermute | solution.py:26
  18.6 8.1 %collective-permute-start.5 = (bf16[384,256]{1,0:T(8,128)(2,1)S(1)}, bf16[384,256]{1,0:T(8,128)(2,1)S(1)}, u32[]{:S(2)}, u32[]{:S(2)}) collective-permute-start(bf16[384,256]{1,0:T(8,128)(2,1)S(1)} %collective-permute-done.refs_1_), channel_id=1, source_target_pairs={{0,1},{1,0},{2,3},{3,2},{4,5},{5,4},{6,7},{7,6},{8,9},{9,8},{10,11... | collective-permute-start | bytes 589832 | tf_op jit(solution)/shard_map/ppermute | solution.py:26
  18.7 8.0 %collective-permute-start.6 = (bf16[384,256]{1,0:T(8,128)(2,1)S(1)}, bf16[384,256]{1,0:T(8,128)(2,1)S(1)}, u32[]{:S(2)}, u32[]{:S(2)}) collective-permute-start(bf16[384,256]{1,0:T(8,128)(2,1)S(1)} %collective-permute-done.refs_1_), channel_id=1, source_target_pairs={{0,8},{8,0},{16,24},{24,16},{1,9},{9,1},{17,25},{25,17},{2,10},{10... | collective-permute-start | bytes 589832 | tf_op jit(solution)/shard_map/ppermute | solution.py:26
  19.1 11.9 %collective-permute-start.10 = (bf16[384,512]{1,0:T(8,128)(2,1)S(1)}, bf16[384,512]{1,0:T(8,128)(2,1)S(1)}, u32[]{:S(2)}, u32[]{:S(2)}) collective-permute-start(bf16[384,512]{1,0:T(8,128)(2,1)S(1)} %get-tuple-element.60), channel_id=1, source_target_pairs={{0,16},{8,24},{16,0},{24,8},{1,17},{9,25},{17,1},{25,9},{2,18},{10... | collective-permute-start | bytes 1179656 | tf_op jit(solution)/shard_map/ppermute | solution.py:26
  26.7 1.4 %collective-permute-start.9 = (bf16[384,256]{1,0:T(8,128)(2,1)S(1)}, bf16[384,256]{1,0:T(8,128)(2,1)S(1)}, u32[]{:S(2)}, u32[]{:S(2)}) collective-permute-start(bf16[384,256]{1,0:T(8,128)(2,1)S(1)} %collective-permute-done.5.refs_2_), channel_id=1, source_target_pairs={{0,8},{8,0},{16,24},{24,16},{1,9},{9,1},{17,25},{25,17},{2,10},{10... | collective-permute-start | bytes 589832 | tf_op jit(solution)/shard_map/ppermute | solution.py:26
  26.7 4.4 %collective-permute-start.11 = (bf16[384,256]{1,0:T(8,128)(2,1)S(1)}, bf16[384,256]{1,0:T(8,128)(2,1)S(1)}, u32[]{:S(2)}, u32[]{:S(2)}) collective-permute-start(bf16[384,256]{1,0:T(8,128)(2,1)S(1)} %collective-permute-done.7.refs_2_), channel_id=1, source_target_pairs={{0,8},{8,0},{16,24},{24,16},{1,9},{9,1},{17,25},{25,17},{2,10},{10... | collective-permute-start | bytes 589832 | tf_op jit(solution)/shard_map/ppermute | solution.py:26
  34.0 15.4 %collective-permute-start.21 = (bf16[192,1536]{1,0:T(8,128)(2,1)S(1)}, bf16[192,1536]{1,0:T(8,128)(2,1)S(1)}, u32[]{:S(2)}, u32[]{:S(2)}) collective-permute-start(bf16[192,1536]{1,0:T(8,128)(2,1)S(1)} %copy-done.4), channel_id=1, source_target_pairs={{0,16},{8,24},{16,0},{24,8},{1,17},{9,25},{17,1},{25,9},{2,18},{10... | collective-permute-start | bytes 1769480 | tf_op jit(solution)/shard_map/ppermute | solution.py:26
  35.7 1.7 %collective-permute-start.12 = (bf16[384,512]{1,0:T(8,128)(2,1)S(1)}, bf16[384,512]{1,0:T(8,128)(2,1)S(1)}, u32[]{:S(2)}, u32[]{:S(2)}) collective-permute-start(bf16[384,512]{1,0:T(8,128)(2,1)S(1)} %collective-permute-done.10.refs_3_), channel_id=1, source_target_pairs={{0,8},{8,0},{16,24},{24,16},{1,9},{9,1},{17,25},{25,17},{2,10},{10... | collective-permute-start | bytes 1179656 | tf_op jit(solution)/shard_map/ppermute | solution.py:26
  37.4 26.9 %copy-start.7 = (f32[768]{0:T(1024)S(1)}, f32[768]{0:T(1024)}, u32[]{:S(2)}) copy-start(f32[768]{0:T(1024)} %param.14) | copy-start | bytes 9220
  40.3 9.1 %collective-permute-start.13 = (f32[1,3,768]{2,1,0:T(4,128)S(1)}, f32[1,3,768]{2,1,0:T(4,128)S(1)}, u32[]{:S(2)}, u32[]{:S(2)}) collective-permute-start(f32[1,3,768]{2,1,0:T(4,128)S(1)} %get-tuple-element.68), channel_id=1, source_target_pairs={{0,8},{1,9},{2,10},{3,11},{4,12},{5,13},{6,14},{7,15},{8,0},{9,1},... | collective-permute-start | bytes 27656 | tf_op jit(solution)/shard_map/ppermute | solution.py:378
  40.5 26.6 %collective-permute-start.20 = (bf16[192,1536]{1,0:T(8,128)(2,1)S(1)}, bf16[192,1536]{1,0:T(8,128)(2,1)S(1)}, u32[]{:S(2)}, u32[]{:S(2)}) collective-permute-start(bf16[192,1536]{1,0:T(8,128)(2,1)S(1)} %copy-done.4), channel_id=1, source_target_pairs={{0,8},{8,0},{16,24},{24,16},{1,9},{9,1},{17,25},{25,17},{2,10},{10... | collective-permute-start | bytes 1769480 | tf_op jit(solution)/shard_map/ppermute | solution.py:26
  49.4 17.7 %collective-permute-start.22 = (bf16[192,1536]{1,0:T(8,128)(2,1)S(1)}, bf16[192,1536]{1,0:T(8,128)(2,1)S(1)}, u32[]{:S(2)}, u32[]{:S(2)}) collective-permute-start(bf16[192,1536]{1,0:T(8,128)(2,1)S(1)} %collective-permute-done.21.refs_9_), channel_id=1, source_target_pairs={{0,8},{8,0},{16,24},{24,16},{1,9},{9,1},{17,25},{25,17},{2,10},{10... | collective-permute-start | bytes 1769480 | tf_op jit(solution)/shard_map/ppermute | solution.py:26
  49.5 5.8 %collective-permute-start.14 = (f32[1,3,768]{2,1,0:T(4,128)S(1)}, f32[1,3,768]{2,1,0:T(4,128)S(1)}, u32[]{:S(2)}, u32[]{:S(2)}) collective-permute-start(f32[1,3,768]{2,1,0:T(4,128)S(1)} %pad_maximum_fusion), channel_id=1, source_target_pairs={{0,2},{1,3},{2,0},{3,1},{4,6},{5,7},{6,4},{7,5},{8,10},{9,11},{10,... | collective-permute-start | bytes 27656 | tf_op jit(solution)/shard_map/ppermute | solution.py:378
  52.8 4.6 %collective-permute-start.15 = (f32[1,3,768]{2,1,0:T(4,128)S(1)}, f32[1,3,768]{2,1,0:T(4,128)S(1)}, u32[]{:S(2)}, u32[]{:S(2)}) collective-permute-start(f32[1,3,768]{2,1,0:T(4,128)S(1)} %pad_maximum_fusion), channel_id=1, source_target_pairs={{0,4},{1,5},{2,6},{3,7},{4,0},{5,1},{6,2},{7,3},{8,12},{9,13},{10,... | collective-permute-start | bytes 27656 | tf_op jit(solution)/shard_map/ppermute | solution.py:378
  55.2 5.5 %collective-permute-start.16 = (f32[1,3,768]{2,1,0:T(4,128)S(1)}, f32[1,3,768]{2,1,0:T(4,128)S(1)}, u32[]{:S(2)}, u32[]{:S(2)}) collective-permute-start(f32[1,3,768]{2,1,0:T(4,128)S(1)} %pad_maximum_fusion), channel_id=1, source_target_pairs={{0,6},{1,7},{2,4},{3,5},{4,2},{5,3},{6,0},{7,1},{8,14},{9,15},{10,... | collective-permute-start | bytes 27656 | tf_op jit(solution)/shard_map/ppermute | solution.py:378
  60.8 3.8 %collective-permute-start.17 = (f32[1,3,768]{2,1,0:T(4,128)S(1)}, f32[1,3,768]{2,1,0:T(4,128)S(1)}, u32[]{:S(2)}, u32[]{:S(2)}) collective-permute-start(f32[1,3,768]{2,1,0:T(4,128)S(1)} %pad_maximum_fusion.1.refs_0_), channel_id=1, source_target_pairs={{0,16},{1,17},{2,18},{3,19},{4,20},{5,21},{6,22},{7,23},{8,24},{9,... | collective-permute-start | bytes 27656 | tf_op jit(solution)/shard_map/ppermute | solution.py:378
  62.3 3.7 %collective-permute-start.18 = (f32[1,3,768]{2,1,0:T(4,128)S(1)}, f32[1,3,768]{2,1,0:T(4,128)S(1)}, u32[]{:S(2)}, u32[]{:S(2)}) collective-permute-start(f32[1,3,768]{2,1,0:T(4,128)S(1)} %pad_maximum_fusion.1.refs_0_), channel_id=1, source_target_pairs={{0,1},{1,0},{2,3},{3,2},{4,5},{5,4},{6,7},{7,6},{8,9},{9,8},{10,11... | collective-permute-start | bytes 27656 | tf_op jit(solution)/shard_map/ppermute | solution.py:378
  62.5 4.6 %collective-permute-start.19 = (f32[1,3,768]{2,1,0:T(4,128)S(1)}, f32[1,3,768]{2,1,0:T(4,128)S(1)}, u32[]{:S(2)}, u32[]{:S(2)}) collective-permute-start(f32[1,3,768]{2,1,0:T(4,128)S(1)} %pad_maximum_fusion.1.refs_0_), channel_id=1, source_target_pairs={{0,17},{1,16},{2,19},{3,18},{4,21},{5,20},{6,23},{7,22},{8,25},{9,... | collective-permute-start | bytes 27656 | tf_op jit(solution)/shard_map/ppermute | solution.py:378
  (7 other events, 65.8 us)

commit v6 on v5

--- a/solution.py
+++ b/solution.py
@@ -26,29 +26,33 @@
     return lax.ppermute(value, axis, [(i, i ^ bit) for i in range(lax.axis_size(axis))])
 
 
-def cut_kernel(place_ref, shard_ref, two_ref, zero_ref, one_ref):
+def cut_kernel(place_ref, shard_ref, out_shard_ref, two_ref, zero_ref, one_ref, half_ref):
     wide = two_ref.shape[1]
     channels = shard_ref.shape[1] // 2
+    odd = place_ref[3]
     for block, ref in ((2, two_ref), (0, zero_ref)):
-        at = pl.multiple_of(place_ref[3] * channels + block * wide, wide)
+        at = pl.multiple_of(odd * channels + block * wide, wide)
         ref[...] = shard_ref[:, pl.ds(at, wide)]
     for i in range(2):
         at = i * channels + wide
         one_ref[:, i * wide : (i + 1) * wide] = shard_ref[:, at : at + wide]
-
-
-def cut(place, shard, wide):
+    rows = half_ref.shape[0]
+    half_ref[...] = out_shard_ref[pl.ds(pl.multiple_of(odd * rows, rows), rows), :]
+
+
+def cut(place, shard, out_shard, wide):
     depth = shard.shape[0]
     shapes = [(depth, wide), (depth, wide), (depth, 2 * wide)]
+    shapes.append((out_shard.shape[0] // 2, out_shard.shape[1]))
     return pl.pallas_call(
         cut_kernel,
         out_shape=[jax.ShapeDtypeStruct(shape, jnp.bfloat16) for shape in shapes],
-        in_specs=[pl.BlockSpec(memory_space=pltpu.SMEM), pl.BlockSpec(memory_space=VMEM)],
-        out_specs=[pl.BlockSpec(memory_space=VMEM)] * 3,
+        in_specs=[pl.BlockSpec(memory_space=pltpu.SMEM)] + [pl.BlockSpec(memory_space=VMEM)] * 2,
+        out_specs=[pl.BlockSpec(memory_space=VMEM)] * len(shapes),
         compiler_params=params(4),
         cost_estimate=cost(10**8),
         name="cut",
-    )(place, shard)
+    )(place, shard, out_shard)
 
 
 def normalize(values, gain):
@@ -172,7 +176,7 @@
     kept = jnp.where(valid, value * jax.nn.sigmoid(gate), 0.0)
     kept = kept.astype(jnp.bfloat16).astype(jnp.float32)
     first = HALO - (taps - 1) // 2
-    step = 64
+    step = 128
     for unit in range(wide // LANES):
         lanes = slice(unit * LANES, (unit + 1) * LANES)
         tap_lanes = slice(block * wide + unit * LANES, block * wide + (unit + 1) * LANES)
@@ -182,10 +186,15 @@
             gated[phase] = pltpu.roll(column, ext_rows - phase, 0)
         for at in range(0, row_count, step):
             acc = None
-            for tap in range(taps):
-                base = at + (first + tap) // 8 * 8
-                term = gated[(first + tap) % 8, base : base + step, :] * taps_ref[tap : tap + 1, tap_lanes]
-                acc = term if acc is None else acc + term
+            for phase in range(8):
+                offsets = [k for k in range(phase, first + taps, 8) if k >= first]
+                low = offsets[0] - phase
+                tiles = gated[phase, at + low : at + offsets[-1] - phase + step, :]
+                for offset in offsets:
+                    base = offset - phase - low
+                    tap = offset - first
+                    term = tiles[base : base + step] * taps_ref[tap : tap + 1, tap_lanes]
+                    acc = term if acc is None else acc + term
             conv_ref[at : at + step, lanes] = acc
     here = start + lax.broadcasted_iota(jnp.int32, (row_count, 1), 0) < length
     count = jnp.clip(length - start, 0, row_count).astype(jnp.float32)
@@ -224,7 +233,7 @@
             VMEM((8, ext_rows, LANES), jnp.float32),
         ],
         compiler_params=params(10),
-        cost_estimate=cost(10**8),
+        cost_estimate=cost(4 * 10**9 if block == ORDER[1] else 10**8),
         name="front",
     )(place, normed, *earlier, *weights, dw_kernel)
 
@@ -266,9 +275,14 @@
     row_count, wide = convs[0].shape
     if len(weight_refs) > 1:
         depth = weight_refs[0].shape[0]
-        for i, weight_ref in enumerate(weight_refs):
+        for i, weight_ref in enumerate(weight_refs[:2]):
             at = pl.multiple_of(lax.bitwise_xor(place_ref[0], i) * depth, depth)
             weights[pl.ds(at, depth), :] = weight_ref[...]
+        half = depth // 2
+        for i, weight_ref in enumerate(weight_refs[2:]):
+            at = lax.bitwise_xor(place_ref[0], 2 + i // 2) * depth
+            at += lax.bitwise_xor(place_ref[3], i % 2) * half
+            weights[pl.ds(pl.multiple_of(at, half), half), :] = weight_ref[...]
     else:
         weights[...] = weight_refs[0][...]
     mean, square, count = merged(rows_of(stat_refs))
@@ -347,7 +361,7 @@
         return front_block(block, wide, place, normed, weights, dw_kernel, *extra)
 
     if direct:
-        two, zero, one = (swap(part, "fsdp", 2) for part in cut(place, w_in, wide))
+        two, zero, one, half = (swap(part, "fsdp", 2) for part in cut(place, w_in, w_out, wide))
         across = swap(w_in, "fsdp", 1)
         normed, inner, outer = normalize_rows(place, rows, gain)
         normed, two = tie(normed, two)
@@ -355,21 +369,21 @@
         inner = swap(inner, "ctx", 1)
         pairs = [(i, i + 1) for i in range(1, ends, 2)]
         outer = lax.ppermute(outer, "ctx", pairs + [(j, i) for i, j in pairs])
-        normed, inner, outer, zero = tie(normed, inner, outer, zero)
+        normed, inner, outer, two[1], zero = tie(normed, inner, outer, two[1], zero)
         zero = [zero, swap(zero, "ctx", 1)]
         two.append(swap(two[0], "fsdp", 1))
         zero.append(swap(zero[0], "fsdp", 1))
         normed, *partials = near_product(place, normed, inner, outer, gain, w_in, across)
-        partials[2], *parts = tie(partials[2], *two, *zero, w_out)
-        two, zero, w_out = parts[:3], parts[3:6], parts[6]
+        partials[2], *parts = tie(partials[2], *two, *zero, half, w_out)
+        two, zero, half, w_out = parts[:3], parts[3:6], *parts[6:]
+        halves = [half, swap(half, "ctx", 1)]
         two.append(swap(two[1], "fsdp", 1))
         zero.append(swap(zero[1], "fsdp", 1))
         conv_two, stat_two = front(2, [partials[2], *two])
         conv_two, partials[0], one = tie(conv_two, partials[0], one)
         beyond_one = swap(one, "fsdp", 1)
         conv_zero, stat_zero = front(0, [partials[0], *zero])
-        conv_zero, w_out = tie(conv_zero, w_out)
-        remote_out, across_out = swap(w_out, "fsdp", 2), swap(w_out, "fsdp", 1)
+        across_out, beyond_half = swap(w_out, "fsdp", 1), swap(half, "fsdp", 1)
         conv_one, stats = front(1, [partials[1], one, beyond_one], (stat_two, stat_zero), 1)
         convs = [conv_zero, conv_one, conv_two]
 
@@ -386,10 +400,14 @@
         def union(parts):
             return jnp.stack(merged([[part[:, i] for i in range(3)] for part in parts]), 1)
 
+        stats, halves[1], across_out, beyond_half = tie(stats, halves[1], across_out, beyond_half)
+        beyond_rest = swap(halves[1], "fsdp", 1)
         stats = union([stats] + others([(1, 0)]))
-        stats = union([stats] + others([(0, 2), (0, 4), (0, 6)]))
-        stats = [stats] + others([(2, 0), (0, 1), (2, 1)])
-        out_weights = [w_out, across_out, remote_out, swap(remote_out, "fsdp", 1)]
+        stats, beyond_rest = tie(stats, beyond_rest)
+        out_weights = [w_out, across_out, *halves, beyond_half, beyond_rest]
+        stats = union([stats] + others([(0, 2)]))
+        stats = union([stats] + others([(0, 4)]))
+        stats = [stats] + others([(0, 1), (2, 0), (2, 1)])
     else:
         full_in = lax.all_gather(w_in, "fsdp", axis=0, tiled=True)
         out_weights = [lax.all_gather(w_out, "fsdp", axis=0, tiled=True)]

time: 70.3 us -> 69.3 us (0.986)
  waiting for transfers between devices: 25.8 us -> 21.8 us
  starting transfers between devices: 23.6 us -> 26.6 us
    ppermute x15 -> x17, starting transfers between devices: 13.4 us -> 18.1 us  [swap(): lax.ppermute(value, axis, [(i, i ^ bit) for i in range(lax.axis_size(axis...]
    ppermute x15 -> x17, waiting for transfers between devices: 17.6 us -> 14.1 us  [swap(): lax.ppermute(value, axis, [(i, i ^ bit) for i in range(lax.axis_size(axis...]
    ppermute x7 -> x6, starting transfers between devices: 9.56 us -> 7.8 us  [others(): lax.ppermute(stats, both, [(member(f, p), member(f ^ df, p ^ dp)) for f i...]
    ppermute x7 -> x6, waiting for transfers between devices: 8.18 us -> 7.65 us  [others(): lax.ppermute(stats, both, [(member(f, p), member(f ^ df, p ^ dp)) for f i...]
    unnamed x16 -> x18, local copies, waits for them, and re-layouts: 2.7 us -> 2.37 us
  transfers between devices with their start and end apart: 23 -> 24, of which waited for: 12 -> 13; matrix products, arithmetic and copies ran while one was open for 0% -> 0% of each run, Pallas kernels for 16% -> 21%
where the time goes in v6:
time: 69.3 us; the launch traced here: 69.1 us
  starting transfers between devices  26.6 us (38%)
  waiting for transfers between devices  21.8 us (31%)
  Pallas kernels  17.3 us (25%)
  local copies, waits for them, and re-layouts  2.38 us (3%)
  between operations  0.85 us (1%)
    ppermute x17, starting transfers between devices, swap(): lax.ppermute(value, axis, [(i, i ^ bit) for i in range(lax.axis_size(axis...  18.1 us
    ppermute x17, waiting for transfers between devices, swap(): lax.ppermute(value, axis, [(i, i ^ bit) for i in range(lax.axis_size(axis...  14.1 us
    pallas_call x3, Pallas kernels, front_block(): pl.pallas_call(functools.partial(front_kernel, block, len(earlier)), out_...  8.97 us
    ppermute x6, starting transfers between devices, others(): lax.ppermute(stats, both, [(member(f, p), member(f ^ df, p ^ dp)) for f i...  7.8 us
    ppermute x6, waiting for transfers between devices, others(): lax.ppermute(stats, both, [(member(f, p), member(f ^ df, p ^ dp)) for f i...  7.65 us
    pallas_call x1, Pallas kernels, back(): pl.pallas_call(functools.partial(back_kernel, len(stats)), out_shape=jax....  2.95 us
    pallas_call x1, Pallas kernels, normalize_rows(): pl.pallas_call(norm_kernel, out_shape=[jax.ShapeDtypeStruct(shape, jnp.bf...  2.46 us
    unnamed x18, local copies, waits for them, and re-layouts  2.37 us
  transfers between devices with their start and end apart: 24, of which 13 were waited for; matrix products, arithmetic and copies ran while one was open for 0% of the time, Pallas kernels for 21%

profile of v6, /device:TPU:0, one launch (start us, length us, event | category | flops | bytes accessed | tf_op | source)
XLA Modules:
  0.0 69.1 jit_solution(11857722888156893843)
XLA Ops:
  1.2 1.3 %copy-done = bf16[384,1536]{1,0:T(8,128)(2,1)S(1)} copy-done((bf16[384,1536]{1,0:T(8,128)(2,1)S(1)}, bf16[384,1536]{1,0:T(8,128)(2,1)}, u32[]{:S(2)}) %copy-start) | copy-done | bytes 1179672
  4.2 2.6 %collective-permute-start = (bf16[384,256]{1,0:T(8,128)(2,1)S(1)}, bf16[384,256]{1,0:T(8,128)(2,1)S(1)}, u32[]{:S(2)}, u32[]{:S(2)}) collective-permute-start(bf16[384,256]{1,0:T(8,128)(2,1)S(1)} %get-tuple-element.48), channel_id=1, source_target_pairs={{0,16},{8,24},{16,0},{24,8},{1,17},{9,25},{17,1},{25,9},{2,18},{10... | collective-permute-start | bytes 589832 | tf_op jit(solution)/shard_map/ppermute | solution.py:26
  6.8 2.5 %layer_norm.1 = (bf16[512,1536]{1,0:T(8,128)(2,1)S(1)}, bf16[16,1536]{1,0:T(8,128)(2,1)S(1)}, bf16[16,1536]{1,0:T(8,128)(2,1)S(1)}) custom-call(s32[4]{0:T(128)S(1)} %pad_add_fusion.place_ref, bf16[512,1536]{1,0:T(8,128)(2,1)S(1)} %bitcast.5, f32[1,1536]{1,0:T(1,128)S(1)} %broadcast_in_dim.14.gain_ref), custom_call_target="tpu_custom_call" | custom-call | flops 100000000 | tf_op jit(solution)/shard_map/layer_norm/pallas_call | solution.py:84
  9.3 3.2 %collective-permute-done.refs_1_ = bf16[384,256]{1,0:T(8,128)(2,1)S(1)} collective-permute-done((bf16[384,256]{1,0:T(8,128)(2,1)S(1)}, bf16[384,256]{1,0:T(8,128)(2,1)S(1)}, u32[]{:S(2)}, u32[]{:S(2)}) %collective-permute-start) | collective-permute-done | bytes 196640 | tf_op jit(solution)/shard_map/ppermute | solution.py:26
  12.5 2.0 %collective-permute-start.3 = (bf16[384,256]{1,0:T(8,128)(2,1)S(1)}, bf16[384,256]{1,0:T(8,128)(2,1)S(1)}, u32[]{:S(2)}, u32[]{:S(2)}) collective-permute-start(bf16[384,256]{1,0:T(8,128)(2,1)S(1)} %collective-permute-done.refs_1_), channel_id=1, source_target_pairs={{0,1},{1,0},{2,3},{3,2},{4,5},{5,4},{6,7},{7,6},{8,9},{9,8},{10,11... | collective-permute-start | bytes 589832 | tf_op jit(solution)/shard_map/ppermute | solution.py:26
  14.5 1.9 %collective-permute-start.9 = (bf16[96,1536]{1,0:T(8,128)(2,1)S(1)}, bf16[96,1536]{1,0:T(8,128)(2,1)S(1)}, u32[]{:S(2)}, u32[]{:S(2)}) collective-permute-start(bf16[96,1536]{1,0:T(8,128)(2,1)S(1)} %get-tuple-element.61), channel_id=1, source_target_pairs={{0,16},{8,24},{16,0},{24,8},{1,17},{9,25},{17,1},{25,9},{2,18},{10... | collective-permute-start | bytes 884744 | tf_op jit(solution)/shard_map/ppermute | solution.py:26
  16.4 3.6 %collective-permute-done.1.inner_ref = bf16[16,1536]{1,0:T(8,128)(2,1)S(1)} collective-permute-done((bf16[16,1536]{1,0:T(8,128)(2,1)S(1)}, bf16[16,1536]{1,0:T(8,128)(2,1)S(1)}, u32[]{:S(2)}, u32[]{:S(2)}) %collective-permute-start.1) | collective-permute-done | bytes 49184 | tf_op jit(solution)/shard_map/ppermute | solution.py:26
  20.8 7.7 %collective-permute-start.7 = (bf16[384,256]{1,0:T(8,128)(2,1)S(1)}, bf16[384,256]{1,0:T(8,128)(2,1)S(1)}, u32[]{:S(2)}, u32[]{:S(2)}) collective-permute-start(bf16[384,256]{1,0:T(8,128)(2,1)S(1)} %collective-permute-done.4.refs_1_), channel_id=1, source_target_pairs={{0,1},{1,0},{2,3},{3,2},{4,5},{5,4},{6,7},{7,6},{8,9},{9,8},{10,11... | collective-permute-start | bytes 589832 | tf_op jit(solution)/shard_map/ppermute | solution.py:26
  28.7 1.5 %collective-permute-start.11 = (bf16[384,512]{1,0:T(8,128)(2,1)S(1)}, bf16[384,512]{1,0:T(8,128)(2,1)S(1)}, u32[]{:S(2)}, u32[]{:S(2)}) collective-permute-start(bf16[384,512]{1,0:T(8,128)(2,1)S(1)} %get-tuple-element.69), channel_id=1, source_target_pairs={{0,16},{8,24},{16,0},{24,8},{1,17},{9,25},{17,1},{25,9},{2,18},{10... | collective-permute-start | bytes 1179656 | tf_op jit(solution)/shard_map/ppermute | solution.py:26
  30.3 2.3 %near.1 = (bf16[544,1536]{1,0:T(8,128)(2,1)S(1)}, f32[544,512]{1,0:T(8,128)S(1)}, f32[544,512]{1,0:T(8,128)S(1)}, f32[544,512]{1,0:T(8,128)S(1)}) custom-call(s32[4]{0:T(128)S(1)} %pad_add_fusion.place_ref, bf16[512,1536]{1,0:T(8,128)(2,1)S(1)} %get-tuple-element.54.rows_ref, bf16[16,1536]{1,0:T(8,128)(2,1)S(1)} %collective-permute-done.1.inner_ref, ...), custom_call_target="tpu_custom_call" | custom-call | flops 100000000 | tf_op jit(solution)/shard_map/near/pallas_call | solution.py:132
  32.6 1.5 %collective-permute-done.7.refs_2_ = bf16[384,256]{1,0:T(8,128)(2,1)S(1)} collective-permute-done((bf16[384,256]{1,0:T(8,128)(2,1)S(1)}, bf16[384,256]{1,0:T(8,128)(2,1)S(1)}, u32[]{:S(2)}, u32[]{:S(2)}) %collective-permute-start.7) | collective-permute-done | bytes 196640 | tf_op jit(solution)/shard_map/ppermute | solution.py:26
  35.5 3.0 %front.3 = (f32[512,256]{1,0:T(8,128)S(1)}, f32[3,256]{1,0:T(4,128)S(1)}) custom-call(s32[4]{0:T(128)S(1)} %pad_add_fusion.place_ref, bf16[544,1536]{1,0:T(8,128)(2,1)S(1)} %get-tuple-element.57.normed_ref, f32[544,512]{1,0:T(8,128)S(1)} %get-tuple-element.62.refs_0_, bf16[384,256]{1,0:T(8,128)(2,1)S(1)} %collective-permute-done.refs_1_, ...), custom_call_target="tpu_custom_call" | custom-call | flops 100000000 | tf_op jit(solution)/shard_map/front/pallas_call | solution.py:222
  38.5 1.6 %collective-permute-done.11.refs_3_ = bf16[384,512]{1,0:T(8,128)(2,1)S(1)} collective-permute-done((bf16[384,512]{1,0:T(8,128)(2,1)S(1)}, bf16[384,512]{1,0:T(8,128)(2,1)S(1)}, u32[]{:S(2)}, u32[]{:S(2)}) %collective-permute-start.11) | collective-permute-done | bytes 393248 | tf_op jit(solution)/shard_map/ppermute | solution.py:26
  40.6 3.0 %front.4 = (f32[512,256]{1,0:T(8,128)S(1)}, f32[3,256]{1,0:T(4,128)S(1)}) custom-call(s32[4]{0:T(128)S(1)} %pad_add_fusion.place_ref, bf16[544,1536]{1,0:T(8,128)(2,1)S(1)} %get-tuple-element.57.normed_ref, f32[544,512]{1,0:T(8,128)S(1)} %get-tuple-element.70.refs_0_, bf16[384,256]{1,0:T(8,128)(2,1)S(1)} %collective-permute-done.4.refs_1_, ...), custom_call_target="tpu_custom_call" | custom-call | flops 4000000000 | tf_op jit(solution)/shard_map/front/pallas_call | solution.py:222
  43.6 3.0 %front.5 = (f32[512,256]{1,0:T(8,128)S(1)}, f32[1,3,768]{2,1,0:T(4,128)S(1)}) custom-call(s32[4]{0:T(128)S(1)} %pad_add_fusion.place_ref, bf16[544,1536]{1,0:T(8,128)(2,1)S(1)} %get-tuple-element.57.normed_ref, f32[3,256]{1,0:T(4,128)S(1)} %get-tuple-element.66.refs_0_, f32[3,256]{1,0:T(4,128)S(1)} %get-tuple-element.74.refs_1_, ...), custom_call_target="tpu_custom_call" | custom-call | flops 100000000 | tf_op jit(solution)/shard_map/front/pallas_call | solution.py:222
  46.6 2.9 %collective-permute-done.14.refs_10_ = bf16[96,1536]{1,0:T(8,128)(2,1)S(1)} collective-permute-done((bf16[96,1536]{1,0:T(8,128)(2,1)S(1)}, bf16[96,1536]{1,0:T(8,128)(2,1)S(1)}, u32[]{:S(2)}, u32[]{:S(2)}) %collective-permute-start.14) | collective-permute-done | bytes 294944 | tf_op jit(solution)/shard_map/ppermute | solution.py:26
  51.3 1.6 %collective-permute-start.19 = (f32[1,3,768]{2,1,0:T(4,128)S(1)}, f32[1,3,768]{2,1,0:T(4,128)S(1)}, u32[]{:S(2)}, u32[]{:S(2)}) collective-permute-start(f32[1,3,768]{2,1,0:T(4,128)S(1)} %pad_maximum_fusion), channel_id=1, source_target_pairs={{0,2},{1,3},{2,0},{3,1},{4,6},{5,7},{6,4},{7,5},{8,10},{9,11},{10,... | collective-permute-start | bytes 27656 | tf_op jit(solution)/shard_map/ppermute | solution.py:392
  52.9 2.1 %collective-permute-done.19 = f32[1,3,768]{2,1,0:T(4,128)S(1)} collective-permute-done((f32[1,3,768]{2,1,0:T(4,128)S(1)}, f32[1,3,768]{2,1,0:T(4,128)S(1)}, u32[]{:S(2)}, u32[]{:S(2)}) %collective-permute-start.19) | collective-permute-done | bytes 9248 | tf_op jit(solution)/shard_map/ppermute | solution.py:392
  55.0 2.7 %collective-permute-start.20 = (f32[1,3,768]{2,1,0:T(4,128)S(1)}, f32[1,3,768]{2,1,0:T(4,128)S(1)}, u32[]{:S(2)}, u32[]{:S(2)}) collective-permute-start(f32[1,3,768]{2,1,0:T(4,128)S(1)} %pad_maximum_fusion.1), channel_id=1, source_target_pairs={{0,4},{1,5},{2,6},{3,7},{4,0},{5,1},{6,2},{7,3},{8,12},{9,13},{10,... | collective-permute-start | bytes 27656 | tf_op jit(solution)/shard_map/ppermute | solution.py:392
  57.7 2.0 %collective-permute-done.20 = f32[1,3,768]{2,1,0:T(4,128)S(1)} collective-permute-done((f32[1,3,768]{2,1,0:T(4,128)S(1)}, f32[1,3,768]{2,1,0:T(4,128)S(1)}, u32[]{:S(2)}, u32[]{:S(2)}) %collective-permute-start.20) | collective-permute-done | bytes 9248 | tf_op jit(solution)/shard_map/ppermute | solution.py:392
  60.1 1.5 %collective-permute-start.22 = (f32[1,3,768]{2,1,0:T(4,128)S(1)}, f32[1,3,768]{2,1,0:T(4,128)S(1)}, u32[]{:S(2)}, u32[]{:S(2)}) collective-permute-start(f32[1,3,768]{2,1,0:T(4,128)S(1)} %pad_maximum_fusion.2.refs_0_), channel_id=1, source_target_pairs={{0,16},{1,17},{2,18},{3,19},{4,20},{5,21},{6,22},{7,23},{8,24},{9,... | collective-permute-start | bytes 27656 | tf_op jit(solution)/shard_map/ppermute | solution.py:392
  61.6 1.7 %collective-permute-start.23 = (f32[1,3,768]{2,1,0:T(4,128)S(1)}, f32[1,3,768]{2,1,0:T(4,128)S(1)}, u32[]{:S(2)}, u32[]{:S(2)}) collective-permute-start(f32[1,3,768]{2,1,0:T(4,128)S(1)} %pad_maximum_fusion.2.refs_0_), channel_id=1, source_target_pairs={{0,17},{1,16},{2,19},{3,18},{4,21},{5,20},{6,23},{7,22},{8,25},{9,... | collective-permute-start | bytes 27656 | tf_op jit(solution)/shard_map/ppermute | solution.py:392
  63.8 2.4 %collective-permute-done.23.refs_3_ = f32[1,3,768]{2,1,0:T(4,128)S(1)} collective-permute-done((f32[1,3,768]{2,1,0:T(4,128)S(1)}, f32[1,3,768]{2,1,0:T(4,128)S(1)}, u32[]{:S(2)}, u32[]{:S(2)}) %collective-permute-start.23) | collective-permute-done | bytes 9248 | tf_op jit(solution)/shard_map/ppermute | solution.py:392
  66.2 2.9 %back.1 = bf16[512,1536]{1,0:T(8,128)(2,1)} custom-call(s32[4]{0:T(128)S(1)} %pad_add_fusion.place_ref, f32[1,768]{1,0:T(1,128)S(1)} %broadcast_in_dim.12.gain_ref, f32[1,768]{1,0:T(1,128)S(1)} %broadcast_in_dim.13.shift_ref, f32[1,3,768]{2,1,0:T(4,128)S(1)} %pad_maximum_fusion.2.refs_0_, f32[1,3,768]{2,1,0:T(4,128)S(1)} %collective-permute-done.21.refs_1_, ...), custom_call_target="tpu_custom_call" | custom-call | flops 1000000000 | tf_op jit(solution)/shard_map/back/pallas_call | solution.py:319
  (59 shorter events, 7.8 us)
Async XLA Ops:
  0.0 28.7 %collective-permute-start.5 = (bf16[384,1536]{1,0:T(8,128)(2,1)}, bf16[384,1536]{1,0:T(8,128)(2,1)S(1)}, u32[]{:S(2)}, u32[]{:S(2)}) collective-permute-start(bf16[384,1536]{1,0:T(8,128)(2,1)} %refs_0_.1), channel_id=1, source_target_pairs={{0,8},{8,0},{16,24},{24,16},{1,9},{9,1},{17,25},{25,17},{2,10},{10... | collective-permute-start | bytes 3538952 | tf_op jit(solution)/shard_map/ppermute | solution.py:26
  4.2 8.3 %collective-permute-start = (bf16[384,256]{1,0:T(8,128)(2,1)S(1)}, bf16[384,256]{1,0:T(8,128)(2,1)S(1)}, u32[]{:S(2)}, u32[]{:S(2)}) collective-permute-start(bf16[384,256]{1,0:T(8,128)(2,1)S(1)} %get-tuple-element.48), channel_id=1, source_target_pairs={{0,16},{8,24},{16,0},{24,8},{1,17},{9,25},{17,1},{25,9},{2,18},{10... | collective-permute-start | bytes 589832 | tf_op jit(solution)/shard_map/ppermute | solution.py:26
  6.7 14.1 %collective-permute-start.4 = (bf16[384,256]{1,0:T(8,128)(2,1)S(1)}, bf16[384,256]{1,0:T(8,128)(2,1)S(1)}, u32[]{:S(2)}, u32[]{:S(2)}) collective-permute-start(bf16[384,256]{1,0:T(8,128)(2,1)S(1)} %get-tuple-element.53), channel_id=1, source_target_pairs={{0,16},{8,24},{16,0},{24,8},{1,17},{9,25},{17,1},{25,9},{2,18},{10... | collective-permute-start | bytes 589832 | tf_op jit(solution)/shard_map/ppermute | solution.py:26
  12.5 8.3 %collective-permute-start.3 = (bf16[384,256]{1,0:T(8,128)(2,1)S(1)}, bf16[384,256]{1,0:T(8,128)(2,1)S(1)}, u32[]{:S(2)}, u32[]{:S(2)}) collective-permute-start(bf16[384,256]{1,0:T(8,128)(2,1)S(1)} %collective-permute-done.refs_1_), channel_id=1, source_target_pairs={{0,1},{1,0},{2,3},{3,2},{4,5},{5,4},{6,7},{7,6},{8,9},{9,8},{10,11... | collective-permute-start | bytes 589832 | tf_op jit(solution)/shard_map/ppermute | solution.py:26
  14.4 5.6 %collective-permute-start.1 = (bf16[16,1536]{1,0:T(8,128)(2,1)S(1)}, bf16[16,1536]{1,0:T(8,128)(2,1)S(1)}, u32[]{:S(2)}, u32[]{:S(2)}) collective-permute-start(bf16[16,1536]{1,0:T(8,128)(2,1)S(1)} %get-tuple-element.50), channel_id=1, source_target_pairs={{0,1},{1,0},{2,3},{3,2},{4,5},{5,4},{6,7},{7,6},{8,9},{9,8},{10,11... | collective-permute-start | bytes 147464 | tf_op jit(solution)/shard_map/ppermute | solution.py:26
  14.5 18.1 %collective-permute-start.9 = (bf16[96,1536]{1,0:T(8,128)(2,1)S(1)}, bf16[96,1536]{1,0:T(8,128)(2,1)S(1)}, u32[]{:S(2)}, u32[]{:S(2)}) collective-permute-start(bf16[96,1536]{1,0:T(8,128)(2,1)S(1)} %get-tuple-element.61), channel_id=1, source_target_pairs={{0,16},{8,24},{16,0},{24,8},{1,17},{9,25},{17,1},{25,9},{2,18},{10... | collective-permute-start | bytes 884744 | tf_op jit(solution)/shard_map/ppermute | solution.py:26
  20.1 0.7 collective-permute-start.2
  20.7 11.9 %collective-permute-start.6 = (bf16[384,256]{1,0:T(8,128)(2,1)S(1)}, bf16[384,256]{1,0:T(8,128)(2,1)S(1)}, u32[]{:S(2)}, u32[]{:S(2)}) collective-permute-start(bf16[384,256]{1,0:T(8,128)(2,1)S(1)} %collective-permute-done.refs_1_), channel_id=1, source_target_pairs={{0,8},{8,0},{16,24},{24,16},{1,9},{9,1},{17,25},{25,17},{2,10},{10... | collective-permute-start | bytes 589832 | tf_op jit(solution)/shard_map/ppermute | solution.py:26
  20.8 13.2 %collective-permute-start.7 = (bf16[384,256]{1,0:T(8,128)(2,1)S(1)}, bf16[384,256]{1,0:T(8,128)(2,1)S(1)}, u32[]{:S(2)}, u32[]{:S(2)}) collective-permute-start(bf16[384,256]{1,0:T(8,128)(2,1)S(1)} %collective-permute-done.4.refs_1_), channel_id=1, source_target_pairs={{0,1},{1,0},{2,3},{3,2},{4,5},{5,4},{6,7},{7,6},{8,9},{9,8},{10,11... | collective-permute-start | bytes 589832 | tf_op jit(solution)/shard_map/ppermute | solution.py:26
  28.6 5.5 %collective-permute-start.8 = (bf16[384,256]{1,0:T(8,128)(2,1)S(1)}, bf16[384,256]{1,0:T(8,128)(2,1)S(1)}, u32[]{:S(2)}, u32[]{:S(2)}) collective-permute-start(bf16[384,256]{1,0:T(8,128)(2,1)S(1)} %collective-permute-done.4.refs_1_), channel_id=1, source_target_pairs={{0,8},{8,0},{16,24},{24,16},{1,9},{9,1},{17,25},{25,17},{2,10},{10... | collective-permute-start | bytes 589832 | tf_op jit(solution)/shard_map/ppermute | solution.py:26
  28.7 11.4 %collective-permute-start.11 = (bf16[384,512]{1,0:T(8,128)(2,1)S(1)}, bf16[384,512]{1,0:T(8,128)(2,1)S(1)}, u32[]{:S(2)}, u32[]{:S(2)}) collective-permute-start(bf16[384,512]{1,0:T(8,128)(2,1)S(1)} %get-tuple-element.69), channel_id=1, source_target_pairs={{0,16},{8,24},{16,0},{24,8},{1,17},{9,25},{17,1},{25,9},{2,18},{10... | collective-permute-start | bytes 1179656 | tf_op jit(solution)/shard_map/ppermute | solution.py:26
  34.1 1.4 %collective-permute-start.10 = (bf16[384,256]{1,0:T(8,128)(2,1)S(1)}, bf16[384,256]{1,0:T(8,128)(2,1)S(1)}, u32[]{:S(2)}, u32[]{:S(2)}) collective-permute-start(bf16[384,256]{1,0:T(8,128)(2,1)S(1)} %collective-permute-done.3.refs_2_), channel_id=1, source_target_pairs={{0,8},{8,0},{16,24},{24,16},{1,9},{9,1},{17,25},{25,17},{2,10},{10... | collective-permute-start | bytes 589832 | tf_op jit(solution)/shard_map/ppermute | solution.py:26
  34.1 15.5 %collective-permute-start.15 = (bf16[192,1536]{1,0:T(8,128)(2,1)S(1)}, bf16[192,1536]{1,0:T(8,128)(2,1)S(1)}, u32[]{:S(2)}, u32[]{:S(2)}) collective-permute-start(bf16[192,1536]{1,0:T(8,128)(2,1)S(1)} %copy-done.3), channel_id=1, source_target_pairs={{0,8},{8,0},{16,24},{24,16},{1,9},{9,1},{17,25},{25,17},{2,10},{10... | collective-permute-start | bytes 1769480 | tf_op jit(solution)/shard_map/ppermute | solution.py:26
  34.6 6.0 %collective-permute-start.12 = (bf16[384,256]{1,0:T(8,128)(2,1)S(1)}, bf16[384,256]{1,0:T(8,128)(2,1)S(1)}, u32[]{:S(2)}, u32[]{:S(2)}) collective-permute-start(bf16[384,256]{1,0:T(8,128)(2,1)S(1)} %collective-permute-done.7.refs_2_), channel_id=1, source_target_pairs={{0,8},{8,0},{16,24},{24,16},{1,9},{9,1},{17,25},{25,17},{2,10},{10... | collective-permute-start | bytes 589832 | tf_op jit(solution)/shard_map/ppermute | solution.py:26
  40.1 3.5 %collective-permute-start.13 = (bf16[384,512]{1,0:T(8,128)(2,1)S(1)}, bf16[384,512]{1,0:T(8,128)(2,1)S(1)}, u32[]{:S(2)}, u32[]{:S(2)}) collective-permute-start(bf16[384,512]{1,0:T(8,128)(2,1)S(1)} %collective-permute-done.11.refs_3_), channel_id=1, source_target_pairs={{0,8},{8,0},{16,24},{24,16},{1,9},{9,1},{17,25},{25,17},{2,10},{10... | collective-permute-start | bytes 1179656 | tf_op jit(solution)/shard_map/ppermute | solution.py:26
  40.1 9.4 %collective-permute-start.14 = (bf16[96,1536]{1,0:T(8,128)(2,1)S(1)}, bf16[96,1536]{1,0:T(8,128)(2,1)S(1)}, u32[]{:S(2)}, u32[]{:S(2)}) collective-permute-start(bf16[96,1536]{1,0:T(8,128)(2,1)S(1)} %collective-permute-done.9.refs_9_), channel_id=1, source_target_pairs={{0,1},{1,0},{2,3},{3,2},{4,5},{5,4},{6,7},{7,6},{8,9},{9,8},{10,11... | collective-permute-start | bytes 884744 | tf_op jit(solution)/shard_map/ppermute | solution.py:26
  40.5 9.0 %collective-permute-start.16 = (bf16[96,1536]{1,0:T(8,128)(2,1)S(1)}, bf16[96,1536]{1,0:T(8,128)(2,1)S(1)}, u32[]{:S(2)}, u32[]{:S(2)}) collective-permute-start(bf16[96,1536]{1,0:T(8,128)(2,1)S(1)} %collective-permute-done.9.refs_9_), channel_id=1, source_target_pairs={{0,8},{8,0},{16,24},{24,16},{1,9},{9,1},{17,25},{25,17},{2,10},{10... | collective-permute-start | bytes 884744 | tf_op jit(solution)/shard_map/ppermute | solution.py:26
  49.5 1.2 %collective-permute-start.17 = (f32[1,3,768]{2,1,0:T(4,128)S(1)}, f32[1,3,768]{2,1,0:T(4,128)S(1)}, u32[]{:S(2)}, u32[]{:S(2)}) collective-permute-start(f32[1,3,768]{2,1,0:T(4,128)S(1)} %get-tuple-element.80), channel_id=1, source_target_pairs={{0,8},{1,9},{2,10},{3,11},{4,12},{5,13},{6,14},{7,15},{8,0},{9,1},... | collective-permute-start | bytes 27656 | tf_op jit(solution)/shard_map/ppermute | solution.py:392
  49.6 1.7 %collective-permute-start.18 = (bf16[96,1536]{1,0:T(8,128)(2,1)S(1)}, bf16[96,1536]{1,0:T(8,128)(2,1)S(1)}, u32[]{:S(2)}, u32[]{:S(2)}) collective-permute-start(bf16[96,1536]{1,0:T(8,128)(2,1)S(1)} %collective-permute-done.14.refs_10_), channel_id=1, source_target_pairs={{0,8},{8,0},{16,24},{24,16},{1,9},{9,1},{17,25},{25,17},{2,10},{10... | collective-permute-start | bytes 884744 | tf_op jit(solution)/shard_map/ppermute | solution.py:26
  51.3 3.7 %collective-permute-start.19 = (f32[1,3,768]{2,1,0:T(4,128)S(1)}, f32[1,3,768]{2,1,0:T(4,128)S(1)}, u32[]{:S(2)}, u32[]{:S(2)}) collective-permute-start(f32[1,3,768]{2,1,0:T(4,128)S(1)} %pad_maximum_fusion), channel_id=1, source_target_pairs={{0,2},{1,3},{2,0},{3,1},{4,6},{5,7},{6,4},{7,5},{8,10},{9,11},{10,... | collective-permute-start | bytes 27656 | tf_op jit(solution)/shard_map/ppermute | solution.py:392
  55.0 4.7 %collective-permute-start.20 = (f32[1,3,768]{2,1,0:T(4,128)S(1)}, f32[1,3,768]{2,1,0:T(4,128)S(1)}, u32[]{:S(2)}, u32[]{:S(2)}) collective-permute-start(f32[1,3,768]{2,1,0:T(4,128)S(1)} %pad_maximum_fusion.1), channel_id=1, source_target_pairs={{0,4},{1,5},{2,6},{3,7},{4,0},{5,1},{6,2},{7,3},{8,12},{9,13},{10,... | collective-permute-start | bytes 27656 | tf_op jit(solution)/shard_map/ppermute | solution.py:392
  59.7 3.8 %collective-permute-start.21 = (f32[1,3,768]{2,1,0:T(4,128)S(1)}, f32[1,3,768]{2,1,0:T(4,128)S(1)}, u32[]{:S(2)}, u32[]{:S(2)}) collective-permute-start(f32[1,3,768]{2,1,0:T(4,128)S(1)} %pad_maximum_fusion.2.refs_0_), channel_id=1, source_target_pairs={{0,1},{1,0},{2,3},{3,2},{4,5},{5,4},{6,7},{7,6},{8,9},{9,8},{10,11... | collective-permute-start | bytes 27656 | tf_op jit(solution)/shard_map/ppermute | solution.py:392
  60.1 3.7 %collective-permute-start.22 = (f32[1,3,768]{2,1,0:T(4,128)S(1)}, f32[1,3,768]{2,1,0:T(4,128)S(1)}, u32[]{:S(2)}, u32[]{:S(2)}) collective-permute-start(f32[1,3,768]{2,1,0:T(4,128)S(1)} %pad_maximum_fusion.2.refs_0_), channel_id=1, source_target_pairs={{0,16},{1,17},{2,18},{3,19},{4,20},{5,21},{6,22},{7,23},{8,24},{9,... | collective-permute-start | bytes 27656 | tf_op jit(solution)/shard_map/ppermute | solution.py:392
  61.6 4.6 %collective-permute-start.23 = (f32[1,3,768]{2,1,0:T(4,128)S(1)}, f32[1,3,768]{2,1,0:T(4,128)S(1)}, u32[]{:S(2)}, u32[]{:S(2)}) collective-permute-start(f32[1,3,768]{2,1,0:T(4,128)S(1)} %pad_maximum_fusion.2.refs_0_), channel_id=1, source_target_pairs={{0,17},{1,16},{2,19},{3,18},{4,21},{5,20},{6,23},{7,22},{8,25},{9,... | collective-permute-start | bytes 27656 | tf_op jit(solution)/shard_map/ppermute | solution.py:392
  (9 other events, 90.1 us)

commit v7 on v5

--- a/solution.py
+++ b/solution.py
@@ -224,7 +224,7 @@
             VMEM((8, ext_rows, LANES), jnp.float32),
         ],
         compiler_params=params(10),
-        cost_estimate=cost(10**8),
+        cost_estimate=cost(4 * 10**9 if block == ORDER[0] else 10**8),
         name="front",
     )(place, normed, *earlier, *weights, dw_kernel)
 
@@ -350,27 +350,25 @@
         two, zero, one = (swap(part, "fsdp", 2) for part in cut(place, w_in, wide))
         across = swap(w_in, "fsdp", 1)
         normed, inner, outer = normalize_rows(place, rows, gain)
-        normed, two = tie(normed, two)
-        two = [two, swap(two, "ctx", 1)]
         inner = swap(inner, "ctx", 1)
         pairs = [(i, i + 1) for i in range(1, ends, 2)]
         outer = lax.ppermute(outer, "ctx", pairs + [(j, i) for i, j in pairs])
-        normed, inner, outer, zero = tie(normed, inner, outer, zero)
-        zero = [zero, swap(zero, "ctx", 1)]
+        normed, inner, outer, two, zero = tie(normed, inner, outer, two, zero)
+        two, zero = [two, swap(two, "ctx", 1)], [zero, swap(zero, "ctx", 1)]
         two.append(swap(two[0], "fsdp", 1))
         zero.append(swap(zero[0], "fsdp", 1))
         normed, *partials = near_product(place, normed, inner, outer, gain, w_in, across)
-        partials[2], *parts = tie(partials[2], *two, *zero, w_out)
-        two, zero, w_out = parts[:3], parts[3:6], parts[6]
+        partials[2], two[1], two[2], zero[2], w_out = tie(partials[2], two[1], two[2], zero[2], w_out)
         two.append(swap(two[1], "fsdp", 1))
+        partials[2], one, zero[1] = tie(partials[2], one, zero[1])
+        beyond_one = swap(one, "fsdp", 1)
         zero.append(swap(zero[1], "fsdp", 1))
         conv_two, stat_two = front(2, [partials[2], *two])
-        conv_two, partials[0], one = tie(conv_two, partials[0], one)
-        beyond_one = swap(one, "fsdp", 1)
+        conv_two, partials[0] = tie(conv_two, partials[0])
         conv_zero, stat_zero = front(0, [partials[0], *zero])
-        conv_zero, w_out = tie(conv_zero, w_out)
+        conv_zero, partials[1] = tie(conv_zero, partials[1])
+        conv_one, stats = front(1, [partials[1], one, beyond_one], (stat_two, stat_zero), 1)
         remote_out, across_out = swap(w_out, "fsdp", 2), swap(w_out, "fsdp", 1)
-        conv_one, stats = front(1, [partials[1], one, beyond_one], (stat_two, stat_zero), 1)
         convs = [conv_zero, conv_one, conv_two]
 
         def others(flips):
@@ -387,8 +385,10 @@
             return jnp.stack(merged([[part[:, i] for i in range(3)] for part in parts]), 1)
 
         stats = union([stats] + others([(1, 0)]))
-        stats = union([stats] + others([(0, 2), (0, 4), (0, 6)]))
-        stats = [stats] + others([(2, 0), (0, 1), (2, 1)])
+        stats = union([stats] + others([(0, 2)]))
+        stats = union([stats] + others([(0, 4)]))
+        stats = [stats] + others([(0, 1), (2, 0), (2, 1)])
+        stats[1], remote_out = tie(stats[1], remote_out)
         out_weights = [w_out, across_out, remote_out, swap(remote_out, "fsdp", 1)]
     else:
         full_in = lax.all_gather(w_in, "fsdp", axis=0, tiled=True)

time: 70.3 us -> 65 us (0.925)
  waiting for transfers between devices: 25.8 us -> 21.7 us
  starting transfers between devices: 23.6 us -> 22.4 us
    ppermute x15, waiting for transfers between devices: 17.6 us -> 11.4 us  [swap(): lax.ppermute(value, axis, [(i, i ^ bit) for i in range(lax.axis_size(axis...]
    ppermute x7 -> x6, waiting for transfers between devices: 8.18 us -> 10.3 us  [others(): lax.ppermute(stats, both, [(member(f, p), member(f ^ df, p ^ dp)) for f i...]
    ppermute x7 -> x6, starting transfers between devices: 9.56 us -> 9.04 us  [others(): lax.ppermute(stats, both, [(member(f, p), member(f ^ df, p ^ dp)) for f i...]
  transfers between devices with their start and end apart: 23 -> 22, of which waited for: 12 -> 10; matrix products, arithmetic and copies ran while one was open for 0% -> 0% of each run, Pallas kernels for 16% -> 17%
where the time goes in v7:
time: 65 us; the launch traced here: 64.8 us
  starting transfers between devices  22.4 us (34%)
  waiting for transfers between devices  21.7 us (33%)
  Pallas kernels  17 us (26%)
  local copies, waits for them, and re-layouts  2.72 us (4%)
  between operations  0.81 us (1%)
    ppermute x15, starting transfers between devices, swap(): lax.ppermute(value, axis, [(i, i ^ bit) for i in range(lax.axis_size(axis...  12.7 us
    ppermute x15, waiting for transfers between devices, swap(): lax.ppermute(value, axis, [(i, i ^ bit) for i in range(lax.axis_size(axis...  11.4 us
    ppermute x6, waiting for transfers between devices, others(): lax.ppermute(stats, both, [(member(f, p), member(f ^ df, p ^ dp)) for f i...  10.3 us
    ppermute x6, starting transfers between devices, others(): lax.ppermute(stats, both, [(member(f, p), member(f ^ df, p ^ dp)) for f i...  9.04 us
    pallas_call x3, Pallas kernels, front_block(): pl.pallas_call(functools.partial(front_kernel, block, len(earlier)), out_...  8.67 us
    pallas_call x1, Pallas kernels, back(): pl.pallas_call(functools.partial(back_kernel, len(stats)), out_shape=jax....  2.94 us
    unnamed x16, local copies, waits for them, and re-layouts  2.71 us
    pallas_call x1, Pallas kernels, normalize_rows(): pl.pallas_call(norm_kernel, out_shape=[jax.ShapeDtypeStruct(shape, jnp.bf...  2.45 us
  transfers between devices with their start and end apart: 22, of which 10 were waited for; matrix products, arithmetic and copies ran while one was open for 0% of the time, Pallas kernels for 17%

profile of v7, /device:TPU:0, one launch (start us, length us, event | category | flops | bytes accessed | tf_op | source)
XLA Modules:
  0.0 64.8 jit_solution(8686918103081596884)
XLA Ops:
  1.2 1.3 %copy-done = bf16[384,1536]{1,0:T(8,128)(2,1)S(1)} copy-done((bf16[384,1536]{1,0:T(8,128)(2,1)S(1)}, bf16[384,1536]{1,0:T(8,128)(2,1)}, u32[]{:S(2)}) %copy-start) | copy-done | bytes 1179672
  3.1 2.6 %collective-permute-start.2 = (bf16[384,256]{1,0:T(8,128)(2,1)S(1)}, bf16[384,256]{1,0:T(8,128)(2,1)S(1)}, u32[]{:S(2)}, u32[]{:S(2)}) collective-permute-start(bf16[384,256]{1,0:T(8,128)(2,1)S(1)} %get-tuple-element.43), channel_id=1, source_target_pairs={{0,16},{8,24},{16,0},{24,8},{1,17},{9,25},{17,1},{25,9},{2,18},{10... | collective-permute-start | bytes 589832 | tf_op jit(solution)/shard_map/ppermute | solution.py:26
  5.7 1.4 %copy-done.2 = bf16[1,512,1536]{2,1,0:T(8,128)(2,1)S(1)} copy-done((bf16[1,512,1536]{2,1,0:T(8,128)(2,1)S(1)}, bf16[1,512,1536]{2,1,0:T(8,128)(2,1)}, u32[]{:S(2)}) %copy-start.2) | copy-done | bytes 1572888
  7.1 2.5 %layer_norm.1 = (bf16[512,1536]{1,0:T(8,128)(2,1)S(1)}, bf16[16,1536]{1,0:T(8,128)(2,1)S(1)}, bf16[16,1536]{1,0:T(8,128)(2,1)S(1)}) custom-call(s32[4]{0:T(128)S(1)} %pad_add_fusion.place_ref, bf16[512,1536]{1,0:T(8,128)(2,1)S(1)} %bitcast.5, f32[1,1536]{1,0:T(1,128)S(1)} %broadcast_in_dim.14.gain_ref), custom_call_target="tpu_custom_call" | custom-call | flops 100000000 | tf_op jit(solution)/shard_map/layer_norm/pallas_call | solution.py:80
  9.6 2.0 %collective-permute-start = (bf16[16,1536]{1,0:T(8,128)(2,1)S(1)}, bf16[16,1536]{1,0:T(8,128)(2,1)S(1)}, u32[]{:S(2)}, u32[]{:S(2)}) collective-permute-start(bf16[16,1536]{1,0:T(8,128)(2,1)S(1)} %get-tuple-element.41), channel_id=1, source_target_pairs={{0,1},{1,0},{2,3},{3,2},{4,5},{5,4},{6,7},{7,6},{8,9},{9,8},{10,11... | collective-permute-start | bytes 147464 | tf_op jit(solution)/shard_map/ppermute | solution.py:26
  12.3 1.5 %collective-permute-done.inner_ref = bf16[16,1536]{1,0:T(8,128)(2,1)S(1)} collective-permute-done((bf16[16,1536]{1,0:T(8,128)(2,1)S(1)}, bf16[16,1536]{1,0:T(8,128)(2,1)S(1)}, u32[]{:S(2)}, u32[]{:S(2)}) %collective-permute-start) | collective-permute-done | bytes 49184 | tf_op jit(solution)/shard_map/ppermute | solution.py:26
  13.7 1.9 %collective-permute-start.8 = (bf16[384,512]{1,0:T(8,128)(2,1)S(1)}, bf16[384,512]{1,0:T(8,128)(2,1)S(1)}, u32[]{:S(2)}, u32[]{:S(2)}) collective-permute-start(bf16[384,512]{1,0:T(8,128)(2,1)S(1)} %get-tuple-element.53), channel_id=1, source_target_pairs={{0,16},{8,24},{16,0},{24,8},{1,17},{9,25},{17,1},{25,9},{2,18},{10... | collective-permute-start | bytes 1179656 | tf_op jit(solution)/shard_map/ppermute | solution.py:26
  15.7 3.0 %collective-permute-start.5 = (bf16[384,256]{1,0:T(8,128)(2,1)S(1)}, bf16[384,256]{1,0:T(8,128)(2,1)S(1)}, u32[]{:S(2)}, u32[]{:S(2)}) collective-permute-start(bf16[384,256]{1,0:T(8,128)(2,1)S(1)} %collective-permute-done.2.refs_1_), channel_id=1, source_target_pairs={{0,1},{1,0},{2,3},{3,2},{4,5},{5,4},{6,7},{7,6},{8,9},{9,8},{10,11... | collective-permute-start | bytes 589832 | tf_op jit(solution)/shard_map/ppermute | solution.py:26
  19.3 2.3 %near.1 = (bf16[544,1536]{1,0:T(8,128)(2,1)S(1)}, f32[544,512]{1,0:T(8,128)S(1)}, f32[544,512]{1,0:T(8,128)S(1)}, f32[544,512]{1,0:T(8,128)S(1)}) custom-call(s32[4]{0:T(128)S(1)} %pad_add_fusion.place_ref, bf16[512,1536]{1,0:T(8,128)(2,1)S(1)} %get-tuple-element.45.rows_ref, bf16[16,1536]{1,0:T(8,128)(2,1)S(1)} %collective-permute-done.inner_ref, ...), custom_call_target="tpu_custom_call" | custom-call | flops 100000000 | tf_op jit(solution)/shard_map/near/pallas_call | solution.py:128
  21.6 2.3 %collective-permute-done.5.refs_2_ = bf16[384,256]{1,0:T(8,128)(2,1)S(1)} collective-permute-done((bf16[384,256]{1,0:T(8,128)(2,1)S(1)}, bf16[384,256]{1,0:T(8,128)(2,1)S(1)}, u32[]{:S(2)}, u32[]{:S(2)}) %collective-permute-start.5) | collective-permute-done | bytes 196640 | tf_op jit(solution)/shard_map/ppermute | solution.py:26
  23.9 2.8 %collective-permute-done.9.refs_2_ = bf16[384,256]{1,0:T(8,128)(2,1)S(1)} collective-permute-done((bf16[384,256]{1,0:T(8,128)(2,1)S(1)}, bf16[384,256]{1,0:T(8,128)(2,1)S(1)}, u32[]{:S(2)}, u32[]{:S(2)}) %collective-permute-start.9) | collective-permute-done | bytes 196640 | tf_op jit(solution)/shard_map/ppermute | solution.py:26
  27.3 2.9 %front.3 = (f32[512,256]{1,0:T(8,128)S(1)}, f32[3,256]{1,0:T(4,128)S(1)}) custom-call(s32[4]{0:T(128)S(1)} %pad_add_fusion.place_ref, bf16[544,1536]{1,0:T(8,128)(2,1)S(1)} %get-tuple-element.48.normed_ref, f32[544,512]{1,0:T(8,128)S(1)} %get-tuple-element.54.refs_0_, bf16[384,256]{1,0:T(8,128)(2,1)S(1)} %collective-permute-done.2.refs_1_, ...), custom_call_target="tpu_custom_call" | custom-call | flops 4000000000 | tf_op jit(solution)/shard_map/front/pallas_call | solution.py:213
  30.2 2.9 %front.4 = (f32[512,256]{1,0:T(8,128)S(1)}, f32[3,256]{1,0:T(4,128)S(1)}) custom-call(s32[4]{0:T(128)S(1)} %pad_add_fusion.place_ref, bf16[544,1536]{1,0:T(8,128)(2,1)S(1)} %get-tuple-element.48.normed_ref, f32[544,512]{1,0:T(8,128)S(1)} %get-tuple-element.60.refs_0_, bf16[384,256]{1,0:T(8,128)(2,1)S(1)} %collective-permute-done.3.refs_1_, ...), custom_call_target="tpu_custom_call" | custom-call | flops 100000000 | tf_op jit(solution)/shard_map/front/pallas_call | solution.py:213
  33.1 2.9 %front.5 = (f32[512,256]{1,0:T(8,128)S(1)}, f32[1,3,768]{2,1,0:T(4,128)S(1)}) custom-call(s32[4]{0:T(128)S(1)} %pad_add_fusion.place_ref, bf16[544,1536]{1,0:T(8,128)(2,1)S(1)} %get-tuple-element.48.normed_ref, f32[3,256]{1,0:T(4,128)S(1)} %get-tuple-element.57.refs_0_, f32[3,256]{1,0:T(4,128)S(1)} %get-tuple-element.63.refs_1_, ...), custom_call_target="tpu_custom_call" | custom-call | flops 100000000 | tf_op jit(solution)/shard_map/front/pallas_call | solution.py:213
  37.3 3.3 %collective-permute-start.14 = (f32[1,3,768]{2,1,0:T(4,128)S(1)}, f32[1,3,768]{2,1,0:T(4,128)S(1)}, u32[]{:S(2)}, u32[]{:S(2)}) collective-permute-start(f32[1,3,768]{2,1,0:T(4,128)S(1)} %pad_maximum_fusion), channel_id=1, source_target_pairs={{0,2},{1,3},{2,0},{3,1},{4,6},{5,7},{6,4},{7,5},{8,10},{9,11},{10,... | collective-permute-start | bytes 27656 | tf_op jit(solution)/shard_map/ppermute | solution.py:376
  40.6 1.5 %collective-permute-start.17 = (bf16[192,1536]{1,0:T(8,128)(2,1)S(1)}, bf16[192,1536]{1,0:T(8,128)(2,1)S(1)}, u32[]{:S(2)}, u32[]{:S(2)}) collective-permute-start(bf16[192,1536]{1,0:T(8,128)(2,1)S(1)} %copy-done.3), channel_id=1, source_target_pairs={{0,16},{8,24},{16,0},{24,8},{1,17},{9,25},{17,1},{25,9},{2,18},{10... | collective-permute-start | bytes 1769480 | tf_op jit(solution)/shard_map/ppermute | solution.py:26
  42.4 3.1 %collective-permute-start.15 = (f32[1,3,768]{2,1,0:T(4,128)S(1)}, f32[1,3,768]{2,1,0:T(4,128)S(1)}, u32[]{:S(2)}, u32[]{:S(2)}) collective-permute-start(f32[1,3,768]{2,1,0:T(4,128)S(1)} %pad_maximum_fusion.1), channel_id=1, source_target_pairs={{0,4},{1,5},{2,6},{3,7},{4,0},{5,1},{6,2},{7,3},{8,12},{9,13},{10,... | collective-permute-start | bytes 27656 | tf_op jit(solution)/shard_map/ppermute | solution.py:376
  45.5 1.7 %collective-permute-done.15 = f32[1,3,768]{2,1,0:T(4,128)S(1)} collective-permute-done((f32[1,3,768]{2,1,0:T(4,128)S(1)}, f32[1,3,768]{2,1,0:T(4,128)S(1)}, u32[]{:S(2)}, u32[]{:S(2)}) %collective-permute-start.15) | collective-permute-done | bytes 9248 | tf_op jit(solution)/shard_map/ppermute | solution.py:376
  47.8 3.2 %collective-permute-done.16.refs_1_ = f32[1,3,768]{2,1,0:T(4,128)S(1)} collective-permute-done((f32[1,3,768]{2,1,0:T(4,128)S(1)}, f32[1,3,768]{2,1,0:T(4,128)S(1)}, u32[]{:S(2)}, u32[]{:S(2)}) %collective-permute-start.16) | collective-permute-done | bytes 9248 | tf_op jit(solution)/shard_map/ppermute | solution.py:376
  50.9 4.8 %collective-permute-done.17.refs_9_ = bf16[192,1536]{1,0:T(8,128)(2,1)S(1)} collective-permute-done((bf16[192,1536]{1,0:T(8,128)(2,1)S(1)}, bf16[192,1536]{1,0:T(8,128)(2,1)S(1)}, u32[]{:S(2)}, u32[]{:S(2)}) %collective-permute-start.17) | collective-permute-done | bytes 589856 | tf_op jit(solution)/shard_map/ppermute | solution.py:26
  55.8 1.5 %collective-permute-start.18 = (f32[1,3,768]{2,1,0:T(4,128)S(1)}, f32[1,3,768]{2,1,0:T(4,128)S(1)}, u32[]{:S(2)}, u32[]{:S(2)}) collective-permute-start(f32[1,3,768]{2,1,0:T(4,128)S(1)} %pad_maximum_fusion.2.refs_0_), channel_id=1, source_target_pairs={{0,16},{1,17},{2,18},{3,19},{4,20},{5,21},{6,22},{7,23},{8,24},{9,... | collective-permute-start | bytes 27656 | tf_op jit(solution)/shard_map/ppermute | solution.py:376
  57.8 1.7 %collective-permute-done.18.refs_2_ = f32[1,3,768]{2,1,0:T(4,128)S(1)} collective-permute-done((f32[1,3,768]{2,1,0:T(4,128)S(1)}, f32[1,3,768]{2,1,0:T(4,128)S(1)}, u32[]{:S(2)}, u32[]{:S(2)}) %collective-permute-start.18) | collective-permute-done | bytes 9248 | tf_op jit(solution)/shard_map/ppermute | solution.py:376
  59.5 2.4 %collective-permute-done.19.refs_3_ = f32[1,3,768]{2,1,0:T(4,128)S(1)} collective-permute-done((f32[1,3,768]{2,1,0:T(4,128)S(1)}, f32[1,3,768]{2,1,0:T(4,128)S(1)}, u32[]{:S(2)}, u32[]{:S(2)}) %collective-permute-start.19) | collective-permute-done | bytes 9248 | tf_op jit(solution)/shard_map/ppermute | solution.py:376
  61.8 2.9 %back.1 = bf16[512,1536]{1,0:T(8,128)(2,1)} custom-call(s32[4]{0:T(128)S(1)} %pad_add_fusion.place_ref, f32[1,768]{1,0:T(1,128)S(1)} %broadcast_in_dim.12.gain_ref, f32[1,768]{1,0:T(1,128)S(1)} %broadcast_in_dim.13.shift_ref, f32[1,3,768]{2,1,0:T(4,128)S(1)} %pad_maximum_fusion.2.refs_0_, f32[1,3,768]{2,1,0:T(4,128)S(1)} %collective-permute-done.16.refs_1_, ...), custom_call_target="tpu_custom_call" | custom-call | flops 1000000000 | tf_op jit(solution)/shard_map/back/pallas_call | solution.py:305
  (53 shorter events, 5.7 us)
Async XLA Ops:
  0.0 19.2 %collective-permute-start.4 = (bf16[384,1536]{1,0:T(8,128)(2,1)}, bf16[384,1536]{1,0:T(8,128)(2,1)S(1)}, u32[]{:S(2)}, u32[]{:S(2)}) collective-permute-start(bf16[384,1536]{1,0:T(8,128)(2,1)} %refs_0_.1), channel_id=1, source_target_pairs={{0,8},{8,0},{16,24},{24,16},{1,9},{9,1},{17,25},{25,17},{2,10},{10... | collective-permute-start | bytes 3538952 | tf_op jit(solution)/shard_map/ppermute | solution.py:26
  3.1 12.6 %collective-permute-start.2 = (bf16[384,256]{1,0:T(8,128)(2,1)S(1)}, bf16[384,256]{1,0:T(8,128)(2,1)S(1)}, u32[]{:S(2)}, u32[]{:S(2)}) collective-permute-start(bf16[384,256]{1,0:T(8,128)(2,1)S(1)} %get-tuple-element.43), channel_id=1, source_target_pairs={{0,16},{8,24},{16,0},{24,8},{1,17},{9,25},{17,1},{25,9},{2,18},{10... | collective-permute-start | bytes 589832 | tf_op jit(solution)/shard_map/ppermute | solution.py:26
  5.6 10.1 %collective-permute-start.3 = (bf16[384,256]{1,0:T(8,128)(2,1)S(1)}, bf16[384,256]{1,0:T(8,128)(2,1)S(1)}, u32[]{:S(2)}, u32[]{:S(2)}) collective-permute-start(bf16[384,256]{1,0:T(8,128)(2,1)S(1)} %get-tuple-element.44), channel_id=1, source_target_pairs={{0,16},{8,24},{16,0},{24,8},{1,17},{9,25},{17,1},{25,9},{2,18},{10... | collective-permute-start | bytes 589832 | tf_op jit(solution)/shard_map/ppermute | solution.py:26
  9.6 4.2 %collective-permute-start = (bf16[16,1536]{1,0:T(8,128)(2,1)S(1)}, bf16[16,1536]{1,0:T(8,128)(2,1)S(1)}, u32[]{:S(2)}, u32[]{:S(2)}) collective-permute-start(bf16[16,1536]{1,0:T(8,128)(2,1)S(1)} %get-tuple-element.41), channel_id=1, source_target_pairs={{0,1},{1,0},{2,3},{3,2},{4,5},{5,4},{6,7},{7,6},{8,9},{9,8},{10,11... | collective-permute-start | bytes 147464 | tf_op jit(solution)/shard_map/ppermute | solution.py:26
  11.6 4.1 %collective-permute-start.1 = (bf16[16,1536]{1,0:T(8,128)(2,1)S(1)}, bf16[16,1536]{1,0:T(8,128)(2,1)S(1)}, u32[]{:S(2)}, u32[]{:S(2)}) collective-permute-start(bf16[16,1536]{1,0:T(8,128)(2,1)S(1)} %get-tuple-element.42), channel_id=1, source_target_pairs={{1,2},{3,4},{5,6},{2,1},{4,3},{6,5},{9,10},{11,12},{13,14},{10,9},... | collective-permute-start | bytes 147464 | tf_op jit(solution)/shard_map/ppermute | solution.py:355
  13.7 13.0 %collective-permute-start.8 = (bf16[384,512]{1,0:T(8,128)(2,1)S(1)}, bf16[384,512]{1,0:T(8,128)(2,1)S(1)}, u32[]{:S(2)}, u32[]{:S(2)}) collective-permute-start(bf16[384,512]{1,0:T(8,128)(2,1)S(1)} %get-tuple-element.53), channel_id=1, source_target_pairs={{0,16},{8,24},{16,0},{24,8},{1,17},{9,25},{17,1},{25,9},{2,18},{10... | collective-permute-start | bytes 1179656 | tf_op jit(solution)/shard_map/ppermute | solution.py:26
  15.7 8.2 %collective-permute-start.5 = (bf16[384,256]{1,0:T(8,128)(2,1)S(1)}, bf16[384,256]{1,0:T(8,128)(2,1)S(1)}, u32[]{:S(2)}, u32[]{:S(2)}) collective-permute-start(bf16[384,256]{1,0:T(8,128)(2,1)S(1)} %collective-permute-done.2.refs_1_), channel_id=1, source_target_pairs={{0,1},{1,0},{2,3},{3,2},{4,5},{5,4},{6,7},{7,6},{8,9},{9,8},{10,11... | collective-permute-start | bytes 589832 | tf_op jit(solution)/shard_map/ppermute | solution.py:26
  18.7 5.2 %collective-permute-start.6 = (bf16[384,256]{1,0:T(8,128)(2,1)S(1)}, bf16[384,256]{1,0:T(8,128)(2,1)S(1)}, u32[]{:S(2)}, u32[]{:S(2)}) collective-permute-start(bf16[384,256]{1,0:T(8,128)(2,1)S(1)} %collective-permute-done.2.refs_1_), channel_id=1, source_target_pairs={{0,8},{8,0},{16,24},{24,16},{1,9},{9,1},{17,25},{25,17},{2,10},{10... | collective-permute-start | bytes 589832 | tf_op jit(solution)/shard_map/ppermute | solution.py:26
  18.7 5.2 %collective-permute-start.7 = (bf16[384,256]{1,0:T(8,128)(2,1)S(1)}, bf16[384,256]{1,0:T(8,128)(2,1)S(1)}, u32[]{:S(2)}, u32[]{:S(2)}) collective-permute-start(bf16[384,256]{1,0:T(8,128)(2,1)S(1)} %collective-permute-done.3.refs_1_), channel_id=1, source_target_pairs={{0,8},{8,0},{16,24},{24,16},{1,9},{9,1},{17,25},{25,17},{2,10},{10... | collective-permute-start | bytes 589832 | tf_op jit(solution)/shard_map/ppermute | solution.py:26
  19.2 7.6 %collective-permute-start.9 = (bf16[384,256]{1,0:T(8,128)(2,1)S(1)}, bf16[384,256]{1,0:T(8,128)(2,1)S(1)}, u32[]{:S(2)}, u32[]{:S(2)}) collective-permute-start(bf16[384,256]{1,0:T(8,128)(2,1)S(1)} %collective-permute-done.3.refs_1_), channel_id=1, source_target_pairs={{0,1},{1,0},{2,3},{3,2},{4,5},{5,4},{6,7},{7,6},{8,9},{9,8},{10,11... | collective-permute-start | bytes 589832 | tf_op jit(solution)/shard_map/ppermute | solution.py:26
  23.9 3.4 %collective-permute-start.10 = (bf16[384,256]{1,0:T(8,128)(2,1)S(1)}, bf16[384,256]{1,0:T(8,128)(2,1)S(1)}, u32[]{:S(2)}, u32[]{:S(2)}) collective-permute-start(bf16[384,256]{1,0:T(8,128)(2,1)S(1)} %collective-permute-done.5.refs_2_), channel_id=1, source_target_pairs={{0,8},{8,0},{16,24},{24,16},{1,9},{9,1},{17,25},{25,17},{2,10},{10... | collective-permute-start | bytes 589832 | tf_op jit(solution)/shard_map/ppermute | solution.py:26
  26.8 6.3 %collective-permute-start.12 = (bf16[384,512]{1,0:T(8,128)(2,1)S(1)}, bf16[384,512]{1,0:T(8,128)(2,1)S(1)}, u32[]{:S(2)}, u32[]{:S(2)}) collective-permute-start(bf16[384,512]{1,0:T(8,128)(2,1)S(1)} %collective-permute-done.8.refs_3_), channel_id=1, source_target_pairs={{0,8},{8,0},{16,24},{24,16},{1,9},{9,1},{17,25},{25,17},{2,10},{10... | collective-permute-start | bytes 1179656 | tf_op jit(solution)/shard_map/ppermute | solution.py:26
  26.8 3.4 %collective-permute-start.11 = (bf16[384,256]{1,0:T(8,128)(2,1)S(1)}, bf16[384,256]{1,0:T(8,128)(2,1)S(1)}, u32[]{:S(2)}, u32[]{:S(2)}) collective-permute-start(bf16[384,256]{1,0:T(8,128)(2,1)S(1)} %collective-permute-done.9.refs_2_), channel_id=1, source_target_pairs={{0,8},{8,0},{16,24},{24,16},{1,9},{9,1},{17,25},{25,17},{2,10},{10... | collective-permute-start | bytes 589832 | tf_op jit(solution)/shard_map/ppermute | solution.py:26
  33.1 24.6 %copy-start.6 = (f32[768]{0:T(1024)S(1)}, f32[768]{0:T(1024)}, u32[]{:S(2)}) copy-start(f32[768]{0:T(1024)} %param.13) | copy-start | bytes 9220
  33.1 24.6 %copy-start.7 = (f32[768]{0:T(1024)S(1)}, f32[768]{0:T(1024)}, u32[]{:S(2)}) copy-start(f32[768]{0:T(1024)} %param.14) | copy-start | bytes 9220
  36.0 1.2 %collective-permute-start.13 = (f32[1,3,768]{2,1,0:T(4,128)S(1)}, f32[1,3,768]{2,1,0:T(4,128)S(1)}, u32[]{:S(2)}, u32[]{:S(2)}) collective-permute-start(f32[1,3,768]{2,1,0:T(4,128)S(1)} %get-tuple-element.68), channel_id=1, source_target_pairs={{0,8},{1,9},{2,10},{3,11},{4,12},{5,13},{6,14},{7,15},{8,0},{9,1},... | collective-permute-start | bytes 27656 | tf_op jit(solution)/shard_map/ppermute | solution.py:376
  37.3 5.0 %collective-permute-start.14 = (f32[1,3,768]{2,1,0:T(4,128)S(1)}, f32[1,3,768]{2,1,0:T(4,128)S(1)}, u32[]{:S(2)}, u32[]{:S(2)}) collective-permute-start(f32[1,3,768]{2,1,0:T(4,128)S(1)} %pad_maximum_fusion), channel_id=1, source_target_pairs={{0,2},{1,3},{2,0},{3,1},{4,6},{5,7},{6,4},{7,5},{8,10},{9,11},{10,... | collective-permute-start | bytes 27656 | tf_op jit(solution)/shard_map/ppermute | solution.py:376
  40.6 15.1 %collective-permute-start.17 = (bf16[192,1536]{1,0:T(8,128)(2,1)S(1)}, bf16[192,1536]{1,0:T(8,128)(2,1)S(1)}, u32[]{:S(2)}, u32[]{:S(2)}) collective-permute-start(bf16[192,1536]{1,0:T(8,128)(2,1)S(1)} %copy-done.3), channel_id=1, source_target_pairs={{0,16},{8,24},{16,0},{24,8},{1,17},{9,25},{17,1},{25,9},{2,18},{10... | collective-permute-start | bytes 1769480 | tf_op jit(solution)/shard_map/ppermute | solution.py:26
  42.4 4.8 %collective-permute-start.15 = (f32[1,3,768]{2,1,0:T(4,128)S(1)}, f32[1,3,768]{2,1,0:T(4,128)S(1)}, u32[]{:S(2)}, u32[]{:S(2)}) collective-permute-start(f32[1,3,768]{2,1,0:T(4,128)S(1)} %pad_maximum_fusion.1), channel_id=1, source_target_pairs={{0,4},{1,5},{2,6},{3,7},{4,0},{5,1},{6,2},{7,3},{8,12},{9,13},{10,... | collective-permute-start | bytes 27656 | tf_op jit(solution)/shard_map/ppermute | solution.py:376
  47.2 3.8 %collective-permute-start.16 = (f32[1,3,768]{2,1,0:T(4,128)S(1)}, f32[1,3,768]{2,1,0:T(4,128)S(1)}, u32[]{:S(2)}, u32[]{:S(2)}) collective-permute-start(f32[1,3,768]{2,1,0:T(4,128)S(1)} %pad_maximum_fusion.2.refs_0_), channel_id=1, source_target_pairs={{0,1},{1,0},{2,3},{3,2},{4,5},{5,4},{6,7},{7,6},{8,9},{9,8},{10,11... | collective-permute-start | bytes 27656 | tf_op jit(solution)/shard_map/ppermute | solution.py:376
  47.8 14.1 %collective-permute-start.20 = (bf16[192,1536]{1,0:T(8,128)(2,1)S(1)}, bf16[192,1536]{1,0:T(8,128)(2,1)S(1)}, u32[]{:S(2)}, u32[]{:S(2)}) collective-permute-start(bf16[192,1536]{1,0:T(8,128)(2,1)S(1)} %copy-done.3), channel_id=1, source_target_pairs={{0,8},{8,0},{16,24},{24,16},{1,9},{9,1},{17,25},{25,17},{2,10},{10... | collective-permute-start | bytes 1769480 | tf_op jit(solution)/shard_map/ppermute | solution.py:26
  55.8 6.1 %collective-permute-start.21 = (bf16[192,1536]{1,0:T(8,128)(2,1)S(1)}, bf16[192,1536]{1,0:T(8,128)(2,1)S(1)}, u32[]{:S(2)}, u32[]{:S(2)}) collective-permute-start(bf16[192,1536]{1,0:T(8,128)(2,1)S(1)} %collective-permute-done.17.refs_9_), channel_id=1, source_target_pairs={{0,8},{8,0},{16,24},{24,16},{1,9},{9,1},{17,25},{25,17},{2,10},{10... | collective-permute-start | bytes 1769480 | tf_op jit(solution)/shard_map/ppermute | solution.py:26
  55.8 3.7 %collective-permute-start.18 = (f32[1,3,768]{2,1,0:T(4,128)S(1)}, f32[1,3,768]{2,1,0:T(4,128)S(1)}, u32[]{:S(2)}, u32[]{:S(2)}) collective-permute-start(f32[1,3,768]{2,1,0:T(4,128)S(1)} %pad_maximum_fusion.2.refs_0_), channel_id=1, source_target_pairs={{0,16},{1,17},{2,18},{3,19},{4,20},{5,21},{6,22},{7,23},{8,24},{9,... | collective-permute-start | bytes 27656 | tf_op jit(solution)/shard_map/ppermute | solution.py:376
  57.2 4.6 %collective-permute-start.19 = (f32[1,3,768]{2,1,0:T(4,128)S(1)}, f32[1,3,768]{2,1,0:T(4,128)S(1)}, u32[]{:S(2)}, u32[]{:S(2)}) collective-permute-start(f32[1,3,768]{2,1,0:T(4,128)S(1)} %pad_maximum_fusion.2.refs_0_), channel_id=1, source_target_pairs={{0,17},{1,16},{2,19},{3,18},{4,21},{5,20},{6,23},{7,22},{8,25},{9,... | collective-permute-start | bytes 27656 | tf_op jit(solution)/shard_map/ppermute | solution.py:376
  (6 other events, 44.4 us)

commit v8 on v7

--- a/solution.py
+++ b/solution.py
@@ -59,7 +59,7 @@
     return (deviate * lax.rsqrt(spread + 1e-05) * gain).astype(jnp.bfloat16)
 
 
-def norm_kernel(place_ref, rows_ref, gain_ref, out_ref, inner_ref, outer_ref):
+def norm_kernel(place_ref, rows_ref, gain_ref, shard_ref, out_ref, inner_ref, outer_ref, *piece_refs):
     step = 64
     row_count = rows_ref.shape[0]
 
@@ -72,20 +72,23 @@
     last = row_count - HALO
     inner_ref[...] = rows_ref[pl.ds(pl.multiple_of((1 - odd) * last, HALO), HALO), :]
     outer_ref[...] = rows_ref[pl.ds(pl.multiple_of(odd * last, HALO), HALO), :]
-
-
-def normalize_rows(place, rows, gain):
+    for i, ref in enumerate(piece_refs):
+        ref[...] = shard_ref[i * ref.shape[0] : (i + 1) * ref.shape[0], :]
+
+
+def normalize_rows(place, rows, gain, shard, pieces):
     row_count, width = rows.shape
     shapes = [(row_count, width), (HALO, width), (HALO, width)]
+    shapes += [(shard.shape[0] // max(pieces, 1), width)] * pieces
     return pl.pallas_call(
         norm_kernel,
         out_shape=[jax.ShapeDtypeStruct(shape, jnp.bfloat16) for shape in shapes],
-        in_specs=[pl.BlockSpec(memory_space=pltpu.SMEM)] + [pl.BlockSpec(memory_space=VMEM)] * 2,
-        out_specs=[pl.BlockSpec(memory_space=VMEM)] * 3,
+        in_specs=[pl.BlockSpec(memory_space=pltpu.SMEM)] + [pl.BlockSpec(memory_space=VMEM)] * 3,
+        out_specs=[pl.BlockSpec(memory_space=VMEM)] * len(shapes),
         compiler_params=params(4),
         cost_estimate=cost(10**8),
         name="layer_norm",
-    )(place, rows, gain)
+    )(place, rows, gain, shard)
 
 
 def near_kernel(place_ref, rows_ref, inner_ref, outer_ref, gain_ref, *refs):
@@ -224,7 +227,7 @@
             VMEM((8, ext_rows, LANES), jnp.float32),
         ],
         compiler_params=params(10),
-        cost_estimate=cost(4 * 10**9 if block == ORDER[0] else 10**8),
+        cost_estimate=cost(4 * 10**9 if block == ORDER[1] else 10**8),
         name="front",
     )(place, normed, *earlier, *weights, dw_kernel)
 
@@ -266,9 +269,14 @@
     row_count, wide = convs[0].shape
     if len(weight_refs) > 1:
         depth = weight_refs[0].shape[0]
-        for i, weight_ref in enumerate(weight_refs):
+        for i, weight_ref in enumerate(weight_refs[:2]):
             at = pl.multiple_of(lax.bitwise_xor(place_ref[0], i) * depth, depth)
             weights[pl.ds(at, depth), :] = weight_ref[...]
+        rows = weight_refs[2].shape[0]
+        pieces = depth // rows
+        for i, weight_ref in enumerate(weight_refs[2:]):
+            at = lax.bitwise_xor(place_ref[0], 2 + i // pieces) * depth + i % pieces * rows
+            weights[pl.ds(pl.multiple_of(at, rows), rows), :] = weight_ref[...]
     else:
         weights[...] = weight_refs[0][...]
     mean, square, count = merged(rows_of(stat_refs))
@@ -349,7 +357,7 @@
     if direct:
         two, zero, one = (swap(part, "fsdp", 2) for part in cut(place, w_in, wide))
         across = swap(w_in, "fsdp", 1)
-        normed, inner, outer = normalize_rows(place, rows, gain)
+        normed, inner, outer, *pieces = normalize_rows(place, rows, gain, w_out, 3)
         inner = swap(inner, "ctx", 1)
         pairs = [(i, i + 1) for i in range(1, ends, 2)]
         outer = lax.ppermute(outer, "ctx", pairs + [(j, i) for i, j in pairs])
@@ -364,11 +372,15 @@
         beyond_one = swap(one, "fsdp", 1)
         zero.append(swap(zero[1], "fsdp", 1))
         conv_two, stat_two = front(2, [partials[2], *two])
-        conv_two, partials[0] = tie(conv_two, partials[0])
+        pieces = [swap(piece, "fsdp", 2) for piece in pieces]
+        conv_two, partials[0], pieces[0] = tie(conv_two, partials[0], pieces[0])
+        beyond = [swap(pieces[0], "fsdp", 1)]
         conv_zero, stat_zero = front(0, [partials[0], *zero])
         conv_zero, partials[1] = tie(conv_zero, partials[1])
         conv_one, stats = front(1, [partials[1], one, beyond_one], (stat_two, stat_zero), 1)
-        remote_out, across_out = swap(w_out, "fsdp", 2), swap(w_out, "fsdp", 1)
+        across_out = swap(w_out, "fsdp", 1)
+        stats, pieces[1], beyond[0] = tie(stats, pieces[1], beyond[0])
+        beyond.append(swap(pieces[1], "fsdp", 1))
         convs = [conv_zero, conv_one, conv_two]
 
         def others(flips):
@@ -386,10 +398,11 @@
 
         stats = union([stats] + others([(1, 0)]))
         stats = union([stats] + others([(0, 2)]))
+        stats, pieces[2], beyond[1] = tie(stats, pieces[2], beyond[1])
+        beyond.append(swap(pieces[2], "fsdp", 1))
         stats = union([stats] + others([(0, 4)]))
         stats = [stats] + others([(0, 1), (2, 0), (2, 1)])
-        stats[1], remote_out = tie(stats[1], remote_out)
-        out_weights = [w_out, across_out, remote_out, swap(remote_out, "fsdp", 1)]
+        out_weights = [w_out, across_out, *pieces, *beyond]
     else:
         full_in = lax.all_gather(w_in, "fsdp", axis=0, tiled=True)
         out_weights = [lax.all_gather(w_out, "fsdp", axis=0, tiled=True)]
@@ -397,7 +410,7 @@
         after = lax.ppermute(rows[:HALO], "ctx", up)
         inner = jnp.where(parity == 0, after, before)
         outer = jnp.where(parity == 0, before, after)
-        normed, _, _ = normalize_rows(place, rows, gain)
+        normed, _, _ = normalize_rows(place, rows, gain, w_out, 0)
         (normed,) = near_product(place, normed, inner, outer, gain)
         near_by = 2 if ctx_count % 2 == 0 else 1
         groups = [

time: 65 us -> 68.5 us (1.054)
  starting transfers between devices: 22.4 us -> 28 us
  waiting for transfers between devices: 21.7 us -> 19.6 us
    ppermute x15 -> x19, starting transfers between devices: 12.7 us -> 18 us  [swap(): lax.ppermute(value, axis, [(i, i ^ bit) for i in range(lax.axis_size(axis...]
    ppermute x6, waiting for transfers between devices: 10.3 us -> 6.71 us  [others(): lax.ppermute(stats, both, [(member(f, p), member(f ^ df, p ^ dp)) for f i...]
    ppermute x15 -> x19, waiting for transfers between devices: 11.4 us -> 12.9 us  [swap(): lax.ppermute(value, axis, [(i, i ^ bit) for i in range(lax.axis_size(axis...]
  transfers between devices with their start and end apart: 22 -> 26, of which waited for: 10 -> 11; matrix products, arithmetic and copies ran while one was open for 0% -> 0% of each run, Pallas kernels for 17% -> 21%
where the time goes in v8:
time: 68.5 us; the launch traced here: 68.3 us
  starting transfers between devices  28 us (41%)
  waiting for transfers between devices  19.6 us (29%)
  Pallas kernels  17 us (25%)
  local copies, waits for them, and re-layouts  2.72 us (4%)
  between operations  0.85 us (1%)
    ppermute x19, starting transfers between devices, swap(): lax.ppermute(value, axis, [(i, i ^ bit) for i in range(lax.axis_size(axis...  18 us
    ppermute x19, waiting for transfers between devices, swap(): lax.ppermute(value, axis, [(i, i ^ bit) for i in range(lax.axis_size(axis...  12.9 us
    ppermute x6, starting transfers between devices, others(): lax.ppermute(stats, both, [(member(f, p), member(f ^ df, p ^ dp)) for f i...  9.34 us
    pallas_call x3, Pallas kernels, front_block(): pl.pallas_call(functools.partial(front_kernel, block, len(earlier)), out_...  8.63 us
    ppermute x6, waiting for transfers between devices, others(): lax.ppermute(stats, both, [(member(f, p), member(f ^ df, p ^ dp)) for f i...  6.71 us
    pallas_call x1, Pallas kernels, back(): pl.pallas_call(functools.partial(back_kernel, len(stats)), out_shape=jax....  2.95 us
    unnamed x16, local copies, waits for them, and re-layouts  2.71 us
    pallas_call x1, Pallas kernels, normalize_rows(): pl.pallas_call(norm_kernel, out_shape=[jax.ShapeDtypeStruct(shape, jnp.bf...  2.49 us
  transfers between devices with their start and end apart: 26, of which 11 were waited for; matrix products, arithmetic and copies ran while one was open for 0% of the time, Pallas kernels for 21%

profile of v8, /device:TPU:0, one launch (start us, length us, event | category | flops | bytes accessed | tf_op | source)
XLA Modules:
  0.0 68.3 jit_solution(2282958101543317117)
XLA Ops:
  1.2 1.3 %copy-done = bf16[384,1536]{1,0:T(8,128)(2,1)S(1)} copy-done((bf16[384,1536]{1,0:T(8,128)(2,1)S(1)}, bf16[384,1536]{1,0:T(8,128)(2,1)}, u32[]{:S(2)}) %copy-start) | copy-done | bytes 1179672
  3.1 2.6 %collective-permute-start.2 = (bf16[384,256]{1,0:T(8,128)(2,1)S(1)}, bf16[384,256]{1,0:T(8,128)(2,1)S(1)}, u32[]{:S(2)}, u32[]{:S(2)}) collective-permute-start(bf16[384,256]{1,0:T(8,128)(2,1)S(1)} %get-tuple-element.51), channel_id=1, source_target_pairs={{0,16},{8,24},{16,0},{24,8},{1,17},{9,25},{17,1},{25,9},{2,18},{10... | collective-permute-start | bytes 589832 | tf_op jit(solution)/shard_map/ppermute | solution.py:26
  5.7 1.9 %collective-permute-start.8 = (bf16[384,512]{1,0:T(8,128)(2,1)S(1)}, bf16[384,512]{1,0:T(8,128)(2,1)S(1)}, u32[]{:S(2)}, u32[]{:S(2)}) collective-permute-start(bf16[384,512]{1,0:T(8,128)(2,1)S(1)} %get-tuple-element.61), channel_id=1, source_target_pairs={{0,16},{8,24},{16,0},{24,8},{1,17},{9,25},{17,1},{25,9},{2,18},{10... | collective-permute-start | bytes 1179656 | tf_op jit(solution)/shard_map/ppermute | solution.py:26
  7.7 1.4 %copy-done.3 = bf16[1,512,1536]{2,1,0:T(8,128)(2,1)S(1)} copy-done((bf16[1,512,1536]{2,1,0:T(8,128)(2,1)S(1)}, bf16[1,512,1536]{2,1,0:T(8,128)(2,1)}, u32[]{:S(2)}) %copy-start.3) | copy-done | bytes 1572888
  9.1 2.5 %layer_norm.1 = (bf16[512,1536]{1,0:T(8,128)(2,1)S(1)}, bf16[16,1536]{1,0:T(8,128)(2,1)S(1)}, bf16[16,1536]{1,0:T(8,128)(2,1)S(1)}, bf16[64,1536]{1,0:T(8,128)(2...) custom-call(s32[4]{0:T(128)S(1)} %pad_add_fusion.place_ref, bf16[512,1536]{1,0:T(8,128)(2,1)S(1)} %bitcast.5, ...), custom_call_target="tpu_custom_call" | custom-call | flops 100000000 | tf_op jit(solution)/shard_map/layer_norm/pallas_call | solution.py:83
  11.6 1.6 %collective-permute-start = (bf16[16,1536]{1,0:T(8,128)(2,1)S(1)}, bf16[16,1536]{1,0:T(8,128)(2,1)S(1)}, u32[]{:S(2)}, u32[]{:S(2)}) collective-permute-start(bf16[16,1536]{1,0:T(8,128)(2,1)S(1)} %get-tuple-element.49), channel_id=1, source_target_pairs={{0,1},{1,0},{2,3},{3,2},{4,5},{5,4},{6,7},{7,6},{8,9},{9,8},{10,11... | collective-permute-start | bytes 147464 | tf_op jit(solution)/shard_map/ppermute | solution.py:26
  13.2 2.6 %collective-permute-done.inner_ref = bf16[16,1536]{1,0:T(8,128)(2,1)S(1)} collective-permute-done((bf16[16,1536]{1,0:T(8,128)(2,1)S(1)}, bf16[16,1536]{1,0:T(8,128)(2,1)S(1)}, u32[]{:S(2)}, u32[]{:S(2)}) %collective-permute-start) | collective-permute-done | bytes 49184 | tf_op jit(solution)/shard_map/ppermute | solution.py:26
  16.5 7.8 %collective-permute-start.5 = (bf16[384,256]{1,0:T(8,128)(2,1)S(1)}, bf16[384,256]{1,0:T(8,128)(2,1)S(1)}, u32[]{:S(2)}, u32[]{:S(2)}) collective-permute-start(bf16[384,256]{1,0:T(8,128)(2,1)S(1)} %collective-permute-done.2.refs_1_), channel_id=1, source_target_pairs={{0,1},{1,0},{2,3},{3,2},{4,5},{5,4},{6,7},{7,6},{8,9},{9,8},{10,11... | collective-permute-start | bytes 589832 | tf_op jit(solution)/shard_map/ppermute | solution.py:26
  24.8 2.3 %near.1 = (bf16[544,1536]{1,0:T(8,128)(2,1)S(1)}, f32[544,512]{1,0:T(8,128)S(1)}, f32[544,512]{1,0:T(8,128)S(1)}, f32[544,512]{1,0:T(8,128)S(1)}) custom-call(s32[4]{0:T(128)S(1)} %pad_add_fusion.place_ref, bf16[512,1536]{1,0:T(8,128)(2,1)S(1)} %get-tuple-element.53.rows_ref, bf16[16,1536]{1,0:T(8,128)(2,1)S(1)} %collective-permute-done.inner_ref, ...), custom_call_target="tpu_custom_call" | custom-call | flops 100000000 | tf_op jit(solution)/shard_map/near/pallas_call | solution.py:131
  27.2 2.2 %collective-permute-done.5.refs_2_ = bf16[384,256]{1,0:T(8,128)(2,1)S(1)} collective-permute-done((bf16[384,256]{1,0:T(8,128)(2,1)S(1)}, bf16[384,256]{1,0:T(8,128)(2,1)S(1)}, u32[]{:S(2)}, u32[]{:S(2)}) %collective-permute-start.5) | collective-permute-done | bytes 196640 | tf_op jit(solution)/shard_map/ppermute | solution.py:26
  30.0 2.1 %collective-permute-done.9.refs_2_ = bf16[384,256]{1,0:T(8,128)(2,1)S(1)} collective-permute-done((bf16[384,256]{1,0:T(8,128)(2,1)S(1)}, bf16[384,256]{1,0:T(8,128)(2,1)S(1)}, u32[]{:S(2)}, u32[]{:S(2)}) %collective-permute-start.9) | collective-permute-done | bytes 196640 | tf_op jit(solution)/shard_map/ppermute | solution.py:26
  33.1 2.9 %front.3 = (f32[512,256]{1,0:T(8,128)S(1)}, f32[3,256]{1,0:T(4,128)S(1)}) custom-call(s32[4]{0:T(128)S(1)} %pad_add_fusion.place_ref, bf16[544,1536]{1,0:T(8,128)(2,1)S(1)} %get-tuple-element.56.normed_ref, f32[544,512]{1,0:T(8,128)S(1)} %get-tuple-element.62.refs_0_, bf16[384,256]{1,0:T(8,128)(2,1)S(1)} %collective-permute-done.2.refs_1_, ...), custom_call_target="tpu_custom_call" | custom-call | flops 100000000 | tf_op jit(solution)/shard_map/front/pallas_call | solution.py:216
  36.0 1.1 %collective-permute-done.11.refs_9_ = bf16[64,1536]{1,0:T(8,128)(2,1)S(1)} collective-permute-done((bf16[64,1536]{1,0:T(8,128)(2,1)S(1)}, bf16[64,1536]{1,0:T(8,128)(2,1)S(1)}, u32[]{:S(2)}, u32[]{:S(2)}) %collective-permute-start.11) | collective-permute-done | bytes 196640 | tf_op jit(solution)/shard_map/ppermute | solution.py:26
  37.1 2.9 %front.4 = (f32[512,256]{1,0:T(8,128)S(1)}, f32[3,256]{1,0:T(4,128)S(1)}) custom-call(s32[4]{0:T(128)S(1)} %pad_add_fusion.place_ref, bf16[544,1536]{1,0:T(8,128)(2,1)S(1)} %get-tuple-element.56.normed_ref, f32[544,512]{1,0:T(8,128)S(1)} %get-tuple-element.69.refs_0_, bf16[384,256]{1,0:T(8,128)(2,1)S(1)} %collective-permute-done.3.refs_1_, ...), custom_call_target="tpu_custom_call" | custom-call | flops 4000000000 | tf_op jit(solution)/shard_map/front/pallas_call | solution.py:216
  40.0 2.9 %front.5 = (f32[512,256]{1,0:T(8,128)S(1)}, f32[1,3,768]{2,1,0:T(4,128)S(1)}) custom-call(s32[4]{0:T(128)S(1)} %pad_add_fusion.place_ref, bf16[544,1536]{1,0:T(8,128)(2,1)S(1)} %get-tuple-element.56.normed_ref, f32[3,256]{1,0:T(4,128)S(1)} %get-tuple-element.65.refs_0_, f32[3,256]{1,0:T(4,128)S(1)} %get-tuple-element.72.refs_1_, ...), custom_call_target="tpu_custom_call" | custom-call | flops 100000000 | tf_op jit(solution)/shard_map/front/pallas_call | solution.py:216
  44.4 1.8 %collective-permute-start.17 = (f32[1,3,768]{2,1,0:T(4,128)S(1)}, f32[1,3,768]{2,1,0:T(4,128)S(1)}, u32[]{:S(2)}, u32[]{:S(2)}) collective-permute-start(f32[1,3,768]{2,1,0:T(4,128)S(1)} %pad_maximum_fusion), channel_id=1, source_target_pairs={{0,2},{1,3},{2,0},{3,1},{4,6},{5,7},{6,4},{7,5},{8,10},{9,11},{10,... | collective-permute-start | bytes 27656 | tf_op jit(solution)/shard_map/ppermute | solution.py:388
  48.2 4.8 %collective-permute-done.18.refs_11_ = bf16[64,1536]{1,0:T(8,128)(2,1)S(1)} collective-permute-done((bf16[64,1536]{1,0:T(8,128)(2,1)S(1)}, bf16[64,1536]{1,0:T(8,128)(2,1)S(1)}, u32[]{:S(2)}, u32[]{:S(2)}) %collective-permute-start.18) | collective-permute-done | bytes 196640 | tf_op jit(solution)/shard_map/ppermute | solution.py:26
  53.0 3.4 %collective-permute-start.20 = (f32[1,3,768]{2,1,0:T(4,128)S(1)}, f32[1,3,768]{2,1,0:T(4,128)S(1)}, u32[]{:S(2)}, u32[]{:S(2)}) collective-permute-start(f32[1,3,768]{2,1,0:T(4,128)S(1)} %pad_maximum_fusion.1), channel_id=1, source_target_pairs={{0,4},{1,5},{2,6},{3,7},{4,0},{5,1},{6,2},{7,3},{8,12},{9,13},{10,... | collective-permute-start | bytes 27656 | tf_op jit(solution)/shard_map/ppermute | solution.py:388
  56.5 1.7 %collective-permute-done.20 = f32[1,3,768]{2,1,0:T(4,128)S(1)} collective-permute-done((f32[1,3,768]{2,1,0:T(4,128)S(1)}, f32[1,3,768]{2,1,0:T(4,128)S(1)}, u32[]{:S(2)}, u32[]{:S(2)}) %collective-permute-start.20) | collective-permute-done | bytes 9248 | tf_op jit(solution)/shard_map/ppermute | solution.py:388
  58.2 2.0 %collective-permute-start.21 = (f32[1,3,768]{2,1,0:T(4,128)S(1)}, f32[1,3,768]{2,1,0:T(4,128)S(1)}, u32[]{:S(2)}, u32[]{:S(2)}) collective-permute-start(f32[1,3,768]{2,1,0:T(4,128)S(1)} %pad_maximum_fusion.2.refs_0_), channel_id=1, source_target_pairs={{0,1},{1,0},{2,3},{3,2},{4,5},{5,4},{6,7},{7,6},{8,9},{9,8},{10,11... | collective-permute-start | bytes 27656 | tf_op jit(solution)/shard_map/ppermute | solution.py:388
  60.8 1.0 %collective-permute-start.23 = (f32[1,3,768]{2,1,0:T(4,128)S(1)}, f32[1,3,768]{2,1,0:T(4,128)S(1)}, u32[]{:S(2)}, u32[]{:S(2)}) collective-permute-start(f32[1,3,768]{2,1,0:T(4,128)S(1)} %pad_maximum_fusion.2.refs_0_), channel_id=1, source_target_pairs={{0,17},{1,16},{2,19},{3,18},{4,21},{5,20},{6,23},{7,22},{8,25},{9,... | collective-permute-start | bytes 27656 | tf_op jit(solution)/shard_map/ppermute | solution.py:388
  62.0 1.9 %collective-permute-done.22.refs_2_ = f32[1,3,768]{2,1,0:T(4,128)S(1)} collective-permute-done((f32[1,3,768]{2,1,0:T(4,128)S(1)}, f32[1,3,768]{2,1,0:T(4,128)S(1)}, u32[]{:S(2)}, u32[]{:S(2)}) %collective-permute-start.22) | collective-permute-done | bytes 9248 | tf_op jit(solution)/shard_map/ppermute | solution.py:388
  63.9 1.4 %collective-permute-done.23.refs_3_ = f32[1,3,768]{2,1,0:T(4,128)S(1)} collective-permute-done((f32[1,3,768]{2,1,0:T(4,128)S(1)}, f32[1,3,768]{2,1,0:T(4,128)S(1)}, u32[]{:S(2)}, u32[]{:S(2)}) %collective-permute-start.23) | collective-permute-done | bytes 9248 | tf_op jit(solution)/shard_map/ppermute | solution.py:388
  65.4 2.9 %back.1 = bf16[512,1536]{1,0:T(8,128)(2,1)} custom-call(s32[4]{0:T(128)S(1)} %pad_add_fusion.place_ref, f32[1,768]{1,0:T(1,128)S(1)} %broadcast_in_dim.12.gain_ref, f32[1,768]{1,0:T(1,128)S(1)} %broadcast_in_dim.13.shift_ref, f32[1,3,768]{2,1,0:T(4,128)S(1)} %pad_maximum_fusion.2.refs_0_, f32[1,3,768]{2,1,0:T(4,128)S(1)} %collective-permute-done.21.refs_1_, ...), custom_call_target="tpu_custom_call" | custom-call | flops 1000000000 | tf_op jit(solution)/shard_map/back/pallas_call | solution.py:313
  (61 shorter events, 8.5 us)
Async XLA Ops:
  0.0 24.7 %collective-permute-start.4 = (bf16[384,1536]{1,0:T(8,128)(2,1)}, bf16[384,1536]{1,0:T(8,128)(2,1)S(1)}, u32[]{:S(2)}, u32[]{:S(2)}) collective-permute-start(bf16[384,1536]{1,0:T(8,128)(2,1)} %refs_0_.1), channel_id=1, source_target_pairs={{0,8},{8,0},{16,24},{24,16},{1,9},{9,1},{17,25},{25,17},{2,10},{10... | collective-permute-start | bytes 3538952 | tf_op jit(solution)/shard_map/ppermute | solution.py:26
  3.1 13.4 %collective-permute-start.2 = (bf16[384,256]{1,0:T(8,128)(2,1)S(1)}, bf16[384,256]{1,0:T(8,128)(2,1)S(1)}, u32[]{:S(2)}, u32[]{:S(2)}) collective-permute-start(bf16[384,256]{1,0:T(8,128)(2,1)S(1)} %get-tuple-element.51), channel_id=1, source_target_pairs={{0,16},{8,24},{16,0},{24,8},{1,17},{9,25},{17,1},{25,9},{2,18},{10... | collective-permute-start | bytes 589832 | tf_op jit(solution)/shard_map/ppermute | solution.py:26
  5.6 10.8 %collective-permute-start.3 = (bf16[384,256]{1,0:T(8,128)(2,1)S(1)}, bf16[384,256]{1,0:T(8,128)(2,1)S(1)}, u32[]{:S(2)}, u32[]{:S(2)}) collective-permute-start(bf16[384,256]{1,0:T(8,128)(2,1)S(1)} %get-tuple-element.52), channel_id=1, source_target_pairs={{0,16},{8,24},{16,0},{24,8},{1,17},{9,25},{17,1},{25,9},{2,18},{10... | collective-permute-start | bytes 589832 | tf_op jit(solution)/shard_map/ppermute | solution.py:26
  5.7 26.4 %collective-permute-start.8 = (bf16[384,512]{1,0:T(8,128)(2,1)S(1)}, bf16[384,512]{1,0:T(8,128)(2,1)S(1)}, u32[]{:S(2)}, u32[]{:S(2)}) collective-permute-start(bf16[384,512]{1,0:T(8,128)(2,1)S(1)} %get-tuple-element.61), channel_id=1, source_target_pairs={{0,16},{8,24},{16,0},{24,8},{1,17},{9,25},{17,1},{25,9},{2,18},{10... | collective-permute-start | bytes 1179656 | tf_op jit(solution)/shard_map/ppermute | solution.py:26
  11.6 4.2 %collective-permute-start = (bf16[16,1536]{1,0:T(8,128)(2,1)S(1)}, bf16[16,1536]{1,0:T(8,128)(2,1)S(1)}, u32[]{:S(2)}, u32[]{:S(2)}) collective-permute-start(bf16[16,1536]{1,0:T(8,128)(2,1)S(1)} %get-tuple-element.49), channel_id=1, source_target_pairs={{0,1},{1,0},{2,3},{3,2},{4,5},{5,4},{6,7},{7,6},{8,9},{9,8},{10,11... | collective-permute-start | bytes 147464 | tf_op jit(solution)/shard_map/ppermute | solution.py:26
  16.5 12.9 %collective-permute-start.5 = (bf16[384,256]{1,0:T(8,128)(2,1)S(1)}, bf16[384,256]{1,0:T(8,128)(2,1)S(1)}, u32[]{:S(2)}, u32[]{:S(2)}) collective-permute-start(bf16[384,256]{1,0:T(8,128)(2,1)S(1)} %collective-permute-done.2.refs_1_), channel_id=1, source_target_pairs={{0,1},{1,0},{2,3},{3,2},{4,5},{5,4},{6,7},{7,6},{8,9},{9,8},{10,11... | collective-permute-start | bytes 589832 | tf_op jit(solution)/shard_map/ppermute | solution.py:26
  24.2 5.1 %collective-permute-start.6 = (bf16[384,256]{1,0:T(8,128)(2,1)S(1)}, bf16[384,256]{1,0:T(8,128)(2,1)S(1)}, u32[]{:S(2)}, u32[]{:S(2)}) collective-permute-start(bf16[384,256]{1,0:T(8,128)(2,1)S(1)} %collective-permute-done.2.refs_1_), channel_id=1, source_target_pairs={{0,8},{8,0},{16,24},{24,16},{1,9},{9,1},{17,25},{25,17},{2,10},{10... | collective-permute-start | bytes 589832 | tf_op jit(solution)/shard_map/ppermute | solution.py:26
  24.2 5.1 %collective-permute-start.7 = (bf16[384,256]{1,0:T(8,128)(2,1)S(1)}, bf16[384,256]{1,0:T(8,128)(2,1)S(1)}, u32[]{:S(2)}, u32[]{:S(2)}) collective-permute-start(bf16[384,256]{1,0:T(8,128)(2,1)S(1)} %collective-permute-done.3.refs_1_), channel_id=1, source_target_pairs={{0,8},{8,0},{16,24},{24,16},{1,9},{9,1},{17,25},{25,17},{2,10},{10... | collective-permute-start | bytes 589832 | tf_op jit(solution)/shard_map/ppermute | solution.py:26
  24.7 7.3 %collective-permute-start.9 = (bf16[384,256]{1,0:T(8,128)(2,1)S(1)}, bf16[384,256]{1,0:T(8,128)(2,1)S(1)}, u32[]{:S(2)}, u32[]{:S(2)}) collective-permute-start(bf16[384,256]{1,0:T(8,128)(2,1)S(1)} %collective-permute-done.3.refs_1_), channel_id=1, source_target_pairs={{0,1},{1,0},{2,3},{3,2},{4,5},{5,4},{6,7},{7,6},{8,9},{9,8},{10,11... | collective-permute-start | bytes 589832 | tf_op jit(solution)/shard_map/ppermute | solution.py:26
  29.4 3.8 %collective-permute-start.10 = (bf16[384,256]{1,0:T(8,128)(2,1)S(1)}, bf16[384,256]{1,0:T(8,128)(2,1)S(1)}, u32[]{:S(2)}, u32[]{:S(2)}) collective-permute-start(bf16[384,256]{1,0:T(8,128)(2,1)S(1)} %collective-permute-done.5.refs_2_), channel_id=1, source_target_pairs={{0,8},{8,0},{16,24},{24,16},{1,9},{9,1},{17,25},{25,17},{2,10},{10... | collective-permute-start | bytes 589832 | tf_op jit(solution)/shard_map/ppermute | solution.py:26
  29.4 7.8 %collective-permute-start.11 = (bf16[64,1536]{1,0:T(8,128)(2,1)S(1)}, bf16[64,1536]{1,0:T(8,128)(2,1)S(1)}, u32[]{:S(2)}, u32[]{:S(2)}) collective-permute-start(bf16[64,1536]{1,0:T(8,128)(2,1)S(1)} %get-tuple-element.68), channel_id=1, source_target_pairs={{0,16},{8,24},{16,0},{24,8},{1,17},{9,25},{17,1},{25,9},{2,18},{10... | collective-permute-start | bytes 589832 | tf_op jit(solution)/shard_map/ppermute | solution.py:26
  32.1 5.1 %collective-permute-start.12 = (bf16[384,256]{1,0:T(8,128)(2,1)S(1)}, bf16[384,256]{1,0:T(8,128)(2,1)S(1)}, u32[]{:S(2)}, u32[]{:S(2)}) collective-permute-start(bf16[384,256]{1,0:T(8,128)(2,1)S(1)} %collective-permute-done.9.refs_2_), channel_id=1, source_target_pairs={{0,8},{8,0},{16,24},{24,16},{1,9},{9,1},{17,25},{25,17},{2,10},{10... | collective-permute-start | bytes 589832 | tf_op jit(solution)/shard_map/ppermute | solution.py:26
  32.1 7.9 %collective-permute-start.13 = (bf16[384,512]{1,0:T(8,128)(2,1)S(1)}, bf16[384,512]{1,0:T(8,128)(2,1)S(1)}, u32[]{:S(2)}, u32[]{:S(2)}) collective-permute-start(bf16[384,512]{1,0:T(8,128)(2,1)S(1)} %collective-permute-done.8.refs_3_), channel_id=1, source_target_pairs={{0,8},{8,0},{16,24},{24,16},{1,9},{9,1},{17,25},{25,17},{2,10},{10... | collective-permute-start | bytes 1179656 | tf_op jit(solution)/shard_map/ppermute | solution.py:26
  32.6 10.3 %collective-permute-start.14 = (bf16[64,1536]{1,0:T(8,128)(2,1)S(1)}, bf16[64,1536]{1,0:T(8,128)(2,1)S(1)}, u32[]{:S(2)}, u32[]{:S(2)}) collective-permute-start(bf16[64,1536]{1,0:T(8,128)(2,1)S(1)} %get-tuple-element.78), channel_id=1, source_target_pairs={{0,16},{8,24},{16,0},{24,8},{1,17},{9,25},{17,1},{25,9},{2,18},{10... | collective-permute-start | bytes 589832 | tf_op jit(solution)/shard_map/ppermute | solution.py:26
  37.1 5.8 %collective-permute-start.15 = (bf16[64,1536]{1,0:T(8,128)(2,1)S(1)}, bf16[64,1536]{1,0:T(8,128)(2,1)S(1)}, u32[]{:S(2)}, u32[]{:S(2)}) collective-permute-start(bf16[64,1536]{1,0:T(8,128)(2,1)S(1)} %collective-permute-done.11.refs_9_), channel_id=1, source_target_pairs={{0,8},{8,0},{16,24},{24,16},{1,9},{9,1},{17,25},{25,17},{2,10},{10... | collective-permute-start | bytes 589832 | tf_op jit(solution)/shard_map/ppermute | solution.py:26
  44.4 3.8 %collective-permute-start.17 = (f32[1,3,768]{2,1,0:T(4,128)S(1)}, f32[1,3,768]{2,1,0:T(4,128)S(1)}, u32[]{:S(2)}, u32[]{:S(2)}) collective-permute-start(f32[1,3,768]{2,1,0:T(4,128)S(1)} %pad_maximum_fusion), channel_id=1, source_target_pairs={{0,2},{1,3},{2,0},{3,1},{4,6},{5,7},{6,4},{7,5},{8,10},{9,11},{10,... | collective-permute-start | bytes 27656 | tf_op jit(solution)/shard_map/ppermute | solution.py:388
  46.2 6.9 %collective-permute-start.18 = (bf16[64,1536]{1,0:T(8,128)(2,1)S(1)}, bf16[64,1536]{1,0:T(8,128)(2,1)S(1)}, u32[]{:S(2)}, u32[]{:S(2)}) collective-permute-start(bf16[64,1536]{1,0:T(8,128)(2,1)S(1)} %get-tuple-element.81), channel_id=1, source_target_pairs={{0,16},{8,24},{16,0},{24,8},{1,17},{9,25},{17,1},{25,9},{2,18},{10... | collective-permute-start | bytes 589832 | tf_op jit(solution)/shard_map/ppermute | solution.py:26
  47.0 14.8 %collective-permute-start.24 = (bf16[192,1536]{1,0:T(8,128)(2,1)S(1)}, bf16[192,1536]{1,0:T(8,128)(2,1)S(1)}, u32[]{:S(2)}, u32[]{:S(2)}) collective-permute-start(bf16[192,1536]{1,0:T(8,128)(2,1)S(1)} %copy-done.2), channel_id=1, source_target_pairs={{0,8},{8,0},{16,24},{24,16},{1,9},{9,1},{17,25},{25,17},{2,10},{10... | collective-permute-start | bytes 1769480 | tf_op jit(solution)/shard_map/ppermute | solution.py:26
  47.0 6.0 %collective-permute-start.19 = (bf16[64,1536]{1,0:T(8,128)(2,1)S(1)}, bf16[64,1536]{1,0:T(8,128)(2,1)S(1)}, u32[]{:S(2)}, u32[]{:S(2)}) collective-permute-start(bf16[64,1536]{1,0:T(8,128)(2,1)S(1)} %collective-permute-done.14.refs_10_), channel_id=1, source_target_pairs={{0,8},{8,0},{16,24},{24,16},{1,9},{9,1},{17,25},{25,17},{2,10},{10... | collective-permute-start | bytes 589832 | tf_op jit(solution)/shard_map/ppermute | solution.py:26
  53.0 5.1 %collective-permute-start.20 = (f32[1,3,768]{2,1,0:T(4,128)S(1)}, f32[1,3,768]{2,1,0:T(4,128)S(1)}, u32[]{:S(2)}, u32[]{:S(2)}) collective-permute-start(f32[1,3,768]{2,1,0:T(4,128)S(1)} %pad_maximum_fusion.1), channel_id=1, source_target_pairs={{0,4},{1,5},{2,6},{3,7},{4,0},{5,1},{6,2},{7,3},{8,12},{9,13},{10,... | collective-permute-start | bytes 27656 | tf_op jit(solution)/shard_map/ppermute | solution.py:388
  56.5 8.9 %collective-permute-start.25 = (bf16[64,1536]{1,0:T(8,128)(2,1)S(1)}, bf16[64,1536]{1,0:T(8,128)(2,1)S(1)}, u32[]{:S(2)}, u32[]{:S(2)}) collective-permute-start(bf16[64,1536]{1,0:T(8,128)(2,1)S(1)} %collective-permute-done.18.refs_11_), channel_id=1, source_target_pairs={{0,8},{8,0},{16,24},{24,16},{1,9},{9,1},{17,25},{25,17},{2,10},{10... | collective-permute-start | bytes 589832 | tf_op jit(solution)/shard_map/ppermute | solution.py:26
  58.2 3.8 %collective-permute-start.21 = (f32[1,3,768]{2,1,0:T(4,128)S(1)}, f32[1,3,768]{2,1,0:T(4,128)S(1)}, u32[]{:S(2)}, u32[]{:S(2)}) collective-permute-start(f32[1,3,768]{2,1,0:T(4,128)S(1)} %pad_maximum_fusion.2.refs_0_), channel_id=1, source_target_pairs={{0,1},{1,0},{2,3},{3,2},{4,5},{5,4},{6,7},{7,6},{8,9},{9,8},{10,11... | collective-permute-start | bytes 27656 | tf_op jit(solution)/shard_map/ppermute | solution.py:388
  60.2 3.7 %collective-permute-start.22 = (f32[1,3,768]{2,1,0:T(4,128)S(1)}, f32[1,3,768]{2,1,0:T(4,128)S(1)}, u32[]{:S(2)}, u32[]{:S(2)}) collective-permute-start(f32[1,3,768]{2,1,0:T(4,128)S(1)} %pad_maximum_fusion.2.refs_0_), channel_id=1, source_target_pairs={{0,16},{1,17},{2,18},{3,19},{4,20},{5,21},{6,22},{7,23},{8,24},{9,... | collective-permute-start | bytes 27656 | tf_op jit(solution)/shard_map/ppermute | solution.py:388
  60.8 4.6 %collective-permute-start.23 = (f32[1,3,768]{2,1,0:T(4,128)S(1)}, f32[1,3,768]{2,1,0:T(4,128)S(1)}, u32[]{:S(2)}, u32[]{:S(2)}) collective-permute-start(f32[1,3,768]{2,1,0:T(4,128)S(1)} %pad_maximum_fusion.2.refs_0_), channel_id=1, source_target_pairs={{0,17},{1,16},{2,19},{3,18},{4,21},{5,20},{6,23},{7,22},{8,25},{9,... | collective-permute-start | bytes 27656 | tf_op jit(solution)/shard_map/ppermute | solution.py:388
  (10 other events, 99.6 us)

commit v9 on v8

--- a/solution.py
+++ b/solution.py
@@ -59,36 +59,52 @@
     return (deviate * lax.rsqrt(spread + 1e-05) * gain).astype(jnp.bfloat16)
 
 
-def norm_kernel(place_ref, rows_ref, gain_ref, shard_ref, out_ref, inner_ref, outer_ref, *piece_refs):
+def edge_kernel(place_ref, rows_ref, inner_ref, outer_ref):
+    odd = place_ref[3]
+    last = rows_ref.shape[0] - HALO
+    inner_ref[...] = rows_ref[pl.ds(pl.multiple_of((1 - odd) * last, HALO), HALO), :]
+    outer_ref[...] = rows_ref[pl.ds(pl.multiple_of(odd * last, HALO), HALO), :]
+
+
+def edge_rows(place, rows):
+    shape = jax.ShapeDtypeStruct((HALO, rows.shape[1]), rows.dtype)
+    return pl.pallas_call(
+        edge_kernel,
+        out_shape=[shape, shape],
+        in_specs=[pl.BlockSpec(memory_space=pltpu.SMEM), pl.BlockSpec(memory_space=VMEM)],
+        out_specs=[pl.BlockSpec(memory_space=VMEM)] * 2,
+        compiler_params=params(2),
+        cost_estimate=cost(10**8),
+        name="edges",
+    )(place, rows)
+
+
+def norm_kernel(rows_ref, gain_ref, shard_ref, out_ref, *piece_refs):
     step = 64
-    row_count = rows_ref.shape[0]
-
-    @pl.loop(0, row_count // step)
+
+    @pl.loop(0, rows_ref.shape[0] // step)
     def _(i):
         here = pl.ds(pl.multiple_of(i * step, step), step)
         out_ref[here, :] = normalize(rows_ref[here, :], gain_ref[...])
 
-    odd = place_ref[3]
-    last = row_count - HALO
-    inner_ref[...] = rows_ref[pl.ds(pl.multiple_of((1 - odd) * last, HALO), HALO), :]
-    outer_ref[...] = rows_ref[pl.ds(pl.multiple_of(odd * last, HALO), HALO), :]
-    for i, ref in enumerate(piece_refs):
-        ref[...] = shard_ref[i * ref.shape[0] : (i + 1) * ref.shape[0], :]
-
-
-def normalize_rows(place, rows, gain, shard, pieces):
+    at = 0
+    for ref in piece_refs:
+        ref[...] = shard_ref[at : at + ref.shape[0], :]
+        at += ref.shape[0]
+
+
+def normalize_rows(rows, gain, shard, pieces):
     row_count, width = rows.shape
-    shapes = [(row_count, width), (HALO, width), (HALO, width)]
-    shapes += [(shard.shape[0] // max(pieces, 1), width)] * pieces
+    shapes = [(row_count, width)] + [(piece, width) for piece in pieces]
     return pl.pallas_call(
         norm_kernel,
         out_shape=[jax.ShapeDtypeStruct(shape, jnp.bfloat16) for shape in shapes],
-        in_specs=[pl.BlockSpec(memory_space=pltpu.SMEM)] + [pl.BlockSpec(memory_space=VMEM)] * 3,
+        in_specs=[pl.BlockSpec(memory_space=VMEM)] * 3,
         out_specs=[pl.BlockSpec(memory_space=VMEM)] * len(shapes),
         compiler_params=params(4),
         cost_estimate=cost(10**8),
         name="layer_norm",
-    )(place, rows, gain, shard)
+    )(rows, gain, shard)
 
 
 def near_kernel(place_ref, rows_ref, inner_ref, outer_ref, gain_ref, *refs):
@@ -272,11 +288,12 @@
         for i, weight_ref in enumerate(weight_refs[:2]):
             at = pl.multiple_of(lax.bitwise_xor(place_ref[0], i) * depth, depth)
             weights[pl.ds(at, depth), :] = weight_ref[...]
-        rows = weight_refs[2].shape[0]
-        pieces = depth // rows
-        for i, weight_ref in enumerate(weight_refs[2:]):
-            at = lax.bitwise_xor(place_ref[0], 2 + i // pieces) * depth + i % pieces * rows
-            weights[pl.ds(pl.multiple_of(at, rows), rows), :] = weight_ref[...]
+        at, unit = 0, 16
+        for weight_ref in weight_refs[2:]:
+            rows = weight_ref.shape[0]
+            start = lax.bitwise_xor(place_ref[0], 2 + at // depth) * depth + at % depth
+            weights[pl.ds(pl.multiple_of(start, unit), rows), :] = weight_ref[...]
+            at += rows
     else:
         weights[...] = weight_refs[0][...]
     mean, square, count = merged(rows_of(stat_refs))
@@ -357,7 +374,9 @@
     if direct:
         two, zero, one = (swap(part, "fsdp", 2) for part in cut(place, w_in, wide))
         across = swap(w_in, "fsdp", 1)
-        normed, inner, outer, *pieces = normalize_rows(place, rows, gain, w_out, 3)
+        inner, outer = edge_rows(place, rows)
+        part_rows = w_out.shape[0] // 12
+        normed, *pieces = normalize_rows(rows, gain, w_out, [5 * part_rows, 5 * part_rows, 2 * part_rows])
         inner = swap(inner, "ctx", 1)
         pairs = [(i, i + 1) for i in range(1, ends, 2)]
         outer = lax.ppermute(outer, "ctx", pairs + [(j, i) for i, j in pairs])
@@ -365,10 +384,12 @@
         two, zero = [two, swap(two, "ctx", 1)], [zero, swap(zero, "ctx", 1)]
         two.append(swap(two[0], "fsdp", 1))
         zero.append(swap(zero[0], "fsdp", 1))
+        normed, two[1] = tie(normed, two[1])
+        two.append(swap(two[1], "fsdp", 1))
         normed, *partials = near_product(place, normed, inner, outer, gain, w_in, across)
-        partials[2], two[1], two[2], zero[2], w_out = tie(partials[2], two[1], two[2], zero[2], w_out)
-        two.append(swap(two[1], "fsdp", 1))
-        partials[2], one, zero[1] = tie(partials[2], one, zero[1])
+        partials[2], zero[1], *late = tie(partials[2], zero[1], two[2], two[3], zero[2], w_out)
+        two[2], two[3], zero[2], w_out = late
+        partials[2], one = tie(partials[2], one)
         beyond_one = swap(one, "fsdp", 1)
         zero.append(swap(zero[1], "fsdp", 1))
         conv_two, stat_two = front(2, [partials[2], *two])
@@ -410,7 +431,7 @@
         after = lax.ppermute(rows[:HALO], "ctx", up)
         inner = jnp.where(parity == 0, after, before)
         outer = jnp.where(parity == 0, before, after)
-        normed, _, _ = normalize_rows(place, rows, gain, w_out, 0)
+        (normed,) = normalize_rows(rows, gain, w_out, ())
         (normed,) = near_product(place, normed, inner, outer, gain)
         near_by = 2 if ctx_count % 2 == 0 else 1
         groups = [

time: 68.5 us -> 64.4 us (0.940)
  starting transfers between devices: 28 us -> 22.6 us
  waiting for transfers between devices: 19.6 us -> 20.7 us
    ppermute x19, starting transfers between devices: 18 us -> 13.6 us  [swap(): lax.ppermute(value, axis, [(i, i ^ bit) for i in range(lax.axis_size(axis...]
    ppermute x6, starting transfers between devices: 9.34 us -> 8.4 us  [others(): lax.ppermute(stats, both, [(member(f, p), member(f ^ df, p ^ dp)) for f i...]
    ppermute x19, waiting for transfers between devices: 12.9 us -> 13.7 us  [swap(): lax.ppermute(value, axis, [(i, i ^ bit) for i in range(lax.axis_size(axis...]
    unnamed x16 -> x18, local copies, waits for them, and re-layouts: 2.71 us -> 2.71 us
  transfers between devices with their start and end apart: 26 -> 26, of which waited for: 11 -> 11; matrix products, arithmetic and copies ran while one was open for 0% -> 0% of each run, Pallas kernels for 21% -> 22%
where the time goes in v9:
time: 64.4 us; the launch traced here: 64.2 us
  starting transfers between devices  22.6 us (35%)
  waiting for transfers between devices  20.7 us (32%)
  Pallas kernels  17 us (26%)
  local copies, waits for them, and re-layouts  2.73 us (4%)
  between operations  0.89 us (1%)
    ppermute x19, waiting for transfers between devices, swap(): lax.ppermute(value, axis, [(i, i ^ bit) for i in range(lax.axis_size(axis...  13.7 us
    ppermute x19, starting transfers between devices, swap(): lax.ppermute(value, axis, [(i, i ^ bit) for i in range(lax.axis_size(axis...  13.6 us
    pallas_call x3, Pallas kernels, front_block(): pl.pallas_call(functools.partial(front_kernel, block, len(earlier)), out_...  8.63 us
    ppermute x6, starting transfers between devices, others(): lax.ppermute(stats, both, [(member(f, p), member(f ^ df, p ^ dp)) for f i...  8.4 us
    ppermute x6, waiting for transfers between devices, others(): lax.ppermute(stats, both, [(member(f, p), member(f ^ df, p ^ dp)) for f i...  7.01 us
    pallas_call x1, Pallas kernels, back(): pl.pallas_call(functools.partial(back_kernel, len(stats)), out_shape=jax....  2.95 us
    unnamed x18, local copies, waits for them, and re-layouts  2.71 us
    pallas_call x1, Pallas kernels, near_product(): pl.pallas_call(near_kernel, out_shape=shapes, in_specs=[pl.BlockSpec(memo...  2.33 us
  transfers between devices with their start and end apart: 26, of which 11 were waited for; matrix products, arithmetic and copies ran while one was open for 0% of the time, Pallas kernels for 22%

profile of v9, /device:TPU:0, one launch (start us, length us, event | category | flops | bytes accessed | tf_op | source)
XLA Modules:
  0.0 64.2 jit_solution(3104976627335081749)
XLA Ops:
  3.1 2.6 %collective-permute-start.2 = (bf16[384,256]{1,0:T(8,128)(2,1)S(1)}, bf16[384,256]{1,0:T(8,128)(2,1)S(1)}, u32[]{:S(2)}, u32[]{:S(2)}) collective-permute-start(bf16[384,256]{1,0:T(8,128)(2,1)S(1)} %get-tuple-element.53), channel_id=1, source_target_pairs={{0,16},{8,24},{16,0},{24,8},{1,17},{9,25},{17,1},{25,9},{2,18},{10... | collective-permute-start | bytes 589832 | tf_op jit(solution)/shard_map/ppermute | solution.py:26
  5.7 1.4 %copy-done = bf16[1,512,1536]{2,1,0:T(8,128)(2,1)S(1)} copy-done((bf16[1,512,1536]{2,1,0:T(8,128)(2,1)S(1)}, bf16[1,512,1536]{2,1,0:T(8,128)(2,1)}, u32[]{:S(2)}) %copy-start) | copy-done | bytes 1572888
  7.7 2.0 %collective-permute-start = (bf16[16,1536]{1,0:T(8,128)(2,1)S(1)}, bf16[16,1536]{1,0:T(8,128)(2,1)S(1)}, u32[]{:S(2)}, u32[]{:S(2)}) collective-permute-start(bf16[16,1536]{1,0:T(8,128)(2,1)S(1)} %get-tuple-element.51), channel_id=1, source_target_pairs={{0,1},{1,0},{2,3},{3,2},{4,5},{5,4},{6,7},{7,6},{8,9},{9,8},{10,11... | collective-permute-start | bytes 147464 | tf_op jit(solution)/shard_map/ppermute | solution.py:26
  10.4 1.9 %layer_norm.1 = (bf16[512,1536]{1,0:T(8,128)(2,1)S(1)}, bf16[80,1536]{1,0:T(8,128)(2,1)S(1)}, bf16[80,1536]{1,0:T(8,128)(2,1)S(1)}, bf16[32,1536]{1,0:T(8,128)(2,1)S(1)}) custom-call(bf16[512,1536]{1,0:T(8,128)(2,1)S(1)} %bitcast.6, f32[1,1536]{1,0:T(1,128)S(1)} %broadcast_in_dim.14.gain_ref, bf16[192,1536]{1,0:T(8,128)(2,1)S(1)} %copy-done.4), custom_call_target="tpu_custom_call" | custom-call | flops 100000000 | tf_op jit(solution)/shard_map/layer_norm/pallas_call | solution.py:99
  12.4 3.0 %collective-permute-done.3.refs_1_ = bf16[384,256]{1,0:T(8,128)(2,1)S(1)} collective-permute-done((bf16[384,256]{1,0:T(8,128)(2,1)S(1)}, bf16[384,256]{1,0:T(8,128)(2,1)S(1)}, u32[]{:S(2)}, u32[]{:S(2)}) %collective-permute-start.3) | collective-permute-done | bytes 196640 | tf_op jit(solution)/shard_map/ppermute | solution.py:26
  15.4 1.8 %collective-permute-start.4 = (bf16[384,256]{1,0:T(8,128)(2,1)S(1)}, bf16[384,256]{1,0:T(8,128)(2,1)S(1)}, u32[]{:S(2)}, u32[]{:S(2)}) collective-permute-start(bf16[384,256]{1,0:T(8,128)(2,1)S(1)} %collective-permute-done.2.refs_1_), channel_id=1, source_target_pairs={{0,1},{1,0},{2,3},{3,2},{4,5},{5,4},{6,7},{7,6},{8,9},{9,8},{10,11... | collective-permute-start | bytes 589832 | tf_op jit(solution)/shard_map/ppermute | solution.py:26
  17.4 1.8 %collective-permute-start.10 = (bf16[384,512]{1,0:T(8,128)(2,1)S(1)}, bf16[384,512]{1,0:T(8,128)(2,1)S(1)}, u32[]{:S(2)}, u32[]{:S(2)}) collective-permute-start(bf16[384,512]{1,0:T(8,128)(2,1)S(1)} %get-tuple-element.65), channel_id=1, source_target_pairs={{0,16},{8,24},{16,0},{24,8},{1,17},{9,25},{17,1},{25,9},{2,18},{10... | collective-permute-start | bytes 1179656 | tf_op jit(solution)/shard_map/ppermute | solution.py:26
  19.2 4.0 %collective-permute-done.4.refs_2_ = bf16[384,256]{1,0:T(8,128)(2,1)S(1)} collective-permute-done((bf16[384,256]{1,0:T(8,128)(2,1)S(1)}, bf16[384,256]{1,0:T(8,128)(2,1)S(1)}, u32[]{:S(2)}, u32[]{:S(2)}) %collective-permute-start.4) | collective-permute-done | bytes 196640 | tf_op jit(solution)/shard_map/ppermute | solution.py:26
  23.2 3.2 %collective-permute-done.6.refs_2_ = bf16[384,256]{1,0:T(8,128)(2,1)S(1)} collective-permute-done((bf16[384,256]{1,0:T(8,128)(2,1)S(1)}, bf16[384,256]{1,0:T(8,128)(2,1)S(1)}, u32[]{:S(2)}, u32[]{:S(2)}) %collective-permute-start.6) | collective-permute-done | bytes 196640 | tf_op jit(solution)/shard_map/ppermute | solution.py:26
  26.4 1.6 %collective-permute-start.11 = (bf16[80,1536]{1,0:T(8,128)(2,1)S(1)}, bf16[80,1536]{1,0:T(8,128)(2,1)S(1)}, u32[]{:S(2)}, u32[]{:S(2)}) collective-permute-start(bf16[80,1536]{1,0:T(8,128)(2,1)S(1)} %get-tuple-element.72), channel_id=1, source_target_pairs={{0,16},{8,24},{16,0},{24,8},{1,17},{9,25},{17,1},{25,9},{2,18},{10... | collective-permute-start | bytes 737288 | tf_op jit(solution)/shard_map/ppermute | solution.py:26
  28.0 2.3 %near.1 = (bf16[544,1536]{1,0:T(8,128)(2,1)S(1)}, f32[544,512]{1,0:T(8,128)S(1)}, f32[544,512]{1,0:T(8,128)S(1)}, f32[544,512]{1,0:T(8,128)S(1)}) custom-call(s32[4]{0:T(128)S(1)} %pad_add_fusion.place_ref, bf16[512,1536]{1,0:T(8,128)(2,1)S(1)} %get-tuple-element.57.rows_ref, bf16[16,1536]{1,0:T(8,128)(2,1)S(1)} %collective-permute-done.inner_ref, ...), custom_call_target="tpu_custom_call" | custom-call | flops 100000000 | tf_op jit(solution)/shard_map/near/pallas_call | solution.py:147
  31.4 2.9 %front.3 = (f32[512,256]{1,0:T(8,128)S(1)}, f32[3,256]{1,0:T(4,128)S(1)}) custom-call(s32[4]{0:T(128)S(1)} %pad_add_fusion.place_ref, bf16[544,1536]{1,0:T(8,128)(2,1)S(1)} %get-tuple-element.60.normed_ref, f32[544,512]{1,0:T(8,128)S(1)} %get-tuple-element.66.refs_0_, bf16[384,256]{1,0:T(8,128)(2,1)S(1)} %collective-permute-done.2.refs_1_, ...), custom_call_target="tpu_custom_call" | custom-call | flops 100000000 | tf_op jit(solution)/shard_map/front/pallas_call | solution.py:232
  35.2 2.9 %front.4 = (f32[512,256]{1,0:T(8,128)S(1)}, f32[3,256]{1,0:T(4,128)S(1)}) custom-call(s32[4]{0:T(128)S(1)} %pad_add_fusion.place_ref, bf16[544,1536]{1,0:T(8,128)(2,1)S(1)} %get-tuple-element.60.normed_ref, f32[544,512]{1,0:T(8,128)S(1)} %get-tuple-element.73.refs_0_, bf16[384,256]{1,0:T(8,128)(2,1)S(1)} %collective-permute-done.3.refs_1_, ...), custom_call_target="tpu_custom_call" | custom-call | flops 4000000000 | tf_op jit(solution)/shard_map/front/pallas_call | solution.py:232
  38.1 2.9 %front.5 = (f32[512,256]{1,0:T(8,128)S(1)}, f32[1,3,768]{2,1,0:T(4,128)S(1)}) custom-call(s32[4]{0:T(128)S(1)} %pad_add_fusion.place_ref, bf16[544,1536]{1,0:T(8,128)(2,1)S(1)} %get-tuple-element.60.normed_ref, f32[3,256]{1,0:T(4,128)S(1)} %get-tuple-element.69.refs_0_, f32[3,256]{1,0:T(4,128)S(1)} %get-tuple-element.76.refs_1_, ...), custom_call_target="tpu_custom_call" | custom-call | flops 100000000 | tf_op jit(solution)/shard_map/front/pallas_call | solution.py:232
  42.5 1.7 %collective-permute-start.17 = (f32[1,3,768]{2,1,0:T(4,128)S(1)}, f32[1,3,768]{2,1,0:T(4,128)S(1)}, u32[]{:S(2)}, u32[]{:S(2)}) collective-permute-start(f32[1,3,768]{2,1,0:T(4,128)S(1)} %pad_maximum_fusion), channel_id=1, source_target_pairs={{0,2},{1,3},{2,0},{3,1},{4,6},{5,7},{6,4},{7,5},{8,10},{9,11},{10,... | collective-permute-start | bytes 27656 | tf_op jit(solution)/shard_map/ppermute | solution.py:409
  44.1 1.5 %collective-permute-start.18 = (bf16[32,1536]{1,0:T(8,128)(2,1)S(1)}, bf16[32,1536]{1,0:T(8,128)(2,1)S(1)}, u32[]{:S(2)}, u32[]{:S(2)}) collective-permute-start(bf16[32,1536]{1,0:T(8,128)(2,1)S(1)} %get-tuple-element.85), channel_id=1, source_target_pairs={{0,16},{8,24},{16,0},{24,8},{1,17},{9,25},{17,1},{25,9},{2,18},{10... | collective-permute-start | bytes 294920 | tf_op jit(solution)/shard_map/ppermute | solution.py:26
  46.3 2.6 %collective-permute-done.18.refs_11_ = bf16[32,1536]{1,0:T(8,128)(2,1)S(1)} collective-permute-done((bf16[32,1536]{1,0:T(8,128)(2,1)S(1)}, bf16[32,1536]{1,0:T(8,128)(2,1)S(1)}, u32[]{:S(2)}, u32[]{:S(2)}) %collective-permute-start.18) | collective-permute-done | bytes 98336 | tf_op jit(solution)/shard_map/ppermute | solution.py:26
  48.9 2.6 %collective-permute-start.20 = (f32[1,3,768]{2,1,0:T(4,128)S(1)}, f32[1,3,768]{2,1,0:T(4,128)S(1)}, u32[]{:S(2)}, u32[]{:S(2)}) collective-permute-start(f32[1,3,768]{2,1,0:T(4,128)S(1)} %pad_maximum_fusion.1), channel_id=1, source_target_pairs={{0,4},{1,5},{2,6},{3,7},{4,0},{5,1},{6,2},{7,3},{8,12},{9,13},{10,... | collective-permute-start | bytes 27656 | tf_op jit(solution)/shard_map/ppermute | solution.py:409
  51.5 2.0 %collective-permute-done.20 = f32[1,3,768]{2,1,0:T(4,128)S(1)} collective-permute-done((f32[1,3,768]{2,1,0:T(4,128)S(1)}, f32[1,3,768]{2,1,0:T(4,128)S(1)}, u32[]{:S(2)}, u32[]{:S(2)}) %collective-permute-start.20) | collective-permute-done | bytes 9248 | tf_op jit(solution)/shard_map/ppermute | solution.py:409
  53.6 1.6 %collective-permute-start.21 = (f32[1,3,768]{2,1,0:T(4,128)S(1)}, f32[1,3,768]{2,1,0:T(4,128)S(1)}, u32[]{:S(2)}, u32[]{:S(2)}) collective-permute-start(f32[1,3,768]{2,1,0:T(4,128)S(1)} %pad_maximum_fusion.2.refs_0_), channel_id=1, source_target_pairs={{0,1},{1,0},{2,3},{3,2},{4,5},{5,4},{6,7},{7,6},{8,9},{9,8},{10,11... | collective-permute-start | bytes 27656 | tf_op jit(solution)/shard_map/ppermute | solution.py:409
  55.2 1.5 %collective-permute-start.22 = (f32[1,3,768]{2,1,0:T(4,128)S(1)}, f32[1,3,768]{2,1,0:T(4,128)S(1)}, u32[]{:S(2)}, u32[]{:S(2)}) collective-permute-start(f32[1,3,768]{2,1,0:T(4,128)S(1)} %pad_maximum_fusion.2.refs_0_), channel_id=1, source_target_pairs={{0,16},{1,17},{2,18},{3,19},{4,20},{5,21},{6,22},{7,23},{8,24},{9,... | collective-permute-start | bytes 27656 | tf_op jit(solution)/shard_map/ppermute | solution.py:409
  57.3 1.5 %collective-permute-done.22.refs_2_ = f32[1,3,768]{2,1,0:T(4,128)S(1)} collective-permute-done((f32[1,3,768]{2,1,0:T(4,128)S(1)}, f32[1,3,768]{2,1,0:T(4,128)S(1)}, u32[]{:S(2)}, u32[]{:S(2)}) %collective-permute-start.22) | collective-permute-done | bytes 9248 | tf_op jit(solution)/shard_map/ppermute | solution.py:409
  58.9 2.4 %collective-permute-done.23.refs_3_ = f32[1,3,768]{2,1,0:T(4,128)S(1)} collective-permute-done((f32[1,3,768]{2,1,0:T(4,128)S(1)}, f32[1,3,768]{2,1,0:T(4,128)S(1)}, u32[]{:S(2)}, u32[]{:S(2)}) %collective-permute-start.23) | collective-permute-done | bytes 9248 | tf_op jit(solution)/shard_map/ppermute | solution.py:409
  61.2 2.9 %back.1 = bf16[512,1536]{1,0:T(8,128)(2,1)} custom-call(s32[4]{0:T(128)S(1)} %pad_add_fusion.place_ref, f32[1,768]{1,0:T(1,128)S(1)} %broadcast_in_dim.12.gain_ref, f32[1,768]{1,0:T(1,128)S(1)} %broadcast_in_dim.13.shift_ref, f32[1,3,768]{2,1,0:T(4,128)S(1)} %pad_maximum_fusion.2.refs_0_, f32[1,3,768]{2,1,0:T(4,128)S(1)} %collective-permute-done.21.refs_1_, ...), custom_call_target="tpu_custom_call" | custom-call | flops 1000000000 | tf_op jit(solution)/shard_map/back/pallas_call | solution.py:330
  (64 shorter events, 8.7 us)
Async XLA Ops:
  0.0 26.4 %collective-permute-start.5 = (bf16[384,1536]{1,0:T(8,128)(2,1)}, bf16[384,1536]{1,0:T(8,128)(2,1)S(1)}, u32[]{:S(2)}, u32[]{:S(2)}) collective-permute-start(bf16[384,1536]{1,0:T(8,128)(2,1)} %refs_0_.1), channel_id=1, source_target_pairs={{0,8},{8,0},{16,24},{24,16},{1,9},{9,1},{17,25},{25,17},{2,10},{10... | collective-permute-start | bytes 3538952 | tf_op jit(solution)/shard_map/ppermute | solution.py:26
  3.1 9.3 %collective-permute-start.2 = (bf16[384,256]{1,0:T(8,128)(2,1)S(1)}, bf16[384,256]{1,0:T(8,128)(2,1)S(1)}, u32[]{:S(2)}, u32[]{:S(2)}) collective-permute-start(bf16[384,256]{1,0:T(8,128)(2,1)S(1)} %get-tuple-element.53), channel_id=1, source_target_pairs={{0,16},{8,24},{16,0},{24,8},{1,17},{9,25},{17,1},{25,9},{2,18},{10... | collective-permute-start | bytes 589832 | tf_op jit(solution)/shard_map/ppermute | solution.py:26
  5.6 9.8 %collective-permute-start.3 = (bf16[384,256]{1,0:T(8,128)(2,1)S(1)}, bf16[384,256]{1,0:T(8,128)(2,1)S(1)}, u32[]{:S(2)}, u32[]{:S(2)}) collective-permute-start(bf16[384,256]{1,0:T(8,128)(2,1)S(1)} %get-tuple-element.54), channel_id=1, source_target_pairs={{0,16},{8,24},{16,0},{24,8},{1,17},{9,25},{17,1},{25,9},{2,18},{10... | collective-permute-start | bytes 589832 | tf_op jit(solution)/shard_map/ppermute | solution.py:26
  7.7 4.7 %collective-permute-start = (bf16[16,1536]{1,0:T(8,128)(2,1)S(1)}, bf16[16,1536]{1,0:T(8,128)(2,1)S(1)}, u32[]{:S(2)}, u32[]{:S(2)}) collective-permute-start(bf16[16,1536]{1,0:T(8,128)(2,1)S(1)} %get-tuple-element.51), channel_id=1, source_target_pairs={{0,1},{1,0},{2,3},{3,2},{4,5},{5,4},{6,7},{7,6},{8,9},{9,8},{10,11... | collective-permute-start | bytes 147464 | tf_op jit(solution)/shard_map/ppermute | solution.py:26
  15.4 7.8 %collective-permute-start.4 = (bf16[384,256]{1,0:T(8,128)(2,1)S(1)}, bf16[384,256]{1,0:T(8,128)(2,1)S(1)}, u32[]{:S(2)}, u32[]{:S(2)}) collective-permute-start(bf16[384,256]{1,0:T(8,128)(2,1)S(1)} %collective-permute-done.2.refs_1_), channel_id=1, source_target_pairs={{0,1},{1,0},{2,3},{3,2},{4,5},{5,4},{6,7},{7,6},{8,9},{9,8},{10,11... | collective-permute-start | bytes 589832 | tf_op jit(solution)/shard_map/ppermute | solution.py:26
  17.2 9.2 %collective-permute-start.6 = (bf16[384,256]{1,0:T(8,128)(2,1)S(1)}, bf16[384,256]{1,0:T(8,128)(2,1)S(1)}, u32[]{:S(2)}, u32[]{:S(2)}) collective-permute-start(bf16[384,256]{1,0:T(8,128)(2,1)S(1)} %collective-permute-done.3.refs_1_), channel_id=1, source_target_pairs={{0,1},{1,0},{2,3},{3,2},{4,5},{5,4},{6,7},{7,6},{8,9},{9,8},{10,11... | collective-permute-start | bytes 589832 | tf_op jit(solution)/shard_map/ppermute | solution.py:26
  17.4 13.2 %collective-permute-start.10 = (bf16[384,512]{1,0:T(8,128)(2,1)S(1)}, bf16[384,512]{1,0:T(8,128)(2,1)S(1)}, u32[]{:S(2)}, u32[]{:S(2)}) collective-permute-start(bf16[384,512]{1,0:T(8,128)(2,1)S(1)} %get-tuple-element.65), channel_id=1, source_target_pairs={{0,16},{8,24},{16,0},{24,8},{1,17},{9,25},{17,1},{25,9},{2,18},{10... | collective-permute-start | bytes 1179656 | tf_op jit(solution)/shard_map/ppermute | solution.py:26
  19.2 11.2 %collective-permute-start.7 = (bf16[384,256]{1,0:T(8,128)(2,1)S(1)}, bf16[384,256]{1,0:T(8,128)(2,1)S(1)}, u32[]{:S(2)}, u32[]{:S(2)}) collective-permute-start(bf16[384,256]{1,0:T(8,128)(2,1)S(1)} %collective-permute-done.2.refs_1_), channel_id=1, source_target_pairs={{0,8},{8,0},{16,24},{24,16},{1,9},{9,1},{17,25},{25,17},{2,10},{10... | collective-permute-start | bytes 589832 | tf_op jit(solution)/shard_map/ppermute | solution.py:26
  23.2 7.2 %collective-permute-start.9 = (bf16[384,256]{1,0:T(8,128)(2,1)S(1)}, bf16[384,256]{1,0:T(8,128)(2,1)S(1)}, u32[]{:S(2)}, u32[]{:S(2)}) collective-permute-start(bf16[384,256]{1,0:T(8,128)(2,1)S(1)} %collective-permute-done.3.refs_1_), channel_id=1, source_target_pairs={{0,8},{8,0},{16,24},{24,16},{1,9},{9,1},{17,25},{25,17},{2,10},{10... | collective-permute-start | bytes 589832 | tf_op jit(solution)/shard_map/ppermute | solution.py:26
  26.3 4.0 %collective-permute-start.8 = (bf16[384,256]{1,0:T(8,128)(2,1)S(1)}, bf16[384,256]{1,0:T(8,128)(2,1)S(1)}, u32[]{:S(2)}, u32[]{:S(2)}) collective-permute-start(bf16[384,256]{1,0:T(8,128)(2,1)S(1)} %collective-permute-done.4.refs_2_), channel_id=1, source_target_pairs={{0,8},{8,0},{16,24},{24,16},{1,9},{9,1},{17,25},{25,17},{2,10},{10... | collective-permute-start | bytes 589832 | tf_op jit(solution)/shard_map/ppermute | solution.py:26
  26.4 8.8 %collective-permute-start.11 = (bf16[80,1536]{1,0:T(8,128)(2,1)S(1)}, bf16[80,1536]{1,0:T(8,128)(2,1)S(1)}, u32[]{:S(2)}, u32[]{:S(2)}) collective-permute-start(bf16[80,1536]{1,0:T(8,128)(2,1)S(1)} %get-tuple-element.72), channel_id=1, source_target_pairs={{0,16},{8,24},{16,0},{24,8},{1,17},{9,25},{17,1},{25,9},{2,18},{10... | collective-permute-start | bytes 737288 | tf_op jit(solution)/shard_map/ppermute | solution.py:26
  30.4 4.8 %collective-permute-start.12 = (bf16[384,256]{1,0:T(8,128)(2,1)S(1)}, bf16[384,256]{1,0:T(8,128)(2,1)S(1)}, u32[]{:S(2)}, u32[]{:S(2)}) collective-permute-start(bf16[384,256]{1,0:T(8,128)(2,1)S(1)} %collective-permute-done.6.refs_2_), channel_id=1, source_target_pairs={{0,8},{8,0},{16,24},{24,16},{1,9},{9,1},{17,25},{25,17},{2,10},{10... | collective-permute-start | bytes 589832 | tf_op jit(solution)/shard_map/ppermute | solution.py:26
  30.6 7.5 %collective-permute-start.13 = (bf16[384,512]{1,0:T(8,128)(2,1)S(1)}, bf16[384,512]{1,0:T(8,128)(2,1)S(1)}, u32[]{:S(2)}, u32[]{:S(2)}) collective-permute-start(bf16[384,512]{1,0:T(8,128)(2,1)S(1)} %collective-permute-done.10.refs_3_), channel_id=1, source_target_pairs={{0,8},{8,0},{16,24},{24,16},{1,9},{9,1},{17,25},{25,17},{2,10},{10... | collective-permute-start | bytes 1179656 | tf_op jit(solution)/shard_map/ppermute | solution.py:26
  30.9 10.0 %collective-permute-start.14 = (bf16[80,1536]{1,0:T(8,128)(2,1)S(1)}, bf16[80,1536]{1,0:T(8,128)(2,1)S(1)}, u32[]{:S(2)}, u32[]{:S(2)}) collective-permute-start(bf16[80,1536]{1,0:T(8,128)(2,1)S(1)} %get-tuple-element.82), channel_id=1, source_target_pairs={{0,16},{8,24},{16,0},{24,8},{1,17},{9,25},{17,1},{25,9},{2,18},{10... | collective-permute-start | bytes 737288 | tf_op jit(solution)/shard_map/ppermute | solution.py:26
  35.2 5.8 %collective-permute-start.15 = (bf16[80,1536]{1,0:T(8,128)(2,1)S(1)}, bf16[80,1536]{1,0:T(8,128)(2,1)S(1)}, u32[]{:S(2)}, u32[]{:S(2)}) collective-permute-start(bf16[80,1536]{1,0:T(8,128)(2,1)S(1)} %collective-permute-done.11.refs_9_), channel_id=1, source_target_pairs={{0,8},{8,0},{16,24},{24,16},{1,9},{9,1},{17,25},{25,17},{2,10},{10... | collective-permute-start | bytes 737288 | tf_op jit(solution)/shard_map/ppermute | solution.py:26
  42.5 3.8 %collective-permute-start.17 = (f32[1,3,768]{2,1,0:T(4,128)S(1)}, f32[1,3,768]{2,1,0:T(4,128)S(1)}, u32[]{:S(2)}, u32[]{:S(2)}) collective-permute-start(f32[1,3,768]{2,1,0:T(4,128)S(1)} %pad_maximum_fusion), channel_id=1, source_target_pairs={{0,2},{1,3},{2,0},{3,1},{4,6},{5,7},{6,4},{7,5},{8,10},{9,11},{10,... | collective-permute-start | bytes 27656 | tf_op jit(solution)/shard_map/ppermute | solution.py:409
  44.1 4.8 %collective-permute-start.18 = (bf16[32,1536]{1,0:T(8,128)(2,1)S(1)}, bf16[32,1536]{1,0:T(8,128)(2,1)S(1)}, u32[]{:S(2)}, u32[]{:S(2)}) collective-permute-start(bf16[32,1536]{1,0:T(8,128)(2,1)S(1)} %get-tuple-element.85), channel_id=1, source_target_pairs={{0,16},{8,24},{16,0},{24,8},{1,17},{9,25},{17,1},{25,9},{2,18},{10... | collective-permute-start | bytes 294920 | tf_op jit(solution)/shard_map/ppermute | solution.py:26
  45.6 11.5 %collective-permute-start.24 = (bf16[192,1536]{1,0:T(8,128)(2,1)S(1)}, bf16[192,1536]{1,0:T(8,128)(2,1)S(1)}, u32[]{:S(2)}, u32[]{:S(2)}) collective-permute-start(bf16[192,1536]{1,0:T(8,128)(2,1)S(1)} %copy-done.4), channel_id=1, source_target_pairs={{0,8},{8,0},{16,24},{24,16},{1,9},{9,1},{17,25},{25,17},{2,10},{10... | collective-permute-start | bytes 1769480 | tf_op jit(solution)/shard_map/ppermute | solution.py:26
  45.6 3.3 %collective-permute-start.19 = (bf16[80,1536]{1,0:T(8,128)(2,1)S(1)}, bf16[80,1536]{1,0:T(8,128)(2,1)S(1)}, u32[]{:S(2)}, u32[]{:S(2)}) collective-permute-start(bf16[80,1536]{1,0:T(8,128)(2,1)S(1)} %collective-permute-done.14.refs_10_), channel_id=1, source_target_pairs={{0,8},{8,0},{16,24},{24,16},{1,9},{9,1},{17,25},{25,17},{2,10},{10... | collective-permute-start | bytes 737288 | tf_op jit(solution)/shard_map/ppermute | solution.py:26
  48.9 4.6 %collective-permute-start.20 = (f32[1,3,768]{2,1,0:T(4,128)S(1)}, f32[1,3,768]{2,1,0:T(4,128)S(1)}, u32[]{:S(2)}, u32[]{:S(2)}) collective-permute-start(f32[1,3,768]{2,1,0:T(4,128)S(1)} %pad_maximum_fusion.1), channel_id=1, source_target_pairs={{0,4},{1,5},{2,6},{3,7},{4,0},{5,1},{6,2},{7,3},{8,12},{9,13},{10,... | collective-permute-start | bytes 27656 | tf_op jit(solution)/shard_map/ppermute | solution.py:409
  51.5 9.7 %collective-permute-start.25 = (bf16[32,1536]{1,0:T(8,128)(2,1)S(1)}, bf16[32,1536]{1,0:T(8,128)(2,1)S(1)}, u32[]{:S(2)}, u32[]{:S(2)}) collective-permute-start(bf16[32,1536]{1,0:T(8,128)(2,1)S(1)} %collective-permute-done.18.refs_11_), channel_id=1, source_target_pairs={{0,8},{8,0},{16,24},{24,16},{1,9},{9,1},{17,25},{25,17},{2,10},{10... | collective-permute-start | bytes 294920 | tf_op jit(solution)/shard_map/ppermute | solution.py:26
  53.6 3.8 %collective-permute-start.21 = (f32[1,3,768]{2,1,0:T(4,128)S(1)}, f32[1,3,768]{2,1,0:T(4,128)S(1)}, u32[]{:S(2)}, u32[]{:S(2)}) collective-permute-start(f32[1,3,768]{2,1,0:T(4,128)S(1)} %pad_maximum_fusion.2.refs_0_), channel_id=1, source_target_pairs={{0,1},{1,0},{2,3},{3,2},{4,5},{5,4},{6,7},{7,6},{8,9},{9,8},{10,11... | collective-permute-start | bytes 27656 | tf_op jit(solution)/shard_map/ppermute | solution.py:409
  55.2 3.7 %collective-permute-start.22 = (f32[1,3,768]{2,1,0:T(4,128)S(1)}, f32[1,3,768]{2,1,0:T(4,128)S(1)}, u32[]{:S(2)}, u32[]{:S(2)}) collective-permute-start(f32[1,3,768]{2,1,0:T(4,128)S(1)} %pad_maximum_fusion.2.refs_0_), channel_id=1, source_target_pairs={{0,16},{1,17},{2,18},{3,19},{4,20},{5,21},{6,22},{7,23},{8,24},{9,... | collective-permute-start | bytes 27656 | tf_op jit(solution)/shard_map/ppermute | solution.py:409
  56.6 4.6 %collective-permute-start.23 = (f32[1,3,768]{2,1,0:T(4,128)S(1)}, f32[1,3,768]{2,1,0:T(4,128)S(1)}, u32[]{:S(2)}, u32[]{:S(2)}) collective-permute-start(f32[1,3,768]{2,1,0:T(4,128)S(1)} %pad_maximum_fusion.2.refs_0_), channel_id=1, source_target_pairs={{0,17},{1,16},{2,19},{3,18},{4,21},{5,20},{6,23},{7,22},{8,25},{9,... | collective-permute-start | bytes 27656 | tf_op jit(solution)/shard_map/ppermute | solution.py:409
  (11 other events, 89.4 us)

commit v10 on v9

--- a/solution.py
+++ b/solution.py
@@ -372,36 +372,36 @@
         return front_block(block, wide, place, normed, weights, dw_kernel, *extra)
 
     if direct:
-        two, zero, one = (swap(part, "fsdp", 2) for part in cut(place, w_in, wide))
+        two, zero, one = cut(place, w_in, wide)
+        two, zero = swap(two, "fsdp", 2), swap(zero, "fsdp", 2)
         across = swap(w_in, "fsdp", 1)
         inner, outer = edge_rows(place, rows)
         part_rows = w_out.shape[0] // 12
-        normed, *pieces = normalize_rows(rows, gain, w_out, [5 * part_rows, 5 * part_rows, 2 * part_rows])
+        normed, *pieces = normalize_rows(rows, gain, w_out, [3 * part_rows, 9 * part_rows])
         inner = swap(inner, "ctx", 1)
         pairs = [(i, i + 1) for i in range(1, ends, 2)]
         outer = lax.ppermute(outer, "ctx", pairs + [(j, i) for i, j in pairs])
         normed, inner, outer, two, zero = tie(normed, inner, outer, two, zero)
         two, zero = [two, swap(two, "ctx", 1)], [zero, swap(zero, "ctx", 1)]
+        normed, *partials = near_product(place, normed, inner, outer, gain, w_in, across)
+        partials[2], one, two[0], zero[0] = tie(partials[2], one, two[0], zero[0])
+        one = swap(one, "fsdp", 2)
         two.append(swap(two[0], "fsdp", 1))
         zero.append(swap(zero[0], "fsdp", 1))
-        normed, two[1] = tie(normed, two[1])
+        partials[2], *parts = tie(partials[2], *two, *zero, w_out)
+        two, zero, w_out = parts[:3], parts[3:6], parts[6]
         two.append(swap(two[1], "fsdp", 1))
-        normed, *partials = near_product(place, normed, inner, outer, gain, w_in, across)
-        partials[2], zero[1], *late = tie(partials[2], zero[1], two[2], two[3], zero[2], w_out)
-        two[2], two[3], zero[2], w_out = late
-        partials[2], one = tie(partials[2], one)
-        beyond_one = swap(one, "fsdp", 1)
         zero.append(swap(zero[1], "fsdp", 1))
         conv_two, stat_two = front(2, [partials[2], *two])
+        conv_two, partials[0], one = tie(conv_two, partials[0], one)
+        beyond_one = swap(one, "fsdp", 1)
         pieces = [swap(piece, "fsdp", 2) for piece in pieces]
-        conv_two, partials[0], pieces[0] = tie(conv_two, partials[0], pieces[0])
-        beyond = [swap(pieces[0], "fsdp", 1)]
         conv_zero, stat_zero = front(0, [partials[0], *zero])
         conv_zero, partials[1] = tie(conv_zero, partials[1])
         conv_one, stats = front(1, [partials[1], one, beyond_one], (stat_two, stat_zero), 1)
         across_out = swap(w_out, "fsdp", 1)
-        stats, pieces[1], beyond[0] = tie(stats, pieces[1], beyond[0])
-        beyond.append(swap(pieces[1], "fsdp", 1))
+        stats, pieces[0] = tie(stats, pieces[0])
+        beyond = [swap(pieces[0], "fsdp", 1)]
         convs = [conv_zero, conv_one, conv_two]
 
         def others(flips):
@@ -419,10 +419,10 @@
 
         stats = union([stats] + others([(1, 0)]))
         stats = union([stats] + others([(0, 2)]))
-        stats, pieces[2], beyond[1] = tie(stats, pieces[2], beyond[1])
-        beyond.append(swap(pieces[2], "fsdp", 1))
         stats = union([stats] + others([(0, 4)]))
         stats = [stats] + others([(0, 1), (2, 0), (2, 1)])
+        *stats, pieces[1] = tie(*stats, pieces[1])
+        beyond.append(swap(pieces[1], "fsdp", 1))
         out_weights = [w_out, across_out, *pieces, *beyond]
     else:
         full_in = lax.all_gather(w_in, "fsdp", axis=0, tiled=True)

time: 64.4 us -> 60.6 us (0.941)
  waiting for transfers between devices: 20.7 us -> 16.7 us
    ppermute x6, waiting for transfers between devices: 7.01 us -> 4.06 us  [others(): lax.ppermute(stats, both, [(member(f, p), member(f ^ df, p ^ dp)) for f i...]
    ppermute x6, starting transfers between devices: 8.4 us -> 9.59 us  [others(): lax.ppermute(stats, both, [(member(f, p), member(f ^ df, p ^ dp)) for f i...]
    ppermute x19 -> x17, waiting for transfers between devices: 13.7 us -> 12.6 us  [swap(): lax.ppermute(value, axis, [(i, i ^ bit) for i in range(lax.axis_size(axis...]
    ppermute x19 -> x17, starting transfers between devices: 13.6 us -> 12.8 us  [swap(): lax.ppermute(value, axis, [(i, i ^ bit) for i in range(lax.axis_size(axis...]
  transfers between devices with their start and end apart: 26 -> 24, of which waited for: 11 -> 12; matrix products, arithmetic and copies ran while one was open for 0% -> 0% of each run, Pallas kernels for 22% -> 23%
where the time goes in v10:
time: 60.6 us; the launch traced here: 60.5 us
  starting transfers between devices  23 us (38%)
  Pallas kernels  17 us (28%)
  waiting for transfers between devices  16.7 us (28%)
  local copies, waits for them, and re-layouts  2.73 us (5%)
  between operations  0.87 us (1%)
    ppermute x17, starting transfers between devices, swap(): lax.ppermute(value, axis, [(i, i ^ bit) for i in range(lax.axis_size(axis...  12.8 us
    ppermute x17, waiting for transfers between devices, swap(): lax.ppermute(value, axis, [(i, i ^ bit) for i in range(lax.axis_size(axis...  12.6 us
    ppermute x6, starting transfers between devices, others(): lax.ppermute(stats, both, [(member(f, p), member(f ^ df, p ^ dp)) for f i...  9.59 us
    pallas_call x3, Pallas kernels, front_block(): pl.pallas_call(functools.partial(front_kernel, block, len(earlier)), out_...  8.63 us
    ppermute x6, waiting for transfers between devices, others(): lax.ppermute(stats, both, [(member(f, p), member(f ^ df, p ^ dp)) for f i...  4.06 us
    pallas_call x1, Pallas kernels, back(): pl.pallas_call(functools.partial(back_kernel, len(stats)), out_shape=jax....  2.93 us
    unnamed x18, local copies, waits for them, and re-layouts  2.71 us
    pallas_call x1, Pallas kernels, near_product(): pl.pallas_call(near_kernel, out_shape=shapes, in_specs=[pl.BlockSpec(memo...  2.33 us
  transfers between devices with their start and end apart: 24, of which 12 were waited for; matrix products, arithmetic and copies ran while one was open for 0% of the time, Pallas kernels for 23%

profile of v10, /device:TPU:0, one launch (start us, length us, event | category | flops | bytes accessed | tf_op | source)
XLA Modules:
  0.0 60.5 jit_solution(7984521018896753399)
XLA Ops:
  1.2 1.3 %copy-done.2 = bf16[384,1536]{1,0:T(8,128)(2,1)S(1)} copy-done((bf16[384,1536]{1,0:T(8,128)(2,1)S(1)}, bf16[384,1536]{1,0:T(8,128)(2,1)}, u32[]{:S(2)}) %copy-start.2) | copy-done | bytes 1179672
  3.1 2.6 %collective-permute-start.2 = (bf16[384,256]{1,0:T(8,128)(2,1)S(1)}, bf16[384,256]{1,0:T(8,128)(2,1)S(1)}, u32[]{:S(2)}, u32[]{:S(2)}) collective-permute-start(bf16[384,256]{1,0:T(8,128)(2,1)S(1)} %get-tuple-element.55), channel_id=1, source_target_pairs={{0,16},{8,24},{16,0},{24,8},{1,17},{9,25},{17,1},{25,9},{2,18},{10... | collective-permute-start | bytes 589832 | tf_op jit(solution)/shard_map/ppermute | solution.py:26
  5.7 1.4 %copy-done = bf16[1,512,1536]{2,1,0:T(8,128)(2,1)S(1)} copy-done((bf16[1,512,1536]{2,1,0:T(8,128)(2,1)S(1)}, bf16[1,512,1536]{2,1,0:T(8,128)(2,1)}, u32[]{:S(2)}) %copy-start) | copy-done | bytes 1572888
  7.7 2.0 %collective-permute-start = (bf16[16,1536]{1,0:T(8,128)(2,1)S(1)}, bf16[16,1536]{1,0:T(8,128)(2,1)S(1)}, u32[]{:S(2)}, u32[]{:S(2)}) collective-permute-start(bf16[16,1536]{1,0:T(8,128)(2,1)S(1)} %get-tuple-element.53), channel_id=1, source_target_pairs={{0,1},{1,0},{2,3},{3,2},{4,5},{5,4},{6,7},{7,6},{8,9},{9,8},{10,11... | collective-permute-start | bytes 147464 | tf_op jit(solution)/shard_map/ppermute | solution.py:26
  10.4 1.9 %layer_norm.1 = (bf16[512,1536]{1,0:T(8,128)(2,1)S(1)}, bf16[48,1536]{1,0:T(8,128)(2,1)S(1)}, bf16[144,1536]{1,0:T(8,128)(2,1)S(1)}) custom-call(bf16[512,1536]{1,0:T(8,128)(2,1)S(1)} %bitcast.6, f32[1,1536]{1,0:T(1,128)S(1)} %broadcast_in_dim.14.gain_ref, bf16[192,1536]{1,0:T(8,128)(2,1)S(1)} %copy-done.4), custom_call_target="tpu_custom_call" | custom-call | flops 100000000 | tf_op jit(solution)/shard_map/layer_norm/pallas_call | solution.py:99
  12.4 3.0 %collective-permute-done.3.refs_1_ = bf16[384,256]{1,0:T(8,128)(2,1)S(1)} collective-permute-done((bf16[384,256]{1,0:T(8,128)(2,1)S(1)}, bf16[384,256]{1,0:T(8,128)(2,1)S(1)}, u32[]{:S(2)}, u32[]{:S(2)}) %collective-permute-start.3) | collective-permute-done | bytes 196640 | tf_op jit(solution)/shard_map/ppermute | solution.py:26
  15.4 1.8 %collective-permute-start.5 = (bf16[384,256]{1,0:T(8,128)(2,1)S(1)}, bf16[384,256]{1,0:T(8,128)(2,1)S(1)}, u32[]{:S(2)}, u32[]{:S(2)}) collective-permute-start(bf16[384,256]{1,0:T(8,128)(2,1)S(1)} %collective-permute-done.2.refs_1_), channel_id=1, source_target_pairs={{0,1},{1,0},{2,3},{3,2},{4,5},{5,4},{6,7},{7,6},{8,9},{9,8},{10,11... | collective-permute-start | bytes 589832 | tf_op jit(solution)/shard_map/ppermute | solution.py:26
  17.4 2.3 %near.1 = (bf16[544,1536]{1,0:T(8,128)(2,1)S(1)}, f32[544,512]{1,0:T(8,128)S(1)}, f32[544,512]{1,0:T(8,128)S(1)}, f32[544,512]{1,0:T(8,128)S(1)}) custom-call(s32[4]{0:T(128)S(1)} %pad_add_fusion.place_ref, bf16[512,1536]{1,0:T(8,128)(2,1)S(1)} %get-tuple-element.57.rows_ref, bf16[16,1536]{1,0:T(8,128)(2,1)S(1)} %collective-permute-done.inner_ref, ...), custom_call_target="tpu_custom_call" | custom-call | flops 100000000 | tf_op jit(solution)/shard_map/near/pallas_call | solution.py:147
  20.3 1.8 %collective-permute-start.10 = (bf16[384,512]{1,0:T(8,128)(2,1)S(1)}, bf16[384,512]{1,0:T(8,128)(2,1)S(1)}, u32[]{:S(2)}, u32[]{:S(2)}) collective-permute-start(bf16[384,512]{1,0:T(8,128)(2,1)S(1)} %get-tuple-element.75), channel_id=1, source_target_pairs={{0,16},{8,24},{16,0},{24,8},{1,17},{9,25},{17,1},{25,9},{2,18},{10... | collective-permute-start | bytes 1179656 | tf_op jit(solution)/shard_map/ppermute | solution.py:26
  22.1 1.1 %collective-permute-done.5.refs_2_ = bf16[384,256]{1,0:T(8,128)(2,1)S(1)} collective-permute-done((bf16[384,256]{1,0:T(8,128)(2,1)S(1)}, bf16[384,256]{1,0:T(8,128)(2,1)S(1)}, u32[]{:S(2)}, u32[]{:S(2)}) %collective-permute-start.5) | collective-permute-done | bytes 196640 | tf_op jit(solution)/shard_map/ppermute | solution.py:26
  23.2 3.2 %collective-permute-done.7.refs_2_ = bf16[384,256]{1,0:T(8,128)(2,1)S(1)} collective-permute-done((bf16[384,256]{1,0:T(8,128)(2,1)S(1)}, bf16[384,256]{1,0:T(8,128)(2,1)S(1)}, u32[]{:S(2)}, u32[]{:S(2)}) %collective-permute-start.7) | collective-permute-done | bytes 196640 | tf_op jit(solution)/shard_map/ppermute | solution.py:26
  27.8 2.9 %front.3 = (f32[512,256]{1,0:T(8,128)S(1)}, f32[3,256]{1,0:T(4,128)S(1)}) custom-call(s32[4]{0:T(128)S(1)} %pad_add_fusion.place_ref, bf16[544,1536]{1,0:T(8,128)(2,1)S(1)} %get-tuple-element.60.normed_ref, f32[544,512]{1,0:T(8,128)S(1)} %get-tuple-element.68.refs_0_, bf16[384,256]{1,0:T(8,128)(2,1)S(1)} %collective-permute-done.2.refs_1_, ...), custom_call_target="tpu_custom_call" | custom-call | flops 100000000 | tf_op jit(solution)/shard_map/front/pallas_call | solution.py:232
  31.5 1.7 %collective-permute-start.13 = (bf16[48,1536]{1,0:T(8,128)(2,1)S(1)}, bf16[48,1536]{1,0:T(8,128)(2,1)S(1)}, u32[]{:S(2)}, u32[]{:S(2)}) collective-permute-start(bf16[48,1536]{1,0:T(8,128)(2,1)S(1)} %get-tuple-element.86), channel_id=1, source_target_pairs={{0,16},{8,24},{16,0},{24,8},{1,17},{9,25},{17,1},{25,9},{2,18},{10... | collective-permute-start | bytes 442376 | tf_op jit(solution)/shard_map/ppermute | solution.py:26
  33.2 2.9 %front.4 = (f32[512,256]{1,0:T(8,128)S(1)}, f32[3,256]{1,0:T(4,128)S(1)}) custom-call(s32[4]{0:T(128)S(1)} %pad_add_fusion.place_ref, bf16[544,1536]{1,0:T(8,128)(2,1)S(1)} %get-tuple-element.60.normed_ref, f32[544,512]{1,0:T(8,128)S(1)} %get-tuple-element.76.refs_0_, bf16[384,256]{1,0:T(8,128)(2,1)S(1)} %collective-permute-done.3.refs_1_, ...), custom_call_target="tpu_custom_call" | custom-call | flops 4000000000 | tf_op jit(solution)/shard_map/front/pallas_call | solution.py:232
  36.1 2.9 %front.5 = (f32[512,256]{1,0:T(8,128)S(1)}, f32[1,3,768]{2,1,0:T(4,128)S(1)}) custom-call(s32[4]{0:T(128)S(1)} %pad_add_fusion.place_ref, bf16[544,1536]{1,0:T(8,128)(2,1)S(1)} %get-tuple-element.60.normed_ref, f32[3,256]{1,0:T(4,128)S(1)} %get-tuple-element.72.refs_0_, f32[3,256]{1,0:T(4,128)S(1)} %get-tuple-element.80.refs_1_, ...), custom_call_target="tpu_custom_call" | custom-call | flops 100000000 | tf_op jit(solution)/shard_map/front/pallas_call | solution.py:232
  39.3 1.0 %collective-permute-done.14 = f32[1,3,768]{2,1,0:T(4,128)S(1)} collective-permute-done((f32[1,3,768]{2,1,0:T(4,128)S(1)}, f32[1,3,768]{2,1,0:T(4,128)S(1)}, u32[]{:S(2)}, u32[]{:S(2)}) %collective-permute-start.14) | collective-permute-done | bytes 9248 | tf_op jit(solution)/shard_map/ppermute | solution.py:409
  40.3 2.6 %collective-permute-start.15 = (f32[1,3,768]{2,1,0:T(4,128)S(1)}, f32[1,3,768]{2,1,0:T(4,128)S(1)}, u32[]{:S(2)}, u32[]{:S(2)}) collective-permute-start(f32[1,3,768]{2,1,0:T(4,128)S(1)} %pad_maximum_fusion), channel_id=1, source_target_pairs={{0,2},{1,3},{2,0},{3,1},{4,6},{5,7},{6,4},{7,5},{8,10},{9,11},{10,... | collective-permute-start | bytes 27656 | tf_op jit(solution)/shard_map/ppermute | solution.py:409
  43.5 1.1 %collective-permute-done.15 = f32[1,3,768]{2,1,0:T(4,128)S(1)} collective-permute-done((f32[1,3,768]{2,1,0:T(4,128)S(1)}, f32[1,3,768]{2,1,0:T(4,128)S(1)}, u32[]{:S(2)}, u32[]{:S(2)}) %collective-permute-start.15) | collective-permute-done | bytes 9248 | tf_op jit(solution)/shard_map/ppermute | solution.py:409
  44.7 3.1 %collective-permute-start.16 = (f32[1,3,768]{2,1,0:T(4,128)S(1)}, f32[1,3,768]{2,1,0:T(4,128)S(1)}, u32[]{:S(2)}, u32[]{:S(2)}) collective-permute-start(f32[1,3,768]{2,1,0:T(4,128)S(1)} %pad_maximum_fusion.1), channel_id=1, source_target_pairs={{0,4},{1,5},{2,6},{3,7},{4,0},{5,1},{6,2},{7,3},{8,12},{9,13},{10,... | collective-permute-start | bytes 27656 | tf_op jit(solution)/shard_map/ppermute | solution.py:409
  47.8 1.7 %collective-permute-done.16 = f32[1,3,768]{2,1,0:T(4,128)S(1)} collective-permute-done((f32[1,3,768]{2,1,0:T(4,128)S(1)}, f32[1,3,768]{2,1,0:T(4,128)S(1)}, u32[]{:S(2)}, u32[]{:S(2)}) %collective-permute-start.16) | collective-permute-done | bytes 9248 | tf_op jit(solution)/shard_map/ppermute | solution.py:409
  50.9 2.1 %collective-permute-start.19 = (f32[1,3,768]{2,1,0:T(4,128)S(1)}, f32[1,3,768]{2,1,0:T(4,128)S(1)}, u32[]{:S(2)}, u32[]{:S(2)}) collective-permute-start(f32[1,3,768]{2,1,0:T(4,128)S(1)} %pad_maximum_fusion.2.refs_0_), channel_id=1, source_target_pairs={{0,17},{1,16},{2,19},{3,18},{4,21},{5,20},{6,23},{7,22},{8,25},{9,... | collective-permute-start | bytes 27656 | tf_op jit(solution)/shard_map/ppermute | solution.py:409
  53.0 2.2 %collective-permute-done.20.refs_10_ = bf16[144,1536]{1,0:T(8,128)(2,1)S(1)} collective-permute-done((bf16[144,1536]{1,0:T(8,128)(2,1)S(1)}, bf16[144,1536]{1,0:T(8,128)(2,1)S(1)}, u32[]{:S(2)}, u32[]{:S(2)}) %collective-permute-start.20) | collective-permute-done | bytes 442400 | tf_op jit(solution)/shard_map/ppermute | solution.py:26
  56.1 1.5 %collective-permute-done.22.refs_11_ = bf16[48,1536]{1,0:T(8,128)(2,1)S(1)} collective-permute-done((bf16[48,1536]{1,0:T(8,128)(2,1)S(1)}, bf16[48,1536]{1,0:T(8,128)(2,1)S(1)}, u32[]{:S(2)}, u32[]{:S(2)}) %collective-permute-start.22) | collective-permute-done | bytes 147488 | tf_op jit(solution)/shard_map/ppermute | solution.py:26
  57.5 2.9 %back.1 = bf16[512,1536]{1,0:T(8,128)(2,1)} custom-call(s32[4]{0:T(128)S(1)} %pad_add_fusion.place_ref, f32[1,768]{1,0:T(1,128)S(1)} %broadcast_in_dim.12.gain_ref, f32[1,768]{1,0:T(1,128)S(1)} %broadcast_in_dim.13.shift_ref, f32[1,3,768]{2,1,0:T(4,128)S(1)} %pad_maximum_fusion.2.refs_0_, f32[1,3,768]{2,1,0:T(4,128)S(1)} %collective-permute-done.17.refs_1_, ...), custom_call_target="tpu_custom_call" | custom-call | flops 1000000000 | tf_op jit(solution)/shard_map/back/pallas_call | solution.py:330
  (60 shorter events, 8.7 us)
Async XLA Ops:
  0.0 17.4 %collective-permute-start.4 = (bf16[384,1536]{1,0:T(8,128)(2,1)}, bf16[384,1536]{1,0:T(8,128)(2,1)S(1)}, u32[]{:S(2)}, u32[]{:S(2)}) collective-permute-start(bf16[384,1536]{1,0:T(8,128)(2,1)} %refs_0_.1), channel_id=1, source_target_pairs={{0,8},{8,0},{16,24},{24,16},{1,9},{9,1},{17,25},{25,17},{2,10},{10... | collective-permute-start | bytes 3538952 | tf_op jit(solution)/shard_map/ppermute | solution.py:26
  3.1 9.3 %collective-permute-start.2 = (bf16[384,256]{1,0:T(8,128)(2,1)S(1)}, bf16[384,256]{1,0:T(8,128)(2,1)S(1)}, u32[]{:S(2)}, u32[]{:S(2)}) collective-permute-start(bf16[384,256]{1,0:T(8,128)(2,1)S(1)} %get-tuple-element.55), channel_id=1, source_target_pairs={{0,16},{8,24},{16,0},{24,8},{1,17},{9,25},{17,1},{25,9},{2,18},{10... | collective-permute-start | bytes 589832 | tf_op jit(solution)/shard_map/ppermute | solution.py:26
  5.6 9.8 %collective-permute-start.3 = (bf16[384,256]{1,0:T(8,128)(2,1)S(1)}, bf16[384,256]{1,0:T(8,128)(2,1)S(1)}, u32[]{:S(2)}, u32[]{:S(2)}) collective-permute-start(bf16[384,256]{1,0:T(8,128)(2,1)S(1)} %get-tuple-element.56), channel_id=1, source_target_pairs={{0,16},{8,24},{16,0},{24,8},{1,17},{9,25},{17,1},{25,9},{2,18},{10... | collective-permute-start | bytes 589832 | tf_op jit(solution)/shard_map/ppermute | solution.py:26
  7.7 4.7 %collective-permute-start = (bf16[16,1536]{1,0:T(8,128)(2,1)S(1)}, bf16[16,1536]{1,0:T(8,128)(2,1)S(1)}, u32[]{:S(2)}, u32[]{:S(2)}) collective-permute-start(bf16[16,1536]{1,0:T(8,128)(2,1)S(1)} %get-tuple-element.53), channel_id=1, source_target_pairs={{0,1},{1,0},{2,3},{3,2},{4,5},{5,4},{6,7},{7,6},{8,9},{9,8},{10,11... | collective-permute-start | bytes 147464 | tf_op jit(solution)/shard_map/ppermute | solution.py:26
  9.7 2.7 %collective-permute-start.1 = (bf16[16,1536]{1,0:T(8,128)(2,1)S(1)}, bf16[16,1536]{1,0:T(8,128)(2,1)S(1)}, u32[]{:S(2)}, u32[]{:S(2)}) collective-permute-start(bf16[16,1536]{1,0:T(8,128)(2,1)S(1)} %get-tuple-element.54), channel_id=1, source_target_pairs={{1,2},{3,4},{5,6},{2,1},{4,3},{6,5},{9,10},{11,12},{13,14},{10,9},... | collective-permute-start | bytes 147464 | tf_op jit(solution)/shard_map/ppermute | solution.py:383
  15.4 7.8 %collective-permute-start.5 = (bf16[384,256]{1,0:T(8,128)(2,1)S(1)}, bf16[384,256]{1,0:T(8,128)(2,1)S(1)}, u32[]{:S(2)}, u32[]{:S(2)}) collective-permute-start(bf16[384,256]{1,0:T(8,128)(2,1)S(1)} %collective-permute-done.2.refs_1_), channel_id=1, source_target_pairs={{0,1},{1,0},{2,3},{3,2},{4,5},{5,4},{6,7},{7,6},{8,9},{9,8},{10,11... | collective-permute-start | bytes 589832 | tf_op jit(solution)/shard_map/ppermute | solution.py:26
  17.2 9.2 %collective-permute-start.7 = (bf16[384,256]{1,0:T(8,128)(2,1)S(1)}, bf16[384,256]{1,0:T(8,128)(2,1)S(1)}, u32[]{:S(2)}, u32[]{:S(2)}) collective-permute-start(bf16[384,256]{1,0:T(8,128)(2,1)S(1)} %collective-permute-done.3.refs_1_), channel_id=1, source_target_pairs={{0,1},{1,0},{2,3},{3,2},{4,5},{5,4},{6,7},{7,6},{8,9},{9,8},{10,11... | collective-permute-start | bytes 589832 | tf_op jit(solution)/shard_map/ppermute | solution.py:26
  19.8 6.6 %collective-permute-start.6 = (bf16[384,256]{1,0:T(8,128)(2,1)S(1)}, bf16[384,256]{1,0:T(8,128)(2,1)S(1)}, u32[]{:S(2)}, u32[]{:S(2)}) collective-permute-start(bf16[384,256]{1,0:T(8,128)(2,1)S(1)} %collective-permute-done.2.refs_1_), channel_id=1, source_target_pairs={{0,8},{8,0},{16,24},{24,16},{1,9},{9,1},{17,25},{25,17},{2,10},{10... | collective-permute-start | bytes 589832 | tf_op jit(solution)/shard_map/ppermute | solution.py:26
  19.9 6.5 %collective-permute-start.8 = (bf16[384,256]{1,0:T(8,128)(2,1)S(1)}, bf16[384,256]{1,0:T(8,128)(2,1)S(1)}, u32[]{:S(2)}, u32[]{:S(2)}) collective-permute-start(bf16[384,256]{1,0:T(8,128)(2,1)S(1)} %collective-permute-done.3.refs_1_), channel_id=1, source_target_pairs={{0,8},{8,0},{16,24},{24,16},{1,9},{9,1},{17,25},{25,17},{2,10},{10... | collective-permute-start | bytes 589832 | tf_op jit(solution)/shard_map/ppermute | solution.py:26
  20.3 11.1 %collective-permute-start.10 = (bf16[384,512]{1,0:T(8,128)(2,1)S(1)}, bf16[384,512]{1,0:T(8,128)(2,1)S(1)}, u32[]{:S(2)}, u32[]{:S(2)}) collective-permute-start(bf16[384,512]{1,0:T(8,128)(2,1)S(1)} %get-tuple-element.75), channel_id=1, source_target_pairs={{0,16},{8,24},{16,0},{24,8},{1,17},{9,25},{17,1},{25,9},{2,18},{10... | collective-permute-start | bytes 1179656 | tf_op jit(solution)/shard_map/ppermute | solution.py:26
  26.4 1.4 %collective-permute-start.9 = (bf16[384,256]{1,0:T(8,128)(2,1)S(1)}, bf16[384,256]{1,0:T(8,128)(2,1)S(1)}, u32[]{:S(2)}, u32[]{:S(2)}) collective-permute-start(bf16[384,256]{1,0:T(8,128)(2,1)S(1)} %collective-permute-done.5.refs_2_), channel_id=1, source_target_pairs={{0,8},{8,0},{16,24},{24,16},{1,9},{9,1},{17,25},{25,17},{2,10},{10... | collective-permute-start | bytes 589832 | tf_op jit(solution)/shard_map/ppermute | solution.py:26
  26.4 6.8 %collective-permute-start.11 = (bf16[384,256]{1,0:T(8,128)(2,1)S(1)}, bf16[384,256]{1,0:T(8,128)(2,1)S(1)}, u32[]{:S(2)}, u32[]{:S(2)}) collective-permute-start(bf16[384,256]{1,0:T(8,128)(2,1)S(1)} %collective-permute-done.7.refs_2_), channel_id=1, source_target_pairs={{0,8},{8,0},{16,24},{24,16},{1,9},{9,1},{17,25},{25,17},{2,10},{10... | collective-permute-start | bytes 589832 | tf_op jit(solution)/shard_map/ppermute | solution.py:26
  31.5 4.6 %collective-permute-start.12 = (bf16[384,512]{1,0:T(8,128)(2,1)S(1)}, bf16[384,512]{1,0:T(8,128)(2,1)S(1)}, u32[]{:S(2)}, u32[]{:S(2)}) collective-permute-start(bf16[384,512]{1,0:T(8,128)(2,1)S(1)} %collective-permute-done.10.refs_3_), channel_id=1, source_target_pairs={{0,8},{8,0},{16,24},{24,16},{1,9},{9,1},{17,25},{25,17},{2,10},{10... | collective-permute-start | bytes 1179656 | tf_op jit(solution)/shard_map/ppermute | solution.py:26
  31.5 7.5 %collective-permute-start.13 = (bf16[48,1536]{1,0:T(8,128)(2,1)S(1)}, bf16[48,1536]{1,0:T(8,128)(2,1)S(1)}, u32[]{:S(2)}, u32[]{:S(2)}) collective-permute-start(bf16[48,1536]{1,0:T(8,128)(2,1)S(1)} %get-tuple-element.86), channel_id=1, source_target_pairs={{0,16},{8,24},{16,0},{24,8},{1,17},{9,25},{17,1},{25,9},{2,18},{10... | collective-permute-start | bytes 442376 | tf_op jit(solution)/shard_map/ppermute | solution.py:26
  39.0 1.2 %collective-permute-start.14 = (f32[1,3,768]{2,1,0:T(4,128)S(1)}, f32[1,3,768]{2,1,0:T(4,128)S(1)}, u32[]{:S(2)}, u32[]{:S(2)}) collective-permute-start(f32[1,3,768]{2,1,0:T(4,128)S(1)} %get-tuple-element.87), channel_id=1, source_target_pairs={{0,8},{1,9},{2,10},{3,11},{4,12},{5,13},{6,14},{7,15},{8,0},{9,1},... | collective-permute-start | bytes 27656 | tf_op jit(solution)/shard_map/ppermute | solution.py:409
  40.3 4.3 %collective-permute-start.15 = (f32[1,3,768]{2,1,0:T(4,128)S(1)}, f32[1,3,768]{2,1,0:T(4,128)S(1)}, u32[]{:S(2)}, u32[]{:S(2)}) collective-permute-start(f32[1,3,768]{2,1,0:T(4,128)S(1)} %pad_maximum_fusion), channel_id=1, source_target_pairs={{0,2},{1,3},{2,0},{3,1},{4,6},{5,7},{6,4},{7,5},{8,10},{9,11},{10,... | collective-permute-start | bytes 27656 | tf_op jit(solution)/shard_map/ppermute | solution.py:409
  42.9 12.3 %collective-permute-start.20 = (bf16[144,1536]{1,0:T(8,128)(2,1)S(1)}, bf16[144,1536]{1,0:T(8,128)(2,1)S(1)}, u32[]{:S(2)}, u32[]{:S(2)}) collective-permute-start(bf16[144,1536]{1,0:T(8,128)(2,1)S(1)} %get-tuple-element.88), channel_id=1, source_target_pairs={{0,16},{8,24},{16,0},{24,8},{1,17},{9,25},{17,1},{25,9},{2,18},{10... | collective-permute-start | bytes 1327112 | tf_op jit(solution)/shard_map/ppermute | solution.py:26
  44.7 4.8 %collective-permute-start.16 = (f32[1,3,768]{2,1,0:T(4,128)S(1)}, f32[1,3,768]{2,1,0:T(4,128)S(1)}, u32[]{:S(2)}, u32[]{:S(2)}) collective-permute-start(f32[1,3,768]{2,1,0:T(4,128)S(1)} %pad_maximum_fusion.1), channel_id=1, source_target_pairs={{0,4},{1,5},{2,6},{3,7},{4,0},{5,1},{6,2},{7,3},{8,12},{9,13},{10,... | collective-permute-start | bytes 27656 | tf_op jit(solution)/shard_map/ppermute | solution.py:409
  47.8 8.3 %collective-permute-start.21 = (bf16[192,1536]{1,0:T(8,128)(2,1)S(1)}, bf16[192,1536]{1,0:T(8,128)(2,1)S(1)}, u32[]{:S(2)}, u32[]{:S(2)}) collective-permute-start(bf16[192,1536]{1,0:T(8,128)(2,1)S(1)} %copy-done.4), channel_id=1, source_target_pairs={{0,8},{8,0},{16,24},{24,16},{1,9},{9,1},{17,25},{25,17},{2,10},{10... | collective-permute-start | bytes 1769480 | tf_op jit(solution)/shard_map/ppermute | solution.py:26
  49.5 5.7 %collective-permute-start.17 = (f32[1,3,768]{2,1,0:T(4,128)S(1)}, f32[1,3,768]{2,1,0:T(4,128)S(1)}, u32[]{:S(2)}, u32[]{:S(2)}) collective-permute-start(f32[1,3,768]{2,1,0:T(4,128)S(1)} %pad_maximum_fusion.2.refs_0_), channel_id=1, source_target_pairs={{0,1},{1,0},{2,3},{3,2},{4,5},{5,4},{6,7},{7,6},{8,9},{9,8},{10,11... | collective-permute-start | bytes 27656 | tf_op jit(solution)/shard_map/ppermute | solution.py:409
  50.4 5.0 %collective-permute-start.18 = (f32[1,3,768]{2,1,0:T(4,128)S(1)}, f32[1,3,768]{2,1,0:T(4,128)S(1)}, u32[]{:S(2)}, u32[]{:S(2)}) collective-permute-start(f32[1,3,768]{2,1,0:T(4,128)S(1)} %pad_maximum_fusion.2.refs_0_), channel_id=1, source_target_pairs={{0,16},{1,17},{2,18},{3,19},{4,20},{5,21},{6,22},{7,23},{8,24},{9,... | collective-permute-start | bytes 27656 | tf_op jit(solution)/shard_map/ppermute | solution.py:409
  50.9 4.6 %collective-permute-start.19 = (f32[1,3,768]{2,1,0:T(4,128)S(1)}, f32[1,3,768]{2,1,0:T(4,128)S(1)}, u32[]{:S(2)}, u32[]{:S(2)}) collective-permute-start(f32[1,3,768]{2,1,0:T(4,128)S(1)} %pad_maximum_fusion.2.refs_0_), channel_id=1, source_target_pairs={{0,17},{1,16},{2,19},{3,18},{4,21},{5,20},{6,23},{7,22},{8,25},{9,... | collective-permute-start | bytes 27656 | tf_op jit(solution)/shard_map/ppermute | solution.py:409
  55.5 2.0 %collective-permute-start.23 = (bf16[144,1536]{1,0:T(8,128)(2,1)S(1)}, bf16[144,1536]{1,0:T(8,128)(2,1)S(1)}, u32[]{:S(2)}, u32[]{:S(2)}) collective-permute-start(bf16[144,1536]{1,0:T(8,128)(2,1)S(1)} %collective-permute-done.20.refs_10_), channel_id=1, source_target_pairs={{0,8},{8,0},{16,24},{24,16},{1,9},{9,1},{17,25},{25,17},{2,10},{10... | collective-permute-start | bytes 1327112 | tf_op jit(solution)/shard_map/ppermute | solution.py:26
  55.5 2.0 %collective-permute-start.22 = (bf16[48,1536]{1,0:T(8,128)(2,1)S(1)}, bf16[48,1536]{1,0:T(8,128)(2,1)S(1)}, u32[]{:S(2)}, u32[]{:S(2)}) collective-permute-start(bf16[48,1536]{1,0:T(8,128)(2,1)S(1)} %collective-permute-done.13.refs_9_), channel_id=1, source_target_pairs={{0,8},{8,0},{16,24},{24,16},{1,9},{9,1},{17,25},{25,17},{2,10},{10... | collective-permute-start | bytes 442376 | tf_op jit(solution)/shard_map/ppermute | solution.py:26
  (9 other events, 83.9 us)

commit v11 on v10

--- a/solution.py
+++ b/solution.py
@@ -12,6 +12,7 @@
 MIB = 1024 * 1024
 VMEM = pltpu.VMEM
 ORDER = (2, 0, 1)
+SHARED = {2: 3, 0: 4}
 
 
 def cost(flops):
@@ -30,7 +31,7 @@
     wide = two_ref.shape[1]
     channels = shard_ref.shape[1] // 2
     for block, ref in ((2, two_ref), (0, zero_ref)):
-        at = pl.multiple_of(place_ref[3] * channels + block * wide, wide)
+        at = pl.multiple_of(place_ref[SHARED[block]] * channels + block * wide, wide)
         ref[...] = shard_ref[:, pl.ds(at, wide)]
     for i in range(2):
         at = i * channels + wide
@@ -174,7 +175,7 @@
                 weights[pl.ds(at, depth), :] = far_refs[i][...]
                 continue
             for j in range(2):
-                column = pl.multiple_of(lax.bitwise_xor(place_ref[3], j) * wide, wide)
+                column = pl.multiple_of(lax.bitwise_xor(place_ref[SHARED[block]], j) * wide, wide)
                 weights[pl.ds(at, depth), pl.ds(column, wide)] = far_refs[2 * i + j][...]
         far = pl.ds(pl.multiple_of((1 - own // 2) * (2 * depth), 2 * depth), 2 * depth)
         normed = normed_ref[:, far]
@@ -361,8 +362,8 @@
     direct = fsdp_count == 4 and ctx_count == 8
     rows = frames[0]
     gain = ln_gain[None]
-    parity = lax.rem(ctx, 2)
-    place = jnp.stack([fsdp, ctx * row_count, lengths[0], parity]).astype(jnp.int32)
+    parity, pair = lax.rem(ctx, 2), lax.rem(ctx // 2, 2)
+    place = jnp.stack([fsdp, ctx * row_count, lengths[0], parity, pair]).astype(jnp.int32)
     ends = ctx_count - 1
     down, up = [(i, i + 1) for i in range(ends)], [(i + 1, i) for i in range(ends)]
     both = ("fsdp", "ctx")
@@ -377,12 +378,12 @@
         across = swap(w_in, "fsdp", 1)
         inner, outer = edge_rows(place, rows)
         part_rows = w_out.shape[0] // 12
-        normed, *pieces = normalize_rows(rows, gain, w_out, [3 * part_rows, 9 * part_rows])
+        normed, *pieces = normalize_rows(rows, gain, w_out, [4 * part_rows, 8 * part_rows])
         inner = swap(inner, "ctx", 1)
         pairs = [(i, i + 1) for i in range(1, ends, 2)]
         outer = lax.ppermute(outer, "ctx", pairs + [(j, i) for i, j in pairs])
         normed, inner, outer, two, zero = tie(normed, inner, outer, two, zero)
-        two, zero = [two, swap(two, "ctx", 1)], [zero, swap(zero, "ctx", 1)]
+        two, zero = [two, swap(two, "ctx", 1)], [zero, swap(zero, "ctx", 2)]
         normed, *partials = near_product(place, normed, inner, outer, gain, w_in, across)
         partials[2], one, two[0], zero[0] = tie(partials[2], one, two[0], zero[0])
         one = swap(one, "fsdp", 2)

time: 60.6 us -> 62.7 us (1.035)
  waiting for transfers between devices: 16.7 us -> 19.5 us
  starting transfers between devices: 23 us -> 22.1 us
    ppermute x6, waiting for transfers between devices: 4.06 us -> 8.82 us  [others(): lax.ppermute(stats, both, [(member(f, p), member(f ^ df, p ^ dp)) for f i...]
    ppermute x6, starting transfers between devices: 9.59 us -> 7 us  [others(): lax.ppermute(stats, both, [(member(f, p), member(f ^ df, p ^ dp)) for f i...]
    ppermute x17, waiting for transfers between devices: 12.6 us -> 10.7 us  [swap(): lax.ppermute(value, axis, [(i, i ^ bit) for i in range(lax.axis_size(axis...]
    ppermute x17, starting transfers between devices: 12.8 us -> 14.5 us  [swap(): lax.ppermute(value, axis, [(i, i ^ bit) for i in range(lax.axis_size(axis...]
  transfers between devices with their start and end apart: 24 -> 24, of which waited for: 12 -> 11; matrix products, arithmetic and copies ran while one was open for 0% -> 0% of each run, Pallas kernels for 23% -> 23%
where the time goes in v11:
time: 62.7 us; the launch traced here: 62.5 us
  starting transfers between devices  22.1 us (35%)
  waiting for transfers between devices  19.5 us (31%)
  Pallas kernels  17 us (27%)
  local copies, waits for them, and re-layouts  2.81 us (4%)
  between operations  0.87 us (1%)
    ppermute x17, starting transfers between devices, swap(): lax.ppermute(value, axis, [(i, i ^ bit) for i in range(lax.axis_size(axis...  14.5 us
    ppermute x17, waiting for transfers between devices, swap(): lax.ppermute(value, axis, [(i, i ^ bit) for i in range(lax.axis_size(axis...  10.7 us
    ppermute x6, waiting for transfers between devices, others(): lax.ppermute(stats, both, [(member(f, p), member(f ^ df, p ^ dp)) for f i...  8.82 us
    pallas_call x3, Pallas kernels, front_block(): pl.pallas_call(functools.partial(front_kernel, block, len(earlier)), out_...  8.64 us
    ppermute x6, starting transfers between devices, others(): lax.ppermute(stats, both, [(member(f, p), member(f ^ df, p ^ dp)) for f i...  7 us
    pallas_call x1, Pallas kernels, back(): pl.pallas_call(functools.partial(back_kernel, len(stats)), out_shape=jax....  2.95 us
    unnamed x18, local copies, waits for them, and re-layouts  2.71 us
    pallas_call x1, Pallas kernels, near_product(): pl.pallas_call(near_kernel, out_shape=shapes, in_specs=[pl.BlockSpec(memo...  2.33 us
  transfers between devices with their start and end apart: 24, of which 11 were waited for; matrix products, arithmetic and copies ran while one was open for 0% of the time, Pallas kernels for 23%

profile of v11, /device:TPU:0, one launch (start us, length us, event | category | flops | bytes accessed | tf_op | source)
XLA Modules:
  0.0 62.5 jit_solution(2536784204786514176)
XLA Ops:
  3.1 2.6 %collective-permute-start.2 = (bf16[384,256]{1,0:T(8,128)(2,1)S(1)}, bf16[384,256]{1,0:T(8,128)(2,1)S(1)}, u32[]{:S(2)}, u32[]{:S(2)}) collective-permute-start(bf16[384,256]{1,0:T(8,128)(2,1)S(1)} %get-tuple-element.55), channel_id=1, source_target_pairs={{0,16},{8,24},{16,0},{24,8},{1,17},{9,25},{17,1},{25,9},{2,18},{10... | collective-permute-start | bytes 589832 | tf_op jit(solution)/shard_map/ppermute | solution.py:27
  5.7 1.4 %copy-done = bf16[1,512,1536]{2,1,0:T(8,128)(2,1)S(1)} copy-done((bf16[1,512,1536]{2,1,0:T(8,128)(2,1)S(1)}, bf16[1,512,1536]{2,1,0:T(8,128)(2,1)}, u32[]{:S(2)}) %copy-start) | copy-done | bytes 1572888
  7.7 2.0 %collective-permute-start = (bf16[16,1536]{1,0:T(8,128)(2,1)S(1)}, bf16[16,1536]{1,0:T(8,128)(2,1)S(1)}, u32[]{:S(2)}, u32[]{:S(2)}) collective-permute-start(bf16[16,1536]{1,0:T(8,128)(2,1)S(1)} %get-tuple-element.53), channel_id=1, source_target_pairs={{0,1},{1,0},{2,3},{3,2},{4,5},{5,4},{6,7},{7,6},{8,9},{9,8},{10,11... | collective-permute-start | bytes 147464 | tf_op jit(solution)/shard_map/ppermute | solution.py:27
  10.4 1.9 %layer_norm.1 = (bf16[512,1536]{1,0:T(8,128)(2,1)S(1)}, bf16[64,1536]{1,0:T(8,128)(2,1)S(1)}, bf16[128,1536]{1,0:T(8,128)(2,1)S(1)}) custom-call(bf16[512,1536]{1,0:T(8,128)(2,1)S(1)} %bitcast.7, f32[1,1536]{1,0:T(1,128)S(1)} %broadcast_in_dim.14.gain_ref, bf16[192,1536]{1,0:T(8,128)(2,1)S(1)} %copy-done.4), custom_call_target="tpu_custom_call" | custom-call | flops 100000000 | tf_op jit(solution)/shard_map/layer_norm/pallas_call | solution.py:100
  12.4 3.0 %collective-permute-done.3.refs_1_ = bf16[384,256]{1,0:T(8,128)(2,1)S(1)} collective-permute-done((bf16[384,256]{1,0:T(8,128)(2,1)S(1)}, bf16[384,256]{1,0:T(8,128)(2,1)S(1)}, u32[]{:S(2)}, u32[]{:S(2)}) %collective-permute-start.3) | collective-permute-done | bytes 196640 | tf_op jit(solution)/shard_map/ppermute | solution.py:27
  15.4 1.8 %collective-permute-start.5 = (bf16[384,256]{1,0:T(8,128)(2,1)S(1)}, bf16[384,256]{1,0:T(8,128)(2,1)S(1)}, u32[]{:S(2)}, u32[]{:S(2)}) collective-permute-start(bf16[384,256]{1,0:T(8,128)(2,1)S(1)} %collective-permute-done.2.refs_1_), channel_id=1, source_target_pairs={{0,1},{1,0},{2,3},{3,2},{4,5},{5,4},{6,7},{7,6},{8,9},{9,8},{10,11... | collective-permute-start | bytes 589832 | tf_op jit(solution)/shard_map/ppermute | solution.py:27
  17.2 1.6 %collective-permute-start.7 = (bf16[384,256]{1,0:T(8,128)(2,1)S(1)}, bf16[384,256]{1,0:T(8,128)(2,1)S(1)}, u32[]{:S(2)}, u32[]{:S(2)}) collective-permute-start(bf16[384,256]{1,0:T(8,128)(2,1)S(1)} %collective-permute-done.3.refs_1_), channel_id=1, source_target_pairs={{0,2},{1,3},{2,0},{3,1},{4,6},{5,7},{6,4},{7,5},{8,10},{9,11},{10,... | collective-permute-start | bytes 589832 | tf_op jit(solution)/shard_map/ppermute | solution.py:27
  18.8 2.3 %near.1 = (bf16[544,1536]{1,0:T(8,128)(2,1)S(1)}, f32[544,512]{1,0:T(8,128)S(1)}, f32[544,512]{1,0:T(8,128)S(1)}, f32[544,512]{1,0:T(8,128)S(1)}) custom-call(s32[5]{0:T(128)S(1)} %stack.37.place_ref, bf16[512,1536]{1,0:T(8,128)(2,1)S(1)} %get-tuple-element.57.rows_ref, bf16[16,1536]{1,0:T(8,128)(2,1)S(1)} %collective-permute-done.inner_ref, ...), custom_call_target="tpu_custom_call" | custom-call | flops 100000000 | tf_op jit(solution)/shard_map/near/pallas_call | solution.py:148
  21.7 1.5 %collective-permute-start.10 = (bf16[384,512]{1,0:T(8,128)(2,1)S(1)}, bf16[384,512]{1,0:T(8,128)(2,1)S(1)}, u32[]{:S(2)}, u32[]{:S(2)}) collective-permute-start(bf16[384,512]{1,0:T(8,128)(2,1)S(1)} %get-tuple-element.75), channel_id=1, source_target_pairs={{0,16},{8,24},{16,0},{24,8},{1,17},{9,25},{17,1},{25,9},{2,18},{10... | collective-permute-start | bytes 1179656 | tf_op jit(solution)/shard_map/ppermute | solution.py:27
  24.9 2.9 %front.3 = (f32[512,256]{1,0:T(8,128)S(1)}, f32[3,256]{1,0:T(4,128)S(1)}) custom-call(s32[5]{0:T(128)S(1)} %stack.37.place_ref, bf16[544,1536]{1,0:T(8,128)(2,1)S(1)} %get-tuple-element.60.normed_ref, f32[544,512]{1,0:T(8,128)S(1)} %get-tuple-element.68.refs_0_, bf16[384,256]{1,0:T(8,128)(2,1)S(1)} %collective-permute-done.2.refs_1_, ...), custom_call_target="tpu_custom_call" | custom-call | flops 100000000 | tf_op jit(solution)/shard_map/front/pallas_call | solution.py:233
  27.8 5.0 %collective-permute-done.10.refs_3_ = bf16[384,512]{1,0:T(8,128)(2,1)S(1)} collective-permute-done((bf16[384,512]{1,0:T(8,128)(2,1)S(1)}, bf16[384,512]{1,0:T(8,128)(2,1)S(1)}, u32[]{:S(2)}, u32[]{:S(2)}) %collective-permute-start.10) | collective-permute-done | bytes 393248 | tf_op jit(solution)/shard_map/ppermute | solution.py:27
  32.8 1.5 %collective-permute-start.13 = (bf16[64,1536]{1,0:T(8,128)(2,1)S(1)}, bf16[64,1536]{1,0:T(8,128)(2,1)S(1)}, u32[]{:S(2)}, u32[]{:S(2)}) collective-permute-start(bf16[64,1536]{1,0:T(8,128)(2,1)S(1)} %get-tuple-element.86), channel_id=1, source_target_pairs={{0,16},{8,24},{16,0},{24,8},{1,17},{9,25},{17,1},{25,9},{2,18},{10... | collective-permute-start | bytes 589832 | tf_op jit(solution)/shard_map/ppermute | solution.py:27
  34.3 2.9 %front.4 = (f32[512,256]{1,0:T(8,128)S(1)}, f32[3,256]{1,0:T(4,128)S(1)}) custom-call(s32[5]{0:T(128)S(1)} %stack.37.place_ref, bf16[544,1536]{1,0:T(8,128)(2,1)S(1)} %get-tuple-element.60.normed_ref, f32[544,512]{1,0:T(8,128)S(1)} %get-tuple-element.76.refs_0_, bf16[384,256]{1,0:T(8,128)(2,1)S(1)} %collective-permute-done.3.refs_1_, ...), custom_call_target="tpu_custom_call" | custom-call | flops 4000000000 | tf_op jit(solution)/shard_map/front/pallas_call | solution.py:233
  37.2 2.9 %front.5 = (f32[512,256]{1,0:T(8,128)S(1)}, f32[1,3,768]{2,1,0:T(4,128)S(1)}) custom-call(s32[5]{0:T(128)S(1)} %stack.37.place_ref, bf16[544,1536]{1,0:T(8,128)(2,1)S(1)} %get-tuple-element.60.normed_ref, f32[3,256]{1,0:T(4,128)S(1)} %get-tuple-element.72.refs_0_, f32[3,256]{1,0:T(4,128)S(1)} %get-tuple-element.80.refs_1_, ...), custom_call_target="tpu_custom_call" | custom-call | flops 100000000 | tf_op jit(solution)/shard_map/front/pallas_call | solution.py:233
  41.9 1.4 %collective-permute-start.20 = (bf16[128,1536]{1,0:T(8,128)(2,1)S(1)}, bf16[128,1536]{1,0:T(8,128)(2,1)S(1)}, u32[]{:S(2)}, u32[]{:S(2)}) collective-permute-start(bf16[128,1536]{1,0:T(8,128)(2,1)S(1)} %get-tuple-element.88), channel_id=1, source_target_pairs={{0,16},{8,24},{16,0},{24,8},{1,17},{9,25},{17,1},{25,9},{2,18},{10... | collective-permute-start | bytes 1179656 | tf_op jit(solution)/shard_map/ppermute | solution.py:27
  43.3 1.8 %collective-permute-done.15 = f32[1,3,768]{2,1,0:T(4,128)S(1)} collective-permute-done((f32[1,3,768]{2,1,0:T(4,128)S(1)}, f32[1,3,768]{2,1,0:T(4,128)S(1)}, u32[]{:S(2)}, u32[]{:S(2)}) %collective-permute-start.15) | collective-permute-done | bytes 9248 | tf_op jit(solution)/shard_map/ppermute | solution.py:410
  45.2 2.7 %collective-permute-start.16 = (f32[1,3,768]{2,1,0:T(4,128)S(1)}, f32[1,3,768]{2,1,0:T(4,128)S(1)}, u32[]{:S(2)}, u32[]{:S(2)}) collective-permute-start(f32[1,3,768]{2,1,0:T(4,128)S(1)} %pad_maximum_fusion.1), channel_id=1, source_target_pairs={{0,4},{1,5},{2,6},{3,7},{4,0},{5,1},{6,2},{7,3},{8,12},{9,13},{10,... | collective-permute-start | bytes 27656 | tf_op jit(solution)/shard_map/ppermute | solution.py:410
  47.8 2.0 %collective-permute-done.16 = f32[1,3,768]{2,1,0:T(4,128)S(1)} collective-permute-done((f32[1,3,768]{2,1,0:T(4,128)S(1)}, f32[1,3,768]{2,1,0:T(4,128)S(1)}, u32[]{:S(2)}, u32[]{:S(2)}) %collective-permute-start.16) | collective-permute-done | bytes 9248 | tf_op jit(solution)/shard_map/ppermute | solution.py:410
  49.9 1.6 %collective-permute-start.17 = (f32[1,3,768]{2,1,0:T(4,128)S(1)}, f32[1,3,768]{2,1,0:T(4,128)S(1)}, u32[]{:S(2)}, u32[]{:S(2)}) collective-permute-start(f32[1,3,768]{2,1,0:T(4,128)S(1)} %pad_maximum_fusion.2.refs_0_), channel_id=1, source_target_pairs={{0,1},{1,0},{2,3},{3,2},{4,5},{5,4},{6,7},{7,6},{8,9},{9,8},{10,11... | collective-permute-start | bytes 27656 | tf_op jit(solution)/shard_map/ppermute | solution.py:410
  51.5 1.4 %collective-permute-start.18 = (f32[1,3,768]{2,1,0:T(4,128)S(1)}, f32[1,3,768]{2,1,0:T(4,128)S(1)}, u32[]{:S(2)}, u32[]{:S(2)}) collective-permute-start(f32[1,3,768]{2,1,0:T(4,128)S(1)} %pad_maximum_fusion.2.refs_0_), channel_id=1, source_target_pairs={{0,16},{1,17},{2,18},{3,19},{4,20},{5,21},{6,22},{7,23},{8,24},{9,... | collective-permute-start | bytes 27656 | tf_op jit(solution)/shard_map/ppermute | solution.py:410
  53.7 1.5 %collective-permute-done.18.refs_2_ = f32[1,3,768]{2,1,0:T(4,128)S(1)} collective-permute-done((f32[1,3,768]{2,1,0:T(4,128)S(1)}, f32[1,3,768]{2,1,0:T(4,128)S(1)}, u32[]{:S(2)}, u32[]{:S(2)}) %collective-permute-start.18) | collective-permute-done | bytes 9248 | tf_op jit(solution)/shard_map/ppermute | solution.py:410
  55.2 2.3 %collective-permute-done.19.refs_3_ = f32[1,3,768]{2,1,0:T(4,128)S(1)} collective-permute-done((f32[1,3,768]{2,1,0:T(4,128)S(1)}, f32[1,3,768]{2,1,0:T(4,128)S(1)}, u32[]{:S(2)}, u32[]{:S(2)}) %collective-permute-start.19) | collective-permute-done | bytes 9248 | tf_op jit(solution)/shard_map/ppermute | solution.py:410
  58.1 1.5 %collective-permute-done.22.refs_11_ = bf16[64,1536]{1,0:T(8,128)(2,1)S(1)} collective-permute-done((bf16[64,1536]{1,0:T(8,128)(2,1)S(1)}, bf16[64,1536]{1,0:T(8,128)(2,1)S(1)}, u32[]{:S(2)}, u32[]{:S(2)}) %collective-permute-start.22) | collective-permute-done | bytes 196640 | tf_op jit(solution)/shard_map/ppermute | solution.py:27
  59.5 2.9 %back.1 = bf16[512,1536]{1,0:T(8,128)(2,1)} custom-call(s32[5]{0:T(128)S(1)} %stack.37.place_ref, f32[1,768]{1,0:T(1,128)S(1)} %broadcast_in_dim.12.gain_ref, f32[1,768]{1,0:T(1,128)S(1)} %broadcast_in_dim.13.shift_ref, f32[1,3,768]{2,1,0:T(4,128)S(1)} %pad_maximum_fusion.2.refs_0_, f32[1,3,768]{2,1,0:T(4,128)S(1)} %collective-permute-done.17.refs_1_, ...), custom_call_target="tpu_custom_call" | custom-call | flops 1000000000 | tf_op jit(solution)/shard_map/back/pallas_call | solution.py:331
  (60 shorter events, 9.2 us)
Async XLA Ops:
  0.0 18.8 %collective-permute-start.4 = (bf16[384,1536]{1,0:T(8,128)(2,1)}, bf16[384,1536]{1,0:T(8,128)(2,1)S(1)}, u32[]{:S(2)}, u32[]{:S(2)}) collective-permute-start(bf16[384,1536]{1,0:T(8,128)(2,1)} %refs_0_.1), channel_id=1, source_target_pairs={{0,8},{8,0},{16,24},{24,16},{1,9},{9,1},{17,25},{25,17},{2,10},{10... | collective-permute-start | bytes 3538952 | tf_op jit(solution)/shard_map/ppermute | solution.py:27
  3.1 9.3 %collective-permute-start.2 = (bf16[384,256]{1,0:T(8,128)(2,1)S(1)}, bf16[384,256]{1,0:T(8,128)(2,1)S(1)}, u32[]{:S(2)}, u32[]{:S(2)}) collective-permute-start(bf16[384,256]{1,0:T(8,128)(2,1)S(1)} %get-tuple-element.55), channel_id=1, source_target_pairs={{0,16},{8,24},{16,0},{24,8},{1,17},{9,25},{17,1},{25,9},{2,18},{10... | collective-permute-start | bytes 589832 | tf_op jit(solution)/shard_map/ppermute | solution.py:27
  5.6 9.8 %collective-permute-start.3 = (bf16[384,256]{1,0:T(8,128)(2,1)S(1)}, bf16[384,256]{1,0:T(8,128)(2,1)S(1)}, u32[]{:S(2)}, u32[]{:S(2)}) collective-permute-start(bf16[384,256]{1,0:T(8,128)(2,1)S(1)} %get-tuple-element.56), channel_id=1, source_target_pairs={{0,16},{8,24},{16,0},{24,8},{1,17},{9,25},{17,1},{25,9},{2,18},{10... | collective-permute-start | bytes 589832 | tf_op jit(solution)/shard_map/ppermute | solution.py:27
  7.7 4.7 %collective-permute-start = (bf16[16,1536]{1,0:T(8,128)(2,1)S(1)}, bf16[16,1536]{1,0:T(8,128)(2,1)S(1)}, u32[]{:S(2)}, u32[]{:S(2)}) collective-permute-start(bf16[16,1536]{1,0:T(8,128)(2,1)S(1)} %get-tuple-element.53), channel_id=1, source_target_pairs={{0,1},{1,0},{2,3},{3,2},{4,5},{5,4},{6,7},{7,6},{8,9},{9,8},{10,11... | collective-permute-start | bytes 147464 | tf_op jit(solution)/shard_map/ppermute | solution.py:27
  9.7 2.7 %collective-permute-start.1 = (bf16[16,1536]{1,0:T(8,128)(2,1)S(1)}, bf16[16,1536]{1,0:T(8,128)(2,1)S(1)}, u32[]{:S(2)}, u32[]{:S(2)}) collective-permute-start(bf16[16,1536]{1,0:T(8,128)(2,1)S(1)} %get-tuple-element.54), channel_id=1, source_target_pairs={{1,2},{3,4},{5,6},{2,1},{4,3},{6,5},{9,10},{11,12},{13,14},{10,9},... | collective-permute-start | bytes 147464 | tf_op jit(solution)/shard_map/ppermute | solution.py:384
  15.4 7.8 %collective-permute-start.5 = (bf16[384,256]{1,0:T(8,128)(2,1)S(1)}, bf16[384,256]{1,0:T(8,128)(2,1)S(1)}, u32[]{:S(2)}, u32[]{:S(2)}) collective-permute-start(bf16[384,256]{1,0:T(8,128)(2,1)S(1)} %collective-permute-done.2.refs_1_), channel_id=1, source_target_pairs={{0,1},{1,0},{2,3},{3,2},{4,5},{5,4},{6,7},{7,6},{8,9},{9,8},{10,11... | collective-permute-start | bytes 589832 | tf_op jit(solution)/shard_map/ppermute | solution.py:27
  17.2 6.3 %collective-permute-start.7 = (bf16[384,256]{1,0:T(8,128)(2,1)S(1)}, bf16[384,256]{1,0:T(8,128)(2,1)S(1)}, u32[]{:S(2)}, u32[]{:S(2)}) collective-permute-start(bf16[384,256]{1,0:T(8,128)(2,1)S(1)} %collective-permute-done.3.refs_1_), channel_id=1, source_target_pairs={{0,2},{1,3},{2,0},{3,1},{4,6},{5,7},{6,4},{7,5},{8,10},{9,11},{10,... | collective-permute-start | bytes 589832 | tf_op jit(solution)/shard_map/ppermute | solution.py:27
  21.1 2.3 %collective-permute-start.6 = (bf16[384,256]{1,0:T(8,128)(2,1)S(1)}, bf16[384,256]{1,0:T(8,128)(2,1)S(1)}, u32[]{:S(2)}, u32[]{:S(2)}) collective-permute-start(bf16[384,256]{1,0:T(8,128)(2,1)S(1)} %collective-permute-done.2.refs_1_), channel_id=1, source_target_pairs={{0,8},{8,0},{16,24},{24,16},{1,9},{9,1},{17,25},{25,17},{2,10},{10... | collective-permute-start | bytes 589832 | tf_op jit(solution)/shard_map/ppermute | solution.py:27
  21.2 2.3 %collective-permute-start.8 = (bf16[384,256]{1,0:T(8,128)(2,1)S(1)}, bf16[384,256]{1,0:T(8,128)(2,1)S(1)}, u32[]{:S(2)}, u32[]{:S(2)}) collective-permute-start(bf16[384,256]{1,0:T(8,128)(2,1)S(1)} %collective-permute-done.3.refs_1_), channel_id=1, source_target_pairs={{0,8},{8,0},{16,24},{24,16},{1,9},{9,1},{17,25},{25,17},{2,10},{10... | collective-permute-start | bytes 589832 | tf_op jit(solution)/shard_map/ppermute | solution.py:27
  21.7 11.1 %collective-permute-start.10 = (bf16[384,512]{1,0:T(8,128)(2,1)S(1)}, bf16[384,512]{1,0:T(8,128)(2,1)S(1)}, u32[]{:S(2)}, u32[]{:S(2)}) collective-permute-start(bf16[384,512]{1,0:T(8,128)(2,1)S(1)} %get-tuple-element.75), channel_id=1, source_target_pairs={{0,16},{8,24},{16,0},{24,8},{1,17},{9,25},{17,1},{25,9},{2,18},{10... | collective-permute-start | bytes 1179656 | tf_op jit(solution)/shard_map/ppermute | solution.py:27
  23.4 1.4 %collective-permute-start.9 = (bf16[384,256]{1,0:T(8,128)(2,1)S(1)}, bf16[384,256]{1,0:T(8,128)(2,1)S(1)}, u32[]{:S(2)}, u32[]{:S(2)}) collective-permute-start(bf16[384,256]{1,0:T(8,128)(2,1)S(1)} %collective-permute-done.5.refs_2_), channel_id=1, source_target_pairs={{0,8},{8,0},{16,24},{24,16},{1,9},{9,1},{17,25},{25,17},{2,10},{10... | collective-permute-start | bytes 589832 | tf_op jit(solution)/shard_map/ppermute | solution.py:27
  23.4 10.8 %collective-permute-start.11 = (bf16[384,256]{1,0:T(8,128)(2,1)S(1)}, bf16[384,256]{1,0:T(8,128)(2,1)S(1)}, u32[]{:S(2)}, u32[]{:S(2)}) collective-permute-start(bf16[384,256]{1,0:T(8,128)(2,1)S(1)} %collective-permute-done.7.refs_2_), channel_id=1, source_target_pairs={{0,8},{8,0},{16,24},{24,16},{1,9},{9,1},{17,25},{25,17},{2,10},{10... | collective-permute-start | bytes 589832 | tf_op jit(solution)/shard_map/ppermute | solution.py:27
  32.8 4.4 %collective-permute-start.12 = (bf16[384,512]{1,0:T(8,128)(2,1)S(1)}, bf16[384,512]{1,0:T(8,128)(2,1)S(1)}, u32[]{:S(2)}, u32[]{:S(2)}) collective-permute-start(bf16[384,512]{1,0:T(8,128)(2,1)S(1)} %collective-permute-done.10.refs_3_), channel_id=1, source_target_pairs={{0,8},{8,0},{16,24},{24,16},{1,9},{9,1},{17,25},{25,17},{2,10},{10... | collective-permute-start | bytes 1179656 | tf_op jit(solution)/shard_map/ppermute | solution.py:27
  32.8 7.3 %collective-permute-start.13 = (bf16[64,1536]{1,0:T(8,128)(2,1)S(1)}, bf16[64,1536]{1,0:T(8,128)(2,1)S(1)}, u32[]{:S(2)}, u32[]{:S(2)}) collective-permute-start(bf16[64,1536]{1,0:T(8,128)(2,1)S(1)} %get-tuple-element.86), channel_id=1, source_target_pairs={{0,16},{8,24},{16,0},{24,8},{1,17},{9,25},{17,1},{25,9},{2,18},{10... | collective-permute-start | bytes 589832 | tf_op jit(solution)/shard_map/ppermute | solution.py:27
  40.1 1.2 %collective-permute-start.14 = (f32[1,3,768]{2,1,0:T(4,128)S(1)}, f32[1,3,768]{2,1,0:T(4,128)S(1)}, u32[]{:S(2)}, u32[]{:S(2)}) collective-permute-start(f32[1,3,768]{2,1,0:T(4,128)S(1)} %get-tuple-element.87), channel_id=1, source_target_pairs={{0,8},{1,9},{2,10},{3,11},{4,12},{5,13},{6,14},{7,15},{8,0},{9,1},... | collective-permute-start | bytes 27656 | tf_op jit(solution)/shard_map/ppermute | solution.py:410
  41.4 3.8 %collective-permute-start.15 = (f32[1,3,768]{2,1,0:T(4,128)S(1)}, f32[1,3,768]{2,1,0:T(4,128)S(1)}, u32[]{:S(2)}, u32[]{:S(2)}) collective-permute-start(f32[1,3,768]{2,1,0:T(4,128)S(1)} %pad_maximum_fusion), channel_id=1, source_target_pairs={{0,2},{1,3},{2,0},{3,1},{4,6},{5,7},{6,4},{7,5},{8,10},{9,11},{10,... | collective-permute-start | bytes 27656 | tf_op jit(solution)/shard_map/ppermute | solution.py:410
  41.9 11.6 %collective-permute-start.20 = (bf16[128,1536]{1,0:T(8,128)(2,1)S(1)}, bf16[128,1536]{1,0:T(8,128)(2,1)S(1)}, u32[]{:S(2)}, u32[]{:S(2)}) collective-permute-start(bf16[128,1536]{1,0:T(8,128)(2,1)S(1)} %get-tuple-element.88), channel_id=1, source_target_pairs={{0,16},{8,24},{16,0},{24,8},{1,17},{9,25},{17,1},{25,9},{2,18},{10... | collective-permute-start | bytes 1179656 | tf_op jit(solution)/shard_map/ppermute | solution.py:27
  45.2 4.7 %collective-permute-start.16 = (f32[1,3,768]{2,1,0:T(4,128)S(1)}, f32[1,3,768]{2,1,0:T(4,128)S(1)}, u32[]{:S(2)}, u32[]{:S(2)}) collective-permute-start(f32[1,3,768]{2,1,0:T(4,128)S(1)} %pad_maximum_fusion.1), channel_id=1, source_target_pairs={{0,4},{1,5},{2,6},{3,7},{4,0},{5,1},{6,2},{7,3},{8,12},{9,13},{10,... | collective-permute-start | bytes 27656 | tf_op jit(solution)/shard_map/ppermute | solution.py:410
  47.8 10.2 %collective-permute-start.21 = (bf16[192,1536]{1,0:T(8,128)(2,1)S(1)}, bf16[192,1536]{1,0:T(8,128)(2,1)S(1)}, u32[]{:S(2)}, u32[]{:S(2)}) collective-permute-start(bf16[192,1536]{1,0:T(8,128)(2,1)S(1)} %copy-done.4), channel_id=1, source_target_pairs={{0,8},{8,0},{16,24},{24,16},{1,9},{9,1},{17,25},{25,17},{2,10},{10... | collective-permute-start | bytes 1769480 | tf_op jit(solution)/shard_map/ppermute | solution.py:27
  49.9 3.8 %collective-permute-start.17 = (f32[1,3,768]{2,1,0:T(4,128)S(1)}, f32[1,3,768]{2,1,0:T(4,128)S(1)}, u32[]{:S(2)}, u32[]{:S(2)}) collective-permute-start(f32[1,3,768]{2,1,0:T(4,128)S(1)} %pad_maximum_fusion.2.refs_0_), channel_id=1, source_target_pairs={{0,1},{1,0},{2,3},{3,2},{4,5},{5,4},{6,7},{7,6},{8,9},{9,8},{10,11... | collective-permute-start | bytes 27656 | tf_op jit(solution)/shard_map/ppermute | solution.py:410
  51.5 3.7 %collective-permute-start.18 = (f32[1,3,768]{2,1,0:T(4,128)S(1)}, f32[1,3,768]{2,1,0:T(4,128)S(1)}, u32[]{:S(2)}, u32[]{:S(2)}) collective-permute-start(f32[1,3,768]{2,1,0:T(4,128)S(1)} %pad_maximum_fusion.2.refs_0_), channel_id=1, source_target_pairs={{0,16},{1,17},{2,18},{3,19},{4,20},{5,21},{6,22},{7,23},{8,24},{9,... | collective-permute-start | bytes 27656 | tf_op jit(solution)/shard_map/ppermute | solution.py:410
  52.9 4.6 %collective-permute-start.19 = (f32[1,3,768]{2,1,0:T(4,128)S(1)}, f32[1,3,768]{2,1,0:T(4,128)S(1)}, u32[]{:S(2)}, u32[]{:S(2)}) collective-permute-start(f32[1,3,768]{2,1,0:T(4,128)S(1)} %pad_maximum_fusion.2.refs_0_), channel_id=1, source_target_pairs={{0,17},{1,16},{2,19},{3,18},{4,21},{5,20},{6,23},{7,22},{8,25},{9,... | collective-permute-start | bytes 27656 | tf_op jit(solution)/shard_map/ppermute | solution.py:410
  57.5 2.0 %collective-permute-start.23 = (bf16[128,1536]{1,0:T(8,128)(2,1)S(1)}, bf16[128,1536]{1,0:T(8,128)(2,1)S(1)}, u32[]{:S(2)}, u32[]{:S(2)}) collective-permute-start(bf16[128,1536]{1,0:T(8,128)(2,1)S(1)} %collective-permute-done.20.refs_10_), channel_id=1, source_target_pairs={{0,8},{8,0},{16,24},{24,16},{1,9},{9,1},{17,25},{25,17},{2,10},{10... | collective-permute-start | bytes 1179656 | tf_op jit(solution)/shard_map/ppermute | solution.py:27
  57.5 2.0 %collective-permute-start.22 = (bf16[64,1536]{1,0:T(8,128)(2,1)S(1)}, bf16[64,1536]{1,0:T(8,128)(2,1)S(1)}, u32[]{:S(2)}, u32[]{:S(2)}) collective-permute-start(bf16[64,1536]{1,0:T(8,128)(2,1)S(1)} %collective-permute-done.13.refs_9_), channel_id=1, source_target_pairs={{0,8},{8,0},{16,24},{24,16},{1,9},{9,1},{17,25},{25,17},{2,10},{10... | collective-permute-start | bytes 589832 | tf_op jit(solution)/shard_map/ppermute | solution.py:27
  (9 other events, 84.2 us)

commit v12 on v11

--- a/solution.py
+++ b/solution.py
@@ -374,7 +374,7 @@
 
     if direct:
         two, zero, one = cut(place, w_in, wide)
-        two, zero = swap(two, "fsdp", 2), swap(zero, "fsdp", 2)
+        two, zero, one = (swap(part, "fsdp", 2) for part in (two, zero, one))
         across = swap(w_in, "fsdp", 1)
         inner, outer = edge_rows(place, rows)
         part_rows = w_out.shape[0] // 12
@@ -385,17 +385,17 @@
         normed, inner, outer, two, zero = tie(normed, inner, outer, two, zero)
         two, zero = [two, swap(two, "ctx", 1)], [zero, swap(zero, "ctx", 2)]
         normed, *partials = near_product(place, normed, inner, outer, gain, w_in, across)
-        partials[2], one, two[0], zero[0] = tie(partials[2], one, two[0], zero[0])
-        one = swap(one, "fsdp", 2)
+        partials[2], two[0], zero[0] = tie(partials[2], two[0], zero[0])
         two.append(swap(two[0], "fsdp", 1))
         zero.append(swap(zero[0], "fsdp", 1))
         partials[2], *parts = tie(partials[2], *two, *zero, w_out)
         two, zero, w_out = parts[:3], parts[3:6], parts[6]
         two.append(swap(two[1], "fsdp", 1))
         zero.append(swap(zero[1], "fsdp", 1))
+        partials[2], one = tie(partials[2], one)
+        beyond_one = swap(one, "fsdp", 1)
         conv_two, stat_two = front(2, [partials[2], *two])
-        conv_two, partials[0], one = tie(conv_two, partials[0], one)
-        beyond_one = swap(one, "fsdp", 1)
+        conv_two, partials[0] = tie(conv_two, partials[0])
         pieces = [swap(piece, "fsdp", 2) for piece in pieces]
         conv_zero, stat_zero = front(0, [partials[0], *zero])
         conv_zero, partials[1] = tie(conv_zero, partials[1])

time: 62.7 us -> 57.5 us (0.917)
  waiting for transfers between devices: 19.5 us -> 11.7 us
  starting transfers between devices: 22.1 us -> 24.8 us
    ppermute x17, waiting for transfers between devices: 10.7 us -> 4.58 us  [swap(): lax.ppermute(value, axis, [(i, i ^ bit) for i in range(lax.axis_size(axis...]
    ppermute x6, starting transfers between devices: 7 us -> 10 us  [others(): lax.ppermute(stats, both, [(member(f, p), member(f ^ df, p ^ dp)) for f i...]
    ppermute x6, waiting for transfers between devices: 8.82 us -> 7.17 us  [others(): lax.ppermute(stats, both, [(member(f, p), member(f ^ df, p ^ dp)) for f i...]
  transfers between devices with their start and end apart: 24 -> 24, of which waited for: 11 -> 9; matrix products, arithmetic and copies ran while one was open for 0% -> 0% of each run, Pallas kernels for 23% -> 25%
where the time goes in v12:
time: 57.5 us; the launch traced here: 57.3 us
  starting transfers between devices  24.8 us (43%)
  Pallas kernels  17 us (30%)
  waiting for transfers between devices  11.7 us (20%)
  local copies, waits for them, and re-layouts  2.81 us (5%)
  between operations  0.85 us (1%)
    ppermute x17, starting transfers between devices, swap(): lax.ppermute(value, axis, [(i, i ^ bit) for i in range(lax.axis_size(axis...  14.1 us
    ppermute x6, starting transfers between devices, others(): lax.ppermute(stats, both, [(member(f, p), member(f ^ df, p ^ dp)) for f i...  10 us
    pallas_call x3, Pallas kernels, front_block(): pl.pallas_call(functools.partial(front_kernel, block, len(earlier)), out_...  8.64 us
    ppermute x6, waiting for transfers between devices, others(): lax.ppermute(stats, both, [(member(f, p), member(f ^ df, p ^ dp)) for f i...  7.17 us
    ppermute x17, waiting for transfers between devices, swap(): lax.ppermute(value, axis, [(i, i ^ bit) for i in range(lax.axis_size(axis...  4.58 us
    pallas_call x1, Pallas kernels, back(): pl.pallas_call(functools.partial(back_kernel, len(stats)), out_shape=jax....  2.95 us
    unnamed x18, local copies, waits for them, and re-layouts  2.71 us
    pallas_call x1, Pallas kernels, near_product(): pl.pallas_call(near_kernel, out_shape=shapes, in_specs=[pl.BlockSpec(memo...  2.34 us
  transfers between devices with their start and end apart: 24, of which 9 were waited for; matrix products, arithmetic and copies ran while one was open for 0% of the time, Pallas kernels for 25%

profile of v12, /device:TPU:0, one launch (start us, length us, event | category | flops | bytes accessed | tf_op | source)
XLA Modules:
  0.0 57.3 jit_solution(10083815830269080129)
XLA Ops:
  1.2 1.3 %copy-done.2 = bf16[384,1536]{1,0:T(8,128)(2,1)S(1)} copy-done((bf16[384,1536]{1,0:T(8,128)(2,1)S(1)}, bf16[384,1536]{1,0:T(8,128)(2,1)}, u32[]{:S(2)}) %copy-start.2) | copy-done | bytes 1179672
  3.1 2.6 %collective-permute-start.2 = (bf16[384,256]{1,0:T(8,128)(2,1)S(1)}, bf16[384,256]{1,0:T(8,128)(2,1)S(1)}, u32[]{:S(2)}, u32[]{:S(2)}) collective-permute-start(bf16[384,256]{1,0:T(8,128)(2,1)S(1)} %get-tuple-element.55), channel_id=1, source_target_pairs={{0,16},{8,24},{16,0},{24,8},{1,17},{9,25},{17,1},{25,9},{2,18},{10... | collective-permute-start | bytes 589832 | tf_op jit(solution)/shard_map/ppermute | solution.py:27
  5.7 1.4 %copy-done = bf16[1,512,1536]{2,1,0:T(8,128)(2,1)S(1)} copy-done((bf16[1,512,1536]{2,1,0:T(8,128)(2,1)S(1)}, bf16[1,512,1536]{2,1,0:T(8,128)(2,1)}, u32[]{:S(2)}) %copy-start) | copy-done | bytes 1572888
  7.7 2.0 %collective-permute-start = (bf16[16,1536]{1,0:T(8,128)(2,1)S(1)}, bf16[16,1536]{1,0:T(8,128)(2,1)S(1)}, u32[]{:S(2)}, u32[]{:S(2)}) collective-permute-start(bf16[16,1536]{1,0:T(8,128)(2,1)S(1)} %get-tuple-element.53), channel_id=1, source_target_pairs={{0,1},{1,0},{2,3},{3,2},{4,5},{5,4},{6,7},{7,6},{8,9},{9,8},{10,11... | collective-permute-start | bytes 147464 | tf_op jit(solution)/shard_map/ppermute | solution.py:27
  10.4 1.9 %layer_norm.1 = (bf16[512,1536]{1,0:T(8,128)(2,1)S(1)}, bf16[64,1536]{1,0:T(8,128)(2,1)S(1)}, bf16[128,1536]{1,0:T(8,128)(2,1)S(1)}) custom-call(bf16[512,1536]{1,0:T(8,128)(2,1)S(1)} %bitcast.7, f32[1,1536]{1,0:T(1,128)S(1)} %broadcast_in_dim.14.gain_ref, bf16[192,1536]{1,0:T(8,128)(2,1)S(1)} %copy-done.4), custom_call_target="tpu_custom_call" | custom-call | flops 100000000 | tf_op jit(solution)/shard_map/layer_norm/pallas_call | solution.py:100
  12.4 1.6 %collective-permute-start.9 = (bf16[384,512]{1,0:T(8,128)(2,1)S(1)}, bf16[384,512]{1,0:T(8,128)(2,1)S(1)}, u32[]{:S(2)}, u32[]{:S(2)}) collective-permute-start(bf16[384,512]{1,0:T(8,128)(2,1)S(1)} %get-tuple-element.68), channel_id=1, source_target_pairs={{0,16},{8,24},{16,0},{24,8},{1,17},{9,25},{17,1},{25,9},{2,18},{10... | collective-permute-start | bytes 1179656 | tf_op jit(solution)/shard_map/ppermute | solution.py:27
  14.0 1.6 %collective-permute-done.3.refs_1_ = bf16[384,256]{1,0:T(8,128)(2,1)S(1)} collective-permute-done((bf16[384,256]{1,0:T(8,128)(2,1)S(1)}, bf16[384,256]{1,0:T(8,128)(2,1)S(1)}, u32[]{:S(2)}, u32[]{:S(2)}) %collective-permute-start.3) | collective-permute-done | bytes 196640 | tf_op jit(solution)/shard_map/ppermute | solution.py:27
  15.6 2.7 %collective-permute-start.5 = (bf16[384,256]{1,0:T(8,128)(2,1)S(1)}, bf16[384,256]{1,0:T(8,128)(2,1)S(1)}, u32[]{:S(2)}, u32[]{:S(2)}) collective-permute-start(bf16[384,256]{1,0:T(8,128)(2,1)S(1)} %collective-permute-done.2.refs_1_), channel_id=1, source_target_pairs={{0,1},{1,0},{2,3},{3,2},{4,5},{5,4},{6,7},{7,6},{8,9},{9,8},{10,11... | collective-permute-start | bytes 589832 | tf_op jit(solution)/shard_map/ppermute | solution.py:27
  18.3 1.6 %collective-permute-start.7 = (bf16[384,256]{1,0:T(8,128)(2,1)S(1)}, bf16[384,256]{1,0:T(8,128)(2,1)S(1)}, u32[]{:S(2)}, u32[]{:S(2)}) collective-permute-start(bf16[384,256]{1,0:T(8,128)(2,1)S(1)} %collective-permute-done.3.refs_1_), channel_id=1, source_target_pairs={{0,2},{1,3},{2,0},{3,1},{4,6},{5,7},{6,4},{7,5},{8,10},{9,11},{10,... | collective-permute-start | bytes 589832 | tf_op jit(solution)/shard_map/ppermute | solution.py:27
  19.9 2.3 %near.1 = (bf16[544,1536]{1,0:T(8,128)(2,1)S(1)}, f32[544,512]{1,0:T(8,128)S(1)}, f32[544,512]{1,0:T(8,128)S(1)}, f32[544,512]{1,0:T(8,128)S(1)}) custom-call(s32[5]{0:T(128)S(1)} %stack.37.place_ref, bf16[512,1536]{1,0:T(8,128)(2,1)S(1)} %get-tuple-element.57.rows_ref, bf16[16,1536]{1,0:T(8,128)(2,1)S(1)} %collective-permute-done.inner_ref, ...), custom_call_target="tpu_custom_call" | custom-call | flops 100000000 | tf_op jit(solution)/shard_map/near/pallas_call | solution.py:148
  22.8 1.2 %collective-permute-done.7.refs_2_ = bf16[384,256]{1,0:T(8,128)(2,1)S(1)} collective-permute-done((bf16[384,256]{1,0:T(8,128)(2,1)S(1)}, bf16[384,256]{1,0:T(8,128)(2,1)S(1)}, u32[]{:S(2)}, u32[]{:S(2)}) %collective-permute-start.7) | collective-permute-done | bytes 196640 | tf_op jit(solution)/shard_map/ppermute | solution.py:27
  25.6 2.9 %front.3 = (f32[512,256]{1,0:T(8,128)S(1)}, f32[3,256]{1,0:T(4,128)S(1)}) custom-call(s32[5]{0:T(128)S(1)} %stack.37.place_ref, bf16[544,1536]{1,0:T(8,128)(2,1)S(1)} %get-tuple-element.60.normed_ref, f32[544,512]{1,0:T(8,128)S(1)} %get-tuple-element.69.refs_0_, bf16[384,256]{1,0:T(8,128)(2,1)S(1)} %collective-permute-done.2.refs_1_, ...), custom_call_target="tpu_custom_call" | custom-call | flops 100000000 | tf_op jit(solution)/shard_map/front/pallas_call | solution.py:233
  28.5 2.9 %front.4 = (f32[512,256]{1,0:T(8,128)S(1)}, f32[3,256]{1,0:T(4,128)S(1)}) custom-call(s32[5]{0:T(128)S(1)} %stack.37.place_ref, bf16[544,1536]{1,0:T(8,128)(2,1)S(1)} %get-tuple-element.60.normed_ref, f32[544,512]{1,0:T(8,128)S(1)} %get-tuple-element.76.refs_0_, bf16[384,256]{1,0:T(8,128)(2,1)S(1)} %collective-permute-done.3.refs_1_, ...), custom_call_target="tpu_custom_call" | custom-call | flops 4000000000 | tf_op jit(solution)/shard_map/front/pallas_call | solution.py:233
  31.4 2.9 %front.5 = (f32[512,256]{1,0:T(8,128)S(1)}, f32[1,3,768]{2,1,0:T(4,128)S(1)}) custom-call(s32[5]{0:T(128)S(1)} %stack.37.place_ref, bf16[544,1536]{1,0:T(8,128)(2,1)S(1)} %get-tuple-element.60.normed_ref, f32[3,256]{1,0:T(4,128)S(1)} %get-tuple-element.73.refs_0_, f32[3,256]{1,0:T(4,128)S(1)} %get-tuple-element.80.refs_1_, ...), custom_call_target="tpu_custom_call" | custom-call | flops 100000000 | tf_op jit(solution)/shard_map/front/pallas_call | solution.py:233
  35.6 2.2 %collective-permute-start.15 = (f32[1,3,768]{2,1,0:T(4,128)S(1)}, f32[1,3,768]{2,1,0:T(4,128)S(1)}, u32[]{:S(2)}, u32[]{:S(2)}) collective-permute-start(f32[1,3,768]{2,1,0:T(4,128)S(1)} %pad_maximum_fusion), channel_id=1, source_target_pairs={{0,2},{1,3},{2,0},{3,1},{4,6},{5,7},{6,4},{7,5},{8,10},{9,11},{10,... | collective-permute-start | bytes 27656 | tf_op jit(solution)/shard_map/ppermute | solution.py:410
  38.3 1.2 %collective-permute-done.15 = f32[1,3,768]{2,1,0:T(4,128)S(1)} collective-permute-done((f32[1,3,768]{2,1,0:T(4,128)S(1)}, f32[1,3,768]{2,1,0:T(4,128)S(1)}, u32[]{:S(2)}, u32[]{:S(2)}) %collective-permute-start.15) | collective-permute-done | bytes 9248 | tf_op jit(solution)/shard_map/ppermute | solution.py:410
  39.5 3.1 %collective-permute-start.16 = (f32[1,3,768]{2,1,0:T(4,128)S(1)}, f32[1,3,768]{2,1,0:T(4,128)S(1)}, u32[]{:S(2)}, u32[]{:S(2)}) collective-permute-start(f32[1,3,768]{2,1,0:T(4,128)S(1)} %pad_maximum_fusion.1), channel_id=1, source_target_pairs={{0,4},{1,5},{2,6},{3,7},{4,0},{5,1},{6,2},{7,3},{8,12},{9,13},{10,... | collective-permute-start | bytes 27656 | tf_op jit(solution)/shard_map/ppermute | solution.py:410
  42.6 1.7 %collective-permute-done.16 = f32[1,3,768]{2,1,0:T(4,128)S(1)} collective-permute-done((f32[1,3,768]{2,1,0:T(4,128)S(1)}, f32[1,3,768]{2,1,0:T(4,128)S(1)}, u32[]{:S(2)}, u32[]{:S(2)}) %collective-permute-start.16) | collective-permute-done | bytes 9248 | tf_op jit(solution)/shard_map/ppermute | solution.py:410
  44.3 2.9 %collective-permute-start.17 = (f32[1,3,768]{2,1,0:T(4,128)S(1)}, f32[1,3,768]{2,1,0:T(4,128)S(1)}, u32[]{:S(2)}, u32[]{:S(2)}) collective-permute-start(f32[1,3,768]{2,1,0:T(4,128)S(1)} %pad_maximum_fusion.2.refs_0_), channel_id=1, source_target_pairs={{0,1},{1,0},{2,3},{3,2},{4,5},{5,4},{6,7},{7,6},{8,9},{9,8},{10,11... | collective-permute-start | bytes 27656 | tf_op jit(solution)/shard_map/ppermute | solution.py:410
  47.8 1.0 %collective-permute-start.19 = (f32[1,3,768]{2,1,0:T(4,128)S(1)}, f32[1,3,768]{2,1,0:T(4,128)S(1)}, u32[]{:S(2)}, u32[]{:S(2)}) collective-permute-start(f32[1,3,768]{2,1,0:T(4,128)S(1)} %pad_maximum_fusion.2.refs_0_), channel_id=1, source_target_pairs={{0,17},{1,16},{2,19},{3,18},{4,21},{5,20},{6,23},{7,22},{8,25},{9,... | collective-permute-start | bytes 27656 | tf_op jit(solution)/shard_map/ppermute | solution.py:410
  49.0 1.9 %collective-permute-done.18.refs_2_ = f32[1,3,768]{2,1,0:T(4,128)S(1)} collective-permute-done((f32[1,3,768]{2,1,0:T(4,128)S(1)}, f32[1,3,768]{2,1,0:T(4,128)S(1)}, u32[]{:S(2)}, u32[]{:S(2)}) %collective-permute-start.18) | collective-permute-done | bytes 9248 | tf_op jit(solution)/shard_map/ppermute | solution.py:410
  50.9 1.4 %collective-permute-done.19.refs_3_ = f32[1,3,768]{2,1,0:T(4,128)S(1)} collective-permute-done((f32[1,3,768]{2,1,0:T(4,128)S(1)}, f32[1,3,768]{2,1,0:T(4,128)S(1)}, u32[]{:S(2)}, u32[]{:S(2)}) %collective-permute-start.19) | collective-permute-done | bytes 9248 | tf_op jit(solution)/shard_map/ppermute | solution.py:410
  52.9 1.5 %collective-permute-done.22.refs_11_ = bf16[64,1536]{1,0:T(8,128)(2,1)S(1)} collective-permute-done((bf16[64,1536]{1,0:T(8,128)(2,1)S(1)}, bf16[64,1536]{1,0:T(8,128)(2,1)S(1)}, u32[]{:S(2)}, u32[]{:S(2)}) %collective-permute-start.22) | collective-permute-done | bytes 196640 | tf_op jit(solution)/shard_map/ppermute | solution.py:27
  54.4 2.9 %back.1 = bf16[512,1536]{1,0:T(8,128)(2,1)} custom-call(s32[5]{0:T(128)S(1)} %stack.37.place_ref, f32[1,768]{1,0:T(1,128)S(1)} %broadcast_in_dim.12.gain_ref, f32[1,768]{1,0:T(1,128)S(1)} %broadcast_in_dim.13.shift_ref, f32[1,3,768]{2,1,0:T(4,128)S(1)} %pad_maximum_fusion.2.refs_0_, f32[1,3,768]{2,1,0:T(4,128)S(1)} %collective-permute-done.17.refs_1_, ...), custom_call_target="tpu_custom_call" | custom-call | flops 1000000000 | tf_op jit(solution)/shard_map/back/pallas_call | solution.py:331
  (60 shorter events, 7.8 us)
Async XLA Ops:
  0.0 19.9 %collective-permute-start.4 = (bf16[384,1536]{1,0:T(8,128)(2,1)}, bf16[384,1536]{1,0:T(8,128)(2,1)S(1)}, u32[]{:S(2)}, u32[]{:S(2)}) collective-permute-start(bf16[384,1536]{1,0:T(8,128)(2,1)} %refs_0_.1), channel_id=1, source_target_pairs={{0,8},{8,0},{16,24},{24,16},{1,9},{9,1},{17,25},{25,17},{2,10},{10... | collective-permute-start | bytes 3538952 | tf_op jit(solution)/shard_map/ppermute | solution.py:27
  3.1 10.9 %collective-permute-start.2 = (bf16[384,256]{1,0:T(8,128)(2,1)S(1)}, bf16[384,256]{1,0:T(8,128)(2,1)S(1)}, u32[]{:S(2)}, u32[]{:S(2)}) collective-permute-start(bf16[384,256]{1,0:T(8,128)(2,1)S(1)} %get-tuple-element.55), channel_id=1, source_target_pairs={{0,16},{8,24},{16,0},{24,8},{1,17},{9,25},{17,1},{25,9},{2,18},{10... | collective-permute-start | bytes 589832 | tf_op jit(solution)/shard_map/ppermute | solution.py:27
  5.6 10.0 %collective-permute-start.3 = (bf16[384,256]{1,0:T(8,128)(2,1)S(1)}, bf16[384,256]{1,0:T(8,128)(2,1)S(1)}, u32[]{:S(2)}, u32[]{:S(2)}) collective-permute-start(bf16[384,256]{1,0:T(8,128)(2,1)S(1)} %get-tuple-element.56), channel_id=1, source_target_pairs={{0,16},{8,24},{16,0},{24,8},{1,17},{9,25},{17,1},{25,9},{2,18},{10... | collective-permute-start | bytes 589832 | tf_op jit(solution)/shard_map/ppermute | solution.py:27
  7.7 4.7 %collective-permute-start = (bf16[16,1536]{1,0:T(8,128)(2,1)S(1)}, bf16[16,1536]{1,0:T(8,128)(2,1)S(1)}, u32[]{:S(2)}, u32[]{:S(2)}) collective-permute-start(bf16[16,1536]{1,0:T(8,128)(2,1)S(1)} %get-tuple-element.53), channel_id=1, source_target_pairs={{0,1},{1,0},{2,3},{3,2},{4,5},{5,4},{6,7},{7,6},{8,9},{9,8},{10,11... | collective-permute-start | bytes 147464 | tf_op jit(solution)/shard_map/ppermute | solution.py:27
  9.7 4.2 %collective-permute-start.1 = (bf16[16,1536]{1,0:T(8,128)(2,1)S(1)}, bf16[16,1536]{1,0:T(8,128)(2,1)S(1)}, u32[]{:S(2)}, u32[]{:S(2)}) collective-permute-start(bf16[16,1536]{1,0:T(8,128)(2,1)S(1)} %get-tuple-element.54), channel_id=1, source_target_pairs={{1,2},{3,4},{5,6},{2,1},{4,3},{6,5},{9,10},{11,12},{13,14},{10,9},... | collective-permute-start | bytes 147464 | tf_op jit(solution)/shard_map/ppermute | solution.py:384
  12.4 12.2 %collective-permute-start.9 = (bf16[384,512]{1,0:T(8,128)(2,1)S(1)}, bf16[384,512]{1,0:T(8,128)(2,1)S(1)}, u32[]{:S(2)}, u32[]{:S(2)}) collective-permute-start(bf16[384,512]{1,0:T(8,128)(2,1)S(1)} %get-tuple-element.68), channel_id=1, source_target_pairs={{0,16},{8,24},{16,0},{24,8},{1,17},{9,25},{17,1},{25,9},{2,18},{10... | collective-permute-start | bytes 1179656 | tf_op jit(solution)/shard_map/ppermute | solution.py:27
  15.6 7.2 %collective-permute-start.5 = (bf16[384,256]{1,0:T(8,128)(2,1)S(1)}, bf16[384,256]{1,0:T(8,128)(2,1)S(1)}, u32[]{:S(2)}, u32[]{:S(2)}) collective-permute-start(bf16[384,256]{1,0:T(8,128)(2,1)S(1)} %collective-permute-done.2.refs_1_), channel_id=1, source_target_pairs={{0,1},{1,0},{2,3},{3,2},{4,5},{5,4},{6,7},{7,6},{8,9},{9,8},{10,11... | collective-permute-start | bytes 589832 | tf_op jit(solution)/shard_map/ppermute | solution.py:27
  18.3 5.7 %collective-permute-start.7 = (bf16[384,256]{1,0:T(8,128)(2,1)S(1)}, bf16[384,256]{1,0:T(8,128)(2,1)S(1)}, u32[]{:S(2)}, u32[]{:S(2)}) collective-permute-start(bf16[384,256]{1,0:T(8,128)(2,1)S(1)} %collective-permute-done.3.refs_1_), channel_id=1, source_target_pairs={{0,2},{1,3},{2,0},{3,1},{4,6},{5,7},{6,4},{7,5},{8,10},{9,11},{10,... | collective-permute-start | bytes 589832 | tf_op jit(solution)/shard_map/ppermute | solution.py:27
  22.2 1.7 %collective-permute-start.6 = (bf16[384,256]{1,0:T(8,128)(2,1)S(1)}, bf16[384,256]{1,0:T(8,128)(2,1)S(1)}, u32[]{:S(2)}, u32[]{:S(2)}) collective-permute-start(bf16[384,256]{1,0:T(8,128)(2,1)S(1)} %collective-permute-done.2.refs_1_), channel_id=1, source_target_pairs={{0,8},{8,0},{16,24},{24,16},{1,9},{9,1},{17,25},{25,17},{2,10},{10... | collective-permute-start | bytes 589832 | tf_op jit(solution)/shard_map/ppermute | solution.py:27
  22.3 1.7 %collective-permute-start.8 = (bf16[384,256]{1,0:T(8,128)(2,1)S(1)}, bf16[384,256]{1,0:T(8,128)(2,1)S(1)}, u32[]{:S(2)}, u32[]{:S(2)}) collective-permute-start(bf16[384,256]{1,0:T(8,128)(2,1)S(1)} %collective-permute-done.3.refs_1_), channel_id=1, source_target_pairs={{0,8},{8,0},{16,24},{24,16},{1,9},{9,1},{17,25},{25,17},{2,10},{10... | collective-permute-start | bytes 589832 | tf_op jit(solution)/shard_map/ppermute | solution.py:27
  24.0 1.6 %collective-permute-start.10 = (bf16[384,256]{1,0:T(8,128)(2,1)S(1)}, bf16[384,256]{1,0:T(8,128)(2,1)S(1)}, u32[]{:S(2)}, u32[]{:S(2)}) collective-permute-start(bf16[384,256]{1,0:T(8,128)(2,1)S(1)} %collective-permute-done.5.refs_2_), channel_id=1, source_target_pairs={{0,8},{8,0},{16,24},{24,16},{1,9},{9,1},{17,25},{25,17},{2,10},{10... | collective-permute-start | bytes 589832 | tf_op jit(solution)/shard_map/ppermute | solution.py:27
  24.3 4.2 %collective-permute-start.11 = (bf16[384,256]{1,0:T(8,128)(2,1)S(1)}, bf16[384,256]{1,0:T(8,128)(2,1)S(1)}, u32[]{:S(2)}, u32[]{:S(2)}) collective-permute-start(bf16[384,256]{1,0:T(8,128)(2,1)S(1)} %collective-permute-done.7.refs_2_), channel_id=1, source_target_pairs={{0,8},{8,0},{16,24},{24,16},{1,9},{9,1},{17,25},{25,17},{2,10},{10... | collective-permute-start | bytes 589832 | tf_op jit(solution)/shard_map/ppermute | solution.py:27
  24.6 6.8 %collective-permute-start.12 = (bf16[384,512]{1,0:T(8,128)(2,1)S(1)}, bf16[384,512]{1,0:T(8,128)(2,1)S(1)}, u32[]{:S(2)}, u32[]{:S(2)}) collective-permute-start(bf16[384,512]{1,0:T(8,128)(2,1)S(1)} %collective-permute-done.9.refs_3_), channel_id=1, source_target_pairs={{0,8},{8,0},{16,24},{24,16},{1,9},{9,1},{17,25},{25,17},{2,10},{10... | collective-permute-start | bytes 1179656 | tf_op jit(solution)/shard_map/ppermute | solution.py:27
  24.8 9.5 %collective-permute-start.13 = (bf16[64,1536]{1,0:T(8,128)(2,1)S(1)}, bf16[64,1536]{1,0:T(8,128)(2,1)S(1)}, u32[]{:S(2)}, u32[]{:S(2)}) collective-permute-start(bf16[64,1536]{1,0:T(8,128)(2,1)S(1)} %get-tuple-element.86), channel_id=1, source_target_pairs={{0,16},{8,24},{16,0},{24,8},{1,17},{9,25},{17,1},{25,9},{2,18},{10... | collective-permute-start | bytes 589832 | tf_op jit(solution)/shard_map/ppermute | solution.py:27
  34.3 1.2 %collective-permute-start.14 = (f32[1,3,768]{2,1,0:T(4,128)S(1)}, f32[1,3,768]{2,1,0:T(4,128)S(1)}, u32[]{:S(2)}, u32[]{:S(2)}) collective-permute-start(f32[1,3,768]{2,1,0:T(4,128)S(1)} %get-tuple-element.87), channel_id=1, source_target_pairs={{0,8},{1,9},{2,10},{3,11},{4,12},{5,13},{6,14},{7,15},{8,0},{9,1},... | collective-permute-start | bytes 27656 | tf_op jit(solution)/shard_map/ppermute | solution.py:410
  35.6 3.9 %collective-permute-start.15 = (f32[1,3,768]{2,1,0:T(4,128)S(1)}, f32[1,3,768]{2,1,0:T(4,128)S(1)}, u32[]{:S(2)}, u32[]{:S(2)}) collective-permute-start(f32[1,3,768]{2,1,0:T(4,128)S(1)} %pad_maximum_fusion), channel_id=1, source_target_pairs={{0,2},{1,3},{2,0},{3,1},{4,6},{5,7},{6,4},{7,5},{8,10},{9,11},{10,... | collective-permute-start | bytes 27656 | tf_op jit(solution)/shard_map/ppermute | solution.py:410
  37.8 11.2 %collective-permute-start.20 = (bf16[128,1536]{1,0:T(8,128)(2,1)S(1)}, bf16[128,1536]{1,0:T(8,128)(2,1)S(1)}, u32[]{:S(2)}, u32[]{:S(2)}) collective-permute-start(bf16[128,1536]{1,0:T(8,128)(2,1)S(1)} %get-tuple-element.88), channel_id=1, source_target_pairs={{0,16},{8,24},{16,0},{24,8},{1,17},{9,25},{17,1},{25,9},{2,18},{10... | collective-permute-start | bytes 1179656 | tf_op jit(solution)/shard_map/ppermute | solution.py:27
  39.5 4.8 %collective-permute-start.16 = (f32[1,3,768]{2,1,0:T(4,128)S(1)}, f32[1,3,768]{2,1,0:T(4,128)S(1)}, u32[]{:S(2)}, u32[]{:S(2)}) collective-permute-start(f32[1,3,768]{2,1,0:T(4,128)S(1)} %pad_maximum_fusion.1), channel_id=1, source_target_pairs={{0,4},{1,5},{2,6},{3,7},{4,0},{5,1},{6,2},{7,3},{8,12},{9,13},{10,... | collective-permute-start | bytes 27656 | tf_op jit(solution)/shard_map/ppermute | solution.py:410
  42.6 11.8 %collective-permute-start.21 = (bf16[192,1536]{1,0:T(8,128)(2,1)S(1)}, bf16[192,1536]{1,0:T(8,128)(2,1)S(1)}, u32[]{:S(2)}, u32[]{:S(2)}) collective-permute-start(bf16[192,1536]{1,0:T(8,128)(2,1)S(1)} %copy-done.4), channel_id=1, source_target_pairs={{0,8},{8,0},{16,24},{24,16},{1,9},{9,1},{17,25},{25,17},{2,10},{10... | collective-permute-start | bytes 1769480 | tf_op jit(solution)/shard_map/ppermute | solution.py:27
  44.3 4.7 %collective-permute-start.17 = (f32[1,3,768]{2,1,0:T(4,128)S(1)}, f32[1,3,768]{2,1,0:T(4,128)S(1)}, u32[]{:S(2)}, u32[]{:S(2)}) collective-permute-start(f32[1,3,768]{2,1,0:T(4,128)S(1)} %pad_maximum_fusion.2.refs_0_), channel_id=1, source_target_pairs={{0,1},{1,0},{2,3},{3,2},{4,5},{5,4},{6,7},{7,6},{8,9},{9,8},{10,11... | collective-permute-start | bytes 27656 | tf_op jit(solution)/shard_map/ppermute | solution.py:410
  47.2 3.7 %collective-permute-start.18 = (f32[1,3,768]{2,1,0:T(4,128)S(1)}, f32[1,3,768]{2,1,0:T(4,128)S(1)}, u32[]{:S(2)}, u32[]{:S(2)}) collective-permute-start(f32[1,3,768]{2,1,0:T(4,128)S(1)} %pad_maximum_fusion.2.refs_0_), channel_id=1, source_target_pairs={{0,16},{1,17},{2,18},{3,19},{4,20},{5,21},{6,22},{7,23},{8,24},{9,... | collective-permute-start | bytes 27656 | tf_op jit(solution)/shard_map/ppermute | solution.py:410
  47.8 4.6 %collective-permute-start.19 = (f32[1,3,768]{2,1,0:T(4,128)S(1)}, f32[1,3,768]{2,1,0:T(4,128)S(1)}, u32[]{:S(2)}, u32[]{:S(2)}) collective-permute-start(f32[1,3,768]{2,1,0:T(4,128)S(1)} %pad_maximum_fusion.2.refs_0_), channel_id=1, source_target_pairs={{0,17},{1,16},{2,19},{3,18},{4,21},{5,20},{6,23},{7,22},{8,25},{9,... | collective-permute-start | bytes 27656 | tf_op jit(solution)/shard_map/ppermute | solution.py:410
  52.4 2.0 %collective-permute-start.23 = (bf16[128,1536]{1,0:T(8,128)(2,1)S(1)}, bf16[128,1536]{1,0:T(8,128)(2,1)S(1)}, u32[]{:S(2)}, u32[]{:S(2)}) collective-permute-start(bf16[128,1536]{1,0:T(8,128)(2,1)S(1)} %collective-permute-done.20.refs_10_), channel_id=1, source_target_pairs={{0,8},{8,0},{16,24},{24,16},{1,9},{9,1},{17,25},{25,17},{2,10},{10... | collective-permute-start | bytes 1179656 | tf_op jit(solution)/shard_map/ppermute | solution.py:27
  52.4 2.0 %collective-permute-start.22 = (bf16[64,1536]{1,0:T(8,128)(2,1)S(1)}, bf16[64,1536]{1,0:T(8,128)(2,1)S(1)}, u32[]{:S(2)}, u32[]{:S(2)}) collective-permute-start(bf16[64,1536]{1,0:T(8,128)(2,1)S(1)} %collective-permute-done.13.refs_9_), channel_id=1, source_target_pairs={{0,8},{8,0},{16,24},{24,16},{1,9},{9,1},{17,25},{25,17},{2,10},{10... | collective-permute-start | bytes 589832 | tf_op jit(solution)/shard_map/ppermute | solution.py:27
  (9 other events, 87.1 us)

commit v13 on v12

--- a/solution.py
+++ b/solution.py
@@ -27,11 +27,11 @@
     return lax.ppermute(value, axis, [(i, i ^ bit) for i in range(lax.axis_size(axis))])
 
 
-def cut_kernel(place_ref, shard_ref, two_ref, zero_ref, one_ref):
+def cut_kernel(pairs_ref, shard_ref, two_ref, zero_ref, one_ref):
     wide = two_ref.shape[1]
     channels = shard_ref.shape[1] // 2
     for block, ref in ((2, two_ref), (0, zero_ref)):
-        at = pl.multiple_of(place_ref[SHARED[block]] * channels + block * wide, wide)
+        at = pl.multiple_of(pairs_ref[SHARED[block] - 3] * channels + block * wide, wide)
         ref[...] = shard_ref[:, pl.ds(at, wide)]
     for i in range(2):
         at = i * channels + wide
@@ -60,8 +60,8 @@
     return (deviate * lax.rsqrt(spread + 1e-05) * gain).astype(jnp.bfloat16)
 
 
-def edge_kernel(place_ref, rows_ref, inner_ref, outer_ref):
-    odd = place_ref[3]
+def edge_kernel(pairs_ref, rows_ref, inner_ref, outer_ref):
+    odd = pairs_ref[0]
     last = rows_ref.shape[0] - HALO
     inner_ref[...] = rows_ref[pl.ds(pl.multiple_of((1 - odd) * last, HALO), HALO), :]
     outer_ref[...] = rows_ref[pl.ds(pl.multiple_of(odd * last, HALO), HALO), :]
@@ -373,10 +373,12 @@
         return front_block(block, wide, place, normed, weights, dw_kernel, *extra)
 
     if direct:
-        two, zero, one = cut(place, w_in, wide)
+        positions = jnp.stack([parity, pair]).astype(jnp.int32)
+        two, zero, one = cut(positions, w_in, wide)
+        one, later_in = tie(one, w_in)
         two, zero, one = (swap(part, "fsdp", 2) for part in (two, zero, one))
-        across = swap(w_in, "fsdp", 1)
-        inner, outer = edge_rows(place, rows)
+        across = swap(later_in, "fsdp", 1)
+        inner, outer = edge_rows(positions, rows)
         part_rows = w_out.shape[0] // 12
         normed, *pieces = normalize_rows(rows, gain, w_out, [4 * part_rows, 8 * part_rows])
         inner = swap(inner, "ctx", 1)
@@ -419,6 +421,7 @@
             return jnp.stack(merged([[part[:, i] for i in range(3)] for part in parts]), 1)
 
         stats = union([stats] + others([(1, 0)]))
+        stats, beyond[0] = tie(stats, beyond[0])
         stats = union([stats] + others([(0, 2)]))
         stats = union([stats] + others([(0, 4)]))
         stats = [stats] + others([(0, 1), (2, 0), (2, 1)])

time: 57.5 us -> 58.9 us (1.024)
  Pallas kernels: 17 us -> 20.4 us
  starting transfers between devices: 24.8 us -> 23.4 us
  local copies, waits for them, and re-layouts: 2.81 us -> 1.54 us
  waiting for transfers between devices: 11.7 us -> 12.3 us
    ppermute x6, starting transfers between devices: 10 us -> 7.31 us  [others(): lax.ppermute(stats, both, [(member(f, p), member(f ^ df, p ^ dp)) for f i...]
    pallas_call x1, Pallas kernels: 0.59 us -> 2.14 us  [cut(): pl.pallas_call(cut_kernel, out_shape=[jax.ShapeDtypeStruct(shape, jnp.bfl...]
    unnamed x18, local copies, waits for them, and re-layouts: 2.71 us -> 1.44 us
    ppermute x6, waiting for transfers between devices: 7.17 us -> 8.41 us  [others(): lax.ppermute(stats, both, [(member(f, p), member(f ^ df, p ^ dp)) for f i...]
    pallas_call x1, Pallas kernels: 2.34 us -> 3.13 us  [near_product(): pl.pallas_call(near_kernel, out_shape=shapes, in_specs=[pl.BlockSpec(memo...]
    ppermute x17, starting transfers between devices: 14.1 us -> 14.8 us  [swap(): lax.ppermute(value, axis, [(i, i ^ bit) for i in range(lax.axis_size(axis...]
    ppermute x17, waiting for transfers between devices: 4.58 us -> 3.89 us  [swap(): lax.ppermute(value, axis, [(i, i ^ bit) for i in range(lax.axis_size(axis...]
    pallas_call x1, Pallas kernels: 0.55 us -> 1.2 us  [edge_rows(): pl.pallas_call(edge_kernel, out_shape=[shape, shape], in_specs=[pl.BlockS...]
  transfers between devices with their start and end apart: 24 -> 24, of which waited for: 9 -> 12; matrix products, arithmetic and copies ran while one was open for 0% -> 0% of each run, Pallas kernels for 25% -> 26%
where the time goes in v13:
time: 58.9 us; the launch traced here: 58.6 us
  starting transfers between devices  23.4 us (40%)
  Pallas kernels  20.4 us (35%)
  waiting for transfers between devices  12.3 us (21%)
  local copies, waits for them, and re-layouts  1.54 us (3%)
  between operations  0.83 us (1%)
    ppermute x17, starting transfers between devices, swap(): lax.ppermute(value, axis, [(i, i ^ bit) for i in range(lax.axis_size(axis...  14.8 us
    pallas_call x3, Pallas kernels, front_block(): pl.pallas_call(functools.partial(front_kernel, block, len(earlier)), out_...  9.04 us
    ppermute x6, waiting for transfers between devices, others(): lax.ppermute(stats, both, [(member(f, p), member(f ^ df, p ^ dp)) for f i...  8.41 us
    ppermute x6, starting transfers between devices, others(): lax.ppermute(stats, both, [(member(f, p), member(f ^ df, p ^ dp)) for f i...  7.31 us
    ppermute x17, waiting for transfers between devices, swap(): lax.ppermute(value, axis, [(i, i ^ bit) for i in range(lax.axis_size(axis...  3.89 us
    pallas_call x1, Pallas kernels, near_product(): pl.pallas_call(near_kernel, out_shape=shapes, in_specs=[pl.BlockSpec(memo...  3.13 us
    pallas_call x1, Pallas kernels, back(): pl.pallas_call(functools.partial(back_kernel, len(stats)), out_shape=jax....  2.95 us
    pallas_call x1, Pallas kernels, cut(): pl.pallas_call(cut_kernel, out_shape=[jax.ShapeDtypeStruct(shape, jnp.bfl...  2.14 us
  transfers between devices with their start and end apart: 24, of which 12 were waited for; matrix products, arithmetic and copies ran while one was open for 0% of the time, Pallas kernels for 26%

profile of v13, /device:TPU:0, one launch (start us, length us, event | category | flops | bytes accessed | tf_op | source)
XLA Modules:
  0.0 58.6 jit_solution(7511499142790530607)
XLA Ops:
  0.1 2.1 %cut.1 = (bf16[384,256]{1,0:T(8,128)(2,1)}, bf16[384,256]{1,0:T(8,128)(2,1)}, bf16[384,512]{1,0:T(8,128)(2,1)S(1)}) custom-call(s32[2]{0:T(128)S(1)} %pad_add_fusion.pairs_ref, bf16[384,1536]{1,0:T(8,128)(2,1)} %refs_0_.1), custom_call_target="tpu_custom_call" | custom-call | flops 100000000 | tf_op jit(solution)/shard_map/cut/pallas_call | solution.py:44
  2.7 2.5 %collective-permute-start.2 = (bf16[384,256]{1,0:T(8,128)(2,1)}, bf16[384,256]{1,0:T(8,128)(2,1)S(1)}, u32[]{:S(2)}, u32[]{:S(2)}) collective-permute-start(bf16[384,256]{1,0:T(8,128)(2,1)} %get-tuple-element.59), channel_id=1, source_target_pairs={{0,16},{8,24},{16,0},{24,8},{1,17},{9,25},{17,1},{25,9},{2,18},{10... | collective-permute-start | bytes 589832 | tf_op jit(solution)/shard_map/ppermute | solution.py:27
  5.3 1.4 %copy-done = bf16[1,512,1536]{2,1,0:T(8,128)(2,1)S(1)} copy-done((bf16[1,512,1536]{2,1,0:T(8,128)(2,1)S(1)}, bf16[1,512,1536]{2,1,0:T(8,128)(2,1)}, u32[]{:S(2)}) %copy-start) | copy-done | bytes 1572888
  6.7 1.2 %edges.1 = (bf16[16,1536]{1,0:T(8,128)(2,1)}, bf16[16,1536]{1,0:T(8,128)(2,1)}) custom-call(s32[2]{0:T(128)S(1)} %pad_add_fusion.pairs_ref, bf16[512,1536]{1,0:T(8,128)(2,1)S(1)} %bitcast.6), custom_call_target="tpu_custom_call" | custom-call | flops 100000000 | tf_op jit(solution)/shard_map/edges/pallas_call | solution.py:72
  7.9 2.0 %collective-permute-start = (bf16[16,1536]{1,0:T(8,128)(2,1)}, bf16[16,1536]{1,0:T(8,128)(2,1)}, u32[]{:S(2)}, u32[]{:S(2)}) collective-permute-start(bf16[16,1536]{1,0:T(8,128)(2,1)} %get-tuple-element.57), channel_id=1, source_target_pairs={{0,1},{1,0},{2,3},{3,2},{4,5},{5,4},{6,7},{7,6},{8,9},{9,8},{10,11... | collective-permute-start | bytes 147464 | tf_op jit(solution)/shard_map/ppermute | solution.py:27
  9.9 1.3 %collective-permute-start.1 = (bf16[16,1536]{1,0:T(8,128)(2,1)}, bf16[16,1536]{1,0:T(8,128)(2,1)}, u32[]{:S(2)}, u32[]{:S(2)}) collective-permute-start(bf16[16,1536]{1,0:T(8,128)(2,1)} %get-tuple-element.58), channel_id=1, source_target_pairs={{1,2},{3,4},{5,6},{2,1},{4,3},{6,5},{9,10},{11,12},{13,14},{10,9},... | collective-permute-start | bytes 147464 | tf_op jit(solution)/shard_map/ppermute | solution.py:386
  11.9 1.9 %layer_norm.1 = (bf16[512,1536]{1,0:T(8,128)(2,1)S(1)}, bf16[64,1536]{1,0:T(8,128)(2,1)S(1)}, bf16[128,1536]{1,0:T(8,128)(2,1)S(1)}) custom-call(bf16[512,1536]{1,0:T(8,128)(2,1)S(1)} %bitcast.7, f32[1,1536]{1,0:T(1,128)S(1)} %broadcast_in_dim.14.gain_ref, bf16[192,1536]{1,0:T(8,128)(2,1)S(1)} %copy-done.2), custom_call_target="tpu_custom_call" | custom-call | flops 100000000 | tf_op jit(solution)/shard_map/layer_norm/pallas_call | solution.py:100
  13.8 1.6 %collective-permute-start.9 = (bf16[384,512]{1,0:T(8,128)(2,1)S(1)}, bf16[384,512]{1,0:T(8,128)(2,1)S(1)}, u32[]{:S(2)}, u32[]{:S(2)}) collective-permute-start(bf16[384,512]{1,0:T(8,128)(2,1)S(1)} %copy-done.5), channel_id=1, source_target_pairs={{0,16},{8,24},{16,0},{24,8},{1,17},{9,25},{17,1},{25,9},{2,18},{10... | collective-permute-start | bytes 1179656 | tf_op jit(solution)/shard_map/ppermute | solution.py:27
  15.4 3.8 %collective-permute-start.5 = (bf16[384,256]{1,0:T(8,128)(2,1)S(1)}, bf16[384,256]{1,0:T(8,128)(2,1)S(1)}, u32[]{:S(2)}, u32[]{:S(2)}) collective-permute-start(bf16[384,256]{1,0:T(8,128)(2,1)S(1)} %collective-permute-done.2.refs_1_), channel_id=1, source_target_pairs={{0,1},{1,0},{2,3},{3,2},{4,5},{5,4},{6,7},{7,6},{8,9},{9,8},{10,11... | collective-permute-start | bytes 589832 | tf_op jit(solution)/shard_map/ppermute | solution.py:27
  19.2 1.6 %collective-permute-start.7 = (bf16[384,256]{1,0:T(8,128)(2,1)}, bf16[384,256]{1,0:T(8,128)(2,1)S(1)}, u32[]{:S(2)}, u32[]{:S(2)}) collective-permute-start(bf16[384,256]{1,0:T(8,128)(2,1)} %collective-permute-done.3.refs_1_), channel_id=1, source_target_pairs={{0,2},{1,3},{2,0},{3,1},{4,6},{5,7},{6,4},{7,5},{8,10},{9,11},{10,... | collective-permute-start | bytes 589832 | tf_op jit(solution)/shard_map/ppermute | solution.py:27
  20.8 3.1 %near.1 = (bf16[544,1536]{1,0:T(8,128)(2,1)S(1)}, f32[544,512]{1,0:T(8,128)S(1)}, f32[544,512]{1,0:T(8,128)S(1)}, f32[544,512]{1,0:T(8,128)S(1)}) custom-call(s32[5]{0:T(128)S(1)} %stack.42.place_ref, bf16[512,1536]{1,0:T(8,128)(2,1)S(1)} %get-tuple-element.61.rows_ref, bf16[16,1536]{1,0:T(8,128)(2,1)} %collective-permute-done.inner_ref, ...), custom_call_target="tpu_custom_call" | custom-call | flops 100000000 | tf_op jit(solution)/shard_map/near/pallas_call | solution.py:148
  27.3 2.9 %front.3 = (f32[512,256]{1,0:T(8,128)S(1)}, f32[3,256]{1,0:T(4,128)S(1)}) custom-call(s32[5]{0:T(128)S(1)} %stack.42.place_ref, bf16[544,1536]{1,0:T(8,128)(2,1)S(1)} %get-tuple-element.66.normed_ref, f32[544,512]{1,0:T(8,128)S(1)} %get-tuple-element.75.refs_0_, bf16[384,256]{1,0:T(8,128)(2,1)S(1)} %collective-permute-done.2.refs_1_, ...), custom_call_target="tpu_custom_call" | custom-call | flops 100000000 | tf_op jit(solution)/shard_map/front/pallas_call | solution.py:233
  30.2 3.3 %front.4 = (f32[512,256]{1,0:T(8,128)S(1)}, f32[3,256]{1,0:T(4,128)S(1)}) custom-call(s32[5]{0:T(128)S(1)} %stack.42.place_ref, bf16[544,1536]{1,0:T(8,128)(2,1)S(1)} %get-tuple-element.66.normed_ref, f32[544,512]{1,0:T(8,128)S(1)} %get-tuple-element.82.refs_0_, bf16[384,256]{1,0:T(8,128)(2,1)} %collective-permute-done.3.refs_1_, ...), custom_call_target="tpu_custom_call" | custom-call | flops 4000000000 | tf_op jit(solution)/shard_map/front/pallas_call | solution.py:233
  33.5 2.9 %front.5 = (f32[512,256]{1,0:T(8,128)S(1)}, f32[1,3,768]{2,1,0:T(4,128)S(1)}) custom-call(s32[5]{0:T(128)S(1)} %stack.42.place_ref, bf16[544,1536]{1,0:T(8,128)(2,1)S(1)} %get-tuple-element.66.normed_ref, f32[3,256]{1,0:T(4,128)S(1)} %get-tuple-element.79.refs_0_, f32[3,256]{1,0:T(4,128)S(1)} %get-tuple-element.86.refs_1_, ...), custom_call_target="tpu_custom_call" | custom-call | flops 100000000 | tf_op jit(solution)/shard_map/front/pallas_call | solution.py:233
  38.2 1.1 %collective-permute-start.16 = (f32[1,3,768]{2,1,0:T(4,128)S(1)}, f32[1,3,768]{2,1,0:T(4,128)S(1)}, u32[]{:S(2)}, u32[]{:S(2)}) collective-permute-start(f32[1,3,768]{2,1,0:T(4,128)S(1)} %pad_maximum_fusion), channel_id=1, source_target_pairs={{0,2},{1,3},{2,0},{3,1},{4,6},{5,7},{6,4},{7,5},{8,10},{9,11},{10,... | collective-permute-start | bytes 27656 | tf_op jit(solution)/shard_map/ppermute | solution.py:412
  40.0 1.8 %collective-permute-done.16 = f32[1,3,768]{2,1,0:T(4,128)S(1)} collective-permute-done((f32[1,3,768]{2,1,0:T(4,128)S(1)}, f32[1,3,768]{2,1,0:T(4,128)S(1)}, u32[]{:S(2)}, u32[]{:S(2)}) %collective-permute-start.16) | collective-permute-done | bytes 9248 | tf_op jit(solution)/shard_map/ppermute | solution.py:412
  41.9 2.2 %collective-permute-start.17 = (f32[1,3,768]{2,1,0:T(4,128)S(1)}, f32[1,3,768]{2,1,0:T(4,128)S(1)}, u32[]{:S(2)}, u32[]{:S(2)}) collective-permute-start(f32[1,3,768]{2,1,0:T(4,128)S(1)} %pad_maximum_fusion.1), channel_id=1, source_target_pairs={{0,4},{1,5},{2,6},{3,7},{4,0},{5,1},{6,2},{7,3},{8,12},{9,13},{10,... | collective-permute-start | bytes 27656 | tf_op jit(solution)/shard_map/ppermute | solution.py:412
  44.1 2.5 %collective-permute-done.17 = f32[1,3,768]{2,1,0:T(4,128)S(1)} collective-permute-done((f32[1,3,768]{2,1,0:T(4,128)S(1)}, f32[1,3,768]{2,1,0:T(4,128)S(1)}, u32[]{:S(2)}, u32[]{:S(2)}) %collective-permute-start.17) | collective-permute-done | bytes 9248 | tf_op jit(solution)/shard_map/ppermute | solution.py:412
  46.6 2.2 %collective-permute-start.18 = (f32[1,3,768]{2,1,0:T(4,128)S(1)}, f32[1,3,768]{2,1,0:T(4,128)S(1)}, u32[]{:S(2)}, u32[]{:S(2)}) collective-permute-start(f32[1,3,768]{2,1,0:T(4,128)S(1)} %pad_maximum_fusion.2.refs_0_), channel_id=1, source_target_pairs={{0,1},{1,0},{2,3},{3,2},{4,5},{5,4},{6,7},{7,6},{8,9},{9,8},{10,11... | collective-permute-start | bytes 27656 | tf_op jit(solution)/shard_map/ppermute | solution.py:412
  49.4 1.0 %collective-permute-start.20 = (f32[1,3,768]{2,1,0:T(4,128)S(1)}, f32[1,3,768]{2,1,0:T(4,128)S(1)}, u32[]{:S(2)}, u32[]{:S(2)}) collective-permute-start(f32[1,3,768]{2,1,0:T(4,128)S(1)} %pad_maximum_fusion.2.refs_0_), channel_id=1, source_target_pairs={{0,17},{1,16},{2,19},{3,18},{4,21},{5,20},{6,23},{7,22},{8,25},{9,... | collective-permute-start | bytes 27656 | tf_op jit(solution)/shard_map/ppermute | solution.py:412
  50.6 2.0 %collective-permute-done.19.refs_2_ = f32[1,3,768]{2,1,0:T(4,128)S(1)} collective-permute-done((f32[1,3,768]{2,1,0:T(4,128)S(1)}, f32[1,3,768]{2,1,0:T(4,128)S(1)}, u32[]{:S(2)}, u32[]{:S(2)}) %collective-permute-start.19) | collective-permute-done | bytes 9248 | tf_op jit(solution)/shard_map/ppermute | solution.py:412
  52.5 1.4 %collective-permute-done.20.refs_3_ = f32[1,3,768]{2,1,0:T(4,128)S(1)} collective-permute-done((f32[1,3,768]{2,1,0:T(4,128)S(1)}, f32[1,3,768]{2,1,0:T(4,128)S(1)}, u32[]{:S(2)}, u32[]{:S(2)}) %collective-permute-start.20) | collective-permute-done | bytes 9248 | tf_op jit(solution)/shard_map/ppermute | solution.py:412
  54.0 1.7 %collective-permute-done.23.refs_12_ = bf16[128,1536]{1,0:T(8,128)(2,1)S(1)} collective-permute-done((bf16[128,1536]{1,0:T(8,128)(2,1)S(1)}, bf16[128,1536]{1,0:T(8,128)(2,1)S(1)}, u32[]{:S(2)}, u32[]{:S(2)}) %collective-permute-start.23) | collective-permute-done | bytes 393248 | tf_op jit(solution)/shard_map/ppermute | solution.py:27
  55.7 2.9 %back.1 = bf16[512,1536]{1,0:T(8,128)(2,1)} custom-call(s32[5]{0:T(128)S(1)} %stack.42.place_ref, f32[1,768]{1,0:T(1,128)S(1)} %broadcast_in_dim.12.gain_ref, f32[1,768]{1,0:T(1,128)S(1)} %broadcast_in_dim.13.shift_ref, f32[1,3,768]{2,1,0:T(4,128)S(1)} %pad_maximum_fusion.2.refs_0_, f32[1,3,768]{2,1,0:T(4,128)S(1)} %collective-permute-done.18.refs_1_, ...), custom_call_target="tpu_custom_call" | custom-call | flops 1000000000 | tf_op jit(solution)/shard_map/back/pallas_call | solution.py:331
  (61 shorter events, 7.5 us)
Async XLA Ops:
  2.2 18.5 %collective-permute-start.4 = (bf16[384,1536]{1,0:T(8,128)(2,1)}, bf16[384,1536]{1,0:T(8,128)(2,1)S(1)}, u32[]{:S(2)}, u32[]{:S(2)}) collective-permute-start(bf16[384,1536]{1,0:T(8,128)(2,1)} %refs_0_.1), channel_id=1, source_target_pairs={{0,8},{8,0},{16,24},{24,16},{1,9},{9,1},{17,25},{25,17},{2,10},{10... | collective-permute-start | bytes 3538952 | tf_op jit(solution)/shard_map/ppermute | solution.py:27
  2.7 12.7 %collective-permute-start.2 = (bf16[384,256]{1,0:T(8,128)(2,1)}, bf16[384,256]{1,0:T(8,128)(2,1)S(1)}, u32[]{:S(2)}, u32[]{:S(2)}) collective-permute-start(bf16[384,256]{1,0:T(8,128)(2,1)} %get-tuple-element.59), channel_id=1, source_target_pairs={{0,16},{8,24},{16,0},{24,8},{1,17},{9,25},{17,1},{25,9},{2,18},{10... | collective-permute-start | bytes 589832 | tf_op jit(solution)/shard_map/ppermute | solution.py:27
  5.2 10.2 %collective-permute-start.3 = (bf16[384,256]{1,0:T(8,128)(2,1)}, bf16[384,256]{1,0:T(8,128)(2,1)}, u32[]{:S(2)}, u32[]{:S(2)}) collective-permute-start(bf16[384,256]{1,0:T(8,128)(2,1)} %get-tuple-element.60), channel_id=1, source_target_pairs={{0,16},{8,24},{16,0},{24,8},{1,17},{9,25},{17,1},{25,9},{2,18},{10... | collective-permute-start | bytes 589832 | tf_op jit(solution)/shard_map/ppermute | solution.py:27
  7.9 6.0 %collective-permute-start = (bf16[16,1536]{1,0:T(8,128)(2,1)}, bf16[16,1536]{1,0:T(8,128)(2,1)}, u32[]{:S(2)}, u32[]{:S(2)}) collective-permute-start(bf16[16,1536]{1,0:T(8,128)(2,1)} %get-tuple-element.57), channel_id=1, source_target_pairs={{0,1},{1,0},{2,3},{3,2},{4,5},{5,4},{6,7},{7,6},{8,9},{9,8},{10,11... | collective-permute-start | bytes 147464 | tf_op jit(solution)/shard_map/ppermute | solution.py:27
  9.9 5.6 %collective-permute-start.1 = (bf16[16,1536]{1,0:T(8,128)(2,1)}, bf16[16,1536]{1,0:T(8,128)(2,1)}, u32[]{:S(2)}, u32[]{:S(2)}) collective-permute-start(bf16[16,1536]{1,0:T(8,128)(2,1)} %get-tuple-element.58), channel_id=1, source_target_pairs={{1,2},{3,4},{5,6},{2,1},{4,3},{6,5},{9,10},{11,12},{13,14},{10,9},... | collective-permute-start | bytes 147464 | tf_op jit(solution)/shard_map/ppermute | solution.py:386
  13.8 12.6 %collective-permute-start.9 = (bf16[384,512]{1,0:T(8,128)(2,1)S(1)}, bf16[384,512]{1,0:T(8,128)(2,1)S(1)}, u32[]{:S(2)}, u32[]{:S(2)}) collective-permute-start(bf16[384,512]{1,0:T(8,128)(2,1)S(1)} %copy-done.5), channel_id=1, source_target_pairs={{0,16},{8,24},{16,0},{24,8},{1,17},{9,25},{17,1},{25,9},{2,18},{10... | collective-permute-start | bytes 1179656 | tf_op jit(solution)/shard_map/ppermute | solution.py:27
  15.4 9.1 %collective-permute-start.5 = (bf16[384,256]{1,0:T(8,128)(2,1)S(1)}, bf16[384,256]{1,0:T(8,128)(2,1)S(1)}, u32[]{:S(2)}, u32[]{:S(2)}) collective-permute-start(bf16[384,256]{1,0:T(8,128)(2,1)S(1)} %collective-permute-done.2.refs_1_), channel_id=1, source_target_pairs={{0,1},{1,0},{2,3},{3,2},{4,5},{5,4},{6,7},{7,6},{8,9},{9,8},{10,11... | collective-permute-start | bytes 589832 | tf_op jit(solution)/shard_map/ppermute | solution.py:27
  19.2 5.9 %collective-permute-start.7 = (bf16[384,256]{1,0:T(8,128)(2,1)}, bf16[384,256]{1,0:T(8,128)(2,1)S(1)}, u32[]{:S(2)}, u32[]{:S(2)}) collective-permute-start(bf16[384,256]{1,0:T(8,128)(2,1)} %collective-permute-done.3.refs_1_), channel_id=1, source_target_pairs={{0,2},{1,3},{2,0},{3,1},{4,6},{5,7},{6,4},{7,5},{8,10},{9,11},{10,... | collective-permute-start | bytes 589832 | tf_op jit(solution)/shard_map/ppermute | solution.py:27
  23.9 1.5 %collective-permute-start.6 = (bf16[384,256]{1,0:T(8,128)(2,1)S(1)}, bf16[384,256]{1,0:T(8,128)(2,1)S(1)}, u32[]{:S(2)}, u32[]{:S(2)}) collective-permute-start(bf16[384,256]{1,0:T(8,128)(2,1)S(1)} %collective-permute-done.2.refs_1_), channel_id=1, source_target_pairs={{0,8},{8,0},{16,24},{24,16},{1,9},{9,1},{17,25},{25,17},{2,10},{10... | collective-permute-start | bytes 589832 | tf_op jit(solution)/shard_map/ppermute | solution.py:27
  24.0 1.9 %collective-permute-start.8 = (bf16[384,256]{1,0:T(8,128)(2,1)}, bf16[384,256]{1,0:T(8,128)(2,1)S(1)}, u32[]{:S(2)}, u32[]{:S(2)}) collective-permute-start(bf16[384,256]{1,0:T(8,128)(2,1)} %collective-permute-done.3.refs_1_), channel_id=1, source_target_pairs={{0,8},{8,0},{16,24},{24,16},{1,9},{9,1},{17,25},{25,17},{2,10},{10... | collective-permute-start | bytes 589832 | tf_op jit(solution)/shard_map/ppermute | solution.py:27
  25.9 1.4 %collective-permute-start.10 = (bf16[384,256]{1,0:T(8,128)(2,1)S(1)}, bf16[384,256]{1,0:T(8,128)(2,1)S(1)}, u32[]{:S(2)}, u32[]{:S(2)}) collective-permute-start(bf16[384,256]{1,0:T(8,128)(2,1)S(1)} %collective-permute-done.5.refs_2_), channel_id=1, source_target_pairs={{0,8},{8,0},{16,24},{24,16},{1,9},{9,1},{17,25},{25,17},{2,10},{10... | collective-permute-start | bytes 589832 | tf_op jit(solution)/shard_map/ppermute | solution.py:27
  26.1 4.1 %collective-permute-start.11 = (bf16[384,256]{1,0:T(8,128)(2,1)S(1)}, bf16[384,256]{1,0:T(8,128)(2,1)S(1)}, u32[]{:S(2)}, u32[]{:S(2)}) collective-permute-start(bf16[384,256]{1,0:T(8,128)(2,1)S(1)} %collective-permute-done.7.refs_2_), channel_id=1, source_target_pairs={{0,8},{8,0},{16,24},{24,16},{1,9},{9,1},{17,25},{25,17},{2,10},{10... | collective-permute-start | bytes 589832 | tf_op jit(solution)/shard_map/ppermute | solution.py:27
  26.4 7.1 %collective-permute-start.12 = (bf16[384,512]{1,0:T(8,128)(2,1)S(1)}, bf16[384,512]{1,0:T(8,128)(2,1)S(1)}, u32[]{:S(2)}, u32[]{:S(2)}) collective-permute-start(bf16[384,512]{1,0:T(8,128)(2,1)S(1)} %collective-permute-done.9.refs_3_), channel_id=1, source_target_pairs={{0,8},{8,0},{16,24},{24,16},{1,9},{9,1},{17,25},{25,17},{2,10},{10... | collective-permute-start | bytes 1179656 | tf_op jit(solution)/shard_map/ppermute | solution.py:27
  26.6 9.8 %collective-permute-start.13 = (bf16[64,1536]{1,0:T(8,128)(2,1)S(1)}, bf16[64,1536]{1,0:T(8,128)(2,1)S(1)}, u32[]{:S(2)}, u32[]{:S(2)}) collective-permute-start(bf16[64,1536]{1,0:T(8,128)(2,1)S(1)} %get-tuple-element.92), channel_id=1, source_target_pairs={{0,16},{8,24},{16,0},{24,8},{1,17},{9,25},{17,1},{25,9},{2,18},{10... | collective-permute-start | bytes 589832 | tf_op jit(solution)/shard_map/ppermute | solution.py:27
  36.4 1.2 %collective-permute-start.14 = (f32[1,3,768]{2,1,0:T(4,128)S(1)}, f32[1,3,768]{2,1,0:T(4,128)S(1)}, u32[]{:S(2)}, u32[]{:S(2)}) collective-permute-start(f32[1,3,768]{2,1,0:T(4,128)S(1)} %get-tuple-element.93), channel_id=1, source_target_pairs={{0,8},{1,9},{2,10},{3,11},{4,12},{5,13},{6,14},{7,15},{8,0},{9,1},... | collective-permute-start | bytes 27656 | tf_op jit(solution)/shard_map/ppermute | solution.py:412
  36.7 1.4 %collective-permute-start.15 = (bf16[64,1536]{1,0:T(8,128)(2,1)S(1)}, bf16[64,1536]{1,0:T(8,128)(2,1)S(1)}, u32[]{:S(2)}, u32[]{:S(2)}) collective-permute-start(bf16[64,1536]{1,0:T(8,128)(2,1)S(1)} %collective-permute-done.13.refs_9_), channel_id=1, source_target_pairs={{0,8},{8,0},{16,24},{24,16},{1,9},{9,1},{17,25},{25,17},{2,10},{10... | collective-permute-start | bytes 589832 | tf_op jit(solution)/shard_map/ppermute | solution.py:27
  38.2 3.7 %collective-permute-start.16 = (f32[1,3,768]{2,1,0:T(4,128)S(1)}, f32[1,3,768]{2,1,0:T(4,128)S(1)}, u32[]{:S(2)}, u32[]{:S(2)}) collective-permute-start(f32[1,3,768]{2,1,0:T(4,128)S(1)} %pad_maximum_fusion), channel_id=1, source_target_pairs={{0,2},{1,3},{2,0},{3,1},{4,6},{5,7},{6,4},{7,5},{8,10},{9,11},{10,... | collective-permute-start | bytes 27656 | tf_op jit(solution)/shard_map/ppermute | solution.py:412
  39.3 11.3 %collective-permute-start.21 = (bf16[128,1536]{1,0:T(8,128)(2,1)S(1)}, bf16[128,1536]{1,0:T(8,128)(2,1)S(1)}, u32[]{:S(2)}, u32[]{:S(2)}) collective-permute-start(bf16[128,1536]{1,0:T(8,128)(2,1)S(1)} %get-tuple-element.96), channel_id=1, source_target_pairs={{0,16},{8,24},{16,0},{24,8},{1,17},{9,25},{17,1},{25,9},{2,18},{10... | collective-permute-start | bytes 1179656 | tf_op jit(solution)/shard_map/ppermute | solution.py:27
  41.9 4.7 %collective-permute-start.17 = (f32[1,3,768]{2,1,0:T(4,128)S(1)}, f32[1,3,768]{2,1,0:T(4,128)S(1)}, u32[]{:S(2)}, u32[]{:S(2)}) collective-permute-start(f32[1,3,768]{2,1,0:T(4,128)S(1)} %pad_maximum_fusion.1), channel_id=1, source_target_pairs={{0,4},{1,5},{2,6},{3,7},{4,0},{5,1},{6,2},{7,3},{8,12},{9,13},{10,... | collective-permute-start | bytes 27656 | tf_op jit(solution)/shard_map/ppermute | solution.py:412
  44.1 9.9 %collective-permute-start.22 = (bf16[192,1536]{1,0:T(8,128)(2,1)S(1)}, bf16[192,1536]{1,0:T(8,128)(2,1)S(1)}, u32[]{:S(2)}, u32[]{:S(2)}) collective-permute-start(bf16[192,1536]{1,0:T(8,128)(2,1)S(1)} %copy-done.2), channel_id=1, source_target_pairs={{0,8},{8,0},{16,24},{24,16},{1,9},{9,1},{17,25},{25,17},{2,10},{10... | collective-permute-start | bytes 1769480 | tf_op jit(solution)/shard_map/ppermute | solution.py:27
  46.6 3.9 %collective-permute-start.18 = (f32[1,3,768]{2,1,0:T(4,128)S(1)}, f32[1,3,768]{2,1,0:T(4,128)S(1)}, u32[]{:S(2)}, u32[]{:S(2)}) collective-permute-start(f32[1,3,768]{2,1,0:T(4,128)S(1)} %pad_maximum_fusion.2.refs_0_), channel_id=1, source_target_pairs={{0,1},{1,0},{2,3},{3,2},{4,5},{5,4},{6,7},{7,6},{8,9},{9,8},{10,11... | collective-permute-start | bytes 27656 | tf_op jit(solution)/shard_map/ppermute | solution.py:412
  48.8 3.7 %collective-permute-start.19 = (f32[1,3,768]{2,1,0:T(4,128)S(1)}, f32[1,3,768]{2,1,0:T(4,128)S(1)}, u32[]{:S(2)}, u32[]{:S(2)}) collective-permute-start(f32[1,3,768]{2,1,0:T(4,128)S(1)} %pad_maximum_fusion.2.refs_0_), channel_id=1, source_target_pairs={{0,16},{1,17},{2,18},{3,19},{4,20},{5,21},{6,22},{7,23},{8,24},{9,... | collective-permute-start | bytes 27656 | tf_op jit(solution)/shard_map/ppermute | solution.py:412
  49.4 4.6 %collective-permute-start.20 = (f32[1,3,768]{2,1,0:T(4,128)S(1)}, f32[1,3,768]{2,1,0:T(4,128)S(1)}, u32[]{:S(2)}, u32[]{:S(2)}) collective-permute-start(f32[1,3,768]{2,1,0:T(4,128)S(1)} %pad_maximum_fusion.2.refs_0_), channel_id=1, source_target_pairs={{0,17},{1,16},{2,19},{3,18},{4,21},{5,20},{6,23},{7,22},{8,25},{9,... | collective-permute-start | bytes 27656 | tf_op jit(solution)/shard_map/ppermute | solution.py:412
  54.0 1.7 %collective-permute-start.23 = (bf16[128,1536]{1,0:T(8,128)(2,1)S(1)}, bf16[128,1536]{1,0:T(8,128)(2,1)S(1)}, u32[]{:S(2)}, u32[]{:S(2)}) collective-permute-start(bf16[128,1536]{1,0:T(8,128)(2,1)S(1)} %collective-permute-done.21.refs_10_), channel_id=1, source_target_pairs={{0,8},{8,0},{16,24},{24,16},{1,9},{9,1},{17,25},{25,17},{2,10},{10... | collective-permute-start | bytes 1179656 | tf_op jit(solution)/shard_map/ppermute | solution.py:27
  (9 other events, 91.9 us)

commit v14 on v12

--- a/solution.py
+++ b/solution.py
@@ -377,8 +377,7 @@
         two, zero, one = (swap(part, "fsdp", 2) for part in (two, zero, one))
         across = swap(w_in, "fsdp", 1)
         inner, outer = edge_rows(place, rows)
-        part_rows = w_out.shape[0] // 12
-        normed, *pieces = normalize_rows(rows, gain, w_out, [4 * part_rows, 8 * part_rows])
+        normed, *pieces = normalize_rows(rows, gain, w_out, [w_out.shape[0]])
         inner = swap(inner, "ctx", 1)
         pairs = [(i, i + 1) for i in range(1, ends, 2)]
         outer = lax.ppermute(outer, "ctx", pairs + [(j, i) for i, j in pairs])
@@ -401,8 +400,6 @@
         conv_zero, partials[1] = tie(conv_zero, partials[1])
         conv_one, stats = front(1, [partials[1], one, beyond_one], (stat_two, stat_zero), 1)
         across_out = swap(w_out, "fsdp", 1)
-        stats, pieces[0] = tie(stats, pieces[0])
-        beyond = [swap(pieces[0], "fsdp", 1)]
         convs = [conv_zero, conv_one, conv_two]
 
         def others(flips):
@@ -422,8 +419,8 @@
         stats = union([stats] + others([(0, 2)]))
         stats = union([stats] + others([(0, 4)]))
         stats = [stats] + others([(0, 1), (2, 0), (2, 1)])
-        *stats, pieces[1] = tie(*stats, pieces[1])
-        beyond.append(swap(pieces[1], "fsdp", 1))
+        *stats, pieces[0] = tie(*stats, pieces[0])
+        beyond = [swap(pieces[0], "fsdp", 1)]
         out_weights = [w_out, across_out, *pieces, *beyond]
     else:
         full_in = lax.all_gather(w_in, "fsdp", axis=0, tiled=True)

time: 57.5 us -> 59.3 us (1.031)
  waiting for transfers between devices: 11.7 us -> 16.4 us
  starting transfers between devices: 24.8 us -> 22 us
    ppermute x17 -> x15, waiting for transfers between devices: 4.58 us -> 10.4 us  [swap(): lax.ppermute(value, axis, [(i, i ^ bit) for i in range(lax.axis_size(axis...]
    ppermute x6, starting transfers between devices: 10 us -> 8.08 us  [others(): lax.ppermute(stats, both, [(member(f, p), member(f ^ df, p ^ dp)) for f i...]
    ppermute x6, waiting for transfers between devices: 7.17 us -> 5.96 us  [others(): lax.ppermute(stats, both, [(member(f, p), member(f ^ df, p ^ dp)) for f i...]
    ppermute x17 -> x15, starting transfers between devices: 14.1 us -> 13.2 us  [swap(): lax.ppermute(value, axis, [(i, i ^ bit) for i in range(lax.axis_size(axis...]
  transfers between devices with their start and end apart: 24 -> 22, of which waited for: 9 -> 10; matrix products, arithmetic and copies ran while one was open for 0% -> 0% of each run, Pallas kernels for 25% -> 19%
where the time goes in v14:
time: 59.3 us; the launch traced here: 59.1 us
  starting transfers between devices  22 us (37%)
  Pallas kernels  17 us (29%)
  waiting for transfers between devices  16.4 us (28%)
  local copies, waits for them, and re-layouts  2.81 us (5%)
  between operations  0.86 us (1%)
    ppermute x15, starting transfers between devices, swap(): lax.ppermute(value, axis, [(i, i ^ bit) for i in range(lax.axis_size(axis...  13.2 us
    ppermute x15, waiting for transfers between devices, swap(): lax.ppermute(value, axis, [(i, i ^ bit) for i in range(lax.axis_size(axis...  10.4 us
    pallas_call x3, Pallas kernels, front_block(): pl.pallas_call(functools.partial(front_kernel, block, len(earlier)), out_...  8.65 us
    ppermute x6, starting transfers between devices, others(): lax.ppermute(stats, both, [(member(f, p), member(f ^ df, p ^ dp)) for f i...  8.08 us
    ppermute x6, waiting for transfers between devices, others(): lax.ppermute(stats, both, [(member(f, p), member(f ^ df, p ^ dp)) for f i...  5.96 us
    pallas_call x1, Pallas kernels, back(): pl.pallas_call(functools.partial(back_kernel, len(stats)), out_shape=jax....  2.93 us
    unnamed x18, local copies, waits for them, and re-layouts  2.71 us
    pallas_call x1, Pallas kernels, near_product(): pl.pallas_call(near_kernel, out_shape=shapes, in_specs=[pl.BlockSpec(memo...  2.34 us
  transfers between devices with their start and end apart: 22, of which 10 were waited for; matrix products, arithmetic and copies ran while one was open for 0% of the time, Pallas kernels for 19%

profile of v14, /device:TPU:0, one launch (start us, length us, event | category | flops | bytes accessed | tf_op | source)
XLA Modules:
  0.0 59.1 jit_solution(13407551104843398558)
XLA Ops:
  1.2 1.3 %copy-done.2 = bf16[384,1536]{1,0:T(8,128)(2,1)S(1)} copy-done((bf16[384,1536]{1,0:T(8,128)(2,1)S(1)}, bf16[384,1536]{1,0:T(8,128)(2,1)}, u32[]{:S(2)}) %copy-start.2) | copy-done | bytes 1179672
  3.1 2.6 %collective-permute-start.2 = (bf16[384,256]{1,0:T(8,128)(2,1)S(1)}, bf16[384,256]{1,0:T(8,128)(2,1)S(1)}, u32[]{:S(2)}, u32[]{:S(2)}) collective-permute-start(bf16[384,256]{1,0:T(8,128)(2,1)S(1)} %get-tuple-element.52), channel_id=1, source_target_pairs={{0,16},{8,24},{16,0},{24,8},{1,17},{9,25},{17,1},{25,9},{2,18},{10... | collective-permute-start | bytes 589832 | tf_op jit(solution)/shard_map/ppermute | solution.py:27
  5.7 1.4 %copy-done = bf16[1,512,1536]{2,1,0:T(8,128)(2,1)S(1)} copy-done((bf16[1,512,1536]{2,1,0:T(8,128)(2,1)S(1)}, bf16[1,512,1536]{2,1,0:T(8,128)(2,1)}, u32[]{:S(2)}) %copy-start) | copy-done | bytes 1572888
  7.7 2.0 %collective-permute-start = (bf16[16,1536]{1,0:T(8,128)(2,1)S(1)}, bf16[16,1536]{1,0:T(8,128)(2,1)S(1)}, u32[]{:S(2)}, u32[]{:S(2)}) collective-permute-start(bf16[16,1536]{1,0:T(8,128)(2,1)S(1)} %get-tuple-element.50), channel_id=1, source_target_pairs={{0,1},{1,0},{2,3},{3,2},{4,5},{5,4},{6,7},{7,6},{8,9},{9,8},{10,11... | collective-permute-start | bytes 147464 | tf_op jit(solution)/shard_map/ppermute | solution.py:27
  10.4 1.9 %layer_norm.1 = (bf16[512,1536]{1,0:T(8,128)(2,1)S(1)}, bf16[192,1536]{1,0:T(8,128)(2,1)S(1)}) custom-call(bf16[512,1536]{1,0:T(8,128)(2,1)S(1)} %bitcast.7, f32[1,1536]{1,0:T(1,128)S(1)} %broadcast_in_dim.14.gain_ref, bf16[192,1536]{1,0:T(8,128)(2,1)S(1)} %copy-done.4), custom_call_target="tpu_custom_call" | custom-call | flops 100000000 | tf_op jit(solution)/shard_map/layer_norm/pallas_call | solution.py:100
  12.4 1.6 %collective-permute-start.9 = (bf16[384,512]{1,0:T(8,128)(2,1)S(1)}, bf16[384,512]{1,0:T(8,128)(2,1)S(1)}, u32[]{:S(2)}, u32[]{:S(2)}) collective-permute-start(bf16[384,512]{1,0:T(8,128)(2,1)S(1)} %get-tuple-element.65), channel_id=1, source_target_pairs={{0,16},{8,24},{16,0},{24,8},{1,17},{9,25},{17,1},{25,9},{2,18},{10... | collective-permute-start | bytes 1179656 | tf_op jit(solution)/shard_map/ppermute | solution.py:27
  14.0 1.6 %collective-permute-done.3.refs_1_ = bf16[384,256]{1,0:T(8,128)(2,1)S(1)} collective-permute-done((bf16[384,256]{1,0:T(8,128)(2,1)S(1)}, bf16[384,256]{1,0:T(8,128)(2,1)S(1)}, u32[]{:S(2)}, u32[]{:S(2)}) %collective-permute-start.3) | collective-permute-done | bytes 196640 | tf_op jit(solution)/shard_map/ppermute | solution.py:27
  15.6 2.7 %collective-permute-start.5 = (bf16[384,256]{1,0:T(8,128)(2,1)S(1)}, bf16[384,256]{1,0:T(8,128)(2,1)S(1)}, u32[]{:S(2)}, u32[]{:S(2)}) collective-permute-start(bf16[384,256]{1,0:T(8,128)(2,1)S(1)} %collective-permute-done.2.refs_1_), channel_id=1, source_target_pairs={{0,1},{1,0},{2,3},{3,2},{4,5},{5,4},{6,7},{7,6},{8,9},{9,8},{10,11... | collective-permute-start | bytes 589832 | tf_op jit(solution)/shard_map/ppermute | solution.py:27
  18.3 1.6 %collective-permute-start.7 = (bf16[384,256]{1,0:T(8,128)(2,1)S(1)}, bf16[384,256]{1,0:T(8,128)(2,1)S(1)}, u32[]{:S(2)}, u32[]{:S(2)}) collective-permute-start(bf16[384,256]{1,0:T(8,128)(2,1)S(1)} %collective-permute-done.3.refs_1_), channel_id=1, source_target_pairs={{0,2},{1,3},{2,0},{3,1},{4,6},{5,7},{6,4},{7,5},{8,10},{9,11},{10,... | collective-permute-start | bytes 589832 | tf_op jit(solution)/shard_map/ppermute | solution.py:27
  19.9 2.3 %near.1 = (bf16[544,1536]{1,0:T(8,128)(2,1)S(1)}, f32[544,512]{1,0:T(8,128)S(1)}, f32[544,512]{1,0:T(8,128)S(1)}, f32[544,512]{1,0:T(8,128)S(1)}) custom-call(s32[5]{0:T(128)S(1)} %stack.37.place_ref, bf16[512,1536]{1,0:T(8,128)(2,1)S(1)} %get-tuple-element.54.rows_ref, bf16[16,1536]{1,0:T(8,128)(2,1)S(1)} %collective-permute-done.inner_ref, ...), custom_call_target="tpu_custom_call" | custom-call | flops 100000000 | tf_op jit(solution)/shard_map/near/pallas_call | solution.py:148
  22.8 1.2 %collective-permute-done.7.refs_2_ = bf16[384,256]{1,0:T(8,128)(2,1)S(1)} collective-permute-done((bf16[384,256]{1,0:T(8,128)(2,1)S(1)}, bf16[384,256]{1,0:T(8,128)(2,1)S(1)}, u32[]{:S(2)}, u32[]{:S(2)}) %collective-permute-start.7) | collective-permute-done | bytes 196640 | tf_op jit(solution)/shard_map/ppermute | solution.py:27
  25.5 2.9 %front.3 = (f32[512,256]{1,0:T(8,128)S(1)}, f32[3,256]{1,0:T(4,128)S(1)}) custom-call(s32[5]{0:T(128)S(1)} %stack.37.place_ref, bf16[544,1536]{1,0:T(8,128)(2,1)S(1)} %get-tuple-element.57.normed_ref, f32[544,512]{1,0:T(8,128)S(1)} %get-tuple-element.66.refs_0_, bf16[384,256]{1,0:T(8,128)(2,1)S(1)} %collective-permute-done.2.refs_1_, ...), custom_call_target="tpu_custom_call" | custom-call | flops 100000000 | tf_op jit(solution)/shard_map/front/pallas_call | solution.py:233
  28.4 2.9 %front.4 = (f32[512,256]{1,0:T(8,128)S(1)}, f32[3,256]{1,0:T(4,128)S(1)}) custom-call(s32[5]{0:T(128)S(1)} %stack.37.place_ref, bf16[544,1536]{1,0:T(8,128)(2,1)S(1)} %get-tuple-element.57.normed_ref, f32[544,512]{1,0:T(8,128)S(1)} %get-tuple-element.73.refs_0_, bf16[384,256]{1,0:T(8,128)(2,1)S(1)} %collective-permute-done.3.refs_1_, ...), custom_call_target="tpu_custom_call" | custom-call | flops 4000000000 | tf_op jit(solution)/shard_map/front/pallas_call | solution.py:233
  31.3 2.9 %front.5 = (f32[512,256]{1,0:T(8,128)S(1)}, f32[1,3,768]{2,1,0:T(4,128)S(1)}) custom-call(s32[5]{0:T(128)S(1)} %stack.37.place_ref, bf16[544,1536]{1,0:T(8,128)(2,1)S(1)} %get-tuple-element.57.normed_ref, f32[3,256]{1,0:T(4,128)S(1)} %get-tuple-element.70.refs_0_, f32[3,256]{1,0:T(4,128)S(1)} %get-tuple-element.77.refs_1_, ...), custom_call_target="tpu_custom_call" | custom-call | flops 100000000 | tf_op jit(solution)/shard_map/front/pallas_call | solution.py:233
  35.5 1.6 %collective-permute-start.14 = (f32[1,3,768]{2,1,0:T(4,128)S(1)}, f32[1,3,768]{2,1,0:T(4,128)S(1)}, u32[]{:S(2)}, u32[]{:S(2)}) collective-permute-start(f32[1,3,768]{2,1,0:T(4,128)S(1)} %pad_maximum_fusion), channel_id=1, source_target_pairs={{0,2},{1,3},{2,0},{3,1},{4,6},{5,7},{6,4},{7,5},{8,10},{9,11},{10,... | collective-permute-start | bytes 27656 | tf_op jit(solution)/shard_map/ppermute | solution.py:407
  38.0 1.2 %collective-permute-done.14 = f32[1,3,768]{2,1,0:T(4,128)S(1)} collective-permute-done((f32[1,3,768]{2,1,0:T(4,128)S(1)}, f32[1,3,768]{2,1,0:T(4,128)S(1)}, u32[]{:S(2)}, u32[]{:S(2)}) %collective-permute-start.14) | collective-permute-done | bytes 9248 | tf_op jit(solution)/shard_map/ppermute | solution.py:407
  39.3 2.6 %collective-permute-start.15 = (f32[1,3,768]{2,1,0:T(4,128)S(1)}, f32[1,3,768]{2,1,0:T(4,128)S(1)}, u32[]{:S(2)}, u32[]{:S(2)}) collective-permute-start(f32[1,3,768]{2,1,0:T(4,128)S(1)} %pad_maximum_fusion.1), channel_id=1, source_target_pairs={{0,4},{1,5},{2,6},{3,7},{4,0},{5,1},{6,2},{7,3},{8,12},{9,13},{10,... | collective-permute-start | bytes 27656 | tf_op jit(solution)/shard_map/ppermute | solution.py:407
  41.9 2.0 %collective-permute-done.15 = f32[1,3,768]{2,1,0:T(4,128)S(1)} collective-permute-done((f32[1,3,768]{2,1,0:T(4,128)S(1)}, f32[1,3,768]{2,1,0:T(4,128)S(1)}, u32[]{:S(2)}, u32[]{:S(2)}) %collective-permute-start.15) | collective-permute-done | bytes 9248 | tf_op jit(solution)/shard_map/ppermute | solution.py:407
  44.0 1.9 %collective-permute-start.16 = (f32[1,3,768]{2,1,0:T(4,128)S(1)}, f32[1,3,768]{2,1,0:T(4,128)S(1)}, u32[]{:S(2)}, u32[]{:S(2)}) collective-permute-start(f32[1,3,768]{2,1,0:T(4,128)S(1)} %pad_maximum_fusion.2.refs_0_), channel_id=1, source_target_pairs={{0,1},{1,0},{2,3},{3,2},{4,5},{5,4},{6,7},{7,6},{8,9},{9,8},{10,11... | collective-permute-start | bytes 27656 | tf_op jit(solution)/shard_map/ppermute | solution.py:407
  45.9 1.5 %collective-permute-start.17 = (f32[1,3,768]{2,1,0:T(4,128)S(1)}, f32[1,3,768]{2,1,0:T(4,128)S(1)}, u32[]{:S(2)}, u32[]{:S(2)}) collective-permute-start(f32[1,3,768]{2,1,0:T(4,128)S(1)} %pad_maximum_fusion.2.refs_0_), channel_id=1, source_target_pairs={{0,16},{1,17},{2,18},{3,19},{4,20},{5,21},{6,22},{7,23},{8,24},{9,... | collective-permute-start | bytes 27656 | tf_op jit(solution)/shard_map/ppermute | solution.py:407
  47.5 4.9 %collective-permute-done.19.refs_9_ = bf16[192,1536]{1,0:T(8,128)(2,1)S(1)} collective-permute-done((bf16[192,1536]{1,0:T(8,128)(2,1)S(1)}, bf16[192,1536]{1,0:T(8,128)(2,1)S(1)}, u32[]{:S(2)}, u32[]{:S(2)}) %collective-permute-start.19) | collective-permute-done | bytes 589856 | tf_op jit(solution)/shard_map/ppermute | solution.py:27
  52.6 1.6 %collective-permute-done.18.refs_3_ = f32[1,3,768]{2,1,0:T(4,128)S(1)} collective-permute-done((f32[1,3,768]{2,1,0:T(4,128)S(1)}, f32[1,3,768]{2,1,0:T(4,128)S(1)}, u32[]{:S(2)}, u32[]{:S(2)}) %collective-permute-start.18) | collective-permute-done | bytes 9248 | tf_op jit(solution)/shard_map/ppermute | solution.py:407
  54.3 2.0 %collective-permute-done.21.refs_10_ = bf16[192,1536]{1,0:T(8,128)(2,1)S(1)} collective-permute-done((bf16[192,1536]{1,0:T(8,128)(2,1)S(1)}, bf16[192,1536]{1,0:T(8,128)(2,1)S(1)}, u32[]{:S(2)}, u32[]{:S(2)}) %collective-permute-start.21) | collective-permute-done | bytes 589856 | tf_op jit(solution)/shard_map/ppermute | solution.py:27
  56.2 2.9 %back.1 = bf16[512,1536]{1,0:T(8,128)(2,1)} custom-call(s32[5]{0:T(128)S(1)} %stack.37.place_ref, f32[1,768]{1,0:T(1,128)S(1)} %broadcast_in_dim.12.gain_ref, f32[1,768]{1,0:T(1,128)S(1)} %broadcast_in_dim.13.shift_ref, f32[1,3,768]{2,1,0:T(4,128)S(1)} %pad_maximum_fusion.2.refs_0_, f32[1,3,768]{2,1,0:T(4,128)S(1)} %collective-permute-done.16.refs_1_, ...), custom_call_target="tpu_custom_call" | custom-call | flops 1000000000 | tf_op jit(solution)/shard_map/back/pallas_call | solution.py:331
  (56 shorter events, 7.1 us)
Async XLA Ops:
  0.0 19.9 %collective-permute-start.4 = (bf16[384,1536]{1,0:T(8,128)(2,1)}, bf16[384,1536]{1,0:T(8,128)(2,1)S(1)}, u32[]{:S(2)}, u32[]{:S(2)}) collective-permute-start(bf16[384,1536]{1,0:T(8,128)(2,1)} %refs_0_.1), channel_id=1, source_target_pairs={{0,8},{8,0},{16,24},{24,16},{1,9},{9,1},{17,25},{25,17},{2,10},{10... | collective-permute-start | bytes 3538952 | tf_op jit(solution)/shard_map/ppermute | solution.py:27
  3.1 10.9 %collective-permute-start.2 = (bf16[384,256]{1,0:T(8,128)(2,1)S(1)}, bf16[384,256]{1,0:T(8,128)(2,1)S(1)}, u32[]{:S(2)}, u32[]{:S(2)}) collective-permute-start(bf16[384,256]{1,0:T(8,128)(2,1)S(1)} %get-tuple-element.52), channel_id=1, source_target_pairs={{0,16},{8,24},{16,0},{24,8},{1,17},{9,25},{17,1},{25,9},{2,18},{10... | collective-permute-start | bytes 589832 | tf_op jit(solution)/shard_map/ppermute | solution.py:27
  5.6 10.0 %collective-permute-start.3 = (bf16[384,256]{1,0:T(8,128)(2,1)S(1)}, bf16[384,256]{1,0:T(8,128)(2,1)S(1)}, u32[]{:S(2)}, u32[]{:S(2)}) collective-permute-start(bf16[384,256]{1,0:T(8,128)(2,1)S(1)} %get-tuple-element.53), channel_id=1, source_target_pairs={{0,16},{8,24},{16,0},{24,8},{1,17},{9,25},{17,1},{25,9},{2,18},{10... | collective-permute-start | bytes 589832 | tf_op jit(solution)/shard_map/ppermute | solution.py:27
  7.7 4.7 %collective-permute-start = (bf16[16,1536]{1,0:T(8,128)(2,1)S(1)}, bf16[16,1536]{1,0:T(8,128)(2,1)S(1)}, u32[]{:S(2)}, u32[]{:S(2)}) collective-permute-start(bf16[16,1536]{1,0:T(8,128)(2,1)S(1)} %get-tuple-element.50), channel_id=1, source_target_pairs={{0,1},{1,0},{2,3},{3,2},{4,5},{5,4},{6,7},{7,6},{8,9},{9,8},{10,11... | collective-permute-start | bytes 147464 | tf_op jit(solution)/shard_map/ppermute | solution.py:27
  9.7 4.2 %collective-permute-start.1 = (bf16[16,1536]{1,0:T(8,128)(2,1)S(1)}, bf16[16,1536]{1,0:T(8,128)(2,1)S(1)}, u32[]{:S(2)}, u32[]{:S(2)}) collective-permute-start(bf16[16,1536]{1,0:T(8,128)(2,1)S(1)} %get-tuple-element.51), channel_id=1, source_target_pairs={{1,2},{3,4},{5,6},{2,1},{4,3},{6,5},{9,10},{11,12},{13,14},{10,9},... | collective-permute-start | bytes 147464 | tf_op jit(solution)/shard_map/ppermute | solution.py:383
  12.4 12.2 %collective-permute-start.9 = (bf16[384,512]{1,0:T(8,128)(2,1)S(1)}, bf16[384,512]{1,0:T(8,128)(2,1)S(1)}, u32[]{:S(2)}, u32[]{:S(2)}) collective-permute-start(bf16[384,512]{1,0:T(8,128)(2,1)S(1)} %get-tuple-element.65), channel_id=1, source_target_pairs={{0,16},{8,24},{16,0},{24,8},{1,17},{9,25},{17,1},{25,9},{2,18},{10... | collective-permute-start | bytes 1179656 | tf_op jit(solution)/shard_map/ppermute | solution.py:27
  15.6 7.2 %collective-permute-start.5 = (bf16[384,256]{1,0:T(8,128)(2,1)S(1)}, bf16[384,256]{1,0:T(8,128)(2,1)S(1)}, u32[]{:S(2)}, u32[]{:S(2)}) collective-permute-start(bf16[384,256]{1,0:T(8,128)(2,1)S(1)} %collective-permute-done.2.refs_1_), channel_id=1, source_target_pairs={{0,1},{1,0},{2,3},{3,2},{4,5},{5,4},{6,7},{7,6},{8,9},{9,8},{10,11... | collective-permute-start | bytes 589832 | tf_op jit(solution)/shard_map/ppermute | solution.py:27
  18.3 5.7 %collective-permute-start.7 = (bf16[384,256]{1,0:T(8,128)(2,1)S(1)}, bf16[384,256]{1,0:T(8,128)(2,1)S(1)}, u32[]{:S(2)}, u32[]{:S(2)}) collective-permute-start(bf16[384,256]{1,0:T(8,128)(2,1)S(1)} %collective-permute-done.3.refs_1_), channel_id=1, source_target_pairs={{0,2},{1,3},{2,0},{3,1},{4,6},{5,7},{6,4},{7,5},{8,10},{9,11},{10,... | collective-permute-start | bytes 589832 | tf_op jit(solution)/shard_map/ppermute | solution.py:27
  22.2 1.7 %collective-permute-start.6 = (bf16[384,256]{1,0:T(8,128)(2,1)S(1)}, bf16[384,256]{1,0:T(8,128)(2,1)S(1)}, u32[]{:S(2)}, u32[]{:S(2)}) collective-permute-start(bf16[384,256]{1,0:T(8,128)(2,1)S(1)} %collective-permute-done.2.refs_1_), channel_id=1, source_target_pairs={{0,8},{8,0},{16,24},{24,16},{1,9},{9,1},{17,25},{25,17},{2,10},{10... | collective-permute-start | bytes 589832 | tf_op jit(solution)/shard_map/ppermute | solution.py:27
  22.3 1.7 %collective-permute-start.8 = (bf16[384,256]{1,0:T(8,128)(2,1)S(1)}, bf16[384,256]{1,0:T(8,128)(2,1)S(1)}, u32[]{:S(2)}, u32[]{:S(2)}) collective-permute-start(bf16[384,256]{1,0:T(8,128)(2,1)S(1)} %collective-permute-done.3.refs_1_), channel_id=1, source_target_pairs={{0,8},{8,0},{16,24},{24,16},{1,9},{9,1},{17,25},{25,17},{2,10},{10... | collective-permute-start | bytes 589832 | tf_op jit(solution)/shard_map/ppermute | solution.py:27
  24.0 1.4 %collective-permute-start.10 = (bf16[384,256]{1,0:T(8,128)(2,1)S(1)}, bf16[384,256]{1,0:T(8,128)(2,1)S(1)}, u32[]{:S(2)}, u32[]{:S(2)}) collective-permute-start(bf16[384,256]{1,0:T(8,128)(2,1)S(1)} %collective-permute-done.5.refs_2_), channel_id=1, source_target_pairs={{0,8},{8,0},{16,24},{24,16},{1,9},{9,1},{17,25},{25,17},{2,10},{10... | collective-permute-start | bytes 589832 | tf_op jit(solution)/shard_map/ppermute | solution.py:27
  24.3 4.1 %collective-permute-start.11 = (bf16[384,256]{1,0:T(8,128)(2,1)S(1)}, bf16[384,256]{1,0:T(8,128)(2,1)S(1)}, u32[]{:S(2)}, u32[]{:S(2)}) collective-permute-start(bf16[384,256]{1,0:T(8,128)(2,1)S(1)} %collective-permute-done.7.refs_2_), channel_id=1, source_target_pairs={{0,8},{8,0},{16,24},{24,16},{1,9},{9,1},{17,25},{25,17},{2,10},{10... | collective-permute-start | bytes 589832 | tf_op jit(solution)/shard_map/ppermute | solution.py:27
  24.6 6.7 %collective-permute-start.12 = (bf16[384,512]{1,0:T(8,128)(2,1)S(1)}, bf16[384,512]{1,0:T(8,128)(2,1)S(1)}, u32[]{:S(2)}, u32[]{:S(2)}) collective-permute-start(bf16[384,512]{1,0:T(8,128)(2,1)S(1)} %collective-permute-done.9.refs_3_), channel_id=1, source_target_pairs={{0,8},{8,0},{16,24},{24,16},{1,9},{9,1},{17,25},{25,17},{2,10},{10... | collective-permute-start | bytes 1179656 | tf_op jit(solution)/shard_map/ppermute | solution.py:27
  31.3 23.0 %copy-start.7 = (f32[768]{0:T(1024)S(1)}, f32[768]{0:T(1024)}, u32[]{:S(2)}) copy-start(f32[768]{0:T(1024)} %param.13) | copy-start | bytes 9220
  31.3 23.0 %copy-start.8 = (f32[768]{0:T(1024)S(1)}, f32[768]{0:T(1024)}, u32[]{:S(2)}) copy-start(f32[768]{0:T(1024)} %param.14) | copy-start | bytes 9220
  34.2 1.2 %collective-permute-start.13 = (f32[1,3,768]{2,1,0:T(4,128)S(1)}, f32[1,3,768]{2,1,0:T(4,128)S(1)}, u32[]{:S(2)}, u32[]{:S(2)}) collective-permute-start(f32[1,3,768]{2,1,0:T(4,128)S(1)} %get-tuple-element.82), channel_id=1, source_target_pairs={{0,8},{1,9},{2,10},{3,11},{4,12},{5,13},{6,14},{7,15},{8,0},{9,1},... | collective-permute-start | bytes 27656 | tf_op jit(solution)/shard_map/ppermute | solution.py:407
  35.5 3.8 %collective-permute-start.14 = (f32[1,3,768]{2,1,0:T(4,128)S(1)}, f32[1,3,768]{2,1,0:T(4,128)S(1)}, u32[]{:S(2)}, u32[]{:S(2)}) collective-permute-start(f32[1,3,768]{2,1,0:T(4,128)S(1)} %pad_maximum_fusion), channel_id=1, source_target_pairs={{0,2},{1,3},{2,0},{3,1},{4,6},{5,7},{6,4},{7,5},{8,10},{9,11},{10,... | collective-permute-start | bytes 27656 | tf_op jit(solution)/shard_map/ppermute | solution.py:407
  37.1 15.4 %collective-permute-start.19 = (bf16[192,1536]{1,0:T(8,128)(2,1)S(1)}, bf16[192,1536]{1,0:T(8,128)(2,1)S(1)}, u32[]{:S(2)}, u32[]{:S(2)}) collective-permute-start(bf16[192,1536]{1,0:T(8,128)(2,1)S(1)} %get-tuple-element.83), channel_id=1, source_target_pairs={{0,16},{8,24},{16,0},{24,8},{1,17},{9,25},{17,1},{25,9},{2,18},{10... | collective-permute-start | bytes 1769480 | tf_op jit(solution)/shard_map/ppermute | solution.py:27
  39.3 4.7 %collective-permute-start.15 = (f32[1,3,768]{2,1,0:T(4,128)S(1)}, f32[1,3,768]{2,1,0:T(4,128)S(1)}, u32[]{:S(2)}, u32[]{:S(2)}) collective-permute-start(f32[1,3,768]{2,1,0:T(4,128)S(1)} %pad_maximum_fusion.1), channel_id=1, source_target_pairs={{0,4},{1,5},{2,6},{3,7},{4,0},{5,1},{6,2},{7,3},{8,12},{9,13},{10,... | collective-permute-start | bytes 27656 | tf_op jit(solution)/shard_map/ppermute | solution.py:407
  44.0 8.5 %collective-permute-start.16 = (f32[1,3,768]{2,1,0:T(4,128)S(1)}, f32[1,3,768]{2,1,0:T(4,128)S(1)}, u32[]{:S(2)}, u32[]{:S(2)}) collective-permute-start(f32[1,3,768]{2,1,0:T(4,128)S(1)} %pad_maximum_fusion.2.refs_0_), channel_id=1, source_target_pairs={{0,1},{1,0},{2,3},{3,2},{4,5},{5,4},{6,7},{7,6},{8,9},{9,8},{10,11... | collective-permute-start | bytes 27656 | tf_op jit(solution)/shard_map/ppermute | solution.py:407
  45.9 6.7 %collective-permute-start.17 = (f32[1,3,768]{2,1,0:T(4,128)S(1)}, f32[1,3,768]{2,1,0:T(4,128)S(1)}, u32[]{:S(2)}, u32[]{:S(2)}) collective-permute-start(f32[1,3,768]{2,1,0:T(4,128)S(1)} %pad_maximum_fusion.2.refs_0_), channel_id=1, source_target_pairs={{0,16},{1,17},{2,18},{3,19},{4,20},{5,21},{6,22},{7,23},{8,24},{9,... | collective-permute-start | bytes 27656 | tf_op jit(solution)/shard_map/ppermute | solution.py:407
  47.4 6.8 %collective-permute-start.18 = (f32[1,3,768]{2,1,0:T(4,128)S(1)}, f32[1,3,768]{2,1,0:T(4,128)S(1)}, u32[]{:S(2)}, u32[]{:S(2)}) collective-permute-start(f32[1,3,768]{2,1,0:T(4,128)S(1)} %pad_maximum_fusion.2.refs_0_), channel_id=1, source_target_pairs={{0,17},{1,16},{2,19},{3,18},{4,21},{5,20},{6,23},{7,22},{8,25},{9,... | collective-permute-start | bytes 27656 | tf_op jit(solution)/shard_map/ppermute | solution.py:407
  47.5 6.7 %collective-permute-start.20 = (bf16[192,1536]{1,0:T(8,128)(2,1)S(1)}, bf16[192,1536]{1,0:T(8,128)(2,1)S(1)}, u32[]{:S(2)}, u32[]{:S(2)}) collective-permute-start(bf16[192,1536]{1,0:T(8,128)(2,1)S(1)} %copy-done.4), channel_id=1, source_target_pairs={{0,8},{8,0},{16,24},{24,16},{1,9},{9,1},{17,25},{25,17},{2,10},{10... | collective-permute-start | bytes 1769480 | tf_op jit(solution)/shard_map/ppermute | solution.py:27
  54.2 2.0 %collective-permute-start.21 = (bf16[192,1536]{1,0:T(8,128)(2,1)S(1)}, bf16[192,1536]{1,0:T(8,128)(2,1)S(1)}, u32[]{:S(2)}, u32[]{:S(2)}) collective-permute-start(bf16[192,1536]{1,0:T(8,128)(2,1)S(1)} %collective-permute-done.19.refs_9_), channel_id=1, source_target_pairs={{0,8},{8,0},{16,24},{24,16},{1,9},{9,1},{17,25},{25,17},{2,10},{10... | collective-permute-start | bytes 1769480 | tf_op jit(solution)/shard_map/ppermute | solution.py:27
  (7 other events, 44.0 us)

commit v15 on v12

--- a/solution.py
+++ b/solution.py
@@ -419,6 +419,7 @@
             return jnp.stack(merged([[part[:, i] for i in range(3)] for part in parts]), 1)
 
         stats = union([stats] + others([(1, 0)]))
+        stats, beyond[0] = tie(stats, beyond[0])
         stats = union([stats] + others([(0, 2)]))
         stats = union([stats] + others([(0, 4)]))
         stats = [stats] + others([(0, 1), (2, 0), (2, 1)])

time: 57.5 us -> 57.6 us (level)
    ppermute x17, waiting for transfers between devices: 4.58 us -> 5.27 us  [swap(): lax.ppermute(value, axis, [(i, i ^ bit) for i in range(lax.axis_size(axis...]
  transfers between devices with their start and end apart: 24 -> 24, of which waited for: 9 -> 10; matrix products, arithmetic and copies ran while one was open for 0% -> 0% of each run, Pallas kernels for 25% -> 25%
where the time goes in v15:
time: 57.6 us; the launch traced here: 57.4 us
  starting transfers between devices  24.4 us (42%)
  Pallas kernels  17 us (30%)
  waiting for transfers between devices  12.2 us (21%)
  local copies, waits for them, and re-layouts  2.81 us (5%)
  between operations  0.86 us (1%)
    ppermute x17, starting transfers between devices, swap(): lax.ppermute(value, axis, [(i, i ^ bit) for i in range(lax.axis_size(axis...  13.8 us
    ppermute x6, starting transfers between devices, others(): lax.ppermute(stats, both, [(member(f, p), member(f ^ df, p ^ dp)) for f i...  9.96 us
    pallas_call x3, Pallas kernels, front_block(): pl.pallas_call(functools.partial(front_kernel, block, len(earlier)), out_...  8.64 us
    ppermute x6, waiting for transfers between devices, others(): lax.ppermute(stats, both, [(member(f, p), member(f ^ df, p ^ dp)) for f i...  6.9 us
    ppermute x17, waiting for transfers between devices, swap(): lax.ppermute(value, axis, [(i, i ^ bit) for i in range(lax.axis_size(axis...  5.27 us
    pallas_call x1, Pallas kernels, back(): pl.pallas_call(functools.partial(back_kernel, len(stats)), out_shape=jax....  2.93 us
    unnamed x18, local copies, waits for them, and re-layouts  2.71 us
    pallas_call x1, Pallas kernels, near_product(): pl.pallas_call(near_kernel, out_shape=shapes, in_specs=[pl.BlockSpec(memo...  2.34 us
  transfers between devices with their start and end apart: 24, of which 10 were waited for; matrix products, arithmetic and copies ran while one was open for 0% of the time, Pallas kernels for 25%

profile of v15, /device:TPU:0, one launch (start us, length us, event | category | flops | bytes accessed | tf_op | source)
XLA Modules:
  0.0 57.4 jit_solution(9093476035909310208)
XLA Ops:
  1.2 1.3 %copy-done.2 = bf16[384,1536]{1,0:T(8,128)(2,1)S(1)} copy-done((bf16[384,1536]{1,0:T(8,128)(2,1)S(1)}, bf16[384,1536]{1,0:T(8,128)(2,1)}, u32[]{:S(2)}) %copy-start.2) | copy-done | bytes 1179672
  3.1 2.6 %collective-permute-start.2 = (bf16[384,256]{1,0:T(8,128)(2,1)S(1)}, bf16[384,256]{1,0:T(8,128)(2,1)S(1)}, u32[]{:S(2)}, u32[]{:S(2)}) collective-permute-start(bf16[384,256]{1,0:T(8,128)(2,1)S(1)} %get-tuple-element.57), channel_id=1, source_target_pairs={{0,16},{8,24},{16,0},{24,8},{1,17},{9,25},{17,1},{25,9},{2,18},{10... | collective-permute-start | bytes 589832 | tf_op jit(solution)/shard_map/ppermute | solution.py:27
  5.7 1.4 %copy-done = bf16[1,512,1536]{2,1,0:T(8,128)(2,1)S(1)} copy-done((bf16[1,512,1536]{2,1,0:T(8,128)(2,1)S(1)}, bf16[1,512,1536]{2,1,0:T(8,128)(2,1)}, u32[]{:S(2)}) %copy-start) | copy-done | bytes 1572888
  7.7 2.0 %collective-permute-start = (bf16[16,1536]{1,0:T(8,128)(2,1)S(1)}, bf16[16,1536]{1,0:T(8,128)(2,1)S(1)}, u32[]{:S(2)}, u32[]{:S(2)}) collective-permute-start(bf16[16,1536]{1,0:T(8,128)(2,1)S(1)} %get-tuple-element.55), channel_id=1, source_target_pairs={{0,1},{1,0},{2,3},{3,2},{4,5},{5,4},{6,7},{7,6},{8,9},{9,8},{10,11... | collective-permute-start | bytes 147464 | tf_op jit(solution)/shard_map/ppermute | solution.py:27
  10.4 1.9 %layer_norm.1 = (bf16[512,1536]{1,0:T(8,128)(2,1)S(1)}, bf16[64,1536]{1,0:T(8,128)(2,1)S(1)}, bf16[128,1536]{1,0:T(8,128)(2,1)S(1)}) custom-call(bf16[512,1536]{1,0:T(8,128)(2,1)S(1)} %bitcast.7, f32[1,1536]{1,0:T(1,128)S(1)} %broadcast_in_dim.14.gain_ref, bf16[192,1536]{1,0:T(8,128)(2,1)S(1)} %copy-done.4), custom_call_target="tpu_custom_call" | custom-call | flops 100000000 | tf_op jit(solution)/shard_map/layer_norm/pallas_call | solution.py:100
  12.4 1.6 %collective-permute-start.9 = (bf16[384,512]{1,0:T(8,128)(2,1)S(1)}, bf16[384,512]{1,0:T(8,128)(2,1)S(1)}, u32[]{:S(2)}, u32[]{:S(2)}) collective-permute-start(bf16[384,512]{1,0:T(8,128)(2,1)S(1)} %get-tuple-element.70), channel_id=1, source_target_pairs={{0,16},{8,24},{16,0},{24,8},{1,17},{9,25},{17,1},{25,9},{2,18},{10... | collective-permute-start | bytes 1179656 | tf_op jit(solution)/shard_map/ppermute | solution.py:27
  14.0 1.6 %collective-permute-done.3.refs_1_ = bf16[384,256]{1,0:T(8,128)(2,1)S(1)} collective-permute-done((bf16[384,256]{1,0:T(8,128)(2,1)S(1)}, bf16[384,256]{1,0:T(8,128)(2,1)S(1)}, u32[]{:S(2)}, u32[]{:S(2)}) %collective-permute-start.3) | collective-permute-done | bytes 196640 | tf_op jit(solution)/shard_map/ppermute | solution.py:27
  15.6 2.7 %collective-permute-start.5 = (bf16[384,256]{1,0:T(8,128)(2,1)S(1)}, bf16[384,256]{1,0:T(8,128)(2,1)S(1)}, u32[]{:S(2)}, u32[]{:S(2)}) collective-permute-start(bf16[384,256]{1,0:T(8,128)(2,1)S(1)} %collective-permute-done.2.refs_1_), channel_id=1, source_target_pairs={{0,1},{1,0},{2,3},{3,2},{4,5},{5,4},{6,7},{7,6},{8,9},{9,8},{10,11... | collective-permute-start | bytes 589832 | tf_op jit(solution)/shard_map/ppermute | solution.py:27
  18.3 1.6 %collective-permute-start.7 = (bf16[384,256]{1,0:T(8,128)(2,1)S(1)}, bf16[384,256]{1,0:T(8,128)(2,1)S(1)}, u32[]{:S(2)}, u32[]{:S(2)}) collective-permute-start(bf16[384,256]{1,0:T(8,128)(2,1)S(1)} %collective-permute-done.3.refs_1_), channel_id=1, source_target_pairs={{0,2},{1,3},{2,0},{3,1},{4,6},{5,7},{6,4},{7,5},{8,10},{9,11},{10,... | collective-permute-start | bytes 589832 | tf_op jit(solution)/shard_map/ppermute | solution.py:27
  19.9 2.3 %near.1 = (bf16[544,1536]{1,0:T(8,128)(2,1)S(1)}, f32[544,512]{1,0:T(8,128)S(1)}, f32[544,512]{1,0:T(8,128)S(1)}, f32[544,512]{1,0:T(8,128)S(1)}) custom-call(s32[5]{0:T(128)S(1)} %stack.37.place_ref, bf16[512,1536]{1,0:T(8,128)(2,1)S(1)} %get-tuple-element.59.rows_ref, bf16[16,1536]{1,0:T(8,128)(2,1)S(1)} %collective-permute-done.inner_ref, ...), custom_call_target="tpu_custom_call" | custom-call | flops 100000000 | tf_op jit(solution)/shard_map/near/pallas_call | solution.py:148
  22.8 1.2 %collective-permute-done.7.refs_2_ = bf16[384,256]{1,0:T(8,128)(2,1)S(1)} collective-permute-done((bf16[384,256]{1,0:T(8,128)(2,1)S(1)}, bf16[384,256]{1,0:T(8,128)(2,1)S(1)}, u32[]{:S(2)}, u32[]{:S(2)}) %collective-permute-start.7) | collective-permute-done | bytes 196640 | tf_op jit(solution)/shard_map/ppermute | solution.py:27
  25.6 2.9 %front.3 = (f32[512,256]{1,0:T(8,128)S(1)}, f32[3,256]{1,0:T(4,128)S(1)}) custom-call(s32[5]{0:T(128)S(1)} %stack.37.place_ref, bf16[544,1536]{1,0:T(8,128)(2,1)S(1)} %get-tuple-element.62.normed_ref, f32[544,512]{1,0:T(8,128)S(1)} %get-tuple-element.71.refs_0_, bf16[384,256]{1,0:T(8,128)(2,1)S(1)} %collective-permute-done.2.refs_1_, ...), custom_call_target="tpu_custom_call" | custom-call | flops 100000000 | tf_op jit(solution)/shard_map/front/pallas_call | solution.py:233
  28.5 2.9 %front.4 = (f32[512,256]{1,0:T(8,128)S(1)}, f32[3,256]{1,0:T(4,128)S(1)}) custom-call(s32[5]{0:T(128)S(1)} %stack.37.place_ref, bf16[544,1536]{1,0:T(8,128)(2,1)S(1)} %get-tuple-element.62.normed_ref, f32[544,512]{1,0:T(8,128)S(1)} %get-tuple-element.78.refs_0_, bf16[384,256]{1,0:T(8,128)(2,1)S(1)} %collective-permute-done.3.refs_1_, ...), custom_call_target="tpu_custom_call" | custom-call | flops 4000000000 | tf_op jit(solution)/shard_map/front/pallas_call | solution.py:233
  31.4 2.9 %front.5 = (f32[512,256]{1,0:T(8,128)S(1)}, f32[1,3,768]{2,1,0:T(4,128)S(1)}) custom-call(s32[5]{0:T(128)S(1)} %stack.37.place_ref, bf16[544,1536]{1,0:T(8,128)(2,1)S(1)} %get-tuple-element.62.normed_ref, f32[3,256]{1,0:T(4,128)S(1)} %get-tuple-element.75.refs_0_, f32[3,256]{1,0:T(4,128)S(1)} %get-tuple-element.82.refs_1_, ...), custom_call_target="tpu_custom_call" | custom-call | flops 100000000 | tf_op jit(solution)/shard_map/front/pallas_call | solution.py:233
  36.0 2.1 %collective-permute-start.16 = (f32[1,3,768]{2,1,0:T(4,128)S(1)}, f32[1,3,768]{2,1,0:T(4,128)S(1)}, u32[]{:S(2)}, u32[]{:S(2)}) collective-permute-start(f32[1,3,768]{2,1,0:T(4,128)S(1)} %pad_maximum_fusion), channel_id=1, source_target_pairs={{0,2},{1,3},{2,0},{3,1},{4,6},{5,7},{6,4},{7,5},{8,10},{9,11},{10,... | collective-permute-start | bytes 27656 | tf_op jit(solution)/shard_map/ppermute | solution.py:410
  38.6 1.3 %collective-permute-done.16 = f32[1,3,768]{2,1,0:T(4,128)S(1)} collective-permute-done((f32[1,3,768]{2,1,0:T(4,128)S(1)}, f32[1,3,768]{2,1,0:T(4,128)S(1)}, u32[]{:S(2)}, u32[]{:S(2)}) %collective-permute-start.16) | collective-permute-done | bytes 9248 | tf_op jit(solution)/shard_map/ppermute | solution.py:410
  39.9 3.1 %collective-permute-start.17 = (f32[1,3,768]{2,1,0:T(4,128)S(1)}, f32[1,3,768]{2,1,0:T(4,128)S(1)}, u32[]{:S(2)}, u32[]{:S(2)}) collective-permute-start(f32[1,3,768]{2,1,0:T(4,128)S(1)} %pad_maximum_fusion.1), channel_id=1, source_target_pairs={{0,4},{1,5},{2,6},{3,7},{4,0},{5,1},{6,2},{7,3},{8,12},{9,13},{10,... | collective-permute-start | bytes 27656 | tf_op jit(solution)/shard_map/ppermute | solution.py:410
  43.0 1.7 %collective-permute-done.17 = f32[1,3,768]{2,1,0:T(4,128)S(1)} collective-permute-done((f32[1,3,768]{2,1,0:T(4,128)S(1)}, f32[1,3,768]{2,1,0:T(4,128)S(1)}, u32[]{:S(2)}, u32[]{:S(2)}) %collective-permute-start.17) | collective-permute-done | bytes 9248 | tf_op jit(solution)/shard_map/ppermute | solution.py:410
  44.7 2.9 %collective-permute-start.18 = (f32[1,3,768]{2,1,0:T(4,128)S(1)}, f32[1,3,768]{2,1,0:T(4,128)S(1)}, u32[]{:S(2)}, u32[]{:S(2)}) collective-permute-start(f32[1,3,768]{2,1,0:T(4,128)S(1)} %pad_maximum_fusion.2.refs_0_), channel_id=1, source_target_pairs={{0,1},{1,0},{2,3},{3,2},{4,5},{5,4},{6,7},{7,6},{8,9},{9,8},{10,11... | collective-permute-start | bytes 27656 | tf_op jit(solution)/shard_map/ppermute | solution.py:410
  48.1 1.0 %collective-permute-start.20 = (f32[1,3,768]{2,1,0:T(4,128)S(1)}, f32[1,3,768]{2,1,0:T(4,128)S(1)}, u32[]{:S(2)}, u32[]{:S(2)}) collective-permute-start(f32[1,3,768]{2,1,0:T(4,128)S(1)} %pad_maximum_fusion.2.refs_0_), channel_id=1, source_target_pairs={{0,17},{1,16},{2,19},{3,18},{4,21},{5,20},{6,23},{7,22},{8,25},{9,... | collective-permute-start | bytes 27656 | tf_op jit(solution)/shard_map/ppermute | solution.py:410
  49.4 1.9 %collective-permute-done.19.refs_2_ = f32[1,3,768]{2,1,0:T(4,128)S(1)} collective-permute-done((f32[1,3,768]{2,1,0:T(4,128)S(1)}, f32[1,3,768]{2,1,0:T(4,128)S(1)}, u32[]{:S(2)}, u32[]{:S(2)}) %collective-permute-start.19) | collective-permute-done | bytes 9248 | tf_op jit(solution)/shard_map/ppermute | solution.py:410
  51.3 1.4 %collective-permute-done.20.refs_3_ = f32[1,3,768]{2,1,0:T(4,128)S(1)} collective-permute-done((f32[1,3,768]{2,1,0:T(4,128)S(1)}, f32[1,3,768]{2,1,0:T(4,128)S(1)}, u32[]{:S(2)}, u32[]{:S(2)}) %collective-permute-start.20) | collective-permute-done | bytes 9248 | tf_op jit(solution)/shard_map/ppermute | solution.py:410
  52.8 1.7 %collective-permute-done.23.refs_12_ = bf16[128,1536]{1,0:T(8,128)(2,1)S(1)} collective-permute-done((bf16[128,1536]{1,0:T(8,128)(2,1)S(1)}, bf16[128,1536]{1,0:T(8,128)(2,1)S(1)}, u32[]{:S(2)}, u32[]{:S(2)}) %collective-permute-start.23) | collective-permute-done | bytes 393248 | tf_op jit(solution)/shard_map/ppermute | solution.py:27
  54.5 2.9 %back.1 = bf16[512,1536]{1,0:T(8,128)(2,1)} custom-call(s32[5]{0:T(128)S(1)} %stack.37.place_ref, f32[1,768]{1,0:T(1,128)S(1)} %broadcast_in_dim.12.gain_ref, f32[1,768]{1,0:T(1,128)S(1)} %broadcast_in_dim.13.shift_ref, f32[1,3,768]{2,1,0:T(4,128)S(1)} %pad_maximum_fusion.2.refs_0_, f32[1,3,768]{2,1,0:T(4,128)S(1)} %collective-permute-done.18.refs_1_, ...), custom_call_target="tpu_custom_call" | custom-call | flops 1000000000 | tf_op jit(solution)/shard_map/back/pallas_call | solution.py:331
  (60 shorter events, 7.7 us)
Async XLA Ops:
  0.0 19.9 %collective-permute-start.4 = (bf16[384,1536]{1,0:T(8,128)(2,1)}, bf16[384,1536]{1,0:T(8,128)(2,1)S(1)}, u32[]{:S(2)}, u32[]{:S(2)}) collective-permute-start(bf16[384,1536]{1,0:T(8,128)(2,1)} %refs_0_.1), channel_id=1, source_target_pairs={{0,8},{8,0},{16,24},{24,16},{1,9},{9,1},{17,25},{25,17},{2,10},{10... | collective-permute-start | bytes 3538952 | tf_op jit(solution)/shard_map/ppermute | solution.py:27
  3.1 10.9 %collective-permute-start.2 = (bf16[384,256]{1,0:T(8,128)(2,1)S(1)}, bf16[384,256]{1,0:T(8,128)(2,1)S(1)}, u32[]{:S(2)}, u32[]{:S(2)}) collective-permute-start(bf16[384,256]{1,0:T(8,128)(2,1)S(1)} %get-tuple-element.57), channel_id=1, source_target_pairs={{0,16},{8,24},{16,0},{24,8},{1,17},{9,25},{17,1},{25,9},{2,18},{10... | collective-permute-start | bytes 589832 | tf_op jit(solution)/shard_map/ppermute | solution.py:27
  5.6 10.0 %collective-permute-start.3 = (bf16[384,256]{1,0:T(8,128)(2,1)S(1)}, bf16[384,256]{1,0:T(8,128)(2,1)S(1)}, u32[]{:S(2)}, u32[]{:S(2)}) collective-permute-start(bf16[384,256]{1,0:T(8,128)(2,1)S(1)} %get-tuple-element.58), channel_id=1, source_target_pairs={{0,16},{8,24},{16,0},{24,8},{1,17},{9,25},{17,1},{25,9},{2,18},{10... | collective-permute-start | bytes 589832 | tf_op jit(solution)/shard_map/ppermute | solution.py:27
  7.7 4.7 %collective-permute-start = (bf16[16,1536]{1,0:T(8,128)(2,1)S(1)}, bf16[16,1536]{1,0:T(8,128)(2,1)S(1)}, u32[]{:S(2)}, u32[]{:S(2)}) collective-permute-start(bf16[16,1536]{1,0:T(8,128)(2,1)S(1)} %get-tuple-element.55), channel_id=1, source_target_pairs={{0,1},{1,0},{2,3},{3,2},{4,5},{5,4},{6,7},{7,6},{8,9},{9,8},{10,11... | collective-permute-start | bytes 147464 | tf_op jit(solution)/shard_map/ppermute | solution.py:27
  9.7 4.2 %collective-permute-start.1 = (bf16[16,1536]{1,0:T(8,128)(2,1)S(1)}, bf16[16,1536]{1,0:T(8,128)(2,1)S(1)}, u32[]{:S(2)}, u32[]{:S(2)}) collective-permute-start(bf16[16,1536]{1,0:T(8,128)(2,1)S(1)} %get-tuple-element.56), channel_id=1, source_target_pairs={{1,2},{3,4},{5,6},{2,1},{4,3},{6,5},{9,10},{11,12},{13,14},{10,9},... | collective-permute-start | bytes 147464 | tf_op jit(solution)/shard_map/ppermute | solution.py:384
  12.4 12.2 %collective-permute-start.9 = (bf16[384,512]{1,0:T(8,128)(2,1)S(1)}, bf16[384,512]{1,0:T(8,128)(2,1)S(1)}, u32[]{:S(2)}, u32[]{:S(2)}) collective-permute-start(bf16[384,512]{1,0:T(8,128)(2,1)S(1)} %get-tuple-element.70), channel_id=1, source_target_pairs={{0,16},{8,24},{16,0},{24,8},{1,17},{9,25},{17,1},{25,9},{2,18},{10... | collective-permute-start | bytes 1179656 | tf_op jit(solution)/shard_map/ppermute | solution.py:27
  15.6 7.2 %collective-permute-start.5 = (bf16[384,256]{1,0:T(8,128)(2,1)S(1)}, bf16[384,256]{1,0:T(8,128)(2,1)S(1)}, u32[]{:S(2)}, u32[]{:S(2)}) collective-permute-start(bf16[384,256]{1,0:T(8,128)(2,1)S(1)} %collective-permute-done.2.refs_1_), channel_id=1, source_target_pairs={{0,1},{1,0},{2,3},{3,2},{4,5},{5,4},{6,7},{7,6},{8,9},{9,8},{10,11... | collective-permute-start | bytes 589832 | tf_op jit(solution)/shard_map/ppermute | solution.py:27
  18.3 5.7 %collective-permute-start.7 = (bf16[384,256]{1,0:T(8,128)(2,1)S(1)}, bf16[384,256]{1,0:T(8,128)(2,1)S(1)}, u32[]{:S(2)}, u32[]{:S(2)}) collective-permute-start(bf16[384,256]{1,0:T(8,128)(2,1)S(1)} %collective-permute-done.3.refs_1_), channel_id=1, source_target_pairs={{0,2},{1,3},{2,0},{3,1},{4,6},{5,7},{6,4},{7,5},{8,10},{9,11},{10,... | collective-permute-start | bytes 589832 | tf_op jit(solution)/shard_map/ppermute | solution.py:27
  22.2 1.7 %collective-permute-start.6 = (bf16[384,256]{1,0:T(8,128)(2,1)S(1)}, bf16[384,256]{1,0:T(8,128)(2,1)S(1)}, u32[]{:S(2)}, u32[]{:S(2)}) collective-permute-start(bf16[384,256]{1,0:T(8,128)(2,1)S(1)} %collective-permute-done.2.refs_1_), channel_id=1, source_target_pairs={{0,8},{8,0},{16,24},{24,16},{1,9},{9,1},{17,25},{25,17},{2,10},{10... | collective-permute-start | bytes 589832 | tf_op jit(solution)/shard_map/ppermute | solution.py:27
  22.3 1.7 %collective-permute-start.8 = (bf16[384,256]{1,0:T(8,128)(2,1)S(1)}, bf16[384,256]{1,0:T(8,128)(2,1)S(1)}, u32[]{:S(2)}, u32[]{:S(2)}) collective-permute-start(bf16[384,256]{1,0:T(8,128)(2,1)S(1)} %collective-permute-done.3.refs_1_), channel_id=1, source_target_pairs={{0,8},{8,0},{16,24},{24,16},{1,9},{9,1},{17,25},{25,17},{2,10},{10... | collective-permute-start | bytes 589832 | tf_op jit(solution)/shard_map/ppermute | solution.py:27
  24.0 1.6 %collective-permute-start.10 = (bf16[384,256]{1,0:T(8,128)(2,1)S(1)}, bf16[384,256]{1,0:T(8,128)(2,1)S(1)}, u32[]{:S(2)}, u32[]{:S(2)}) collective-permute-start(bf16[384,256]{1,0:T(8,128)(2,1)S(1)} %collective-permute-done.5.refs_2_), channel_id=1, source_target_pairs={{0,8},{8,0},{16,24},{24,16},{1,9},{9,1},{17,25},{25,17},{2,10},{10... | collective-permute-start | bytes 589832 | tf_op jit(solution)/shard_map/ppermute | solution.py:27
  24.3 4.2 %collective-permute-start.11 = (bf16[384,256]{1,0:T(8,128)(2,1)S(1)}, bf16[384,256]{1,0:T(8,128)(2,1)S(1)}, u32[]{:S(2)}, u32[]{:S(2)}) collective-permute-start(bf16[384,256]{1,0:T(8,128)(2,1)S(1)} %collective-permute-done.7.refs_2_), channel_id=1, source_target_pairs={{0,8},{8,0},{16,24},{24,16},{1,9},{9,1},{17,25},{25,17},{2,10},{10... | collective-permute-start | bytes 589832 | tf_op jit(solution)/shard_map/ppermute | solution.py:27
  24.6 6.8 %collective-permute-start.12 = (bf16[384,512]{1,0:T(8,128)(2,1)S(1)}, bf16[384,512]{1,0:T(8,128)(2,1)S(1)}, u32[]{:S(2)}, u32[]{:S(2)}) collective-permute-start(bf16[384,512]{1,0:T(8,128)(2,1)S(1)} %collective-permute-done.9.refs_3_), channel_id=1, source_target_pairs={{0,8},{8,0},{16,24},{24,16},{1,9},{9,1},{17,25},{25,17},{2,10},{10... | collective-permute-start | bytes 1179656 | tf_op jit(solution)/shard_map/ppermute | solution.py:27
  24.8 9.5 %collective-permute-start.13 = (bf16[64,1536]{1,0:T(8,128)(2,1)S(1)}, bf16[64,1536]{1,0:T(8,128)(2,1)S(1)}, u32[]{:S(2)}, u32[]{:S(2)}) collective-permute-start(bf16[64,1536]{1,0:T(8,128)(2,1)S(1)} %get-tuple-element.88), channel_id=1, source_target_pairs={{0,16},{8,24},{16,0},{24,8},{1,17},{9,25},{17,1},{25,9},{2,18},{10... | collective-permute-start | bytes 589832 | tf_op jit(solution)/shard_map/ppermute | solution.py:27
  34.3 1.2 %collective-permute-start.14 = (f32[1,3,768]{2,1,0:T(4,128)S(1)}, f32[1,3,768]{2,1,0:T(4,128)S(1)}, u32[]{:S(2)}, u32[]{:S(2)}) collective-permute-start(f32[1,3,768]{2,1,0:T(4,128)S(1)} %get-tuple-element.89), channel_id=1, source_target_pairs={{0,8},{1,9},{2,10},{3,11},{4,12},{5,13},{6,14},{7,15},{8,0},{9,1},... | collective-permute-start | bytes 27656 | tf_op jit(solution)/shard_map/ppermute | solution.py:410
  34.6 1.4 %collective-permute-start.15 = (bf16[64,1536]{1,0:T(8,128)(2,1)S(1)}, bf16[64,1536]{1,0:T(8,128)(2,1)S(1)}, u32[]{:S(2)}, u32[]{:S(2)}) collective-permute-start(bf16[64,1536]{1,0:T(8,128)(2,1)S(1)} %collective-permute-done.13.refs_9_), channel_id=1, source_target_pairs={{0,8},{8,0},{16,24},{24,16},{1,9},{9,1},{17,25},{25,17},{2,10},{10... | collective-permute-start | bytes 589832 | tf_op jit(solution)/shard_map/ppermute | solution.py:27
  36.0 3.8 %collective-permute-start.16 = (f32[1,3,768]{2,1,0:T(4,128)S(1)}, f32[1,3,768]{2,1,0:T(4,128)S(1)}, u32[]{:S(2)}, u32[]{:S(2)}) collective-permute-start(f32[1,3,768]{2,1,0:T(4,128)S(1)} %pad_maximum_fusion), channel_id=1, source_target_pairs={{0,2},{1,3},{2,0},{3,1},{4,6},{5,7},{6,4},{7,5},{8,10},{9,11},{10,... | collective-permute-start | bytes 27656 | tf_op jit(solution)/shard_map/ppermute | solution.py:410
  38.2 11.3 %collective-permute-start.21 = (bf16[128,1536]{1,0:T(8,128)(2,1)S(1)}, bf16[128,1536]{1,0:T(8,128)(2,1)S(1)}, u32[]{:S(2)}, u32[]{:S(2)}) collective-permute-start(bf16[128,1536]{1,0:T(8,128)(2,1)S(1)} %get-tuple-element.92), channel_id=1, source_target_pairs={{0,16},{8,24},{16,0},{24,8},{1,17},{9,25},{17,1},{25,9},{2,18},{10... | collective-permute-start | bytes 1179656 | tf_op jit(solution)/shard_map/ppermute | solution.py:27
  39.9 4.8 %collective-permute-start.17 = (f32[1,3,768]{2,1,0:T(4,128)S(1)}, f32[1,3,768]{2,1,0:T(4,128)S(1)}, u32[]{:S(2)}, u32[]{:S(2)}) collective-permute-start(f32[1,3,768]{2,1,0:T(4,128)S(1)} %pad_maximum_fusion.1), channel_id=1, source_target_pairs={{0,4},{1,5},{2,6},{3,7},{4,0},{5,1},{6,2},{7,3},{8,12},{9,13},{10,... | collective-permute-start | bytes 27656 | tf_op jit(solution)/shard_map/ppermute | solution.py:410
  43.0 9.8 %collective-permute-start.22 = (bf16[192,1536]{1,0:T(8,128)(2,1)S(1)}, bf16[192,1536]{1,0:T(8,128)(2,1)S(1)}, u32[]{:S(2)}, u32[]{:S(2)}) collective-permute-start(bf16[192,1536]{1,0:T(8,128)(2,1)S(1)} %copy-done.4), channel_id=1, source_target_pairs={{0,8},{8,0},{16,24},{24,16},{1,9},{9,1},{17,25},{25,17},{2,10},{10... | collective-permute-start | bytes 1769480 | tf_op jit(solution)/shard_map/ppermute | solution.py:27
  44.7 4.8 %collective-permute-start.18 = (f32[1,3,768]{2,1,0:T(4,128)S(1)}, f32[1,3,768]{2,1,0:T(4,128)S(1)}, u32[]{:S(2)}, u32[]{:S(2)}) collective-permute-start(f32[1,3,768]{2,1,0:T(4,128)S(1)} %pad_maximum_fusion.2.refs_0_), channel_id=1, source_target_pairs={{0,1},{1,0},{2,3},{3,2},{4,5},{5,4},{6,7},{7,6},{8,9},{9,8},{10,11... | collective-permute-start | bytes 27656 | tf_op jit(solution)/shard_map/ppermute | solution.py:410
  47.6 3.7 %collective-permute-start.19 = (f32[1,3,768]{2,1,0:T(4,128)S(1)}, f32[1,3,768]{2,1,0:T(4,128)S(1)}, u32[]{:S(2)}, u32[]{:S(2)}) collective-permute-start(f32[1,3,768]{2,1,0:T(4,128)S(1)} %pad_maximum_fusion.2.refs_0_), channel_id=1, source_target_pairs={{0,16},{1,17},{2,18},{3,19},{4,20},{5,21},{6,22},{7,23},{8,24},{9,... | collective-permute-start | bytes 27656 | tf_op jit(solution)/shard_map/ppermute | solution.py:410
  48.1 4.6 %collective-permute-start.20 = (f32[1,3,768]{2,1,0:T(4,128)S(1)}, f32[1,3,768]{2,1,0:T(4,128)S(1)}, u32[]{:S(2)}, u32[]{:S(2)}) collective-permute-start(f32[1,3,768]{2,1,0:T(4,128)S(1)} %pad_maximum_fusion.2.refs_0_), channel_id=1, source_target_pairs={{0,17},{1,16},{2,19},{3,18},{4,21},{5,20},{6,23},{7,22},{8,25},{9,... | collective-permute-start | bytes 27656 | tf_op jit(solution)/shard_map/ppermute | solution.py:410
  52.7 1.7 %collective-permute-start.23 = (bf16[128,1536]{1,0:T(8,128)(2,1)S(1)}, bf16[128,1536]{1,0:T(8,128)(2,1)S(1)}, u32[]{:S(2)}, u32[]{:S(2)}) collective-permute-start(bf16[128,1536]{1,0:T(8,128)(2,1)S(1)} %collective-permute-done.21.refs_10_), channel_id=1, source_target_pairs={{0,8},{8,0},{16,24},{24,16},{1,9},{9,1},{17,25},{25,17},{2,10},{10... | collective-permute-start | bytes 1179656 | tf_op jit(solution)/shard_map/ppermute | solution.py:27
  (9 other events, 86.8 us)

commit v16 on v12

--- a/solution.py
+++ b/solution.py
@@ -327,7 +327,7 @@
 def back(place, stats, gain, shift, convs, weights):
     row_count = convs[0].shape[0]
     channels, width = gain.shape[1], weights[0].shape[1]
-    pieces, across = 4, 2
+    pieces, across = 6, 3
     return pl.pallas_call(
         functools.partial(back_kernel, len(stats)),
         out_shape=jax.ShapeDtypeStruct((row_count, width), jnp.bfloat16),

time: 57.5 us -> 57.5 us (level)
  no operation moved by 1% of the time
where the time goes in v16:
time: 57.5 us; the launch traced here: 57.3 us
  starting transfers between devices  24.8 us (43%)
  Pallas kernels  17 us (30%)
  waiting for transfers between devices  11.7 us (20%)
  local copies, waits for them, and re-layouts  2.81 us (5%)
  between operations  0.85 us (1%)
    ppermute x17, starting transfers between devices, swap(): lax.ppermute(value, axis, [(i, i ^ bit) for i in range(lax.axis_size(axis...  14.1 us
    ppermute x6, starting transfers between devices, others(): lax.ppermute(stats, both, [(member(f, p), member(f ^ df, p ^ dp)) for f i...  10 us
    pallas_call x3, Pallas kernels, front_block(): pl.pallas_call(functools.partial(front_kernel, block, len(earlier)), out_...  8.64 us
    ppermute x6, waiting for transfers between devices, others(): lax.ppermute(stats, both, [(member(f, p), member(f ^ df, p ^ dp)) for f i...  7.17 us
    ppermute x17, waiting for transfers between devices, swap(): lax.ppermute(value, axis, [(i, i ^ bit) for i in range(lax.axis_size(axis...  4.58 us
    pallas_call x1, Pallas kernels, back(): pl.pallas_call(functools.partial(back_kernel, len(stats)), out_shape=jax....  2.92 us
    unnamed x18, local copies, waits for them, and re-layouts  2.71 us
    pallas_call x1, Pallas kernels, near_product(): pl.pallas_call(near_kernel, out_shape=shapes, in_specs=[pl.BlockSpec(memo...  2.34 us
  transfers between devices with their start and end apart: 24, of which 9 were waited for; matrix products, arithmetic and copies ran while one was open for 0% of the time, Pallas kernels for 25%

profile of v16, /device:TPU:0, one launch (start us, length us, event | category | flops | bytes accessed | tf_op | source)
XLA Modules:
  0.0 57.3 jit_solution(14073965003477304773)
XLA Ops:
  1.2 1.3 %copy-done.2 = bf16[384,1536]{1,0:T(8,128)(2,1)S(1)} copy-done((bf16[384,1536]{1,0:T(8,128)(2,1)S(1)}, bf16[384,1536]{1,0:T(8,128)(2,1)}, u32[]{:S(2)}) %copy-start.2) | copy-done | bytes 1179672
  3.1 2.6 %collective-permute-start.2 = (bf16[384,256]{1,0:T(8,128)(2,1)S(1)}, bf16[384,256]{1,0:T(8,128)(2,1)S(1)}, u32[]{:S(2)}, u32[]{:S(2)}) collective-permute-start(bf16[384,256]{1,0:T(8,128)(2,1)S(1)} %get-tuple-element.55), channel_id=1, source_target_pairs={{0,16},{8,24},{16,0},{24,8},{1,17},{9,25},{17,1},{25,9},{2,18},{10... | collective-permute-start | bytes 589832 | tf_op jit(solution)/shard_map/ppermute | solution.py:27
  5.7 1.4 %copy-done = bf16[1,512,1536]{2,1,0:T(8,128)(2,1)S(1)} copy-done((bf16[1,512,1536]{2,1,0:T(8,128)(2,1)S(1)}, bf16[1,512,1536]{2,1,0:T(8,128)(2,1)}, u32[]{:S(2)}) %copy-start) | copy-done | bytes 1572888
  7.7 2.0 %collective-permute-start = (bf16[16,1536]{1,0:T(8,128)(2,1)S(1)}, bf16[16,1536]{1,0:T(8,128)(2,1)S(1)}, u32[]{:S(2)}, u32[]{:S(2)}) collective-permute-start(bf16[16,1536]{1,0:T(8,128)(2,1)S(1)} %get-tuple-element.53), channel_id=1, source_target_pairs={{0,1},{1,0},{2,3},{3,2},{4,5},{5,4},{6,7},{7,6},{8,9},{9,8},{10,11... | collective-permute-start | bytes 147464 | tf_op jit(solution)/shard_map/ppermute | solution.py:27
  10.4 1.9 %layer_norm.1 = (bf16[512,1536]{1,0:T(8,128)(2,1)S(1)}, bf16[64,1536]{1,0:T(8,128)(2,1)S(1)}, bf16[128,1536]{1,0:T(8,128)(2,1)S(1)}) custom-call(bf16[512,1536]{1,0:T(8,128)(2,1)S(1)} %bitcast.7, f32[1,1536]{1,0:T(1,128)S(1)} %broadcast_in_dim.14.gain_ref, bf16[192,1536]{1,0:T(8,128)(2,1)S(1)} %copy-done.4), custom_call_target="tpu_custom_call" | custom-call | flops 100000000 | tf_op jit(solution)/shard_map/layer_norm/pallas_call | solution.py:100
  12.4 1.6 %collective-permute-start.9 = (bf16[384,512]{1,0:T(8,128)(2,1)S(1)}, bf16[384,512]{1,0:T(8,128)(2,1)S(1)}, u32[]{:S(2)}, u32[]{:S(2)}) collective-permute-start(bf16[384,512]{1,0:T(8,128)(2,1)S(1)} %get-tuple-element.68), channel_id=1, source_target_pairs={{0,16},{8,24},{16,0},{24,8},{1,17},{9,25},{17,1},{25,9},{2,18},{10... | collective-permute-start | bytes 1179656 | tf_op jit(solution)/shard_map/ppermute | solution.py:27
  14.0 1.6 %collective-permute-done.3.refs_1_ = bf16[384,256]{1,0:T(8,128)(2,1)S(1)} collective-permute-done((bf16[384,256]{1,0:T(8,128)(2,1)S(1)}, bf16[384,256]{1,0:T(8,128)(2,1)S(1)}, u32[]{:S(2)}, u32[]{:S(2)}) %collective-permute-start.3) | collective-permute-done | bytes 196640 | tf_op jit(solution)/shard_map/ppermute | solution.py:27
  15.6 2.7 %collective-permute-start.5 = (bf16[384,256]{1,0:T(8,128)(2,1)S(1)}, bf16[384,256]{1,0:T(8,128)(2,1)S(1)}, u32[]{:S(2)}, u32[]{:S(2)}) collective-permute-start(bf16[384,256]{1,0:T(8,128)(2,1)S(1)} %collective-permute-done.2.refs_1_), channel_id=1, source_target_pairs={{0,1},{1,0},{2,3},{3,2},{4,5},{5,4},{6,7},{7,6},{8,9},{9,8},{10,11... | collective-permute-start | bytes 589832 | tf_op jit(solution)/shard_map/ppermute | solution.py:27
  18.3 1.6 %collective-permute-start.7 = (bf16[384,256]{1,0:T(8,128)(2,1)S(1)}, bf16[384,256]{1,0:T(8,128)(2,1)S(1)}, u32[]{:S(2)}, u32[]{:S(2)}) collective-permute-start(bf16[384,256]{1,0:T(8,128)(2,1)S(1)} %collective-permute-done.3.refs_1_), channel_id=1, source_target_pairs={{0,2},{1,3},{2,0},{3,1},{4,6},{5,7},{6,4},{7,5},{8,10},{9,11},{10,... | collective-permute-start | bytes 589832 | tf_op jit(solution)/shard_map/ppermute | solution.py:27
  19.9 2.3 %near.1 = (bf16[544,1536]{1,0:T(8,128)(2,1)S(1)}, f32[544,512]{1,0:T(8,128)S(1)}, f32[544,512]{1,0:T(8,128)S(1)}, f32[544,512]{1,0:T(8,128)S(1)}) custom-call(s32[5]{0:T(128)S(1)} %stack.37.place_ref, bf16[512,1536]{1,0:T(8,128)(2,1)S(1)} %get-tuple-element.57.rows_ref, bf16[16,1536]{1,0:T(8,128)(2,1)S(1)} %collective-permute-done.inner_ref, ...), custom_call_target="tpu_custom_call" | custom-call | flops 100000000 | tf_op jit(solution)/shard_map/near/pallas_call | solution.py:148
  22.8 1.2 %collective-permute-done.7.refs_2_ = bf16[384,256]{1,0:T(8,128)(2,1)S(1)} collective-permute-done((bf16[384,256]{1,0:T(8,128)(2,1)S(1)}, bf16[384,256]{1,0:T(8,128)(2,1)S(1)}, u32[]{:S(2)}, u32[]{:S(2)}) %collective-permute-start.7) | collective-permute-done | bytes 196640 | tf_op jit(solution)/shard_map/ppermute | solution.py:27
  25.6 2.9 %front.3 = (f32[512,256]{1,0:T(8,128)S(1)}, f32[3,256]{1,0:T(4,128)S(1)}) custom-call(s32[5]{0:T(128)S(1)} %stack.37.place_ref, bf16[544,1536]{1,0:T(8,128)(2,1)S(1)} %get-tuple-element.60.normed_ref, f32[544,512]{1,0:T(8,128)S(1)} %get-tuple-element.69.refs_0_, bf16[384,256]{1,0:T(8,128)(2,1)S(1)} %collective-permute-done.2.refs_1_, ...), custom_call_target="tpu_custom_call" | custom-call | flops 100000000 | tf_op jit(solution)/shard_map/front/pallas_call | solution.py:233
  28.5 2.9 %front.4 = (f32[512,256]{1,0:T(8,128)S(1)}, f32[3,256]{1,0:T(4,128)S(1)}) custom-call(s32[5]{0:T(128)S(1)} %stack.37.place_ref, bf16[544,1536]{1,0:T(8,128)(2,1)S(1)} %get-tuple-element.60.normed_ref, f32[544,512]{1,0:T(8,128)S(1)} %get-tuple-element.76.refs_0_, bf16[384,256]{1,0:T(8,128)(2,1)S(1)} %collective-permute-done.3.refs_1_, ...), custom_call_target="tpu_custom_call" | custom-call | flops 4000000000 | tf_op jit(solution)/shard_map/front/pallas_call | solution.py:233
  31.4 2.9 %front.5 = (f32[512,256]{1,0:T(8,128)S(1)}, f32[1,3,768]{2,1,0:T(4,128)S(1)}) custom-call(s32[5]{0:T(128)S(1)} %stack.37.place_ref, bf16[544,1536]{1,0:T(8,128)(2,1)S(1)} %get-tuple-element.60.normed_ref, f32[3,256]{1,0:T(4,128)S(1)} %get-tuple-element.73.refs_0_, f32[3,256]{1,0:T(4,128)S(1)} %get-tuple-element.80.refs_1_, ...), custom_call_target="tpu_custom_call" | custom-call | flops 100000000 | tf_op jit(solution)/shard_map/front/pallas_call | solution.py:233
  35.6 2.2 %collective-permute-start.15 = (f32[1,3,768]{2,1,0:T(4,128)S(1)}, f32[1,3,768]{2,1,0:T(4,128)S(1)}, u32[]{:S(2)}, u32[]{:S(2)}) collective-permute-start(f32[1,3,768]{2,1,0:T(4,128)S(1)} %pad_maximum_fusion), channel_id=1, source_target_pairs={{0,2},{1,3},{2,0},{3,1},{4,6},{5,7},{6,4},{7,5},{8,10},{9,11},{10,... | collective-permute-start | bytes 27656 | tf_op jit(solution)/shard_map/ppermute | solution.py:410
  38.3 1.2 %collective-permute-done.15 = f32[1,3,768]{2,1,0:T(4,128)S(1)} collective-permute-done((f32[1,3,768]{2,1,0:T(4,128)S(1)}, f32[1,3,768]{2,1,0:T(4,128)S(1)}, u32[]{:S(2)}, u32[]{:S(2)}) %collective-permute-start.15) | collective-permute-done | bytes 9248 | tf_op jit(solution)/shard_map/ppermute | solution.py:410
  39.5 3.1 %collective-permute-start.16 = (f32[1,3,768]{2,1,0:T(4,128)S(1)}, f32[1,3,768]{2,1,0:T(4,128)S(1)}, u32[]{:S(2)}, u32[]{:S(2)}) collective-permute-start(f32[1,3,768]{2,1,0:T(4,128)S(1)} %pad_maximum_fusion.1), channel_id=1, source_target_pairs={{0,4},{1,5},{2,6},{3,7},{4,0},{5,1},{6,2},{7,3},{8,12},{9,13},{10,... | collective-permute-start | bytes 27656 | tf_op jit(solution)/shard_map/ppermute | solution.py:410
  42.6 1.7 %collective-permute-done.16 = f32[1,3,768]{2,1,0:T(4,128)S(1)} collective-permute-done((f32[1,3,768]{2,1,0:T(4,128)S(1)}, f32[1,3,768]{2,1,0:T(4,128)S(1)}, u32[]{:S(2)}, u32[]{:S(2)}) %collective-permute-start.16) | collective-permute-done | bytes 9248 | tf_op jit(solution)/shard_map/ppermute | solution.py:410
  44.3 2.9 %collective-permute-start.17 = (f32[1,3,768]{2,1,0:T(4,128)S(1)}, f32[1,3,768]{2,1,0:T(4,128)S(1)}, u32[]{:S(2)}, u32[]{:S(2)}) collective-permute-start(f32[1,3,768]{2,1,0:T(4,128)S(1)} %pad_maximum_fusion.2.refs_0_), channel_id=1, source_target_pairs={{0,1},{1,0},{2,3},{3,2},{4,5},{5,4},{6,7},{7,6},{8,9},{9,8},{10,11... | collective-permute-start | bytes 27656 | tf_op jit(solution)/shard_map/ppermute | solution.py:410
  47.8 1.0 %collective-permute-start.19 = (f32[1,3,768]{2,1,0:T(4,128)S(1)}, f32[1,3,768]{2,1,0:T(4,128)S(1)}, u32[]{:S(2)}, u32[]{:S(2)}) collective-permute-start(f32[1,3,768]{2,1,0:T(4,128)S(1)} %pad_maximum_fusion.2.refs_0_), channel_id=1, source_target_pairs={{0,17},{1,16},{2,19},{3,18},{4,21},{5,20},{6,23},{7,22},{8,25},{9,... | collective-permute-start | bytes 27656 | tf_op jit(solution)/shard_map/ppermute | solution.py:410
  49.0 1.9 %collective-permute-done.18.refs_2_ = f32[1,3,768]{2,1,0:T(4,128)S(1)} collective-permute-done((f32[1,3,768]{2,1,0:T(4,128)S(1)}, f32[1,3,768]{2,1,0:T(4,128)S(1)}, u32[]{:S(2)}, u32[]{:S(2)}) %collective-permute-start.18) | collective-permute-done | bytes 9248 | tf_op jit(solution)/shard_map/ppermute | solution.py:410
  50.9 1.4 %collective-permute-done.19.refs_3_ = f32[1,3,768]{2,1,0:T(4,128)S(1)} collective-permute-done((f32[1,3,768]{2,1,0:T(4,128)S(1)}, f32[1,3,768]{2,1,0:T(4,128)S(1)}, u32[]{:S(2)}, u32[]{:S(2)}) %collective-permute-start.19) | collective-permute-done | bytes 9248 | tf_op jit(solution)/shard_map/ppermute | solution.py:410
  52.9 1.5 %collective-permute-done.22.refs_11_ = bf16[64,1536]{1,0:T(8,128)(2,1)S(1)} collective-permute-done((bf16[64,1536]{1,0:T(8,128)(2,1)S(1)}, bf16[64,1536]{1,0:T(8,128)(2,1)S(1)}, u32[]{:S(2)}, u32[]{:S(2)}) %collective-permute-start.22) | collective-permute-done | bytes 196640 | tf_op jit(solution)/shard_map/ppermute | solution.py:27
  54.4 2.9 %back.1 = bf16[512,1536]{1,0:T(8,128)(2,1)} custom-call(s32[5]{0:T(128)S(1)} %stack.37.place_ref, f32[1,768]{1,0:T(1,128)S(1)} %broadcast_in_dim.12.gain_ref, f32[1,768]{1,0:T(1,128)S(1)} %broadcast_in_dim.13.shift_ref, f32[1,3,768]{2,1,0:T(4,128)S(1)} %pad_maximum_fusion.2.refs_0_, f32[1,3,768]{2,1,0:T(4,128)S(1)} %collective-permute-done.17.refs_1_, ...), custom_call_target="tpu_custom_call" | custom-call | flops 1000000000 | tf_op jit(solution)/shard_map/back/pallas_call | solution.py:331
  (60 shorter events, 7.8 us)
Async XLA Ops:
  0.0 19.9 %collective-permute-start.4 = (bf16[384,1536]{1,0:T(8,128)(2,1)}, bf16[384,1536]{1,0:T(8,128)(2,1)S(1)}, u32[]{:S(2)}, u32[]{:S(2)}) collective-permute-start(bf16[384,1536]{1,0:T(8,128)(2,1)} %refs_0_.1), channel_id=1, source_target_pairs={{0,8},{8,0},{16,24},{24,16},{1,9},{9,1},{17,25},{25,17},{2,10},{10... | collective-permute-start | bytes 3538952 | tf_op jit(solution)/shard_map/ppermute | solution.py:27
  3.1 10.9 %collective-permute-start.2 = (bf16[384,256]{1,0:T(8,128)(2,1)S(1)}, bf16[384,256]{1,0:T(8,128)(2,1)S(1)}, u32[]{:S(2)}, u32[]{:S(2)}) collective-permute-start(bf16[384,256]{1,0:T(8,128)(2,1)S(1)} %get-tuple-element.55), channel_id=1, source_target_pairs={{0,16},{8,24},{16,0},{24,8},{1,17},{9,25},{17,1},{25,9},{2,18},{10... | collective-permute-start | bytes 589832 | tf_op jit(solution)/shard_map/ppermute | solution.py:27
  5.6 10.0 %collective-permute-start.3 = (bf16[384,256]{1,0:T(8,128)(2,1)S(1)}, bf16[384,256]{1,0:T(8,128)(2,1)S(1)}, u32[]{:S(2)}, u32[]{:S(2)}) collective-permute-start(bf16[384,256]{1,0:T(8,128)(2,1)S(1)} %get-tuple-element.56), channel_id=1, source_target_pairs={{0,16},{8,24},{16,0},{24,8},{1,17},{9,25},{17,1},{25,9},{2,18},{10... | collective-permute-start | bytes 589832 | tf_op jit(solution)/shard_map/ppermute | solution.py:27
  7.7 4.7 %collective-permute-start = (bf16[16,1536]{1,0:T(8,128)(2,1)S(1)}, bf16[16,1536]{1,0:T(8,128)(2,1)S(1)}, u32[]{:S(2)}, u32[]{:S(2)}) collective-permute-start(bf16[16,1536]{1,0:T(8,128)(2,1)S(1)} %get-tuple-element.53), channel_id=1, source_target_pairs={{0,1},{1,0},{2,3},{3,2},{4,5},{5,4},{6,7},{7,6},{8,9},{9,8},{10,11... | collective-permute-start | bytes 147464 | tf_op jit(solution)/shard_map/ppermute | solution.py:27
  9.7 4.2 %collective-permute-start.1 = (bf16[16,1536]{1,0:T(8,128)(2,1)S(1)}, bf16[16,1536]{1,0:T(8,128)(2,1)S(1)}, u32[]{:S(2)}, u32[]{:S(2)}) collective-permute-start(bf16[16,1536]{1,0:T(8,128)(2,1)S(1)} %get-tuple-element.54), channel_id=1, source_target_pairs={{1,2},{3,4},{5,6},{2,1},{4,3},{6,5},{9,10},{11,12},{13,14},{10,9},... | collective-permute-start | bytes 147464 | tf_op jit(solution)/shard_map/ppermute | solution.py:384
  12.4 12.2 %collective-permute-start.9 = (bf16[384,512]{1,0:T(8,128)(2,1)S(1)}, bf16[384,512]{1,0:T(8,128)(2,1)S(1)}, u32[]{:S(2)}, u32[]{:S(2)}) collective-permute-start(bf16[384,512]{1,0:T(8,128)(2,1)S(1)} %get-tuple-element.68), channel_id=1, source_target_pairs={{0,16},{8,24},{16,0},{24,8},{1,17},{9,25},{17,1},{25,9},{2,18},{10... | collective-permute-start | bytes 1179656 | tf_op jit(solution)/shard_map/ppermute | solution.py:27
  15.6 7.2 %collective-permute-start.5 = (bf16[384,256]{1,0:T(8,128)(2,1)S(1)}, bf16[384,256]{1,0:T(8,128)(2,1)S(1)}, u32[]{:S(2)}, u32[]{:S(2)}) collective-permute-start(bf16[384,256]{1,0:T(8,128)(2,1)S(1)} %collective-permute-done.2.refs_1_), channel_id=1, source_target_pairs={{0,1},{1,0},{2,3},{3,2},{4,5},{5,4},{6,7},{7,6},{8,9},{9,8},{10,11... | collective-permute-start | bytes 589832 | tf_op jit(solution)/shard_map/ppermute | solution.py:27
  18.3 5.7 %collective-permute-start.7 = (bf16[384,256]{1,0:T(8,128)(2,1)S(1)}, bf16[384,256]{1,0:T(8,128)(2,1)S(1)}, u32[]{:S(2)}, u32[]{:S(2)}) collective-permute-start(bf16[384,256]{1,0:T(8,128)(2,1)S(1)} %collective-permute-done.3.refs_1_), channel_id=1, source_target_pairs={{0,2},{1,3},{2,0},{3,1},{4,6},{5,7},{6,4},{7,5},{8,10},{9,11},{10,... | collective-permute-start | bytes 589832 | tf_op jit(solution)/shard_map/ppermute | solution.py:27
  22.2 1.7 %collective-permute-start.6 = (bf16[384,256]{1,0:T(8,128)(2,1)S(1)}, bf16[384,256]{1,0:T(8,128)(2,1)S(1)}, u32[]{:S(2)}, u32[]{:S(2)}) collective-permute-start(bf16[384,256]{1,0:T(8,128)(2,1)S(1)} %collective-permute-done.2.refs_1_), channel_id=1, source_target_pairs={{0,8},{8,0},{16,24},{24,16},{1,9},{9,1},{17,25},{25,17},{2,10},{10... | collective-permute-start | bytes 589832 | tf_op jit(solution)/shard_map/ppermute | solution.py:27
  22.3 1.7 %collective-permute-start.8 = (bf16[384,256]{1,0:T(8,128)(2,1)S(1)}, bf16[384,256]{1,0:T(8,128)(2,1)S(1)}, u32[]{:S(2)}, u32[]{:S(2)}) collective-permute-start(bf16[384,256]{1,0:T(8,128)(2,1)S(1)} %collective-permute-done.3.refs_1_), channel_id=1, source_target_pairs={{0,8},{8,0},{16,24},{24,16},{1,9},{9,1},{17,25},{25,17},{2,10},{10... | collective-permute-start | bytes 589832 | tf_op jit(solution)/shard_map/ppermute | solution.py:27
  24.0 1.6 %collective-permute-start.10 = (bf16[384,256]{1,0:T(8,128)(2,1)S(1)}, bf16[384,256]{1,0:T(8,128)(2,1)S(1)}, u32[]{:S(2)}, u32[]{:S(2)}) collective-permute-start(bf16[384,256]{1,0:T(8,128)(2,1)S(1)} %collective-permute-done.5.refs_2_), channel_id=1, source_target_pairs={{0,8},{8,0},{16,24},{24,16},{1,9},{9,1},{17,25},{25,17},{2,10},{10... | collective-permute-start | bytes 589832 | tf_op jit(solution)/shard_map/ppermute | solution.py:27
  24.3 4.2 %collective-permute-start.11 = (bf16[384,256]{1,0:T(8,128)(2,1)S(1)}, bf16[384,256]{1,0:T(8,128)(2,1)S(1)}, u32[]{:S(2)}, u32[]{:S(2)}) collective-permute-start(bf16[384,256]{1,0:T(8,128)(2,1)S(1)} %collective-permute-done.7.refs_2_), channel_id=1, source_target_pairs={{0,8},{8,0},{16,24},{24,16},{1,9},{9,1},{17,25},{25,17},{2,10},{10... | collective-permute-start | bytes 589832 | tf_op jit(solution)/shard_map/ppermute | solution.py:27
  24.6 6.8 %collective-permute-start.12 = (bf16[384,512]{1,0:T(8,128)(2,1)S(1)}, bf16[384,512]{1,0:T(8,128)(2,1)S(1)}, u32[]{:S(2)}, u32[]{:S(2)}) collective-permute-start(bf16[384,512]{1,0:T(8,128)(2,1)S(1)} %collective-permute-done.9.refs_3_), channel_id=1, source_target_pairs={{0,8},{8,0},{16,24},{24,16},{1,9},{9,1},{17,25},{25,17},{2,10},{10... | collective-permute-start | bytes 1179656 | tf_op jit(solution)/shard_map/ppermute | solution.py:27
  24.8 9.5 %collective-permute-start.13 = (bf16[64,1536]{1,0:T(8,128)(2,1)S(1)}, bf16[64,1536]{1,0:T(8,128)(2,1)S(1)}, u32[]{:S(2)}, u32[]{:S(2)}) collective-permute-start(bf16[64,1536]{1,0:T(8,128)(2,1)S(1)} %get-tuple-element.86), channel_id=1, source_target_pairs={{0,16},{8,24},{16,0},{24,8},{1,17},{9,25},{17,1},{25,9},{2,18},{10... | collective-permute-start | bytes 589832 | tf_op jit(solution)/shard_map/ppermute | solution.py:27
  34.3 1.2 %collective-permute-start.14 = (f32[1,3,768]{2,1,0:T(4,128)S(1)}, f32[1,3,768]{2,1,0:T(4,128)S(1)}, u32[]{:S(2)}, u32[]{:S(2)}) collective-permute-start(f32[1,3,768]{2,1,0:T(4,128)S(1)} %get-tuple-element.87), channel_id=1, source_target_pairs={{0,8},{1,9},{2,10},{3,11},{4,12},{5,13},{6,14},{7,15},{8,0},{9,1},... | collective-permute-start | bytes 27656 | tf_op jit(solution)/shard_map/ppermute | solution.py:410
  35.6 3.9 %collective-permute-start.15 = (f32[1,3,768]{2,1,0:T(4,128)S(1)}, f32[1,3,768]{2,1,0:T(4,128)S(1)}, u32[]{:S(2)}, u32[]{:S(2)}) collective-permute-start(f32[1,3,768]{2,1,0:T(4,128)S(1)} %pad_maximum_fusion), channel_id=1, source_target_pairs={{0,2},{1,3},{2,0},{3,1},{4,6},{5,7},{6,4},{7,5},{8,10},{9,11},{10,... | collective-permute-start | bytes 27656 | tf_op jit(solution)/shard_map/ppermute | solution.py:410
  37.8 11.2 %collective-permute-start.20 = (bf16[128,1536]{1,0:T(8,128)(2,1)S(1)}, bf16[128,1536]{1,0:T(8,128)(2,1)S(1)}, u32[]{:S(2)}, u32[]{:S(2)}) collective-permute-start(bf16[128,1536]{1,0:T(8,128)(2,1)S(1)} %get-tuple-element.88), channel_id=1, source_target_pairs={{0,16},{8,24},{16,0},{24,8},{1,17},{9,25},{17,1},{25,9},{2,18},{10... | collective-permute-start | bytes 1179656 | tf_op jit(solution)/shard_map/ppermute | solution.py:27
  39.5 4.8 %collective-permute-start.16 = (f32[1,3,768]{2,1,0:T(4,128)S(1)}, f32[1,3,768]{2,1,0:T(4,128)S(1)}, u32[]{:S(2)}, u32[]{:S(2)}) collective-permute-start(f32[1,3,768]{2,1,0:T(4,128)S(1)} %pad_maximum_fusion.1), channel_id=1, source_target_pairs={{0,4},{1,5},{2,6},{3,7},{4,0},{5,1},{6,2},{7,3},{8,12},{9,13},{10,... | collective-permute-start | bytes 27656 | tf_op jit(solution)/shard_map/ppermute | solution.py:410
  42.6 11.8 %collective-permute-start.21 = (bf16[192,1536]{1,0:T(8,128)(2,1)S(1)}, bf16[192,1536]{1,0:T(8,128)(2,1)S(1)}, u32[]{:S(2)}, u32[]{:S(2)}) collective-permute-start(bf16[192,1536]{1,0:T(8,128)(2,1)S(1)} %copy-done.4), channel_id=1, source_target_pairs={{0,8},{8,0},{16,24},{24,16},{1,9},{9,1},{17,25},{25,17},{2,10},{10... | collective-permute-start | bytes 1769480 | tf_op jit(solution)/shard_map/ppermute | solution.py:27
  44.3 4.7 %collective-permute-start.17 = (f32[1,3,768]{2,1,0:T(4,128)S(1)}, f32[1,3,768]{2,1,0:T(4,128)S(1)}, u32[]{:S(2)}, u32[]{:S(2)}) collective-permute-start(f32[1,3,768]{2,1,0:T(4,128)S(1)} %pad_maximum_fusion.2.refs_0_), channel_id=1, source_target_pairs={{0,1},{1,0},{2,3},{3,2},{4,5},{5,4},{6,7},{7,6},{8,9},{9,8},{10,11... | collective-permute-start | bytes 27656 | tf_op jit(solution)/shard_map/ppermute | solution.py:410
  47.2 3.7 %collective-permute-start.18 = (f32[1,3,768]{2,1,0:T(4,128)S(1)}, f32[1,3,768]{2,1,0:T(4,128)S(1)}, u32[]{:S(2)}, u32[]{:S(2)}) collective-permute-start(f32[1,3,768]{2,1,0:T(4,128)S(1)} %pad_maximum_fusion.2.refs_0_), channel_id=1, source_target_pairs={{0,16},{1,17},{2,18},{3,19},{4,20},{5,21},{6,22},{7,23},{8,24},{9,... | collective-permute-start | bytes 27656 | tf_op jit(solution)/shard_map/ppermute | solution.py:410
  47.8 4.6 %collective-permute-start.19 = (f32[1,3,768]{2,1,0:T(4,128)S(1)}, f32[1,3,768]{2,1,0:T(4,128)S(1)}, u32[]{:S(2)}, u32[]{:S(2)}) collective-permute-start(f32[1,3,768]{2,1,0:T(4,128)S(1)} %pad_maximum_fusion.2.refs_0_), channel_id=1, source_target_pairs={{0,17},{1,16},{2,19},{3,18},{4,21},{5,20},{6,23},{7,22},{8,25},{9,... | collective-permute-start | bytes 27656 | tf_op jit(solution)/shard_map/ppermute | solution.py:410
  52.4 2.0 %collective-permute-start.23 = (bf16[128,1536]{1,0:T(8,128)(2,1)S(1)}, bf16[128,1536]{1,0:T(8,128)(2,1)S(1)}, u32[]{:S(2)}, u32[]{:S(2)}) collective-permute-start(bf16[128,1536]{1,0:T(8,128)(2,1)S(1)} %collective-permute-done.20.refs_10_), channel_id=1, source_target_pairs={{0,8},{8,0},{16,24},{24,16},{1,9},{9,1},{17,25},{25,17},{2,10},{10... | collective-permute-start | bytes 1179656 | tf_op jit(solution)/shard_map/ppermute | solution.py:27
  52.4 2.0 %collective-permute-start.22 = (bf16[64,1536]{1,0:T(8,128)(2,1)S(1)}, bf16[64,1536]{1,0:T(8,128)(2,1)S(1)}, u32[]{:S(2)}, u32[]{:S(2)}) collective-permute-start(bf16[64,1536]{1,0:T(8,128)(2,1)S(1)} %collective-permute-done.13.refs_9_), channel_id=1, source_target_pairs={{0,8},{8,0},{16,24},{24,16},{1,9},{9,1},{17,25},{25,17},{2,10},{10... | collective-permute-start | bytes 589832 | tf_op jit(solution)/shard_map/ppermute | solution.py:27
  (9 other events, 87.1 us)
